TPU v7x, 512 devices: a whole 4x4x16 slice. The times are simulated.
512 devices in a mesh: space: 128 (over y, z, core), pipe: 4 (over x).
Axes of the slice: x: 4, y: 4, z: 16, core: 2. Of those that a mesh axis runs over, the one named last changes fastest.
Arguments:
- section_input: bfloat16 [4, 128, 96, 512], P('pipe', 'space'), may hold values from -6 to 6
- top_grad: bfloat16 [128, 96, 512], P('space'), may hold values from -6 to 6
- conv_weight: bfloat16 [4, 27, 96, 96], P('pipe'), may hold values from -0.125 to 0.125
- brick_height: int32 [128], P('space'), may hold values from 0 to 4, as said below
Outputs:
- section_grads: bfloat16 [4, 128, 96, 512], P('pipe', 'space')
- weight_grad: float32 [4, 27, 96, 96], P('pipe')
Inputs may be any that keep to these rules, and one draw needn't show every extreme that they name: `brick_height`: columns next to each other along the first or along the second dimension differ in level by at most one; the lowest level is 0 and the highest is 4.
All inputs are finite; a program needn't handle non-finite values.
Results may differ from a plain program's by a relative error of at most 0.007.
Values may be sent and summed in bfloat16 or wider, within the bound.
No kernel may reach another device: no remote copies, remote signals or barrier semaphores. Data moves between devices by JAX's collectives and lax.ppermute only.
A program may use at most 64 MiB of HBM per device.

v0:
```python
import jax
import jax.numpy as jnp
from jax import lax
from jax.sharding import PartitionSpec as P

BE = 8
GRID_W = 8
FX = 1
FY = 1


def shifted(value, axis, steps):
    count = lax.axis_size(axis)
    leading, last = (max(0, -steps), min(count, count - steps))
    return lax.ppermute(value, axis, [(source, source + steps) for source in range(leading, last)])


def edge_index(side):
    return BE - 1 if side > 0 else 0


def take_layer(block, axis, side):
    start = edge_index(side)
    return lax.slice_in_dim(block, start, start + 1, axis=axis)


def put_layer(layer, axis, side):
    start = edge_index(side)
    widths = [(0, 0)] * layer.ndim
    widths[axis] = (start, BE - 1 - start)
    return jnp.pad(layer, widths)


def send_range(side, count):
    if side > 0:
        return (count - 1, count)
    if side < 0:
        return (0, 1)
    return (0, count)


def fill_range(side, count):
    if side > 0:
        return (0, 1)
    if side < 0:
        return (count + 1, count + 2)
    return (1, count + 1)


def frame(grid, heights):
    nx, ny = (grid.shape[0], grid.shape[1])
    ext = (
        jnp.zeros((nx + 2, ny + 2) + grid.shape[2:], grid.dtype)
        .at[1 : nx + 1, 1 : ny + 1]
        .set(grid)
    )
    if heights is None:
        return (ext, None)
    levels = jnp.zeros((nx + 2, ny + 2), jnp.int32).at[1 : nx + 1, 1 : ny + 1].set(heights)
    return (ext, levels)


def direct_halo(grid, heights, mover):
    nx, ny = (grid.shape[0], grid.shape[1])
    ext, levels = frame(grid, heights)
    for ex in (-1, 0, 1):
        for ey in (-1, 0, 1):
            if ex == 0 and ey == 0:
                continue
            low_x, high_x = send_range(ex, nx)
            low_y, high_y = send_range(ey, ny)
            axis = 3 if ex != 0 else 4
            side = ex if ex != 0 else ey
            layer = take_layer(grid, axis, side)
            sent_levels = None if heights is None else heights
            flat = layer.reshape(high_x - low_x, high_y - low_y, -1)
            got, got_levels = mover(flat, sent_levels, ex * GRID_W + ey)
            first_x, last_x = fill_range(ex, nx)
            first_y, last_y = fill_range(ey, ny)
            ext = ext.at[first_x:last_x, first_y:last_y].set(
                put_layer(got.reshape(layer.shape), axis, side)
            )
            if heights is not None:
                levels = levels.at[first_x:last_x, first_y:last_y].set(got_levels)
    return (ext, levels)


def move_input_direct(layers, levels, by):
    return shifted((layers, levels), "space", by)


def move_grad_direct(layers, levels, by):
    return (shifted(layers, "space", by), None)


def input_halo(grid, heights):
    result = direct_halo(grid, heights, move_input_direct)
    return result


def grad_halo(grid):
    result = direct_halo(grid, None, move_grad_direct)
    return result


def pad_bricks(ext, levels, inside):
    nx, ny = (ext.shape[0] - 2, ext.shape[1] - 2)
    base = levels[1 : nx + 1, 1 : ny + 1]
    planes = []
    for dx in (-1, 0, 1):
        lines = []
        for dy in (-1, 0, 1):
            near = ext[1 + dx : 1 + dx + nx, 1 + dy : 1 + dy + ny]
            rise = levels[1 + dx : 1 + dx + nx, 1 + dy : 1 + dy + ny] - base
            valid = inside[1 + dx : 1 + dx + nx, 1 + dy : 1 + dy + ny]
            if dx != 0:
                near = take_layer(near, 3, -dx)
            if dy != 0:
                near = take_layer(near, 4, -dy)
            stacks = []
            for dz in (-1, 0, 1):
                keep = (valid & (rise == dz)).astype(near.dtype)[:, :, None, None, None, None]
                piece = near if dz == 0 else take_layer(near, 5, -dz)
                stacks.append(piece * keep)
            lines.append(jnp.concatenate(stacks, 5))
        planes.append(jnp.concatenate(lines, 4))
    whole = jnp.concatenate(planes, 3)
    return whole.reshape((nx * ny,) + whole.shape[2:])


def gather_cols(padded, group, sign):
    count, channels = (padded.shape[0], padded.shape[1])
    offset_x = group - 1
    pieces = []
    for offset_y in (-1, 0, 1):
        for offset_z in (-1, 0, 1):
            start_x = 1 + sign * offset_x
            start_y = 1 + sign * offset_y
            start_z = 1 + sign * offset_z
            piece = padded[
                :, :, start_x : start_x + BE, start_y : start_y + BE, start_z : start_z + BE
            ]
            pieces.append(piece.reshape(count, channels, BE**3))
    return jnp.concatenate(pieces, 1)


def apply_conv(padded, weight, sign):
    total = None
    for group in range(3):
        cols = gather_cols(padded, group, sign)
        block = weight[9 * group : 9 * group + 9].reshape(-1, weight.shape[2])
        part = jnp.einsum("bkp,kd->bdp", cols, block, preferred_element_type=jnp.float32)
        total = part if total is None else total + part
    return total


def weight_terms(padded, grad_pre):
    blocks = []
    for group in range(3):
        cols = gather_cols(padded, group, 1)
        blocks.append(jnp.einsum("bkp,bdp->kd", cols, grad_pre, preferred_element_type=jnp.float32))
    channels = grad_pre.shape[1]
    return jnp.concatenate(blocks, 0).reshape(27, channels, channels)


def body(section_input, top_grad, conv_weight, brick_height):
    channels = section_input.shape[2]
    devices = lax.axis_size("space")
    position = lax.axis_index("space")
    row_pos = position // GRID_W
    col_pos = position % GRID_W
    column_x = row_pos * FX - 1 + jnp.arange(FX + 2)
    column_y = col_pos * FY - 1 + jnp.arange(FY + 2)
    inside_x = (column_x >= 0) & (column_x < FX * (devices // GRID_W))
    inside_y = (column_y >= 0) & (column_y < FY * GRID_W)
    inside = inside_x[:, None] & inside_y[None, :]
    shape = (FX, FY, channels, BE, BE, BE)
    ext_x, levels = input_halo(section_input[0].reshape(shape), brick_height.reshape(FX, FY))
    padded_x = pad_bricks(ext_x, levels, inside)
    weight = conv_weight[0]
    flipped = jnp.swapaxes(weight, 1, 2)
    pre = apply_conv(padded_x, weight, 1)
    sigma = jax.nn.sigmoid(pre)
    slope = sigma * (1.0 + pre * (1.0 - sigma))
    section = lax.axis_index("pipe")
    sections = lax.axis_size("pipe")
    incoming = top_grad
    kept_pre = jnp.zeros(top_grad.shape, jnp.bfloat16)
    kept_out = jnp.zeros(top_grad.shape, jnp.bfloat16)
    for step in range(sections):
        grad_pre = (incoming.astype(jnp.float32) * slope).astype(jnp.bfloat16)
        ext_g, unused = grad_halo(grad_pre.reshape(shape))
        padded_g = pad_bricks(ext_g, levels, inside)
        result = (incoming.astype(jnp.float32) + apply_conv(padded_g, flipped, -1)).astype(
            jnp.bfloat16
        )
        active = section == sections - 1 - step
        kept_pre = jnp.where(active, grad_pre, kept_pre)
        kept_out = jnp.where(active, result, kept_out)
        if step + 1 < sections:
            incoming = shifted(result, "pipe", -1)
    terms = weight_terms(padded_x, kept_pre)
    total = lax.psum(terms, "space")
    scale = lax.rsqrt(jnp.mean(total * total) + 1e-06)
    return (kept_out[None], (total * scale)[None])


def solution(mesh):
    return jax.shard_map(
        body,
        mesh=mesh,
        in_specs=(
            P("pipe", "space", None, None),
            P("space", None, None),
            P("pipe", None, None, None),
            P("space"),
        ),
        out_specs=(P("pipe", "space", None, None), P("pipe", None, None, None)),
        check_vma=False,
    )
```

profile of v0, /device:TPU:1, one launch (start us, length us, event | category | flops | bytes accessed | tf_op | source)
XLA Modules:
  0.0 928.4 jit_solution(204441999035959480)
XLA Ops:
  11.1 8.8 collective-permute-start.5
  19.9 1.9 collective-permute-start.6
  31.0 10.0 %collective-permute-start.7 = (s32[1,1]{1,0:T(1,128)}, s32[1,1]{1,0:T(1,128)}, u32[]{:S(2)}, u32[]{:S(2)}) collective-permute-start(s32[1,1]{1,0:T(1,128)} %bitcast.1), channel_id=1, source_target_pairs={{0,28},{4,32},{8,36},{12,40},{16,44},{20,48},{24,52},{28,56},{32,6... | collective-permute-start | bytes 20 | tf_op jit(solution)/shard_map/ppermute | solution.py:15
  41.8 7.6 collective-permute-start.8
  56.1 1.9 dynamic-slice.431
  58.0 10.8 %collective-permute-start.1 = (s32[1,1]{1,0:T(1,128)}, s32[1,1]{1,0:T(1,128)}, u32[]{:S(2)}, u32[]{:S(2)}) collective-permute-start(s32[1,1]{1,0:T(1,128)} %bitcast.1), channel_id=1, source_target_pairs={{0,36},{4,40},{8,44},{12,48},{16,52},{20,56},{24,60},{28,64},{32,6... | collective-permute-start | bytes 20 | tf_op jit(solution)/shard_map/ppermute | solution.py:15
  72.0 1.9 dynamic-slice.432
  73.9 7.4 collective-permute-start
  94.1 7.5 collective-permute-start.14
  118.0 6.3 collective-permute-start.15
  124.7 2.7 collective-permute-start.12
  127.4 2.9 collective-permute-start.13
  134.3 1.9 select_dynamic-update-slice_fusion.4
  146.7 2.3 fusion.41
  161.6 11.7 %collective-permute-start.22 = (bf16[1,1,6144]{2,1,0:T(2,128)(2,1)}, bf16[1,1,6144]{2,1,0:T(2,128)(2,1)}, u32[]{:S(2)}, u32[]{:S(2)}) collective-permute-start(bf16[1,1,6144]{2,1,0:T(2,128)(2,1)} %reshape.3356), channel_id=1, source_target_pairs={{0,28},{4,32},{8,36},{12,40},{16,44},{20,48},{24,52},{28,56},{32,6... | collective-permute-start | bytes 36872 | tf_op jit(solution)/shard_map/ppermute | solution.py:15
  173.3 8.5 collective-permute-start.23
  188.4 1.9 collective-permute-start.20
  190.3 3.6 collective-permute-start.21
  205.0 7.3 collective-permute-start.16
  229.7 3.4 select_dynamic-update-slice_fusion.3
  233.1 1.9 pad_dynamic-update-slice_fusion.18
  263.3 2.4 concatenate.392
  265.7 2.3 fusion.29
  268.0 2.4 concatenate.393
  270.4 2.3 convolution_add_fusion.7
  272.7 2.4 concatenate.394
  278.2 4.1 collective-permute-done.24
  295.5 3.7 collective-permute-start.29
  301.2 1.9 collective-permute-start.30
  305.7 10.1 %collective-permute-start.31 = (bf16[1,1,6144]{2,1,0:T(2,128)(2,1)}, bf16[1,1,6144]{2,1,0:T(2,128)(2,1)}, u32[]{:S(2)}, u32[]{:S(2)}) collective-permute-start(bf16[1,1,6144]{2,1,0:T(2,128)(2,1)} %reshape.3403), channel_id=1, source_target_pairs={{0,28},{4,32},{8,36},{12,40},{16,44},{20,48},{24,52},{28,56},{32,6... | collective-permute-start | bytes 36872 | tf_op jit(solution)/shard_map/ppermute | solution.py:15
  315.8 8.8 collective-permute-start.32
  324.6 2.2 scatter.200
  332.4 8.5 collective-permute-start.25
  358.3 3.4 select_dynamic-update-slice_fusion.2
  361.7 1.9 pad_dynamic-update-slice_fusion.12
  391.9 2.4 concatenate.408
  394.3 2.3 fusion.25
  396.6 2.4 concatenate.409
  399.0 2.3 convolution_add_fusion.5
  401.3 2.4 concatenate.410
  406.8 5.2 collective-permute-done.33
  425.2 2.5 collective-permute-start.38
  429.7 3.0 collective-permute-start.39
  435.3 9.5 %collective-permute-start.40 = (bf16[1,1,6144]{2,1,0:T(2,128)(2,1)}, bf16[1,1,6144]{2,1,0:T(2,128)(2,1)}, u32[]{:S(2)}, u32[]{:S(2)}) collective-permute-start(bf16[1,1,6144]{2,1,0:T(2,128)(2,1)} %reshape.3447), channel_id=1, source_target_pairs={{0,28},{4,32},{8,36},{12,40},{16,44},{20,48},{24,52},{28,56},{32,6... | collective-permute-start | bytes 36872 | tf_op jit(solution)/shard_map/ppermute | solution.py:15
  444.8 8.8 collective-permute-start.41
  453.6 2.2 scatter.214
  461.4 7.9 collective-permute-start.34
  486.6 3.4 select_dynamic-update-slice_fusion.1
  490.1 1.9 pad_dynamic-update-slice_fusion.6
  520.2 2.4 concatenate.424
  522.6 2.3 fusion.21
  524.9 2.4 concatenate.425
  527.3 2.3 convolution_add_fusion.3
  529.6 2.4 concatenate.426
  535.1 4.9 collective-permute-done.42
  549.1 10.6 %collective-permute-start.49 = (bf16[1,1,6144]{2,1,0:T(2,128)(2,1)S(1)}, bf16[1,1,6144]{2,1,0:T(2,128)(2,1)}, u32[]{:S(2)}, u32[]{:S(2)}) collective-permute-start(bf16[1,1,6144]{2,1,0:T(2,128)(2,1)S(1)} %reshape.3491), channel_id=1, source_target_pairs={{0,28},{4,32},{8,36},{12,40},{16,44},{20,48},{24,52},{28,56},{32,6... | collective-permute-start | bytes 36872 | tf_op jit(solution)/shard_map/ppermute | solution.py:15
  559.7 9.7 %collective-permute-start.50 = (bf16[1,1,6144]{2,1,0:T(2,128)(2,1)S(1)}, bf16[1,1,6144]{2,1,0:T(2,128)(2,1)}, u32[]{:S(2)}, u32[]{:S(2)}) collective-permute-start(bf16[1,1,6144]{2,1,0:T(2,128)(2,1)S(1)} %reshape.3491), channel_id=1, source_target_pairs={{0,32},{4,36},{8,40},{12,44},{16,48},{20,52},{24,56},{28,60},{32,6... | collective-permute-start | bytes 36872 | tf_op jit(solution)/shard_map/ppermute | solution.py:15
  570.2 2.1 collective-permute-start.47
  572.3 3.6 collective-permute-start.48
  581.9 6.9 collective-permute-start.43
  595.1 1.9 select_dynamic-update-slice_fusion
  608.0 2.0 fusion.14
  610.0 307.1 %all-reduce.43.cloned.1.call-done = f32[27,96,96]{2,1,0:T(8,128)} async-done(((f32[27,96,96]{2,1,0:T(8,128)}), f32[27,96,96]{2,1,0:T(8,128)}) %all-reduce.43.cloned.1.call-update) | async-done | bytes 995344 | tf_op jit(solution)/shard_map/psum | solution.py:203
  917.1 2.4 multiply_reduce_fusion
  (455 shorter events, 293.9 us)
Async XLA Ops:
  7.2 909.9 %all-reduce.43.cloned.1.call-start = ((), (), s32[]{:S(2)}) async-start(), calls=%async_computation | async-start | bytes 2654208 | tf_op jit(solution)/shard_map/psum | solution.py:203
  7.2 23.8 %collective-permute-start.2 = (s32[1,1]{1,0:T(1,128)}, s32[1,1]{1,0:T(1,128)}, u32[]{:S(2)}, u32[]{:S(2)}) collective-permute-start(s32[1,1]{1,0:T(1,128)} %bitcast.1), channel_id=1, source_target_pairs={{36,0},{40,4},{44,8},{48,12},{52,16},{56,20},{60,24},{64,28},{68,3... | collective-permute-start | bytes 20 | tf_op jit(solution)/shard_map/ppermute | solution.py:15
  8.5 33.3 %collective-permute-start.3 = (s32[1,1]{1,0:T(1,128)}, s32[1,1]{1,0:T(1,128)}, u32[]{:S(2)}, u32[]{:S(2)}) collective-permute-start(s32[1,1]{1,0:T(1,128)} %bitcast.1), channel_id=1, source_target_pairs={{32,0},{36,4},{40,8},{44,12},{48,16},{52,20},{56,24},{60,28},{64,3... | collective-permute-start | bytes 20 | tf_op jit(solution)/shard_map/ppermute | solution.py:15
  9.8 40.3 %collective-permute-start.4 = (s32[1,1]{1,0:T(1,128)}, s32[1,1]{1,0:T(1,128)}, u32[]{:S(2)}, u32[]{:S(2)}) collective-permute-start(s32[1,1]{1,0:T(1,128)} %bitcast.1), channel_id=1, source_target_pairs={{28,0},{32,4},{36,8},{40,12},{44,16},{48,20},{52,24},{56,28},{60,3... | collective-permute-start | bytes 20 | tf_op jit(solution)/shard_map/ppermute | solution.py:15
  11.1 41.0 %collective-permute-start.5 = (s32[1,1]{1,0:T(1,128)}, s32[1,1]{1,0:T(1,128)}, u32[]{:S(2)}, u32[]{:S(2)}) collective-permute-start(s32[1,1]{1,0:T(1,128)} %bitcast.1), channel_id=1, source_target_pairs={{4,0},{8,4},{12,8},{16,12},{20,16},{24,20},{28,24},{32,28},{36,32}... | collective-permute-start | bytes 20 | tf_op jit(solution)/shard_map/ppermute | solution.py:15
  19.9 34.2 %collective-permute-start.6 = (s32[1,1]{1,0:T(1,128)}, s32[1,1]{1,0:T(1,128)}, u32[]{:S(2)}, u32[]{:S(2)}) collective-permute-start(s32[1,1]{1,0:T(1,128)} %bitcast.1), channel_id=1, source_target_pairs={{0,4},{4,8},{8,12},{12,16},{16,20},{20,24},{24,28},{28,32},{32,36}... | collective-permute-start | bytes 20 | tf_op jit(solution)/shard_map/ppermute | solution.py:15
  27.4 2.2 copy-start.1
  27.9 2.5 copy-start.20
  31.0 26.9 %collective-permute-start.7 = (s32[1,1]{1,0:T(1,128)}, s32[1,1]{1,0:T(1,128)}, u32[]{:S(2)}, u32[]{:S(2)}) collective-permute-start(s32[1,1]{1,0:T(1,128)} %bitcast.1), channel_id=1, source_target_pairs={{0,28},{4,32},{8,36},{12,40},{16,44},{20,48},{24,52},{28,56},{32,6... | collective-permute-start | bytes 20 | tf_op jit(solution)/shard_map/ppermute | solution.py:15
  41.8 32.1 %collective-permute-start.8 = (s32[1,1]{1,0:T(1,128)}, s32[1,1]{1,0:T(1,128)}, u32[]{:S(2)}, u32[]{:S(2)}) collective-permute-start(s32[1,1]{1,0:T(1,128)} %bitcast.1), channel_id=1, source_target_pairs={{0,32},{4,36},{8,40},{12,44},{16,48},{20,52},{24,56},{28,60},{32,6... | collective-permute-start | bytes 20 | tf_op jit(solution)/shard_map/ppermute | solution.py:15
  50.1 74.6 %collective-permute-start.9 = (bf16[1,1,6144]{2,1,0:T(2,128)(2,1)S(1)}, bf16[1,1,6144]{2,1,0:T(2,128)(2,1)S(1)}, u32[]{:S(2)}, u32[]{:S(2)}) collective-permute-start(bf16[1,1,6144]{2,1,0:T(2,128)(2,1)S(1)} %reshape.3311), channel_id=1, source_target_pairs={{36,0},{40,4},{44,8},{48,12},{52,16},{56,20},{60,24},{64,28},{68,3... | collective-permute-start | bytes 36872 | tf_op jit(solution)/shard_map/ppermute | solution.py:15
  52.1 75.2 %collective-permute-start.10 = (bf16[1,1,6144]{2,1,0:T(2,128)(2,1)S(1)}, bf16[1,1,6144]{2,1,0:T(2,128)(2,1)S(1)}, u32[]{:S(2)}, u32[]{:S(2)}) collective-permute-start(bf16[1,1,6144]{2,1,0:T(2,128)(2,1)S(1)} %reshape.3311), channel_id=1, source_target_pairs={{32,0},{36,4},{40,8},{44,12},{48,16},{52,20},{56,24},{60,28},{64,3... | collective-permute-start | bytes 36872 | tf_op jit(solution)/shard_map/ppermute | solution.py:15
  54.1 77.3 %collective-permute-start.11 = (bf16[1,1,6144]{2,1,0:T(2,128)(2,1)S(1)}, bf16[1,1,6144]{2,1,0:T(2,128)(2,1)S(1)}, u32[]{:S(2)}, u32[]{:S(2)}) collective-permute-start(bf16[1,1,6144]{2,1,0:T(2,128)(2,1)S(1)} %reshape.3311), channel_id=1, source_target_pairs={{28,0},{32,4},{36,8},{40,12},{44,16},{48,20},{52,24},{56,28},{60,3... | collective-permute-start | bytes 36872 | tf_op jit(solution)/shard_map/ppermute | solution.py:15
  58.0 36.1 %collective-permute-start.1 = (s32[1,1]{1,0:T(1,128)}, s32[1,1]{1,0:T(1,128)}, u32[]{:S(2)}, u32[]{:S(2)}) collective-permute-start(s32[1,1]{1,0:T(1,128)} %bitcast.1), channel_id=1, source_target_pairs={{0,36},{4,40},{8,44},{12,48},{16,52},{20,56},{24,60},{28,64},{32,6... | collective-permute-start | bytes 20 | tf_op jit(solution)/shard_map/ppermute | solution.py:15
  73.9 44.1 %collective-permute-start = (bf16[1,1,6144]{2,1,0:T(2,128)(2,1)S(1)}, bf16[1,1,6144]{2,1,0:T(2,128)(2,1)S(1)}, u32[]{:S(2)}, u32[]{:S(2)}) collective-permute-start(bf16[1,1,6144]{2,1,0:T(2,128)(2,1)S(1)} %reshape.3302), channel_id=1, source_target_pairs={{0,36},{4,40},{8,44},{12,48},{16,52},{20,56},{24,60},{28,64},{32,6... | collective-permute-start | bytes 36872 | tf_op jit(solution)/shard_map/ppermute | solution.py:15
  94.1 38.8 %collective-permute-start.14 = (bf16[1,1,6144]{2,1,0:T(2,128)(2,1)S(1)}, bf16[1,1,6144]{2,1,0:T(2,128)(2,1)S(1)}, u32[]{:S(2)}, u32[]{:S(2)}) collective-permute-start(bf16[1,1,6144]{2,1,0:T(2,128)(2,1)S(1)} %reshape.3302), channel_id=1, source_target_pairs={{0,28},{4,32},{8,36},{12,40},{16,44},{20,48},{24,52},{28,56},{32,6... | collective-permute-start | bytes 36872 | tf_op jit(solution)/shard_map/ppermute | solution.py:15
  118.0 15.4 %collective-permute-start.15 = (bf16[1,1,6144]{2,1,0:T(2,128)(2,1)S(1)}, bf16[1,1,6144]{2,1,0:T(2,128)(2,1)S(1)}, u32[]{:S(2)}, u32[]{:S(2)}) collective-permute-start(bf16[1,1,6144]{2,1,0:T(2,128)(2,1)S(1)} %reshape.3302), channel_id=1, source_target_pairs={{0,32},{4,36},{8,40},{12,44},{16,48},{20,52},{24,56},{28,60},{32,6... | collective-permute-start | bytes 36872 | tf_op jit(solution)/shard_map/ppermute | solution.py:15
  124.7 7.3 collective-permute-start.12
  127.4 5.1 collective-permute-start.13
  153.9 34.5 %collective-permute-start.17 = (bf16[1,1,6144]{2,1,0:T(2,128)(2,1)}, bf16[1,1,6144]{2,1,0:T(2,128)(2,1)}, u32[]{:S(2)}, u32[]{:S(2)}) collective-permute-start(bf16[1,1,6144]{2,1,0:T(2,128)(2,1)} %reshape.3358), channel_id=1, source_target_pairs={{36,0},{40,4},{44,8},{48,12},{52,16},{56,20},{60,24},{64,28},{68,3... | collective-permute-start | bytes 36872 | tf_op jit(solution)/shard_map/ppermute | solution.py:15
  155.1 35.1 %collective-permute-start.18 = (bf16[1,1,6144]{2,1,0:T(2,128)(2,1)}, bf16[1,1,6144]{2,1,0:T(2,128)(2,1)}, u32[]{:S(2)}, u32[]{:S(2)}) collective-permute-start(bf16[1,1,6144]{2,1,0:T(2,128)(2,1)} %reshape.3358), channel_id=1, source_target_pairs={{32,0},{36,4},{40,8},{44,12},{48,16},{52,20},{56,24},{60,28},{64,3... | collective-permute-start | bytes 36872 | tf_op jit(solution)/shard_map/ppermute | solution.py:15
  156.4 48.6 %collective-permute-start.19 = (bf16[1,1,6144]{2,1,0:T(2,128)(2,1)}, bf16[1,1,6144]{2,1,0:T(2,128)(2,1)}, u32[]{:S(2)}, u32[]{:S(2)}) collective-permute-start(bf16[1,1,6144]{2,1,0:T(2,128)(2,1)} %reshape.3358), channel_id=1, source_target_pairs={{28,0},{32,4},{36,8},{40,12},{44,16},{48,20},{52,24},{56,28},{60,3... | collective-permute-start | bytes 36872 | tf_op jit(solution)/shard_map/ppermute | solution.py:15
  161.6 59.1 %collective-permute-start.22 = (bf16[1,1,6144]{2,1,0:T(2,128)(2,1)}, bf16[1,1,6144]{2,1,0:T(2,128)(2,1)}, u32[]{:S(2)}, u32[]{:S(2)}) collective-permute-start(bf16[1,1,6144]{2,1,0:T(2,128)(2,1)} %reshape.3356), channel_id=1, source_target_pairs={{0,28},{4,32},{8,36},{12,40},{16,44},{20,48},{24,52},{28,56},{32,6... | collective-permute-start | bytes 36872 | tf_op jit(solution)/shard_map/ppermute | solution.py:15
  173.3 50.2 %collective-permute-start.23 = (bf16[1,1,6144]{2,1,0:T(2,128)(2,1)}, bf16[1,1,6144]{2,1,0:T(2,128)(2,1)}, u32[]{:S(2)}, u32[]{:S(2)}) collective-permute-start(bf16[1,1,6144]{2,1,0:T(2,128)(2,1)} %reshape.3356), channel_id=1, source_target_pairs={{0,32},{4,36},{8,40},{12,44},{16,48},{20,52},{24,56},{28,60},{32,6... | collective-permute-start | bytes 36872 | tf_op jit(solution)/shard_map/ppermute | solution.py:15
  188.4 26.7 %collective-permute-start.20 = (bf16[1,1,6144]{2,1,0:T(2,128)(2,1)}, bf16[1,1,6144]{2,1,0:T(2,128)(2,1)}, u32[]{:S(2)}, u32[]{:S(2)}) collective-permute-start(bf16[1,1,6144]{2,1,0:T(2,128)(2,1)} %reshape.3362), channel_id=1, source_target_pairs={{4,0},{8,4},{12,8},{16,12},{20,16},{24,20},{28,24},{32,28},{36,32}... | collective-permute-start | bytes 36872 | tf_op jit(solution)/shard_map/ppermute | solution.py:15
  190.3 27.6 %collective-permute-start.21 = (bf16[1,1,6144]{2,1,0:T(2,128)(2,1)}, bf16[1,1,6144]{2,1,0:T(2,128)(2,1)}, u32[]{:S(2)}, u32[]{:S(2)}) collective-permute-start(bf16[1,1,6144]{2,1,0:T(2,128)(2,1)} %reshape.3364), channel_id=1, source_target_pairs={{0,4},{4,8},{8,12},{12,16},{16,20},{20,24},{24,28},{28,32},{32,36}... | collective-permute-start | bytes 36872 | tf_op jit(solution)/shard_map/ppermute | solution.py:15
  205.0 40.8 %collective-permute-start.16 = (bf16[1,1,6144]{2,1,0:T(2,128)(2,1)}, bf16[1,1,6144]{2,1,0:T(2,128)(2,1)}, u32[]{:S(2)}, u32[]{:S(2)}) collective-permute-start(bf16[1,1,6144]{2,1,0:T(2,128)(2,1)} %reshape.3356), channel_id=1, source_target_pairs={{0,36},{4,40},{8,44},{12,48},{16,52},{20,56},{24,60},{28,64},{32,6... | collective-permute-start | bytes 36872 | tf_op jit(solution)/shard_map/ppermute | solution.py:15
  275.1 7.8 copy-start.2
  276.9 5.4 copy-start.7
  276.9 5.4 collective-permute-start.24
  282.9 43.9 %copy-start.5 = (bf16[1,96,512]{2,1,0:T(8,128)(2,1)}, bf16[1,96,512]{2,1,0:T(8,128)(2,1)S(1)}, u32[]{:S(2)}) copy-start(bf16[1,96,512]{2,1,0:T(8,128)(2,1)S(1)} %fusion.42) | copy-start | bytes 294916
  287.0 18.7 %collective-permute-start.26 = (bf16[1,1,6144]{2,1,0:T(2,128)(2,1)}, bf16[1,1,6144]{2,1,0:T(2,128)(2,1)}, u32[]{:S(2)}, u32[]{:S(2)}) collective-permute-start(bf16[1,1,6144]{2,1,0:T(2,128)(2,1)} %reshape.3405), channel_id=1, source_target_pairs={{36,0},{40,4},{44,8},{48,12},{52,16},{56,20},{60,24},{64,28},{68,3... | collective-permute-start | bytes 36872 | tf_op jit(solution)/shard_map/ppermute | solution.py:15
  288.3 27.5 %collective-permute-start.27 = (bf16[1,1,6144]{2,1,0:T(2,128)(2,1)}, bf16[1,1,6144]{2,1,0:T(2,128)(2,1)}, u32[]{:S(2)}, u32[]{:S(2)}) collective-permute-start(bf16[1,1,6144]{2,1,0:T(2,128)(2,1)} %reshape.3405), channel_id=1, source_target_pairs={{32,0},{36,4},{40,8},{44,12},{48,16},{52,20},{56,24},{60,28},{64,3... | collective-permute-start | bytes 36872 | tf_op jit(solution)/shard_map/ppermute | solution.py:15
  289.6 42.8 %collective-permute-start.28 = (bf16[1,1,6144]{2,1,0:T(2,128)(2,1)}, bf16[1,1,6144]{2,1,0:T(2,128)(2,1)}, u32[]{:S(2)}, u32[]{:S(2)}) collective-permute-start(bf16[1,1,6144]{2,1,0:T(2,128)(2,1)} %reshape.3405), channel_id=1, source_target_pairs={{28,0},{32,4},{36,8},{40,12},{44,16},{48,20},{52,24},{56,28},{60,3... | collective-permute-start | bytes 36872 | tf_op jit(solution)/shard_map/ppermute | solution.py:15
  295.5 48.2 %collective-permute-start.29 = (bf16[1,1,6144]{2,1,0:T(2,128)(2,1)}, bf16[1,1,6144]{2,1,0:T(2,128)(2,1)}, u32[]{:S(2)}, u32[]{:S(2)}) collective-permute-start(bf16[1,1,6144]{2,1,0:T(2,128)(2,1)} %reshape.3409), channel_id=1, source_target_pairs={{4,0},{8,4},{12,8},{16,12},{20,16},{24,20},{28,24},{32,28},{36,32}... | collective-permute-start | bytes 36872 | tf_op jit(solution)/shard_map/ppermute | solution.py:15
  301.2 45.3 %collective-permute-start.30 = (bf16[1,1,6144]{2,1,0:T(2,128)(2,1)S(1)}, bf16[1,1,6144]{2,1,0:T(2,128)(2,1)}, u32[]{:S(2)}, u32[]{:S(2)}) collective-permute-start(bf16[1,1,6144]{2,1,0:T(2,128)(2,1)S(1)} %reshape.3411), channel_id=1, source_target_pairs={{0,4},{4,8},{8,12},{12,16},{16,20},{20,24},{24,28},{28,32},{32,36}... | collective-permute-start | bytes 36872 | tf_op jit(solution)/shard_map/ppermute | solution.py:15
  305.7 43.6 %collective-permute-start.31 = (bf16[1,1,6144]{2,1,0:T(2,128)(2,1)}, bf16[1,1,6144]{2,1,0:T(2,128)(2,1)}, u32[]{:S(2)}, u32[]{:S(2)}) collective-permute-start(bf16[1,1,6144]{2,1,0:T(2,128)(2,1)} %reshape.3403), channel_id=1, source_target_pairs={{0,28},{4,32},{8,36},{12,40},{16,44},{20,48},{24,52},{28,56},{32,6... | collective-permute-start | bytes 36872 | tf_op jit(solution)/shard_map/ppermute | solution.py:15
  315.8 36.4 %collective-permute-start.32 = (bf16[1,1,6144]{2,1,0:T(2,128)(2,1)}, bf16[1,1,6144]{2,1,0:T(2,128)(2,1)}, u32[]{:S(2)}, u32[]{:S(2)}) collective-permute-start(bf16[1,1,6144]{2,1,0:T(2,128)(2,1)} %reshape.3403), channel_id=1, source_target_pairs={{0,32},{4,36},{8,40},{12,44},{16,48},{20,52},{24,56},{28,60},{32,6... | collective-permute-start | bytes 36872 | tf_op jit(solution)/shard_map/ppermute | solution.py:15
  332.4 42.0 %collective-permute-start.25 = (bf16[1,1,6144]{2,1,0:T(2,128)(2,1)}, bf16[1,1,6144]{2,1,0:T(2,128)(2,1)}, u32[]{:S(2)}, u32[]{:S(2)}) collective-permute-start(bf16[1,1,6144]{2,1,0:T(2,128)(2,1)} %reshape.3403), channel_id=1, source_target_pairs={{0,36},{4,40},{8,44},{12,48},{16,52},{20,56},{24,60},{28,64},{32,6... | collective-permute-start | bytes 36872 | tf_op jit(solution)/shard_map/ppermute | solution.py:15
  403.7 8.9 copy-start.3
  405.5 6.5 collective-permute-start.33
  412.6 43.1 %copy-start.6 = (bf16[1,96,512]{2,1,0:T(8,128)(2,1)}, bf16[1,96,512]{2,1,0:T(8,128)(2,1)S(1)}, u32[]{:S(2)}) copy-start(bf16[1,96,512]{2,1,0:T(8,128)(2,1)S(1)} %fusion.43) | copy-start | bytes 294916
  416.7 18.6 %collective-permute-start.35 = (bf16[1,1,6144]{2,1,0:T(2,128)(2,1)}, bf16[1,1,6144]{2,1,0:T(2,128)(2,1)}, u32[]{:S(2)}, u32[]{:S(2)}) collective-permute-start(bf16[1,1,6144]{2,1,0:T(2,128)(2,1)} %reshape.3449), channel_id=1, source_target_pairs={{36,0},{40,4},{44,8},{48,12},{52,16},{56,20},{60,24},{64,28},{68,3... | collective-permute-start | bytes 36872 | tf_op jit(solution)/shard_map/ppermute | solution.py:15
  418.0 26.8 %collective-permute-start.36 = (bf16[1,1,6144]{2,1,0:T(2,128)(2,1)}, bf16[1,1,6144]{2,1,0:T(2,128)(2,1)}, u32[]{:S(2)}, u32[]{:S(2)}) collective-permute-start(bf16[1,1,6144]{2,1,0:T(2,128)(2,1)} %reshape.3449), channel_id=1, source_target_pairs={{32,0},{36,4},{40,8},{44,12},{48,16},{52,20},{56,24},{60,28},{64,3... | collective-permute-start | bytes 36872 | tf_op jit(solution)/shard_map/ppermute | solution.py:15
  419.3 42.1 %collective-permute-start.37 = (bf16[1,1,6144]{2,1,0:T(2,128)(2,1)}, bf16[1,1,6144]{2,1,0:T(2,128)(2,1)}, u32[]{:S(2)}, u32[]{:S(2)}) collective-permute-start(bf16[1,1,6144]{2,1,0:T(2,128)(2,1)} %reshape.3449), channel_id=1, source_target_pairs={{28,0},{32,4},{36,8},{40,12},{44,16},{48,20},{52,24},{56,28},{60,3... | collective-permute-start | bytes 36872 | tf_op jit(solution)/shard_map/ppermute | solution.py:15
  425.2 46.9 %collective-permute-start.38 = (bf16[1,1,6144]{2,1,0:T(2,128)(2,1)}, bf16[1,1,6144]{2,1,0:T(2,128)(2,1)}, u32[]{:S(2)}, u32[]{:S(2)}) collective-permute-start(bf16[1,1,6144]{2,1,0:T(2,128)(2,1)} %reshape.3453), channel_id=1, source_target_pairs={{4,0},{8,4},{12,8},{16,12},{20,16},{24,20},{28,24},{32,28},{36,32}... | collective-permute-start | bytes 36872 | tf_op jit(solution)/shard_map/ppermute | solution.py:15
  429.7 45.1 %collective-permute-start.39 = (bf16[1,1,6144]{2,1,0:T(2,128)(2,1)S(1)}, bf16[1,1,6144]{2,1,0:T(2,128)(2,1)}, u32[]{:S(2)}, u32[]{:S(2)}) collective-permute-start(bf16[1,1,6144]{2,1,0:T(2,128)(2,1)S(1)} %reshape.3455), channel_id=1, source_target_pairs={{0,4},{4,8},{8,12},{12,16},{16,20},{20,24},{24,28},{28,32},{32,36}... | collective-permute-start | bytes 36872 | tf_op jit(solution)/shard_map/ppermute | solution.py:15
  435.3 42.3 %collective-permute-start.40 = (bf16[1,1,6144]{2,1,0:T(2,128)(2,1)}, bf16[1,1,6144]{2,1,0:T(2,128)(2,1)}, u32[]{:S(2)}, u32[]{:S(2)}) collective-permute-start(bf16[1,1,6144]{2,1,0:T(2,128)(2,1)} %reshape.3447), channel_id=1, source_target_pairs={{0,28},{4,32},{8,36},{12,40},{16,44},{20,48},{24,52},{28,56},{32,6... | collective-permute-start | bytes 36872 | tf_op jit(solution)/shard_map/ppermute | solution.py:15
  444.8 35.6 %collective-permute-start.41 = (bf16[1,1,6144]{2,1,0:T(2,128)(2,1)}, bf16[1,1,6144]{2,1,0:T(2,128)(2,1)}, u32[]{:S(2)}, u32[]{:S(2)}) collective-permute-start(bf16[1,1,6144]{2,1,0:T(2,128)(2,1)} %reshape.3447), channel_id=1, source_target_pairs={{0,32},{4,36},{8,40},{12,44},{16,48},{20,52},{24,56},{28,60},{32,6... | collective-permute-start | bytes 36872 | tf_op jit(solution)/shard_map/ppermute | solution.py:15
  461.4 41.4 %collective-permute-start.34 = (bf16[1,1,6144]{2,1,0:T(2,128)(2,1)}, bf16[1,1,6144]{2,1,0:T(2,128)(2,1)}, u32[]{:S(2)}, u32[]{:S(2)}) collective-permute-start(bf16[1,1,6144]{2,1,0:T(2,128)(2,1)} %reshape.3447), channel_id=1, source_target_pairs={{0,36},{4,40},{8,44},{12,48},{16,52},{20,56},{24,60},{28,64},{32,6... | collective-permute-start | bytes 36872 | tf_op jit(solution)/shard_map/ppermute | solution.py:15
  533.8 1.3 copy-start.11
  533.8 6.2 collective-permute-start.42
  544.8 25.4 %collective-permute-start.44 = (bf16[1,1,6144]{2,1,0:T(2,128)(2,1)}, bf16[1,1,6144]{2,1,0:T(2,128)(2,1)S(1)}, u32[]{:S(2)}, u32[]{:S(2)}) collective-permute-start(bf16[1,1,6144]{2,1,0:T(2,128)(2,1)} %reshape.3493), channel_id=1, source_target_pairs={{36,0},{40,4},{44,8},{48,12},{52,16},{56,20},{60,24},{64,28},{68,3... | collective-permute-start | bytes 36872 | tf_op jit(solution)/shard_map/ppermute | solution.py:15
  546.1 26.1 %collective-permute-start.45 = (bf16[1,1,6144]{2,1,0:T(2,128)(2,1)}, bf16[1,1,6144]{2,1,0:T(2,128)(2,1)S(1)}, u32[]{:S(2)}, u32[]{:S(2)}) collective-permute-start(bf16[1,1,6144]{2,1,0:T(2,128)(2,1)} %reshape.3493), channel_id=1, source_target_pairs={{32,0},{36,4},{40,8},{44,12},{48,16},{52,20},{56,24},{60,28},{64,3... | collective-permute-start | bytes 36872 | tf_op jit(solution)/shard_map/ppermute | solution.py:15
  547.4 34.5 %collective-permute-start.46 = (bf16[1,1,6144]{2,1,0:T(2,128)(2,1)}, bf16[1,1,6144]{2,1,0:T(2,128)(2,1)}, u32[]{:S(2)}, u32[]{:S(2)}) collective-permute-start(bf16[1,1,6144]{2,1,0:T(2,128)(2,1)} %reshape.3493), channel_id=1, source_target_pairs={{28,0},{32,4},{36,8},{40,12},{44,16},{48,20},{52,24},{56,28},{60,3... | collective-permute-start | bytes 36872 | tf_op jit(solution)/shard_map/ppermute | solution.py:15
  549.1 43.4 %collective-permute-start.49 = (bf16[1,1,6144]{2,1,0:T(2,128)(2,1)S(1)}, bf16[1,1,6144]{2,1,0:T(2,128)(2,1)}, u32[]{:S(2)}, u32[]{:S(2)}) collective-permute-start(bf16[1,1,6144]{2,1,0:T(2,128)(2,1)S(1)} %reshape.3491), channel_id=1, source_target_pairs={{0,28},{4,32},{8,36},{12,40},{16,44},{20,48},{24,52},{28,56},{32,6... | collective-permute-start | bytes 36872 | tf_op jit(solution)/shard_map/ppermute | solution.py:15
  559.7 34.0 %collective-permute-start.50 = (bf16[1,1,6144]{2,1,0:T(2,128)(2,1)S(1)}, bf16[1,1,6144]{2,1,0:T(2,128)(2,1)}, u32[]{:S(2)}, u32[]{:S(2)}) collective-permute-start(bf16[1,1,6144]{2,1,0:T(2,128)(2,1)S(1)} %reshape.3491), channel_id=1, source_target_pairs={{0,32},{4,36},{8,40},{12,44},{16,48},{20,52},{24,56},{28,60},{32,6... | collective-permute-start | bytes 36872 | tf_op jit(solution)/shard_map/ppermute | solution.py:15
  570.1 7.1 copy-start.4
  570.2 5.7 copy-start.18
  570.2 19.8 %collective-permute-start.47 = (bf16[1,1,6144]{2,1,0:T(2,128)(2,1)S(1)}, bf16[1,1,6144]{2,1,0:T(2,128)(2,1)}, u32[]{:S(2)}, u32[]{:S(2)}) collective-permute-start(bf16[1,1,6144]{2,1,0:T(2,128)(2,1)S(1)} %reshape.3497), channel_id=1, source_target_pairs={{4,0},{8,4},{12,8},{16,12},{20,16},{24,20},{28,24},{32,28},{36,32}... | collective-permute-start | bytes 36872 | tf_op jit(solution)/shard_map/ppermute | solution.py:15
  572.2 3.7 copy-start.16
  572.3 19.0 %collective-permute-start.48 = (bf16[1,1,6144]{2,1,0:T(2,128)(2,1)S(1)}, bf16[1,1,6144]{2,1,0:T(2,128)(2,1)}, u32[]{:S(2)}, u32[]{:S(2)}) collective-permute-start(bf16[1,1,6144]{2,1,0:T(2,128)(2,1)S(1)} %reshape.3499), channel_id=1, source_target_pairs={{0,4},{4,8},{8,12},{12,16},{16,20},{20,24},{24,28},{28,32},{32,36}... | collective-permute-start | bytes 36872 | tf_op jit(solution)/shard_map/ppermute | solution.py:15
  581.9 16.6 %collective-permute-start.43 = (bf16[1,1,6144]{2,1,0:T(2,128)(2,1)S(1)}, bf16[1,1,6144]{2,1,0:T(2,128)(2,1)S(1)}, u32[]{:S(2)}, u32[]{:S(2)}) collective-permute-start(bf16[1,1,6144]{2,1,0:T(2,128)(2,1)S(1)} %reshape.3491), channel_id=1, source_target_pairs={{0,36},{4,40},{8,44},{12,48},{16,52},{20,56},{24,60},{28,64},{32,6... | collective-permute-start | bytes 36872 | tf_op jit(solution)/shard_map/ppermute | solution.py:15
  917.1 3.1 copy-start
  (9 other events, 8.4 us)
Sparse Core Ops, SparseCore 0:
  580.3 336.7 all-reduce.42
where the time goes:
time: 946 us; the launch traced here: 928 us
  waiting for transfers between devices  321 us (34%)
  starting transfers between devices  224 us (24%)
  local copies, waits for them, and re-layouts  215 us (23%)
  other arithmetic  93.3 us (10%)
  between operations  46.7 us (5%)
  matrix products  28.7 us (3%)
    psum x1, waiting for transfers between devices, body(): total = lax.psum(terms, 'space')  307 us
    ppermute x51, starting transfers between devices, shifted(): lax.ppermute(value, axis, [(source, source + steps) for source in range(l...  224 us
    reshape x75, local copies, waits for them, and re-layouts, direct_halo(): got.reshape(layer.shape)  53 us
    mul x55, other arithmetic, pad_bricks(): stacks.append(piece * keep)  42.1 us
    slice x40, local copies, waits for them, and re-layouts, take_layer(): return lax.slice_in_dim(block, start, start + 1, axis=axis)  31.4 us
    concatenate x15, local copies, waits for them, and re-layouts, gather_cols(): return jnp.concatenate(pieces, 1)  31.3 us
    ppermute x40, other arithmetic, shifted(): lax.ppermute(value, axis, [(source, source + steps) for source in range(l...  26 us
    dot_general x15, matrix products, apply_conv(): jnp.einsum('bkp,kd->bdp', cols, block, preferred_element_type=jnp.float32)  25.6 us
  transfers between devices with their start and end apart: 52, of which 4 were waited for; matrix products, arithmetic and copies ran while one was open for 22% of the time, Pallas kernels for 0%

commit v1 on v0

v1 whole, which is shorter than its diff:
```python
import functools

import jax
import jax.numpy as jnp
from jax import lax
from jax.experimental import pallas as pl
from jax.experimental.pallas import tpu as pltpu
from jax.sharding import PartitionSpec as P

C = 96
CELLS = 512
COLS = 8
ROWS = 16
SECTIONS = 4
TAPS = 27
DEEP = TAPS * C
WIDE = 128
CODE = 8
CHUNK = 336
VMEM_BYTES = 56 * 1024 * 1024
F32 = jnp.float32
BF16 = jnp.bfloat16


def call(kernel, outs, scratch=()):
    return pl.pallas_call(
        kernel,
        out_shape=[jax.ShapeDtypeStruct(shape, dtype) for shape, dtype in outs],
        scratch_shapes=[pltpu.VMEM(shape, dtype) for shape, dtype in scratch],
        compiler_params=pltpu.CompilerParams(vmem_limit_bytes=VMEM_BYTES),
    )


def lane(row, count=1):
    start = row * WIDE
    if not isinstance(start, int):
        start = pl.multiple_of(start, WIDE)
    return pl.ds(start, count * WIDE)


def turn(value, by):
    by = by % value.shape[1]
    return pltpu.roll(value, by, 1) if by else value


def shifted_rows(base_ref, row, tile):
    level = lax.broadcasted_iota(jnp.int32, (C, WIDE), 1) % 8
    for oy in (-1, 0, 1):
        for oz in (-1, 0, 1):
            if oz == 0:
                moved = turn(tile, -8 * oy)
            elif oz > 0:
                moved = jnp.where(level < 7, turn(tile, -8 * oy - 1), turn(tile, -8 * oy + 7))
            else:
                moved = jnp.where(level > 0, turn(tile, -8 * oy + 1), turn(tile, -8 * oy - 7))
            base_ref[3 * (oy + 1) + oz + 1, :, lane(row)] = moved


def make_cols(cols_ref, base_ref, mask_ref, base_row, mask_row, at=0):
    for ox in (-1, 0, 1):
        for j in range(9):
            tap = 9 * (ox + 1) + j
            tile = base_ref[j, :, lane(base_row + ox, 2)].reshape(C // 16, 16, 2 * WIDE)
            kept = tile * mask_ref[tap, :, lane(mask_row, 2)][None]
            cols_ref[C * tap : C * tap + C, lane(at, 2)] = kept.reshape(C, 2 * WIDE)


def product(weight, cols):
    return lax.dot_general(
        weight, cols, (((1,), (0,)), ((), ())), preferred_element_type=F32
    )


def weight_kernel(w_ref, fwd_ref, bwd_ref):
    for q in range(TAPS):
        fwd_ref[:, C * q : C * q + C] = w_ref[q].T
        bwd_ref[:, C * q : C * q + C] = w_ref[TAPS - 1 - q]


def pack_kernel(own_ref, left_ref, right_ref, own_out, up_out, down_out):
    rows = []
    for i in range(8):
        at = 64 * i
        rows.append(
            jnp.concatenate(
                [
                    left_ref[:, at + 32 : at + 64],
                    own_ref[:, at : at + 64],
                    right_ref[:, at : at + 32],
                ],
                1,
            )
        )
        own_out[:, lane(i)] = rows[i]
    codes = jnp.concatenate([rows[0][2 * C :]] * (C // 16), 0)
    for out, first in ((up_out, 3), (down_out, 0)):
        for n in range(5):
            out[:, lane(n)] = rows[first + n][:C]
        for n in range(4):
            row = first + n + (1 if first else 0)
            out[:, lane(5 + n)] = rows[row][C : 2 * C]
        out[:, lane(9)] = codes


def first_kernel(
    own_ref, before_ref, after_ref, fwd_ref, bwd_ref, active_ref,
    result_ref, slope_ref, mask_ref, x_ref, grad_ref, out_ref,
    base_ref, cols_ref, code_ref, top_ref, pre_ref,
):
    active = active_ref[0:1, 0:1]
    own_code = own_ref[2 * C : 2 * C + 8, :WIDE].astype(F32)
    before_code = before_ref[0:8, lane(9)].astype(F32)
    after_code = after_ref[0:8, lane(9)].astype(F32)
    for row in range(18):
        code = before_code if row < 5 else own_code if row < 13 else after_code
        code_ref[:, lane(row)] = code
    for row in range(18):
        if row < 5:
            tile = before_ref[:, lane(row)]
        elif row < 13:
            tile = own_ref[:C, lane(row - 5)]
        else:
            tile = after_ref[:, lane(row - 13)]
        if 4 <= row < 14:
            x_ref[:, lane(row - 4)] = tile
        shifted_rows(base_ref, row, tile)
    for row in range(1, 17):
        if row < 5:
            tile = before_ref[:, lane(4 + row)]
        elif row < 13:
            tile = own_ref[C : 2 * C, lane(row - 5)]
        else:
            tile = after_ref[:, lane(5 + row - 13)]
        top_ref[:, lane(row - 1)] = tile.astype(F32) * active

    level = lax.broadcasted_iota(jnp.int32, (8, WIDE), 1) % 8
    rise_of = {
        -1: jnp.where(level == 0, -1.0, 0.0),
        0: jnp.zeros((8, WIDE), F32),
        1: jnp.where(level == 7, 1.0, 0.0),
    }

    def masks(row, carry):
        here = code_ref[:, lane(row + 1)]
        for ox in (-1, 0, 1):
            near = code_ref[:, lane(row + 1 + ox)]
            for oy in (-1, 0, 1):
                rise = turn(near, -8 * oy) - here
                for oz in (-1, 0, 1):
                    keep = jnp.where(rise == rise_of[oz], 1.0, 0.0)
                    tap = 9 * (ox + 1) + 3 * (oy + 1) + oz + 1
                    mask_ref[tap, :, lane(row)] = jnp.concatenate([keep, keep], 0).astype(BF16)
        return carry

    lax.fori_loop(0, 16, masks, 0)

    def forward(pair, carry):
        make_cols(cols_ref, base_ref, mask_ref, 2 * pair + 1, 2 * pair)
        pre_ref[:, lane(2 * pair, 2)] = product(fwd_ref[...], cols_ref[...])
        return carry

    lax.fori_loop(0, 8, forward, 0)
    for row in range(16):
        pre = pre_ref[:, lane(row)]
        sigma = 1.0 / (1.0 + jnp.exp(-pre))
        slope = sigma * (1.0 + pre * (1.0 - sigma))
        grad = (top_ref[:, lane(row)] * slope).astype(BF16)
        if 1 <= row < 15:
            slope_ref[:, lane(row - 1)] = slope
        if 4 <= row < 12:
            grad_ref[:, lane(row - 4)] = grad
        shifted_rows(base_ref, row, grad)

    def backward(pair, carry):
        make_cols(cols_ref, base_ref, mask_ref, 2 * pair + 1, 2 * pair + 1)
        total = top_ref[:, lane(2 * pair + 1, 2)] + product(bwd_ref[...], cols_ref[...])
        result_ref[:, lane(2 * pair, 2)] = total.astype(BF16)
        return carry

    lax.fori_loop(0, 7, backward, 0)
    for row in range(8):
        out_ref[:, lane(row)] = result_ref[:, lane(row + 3)]


def step_rows(incoming_ref, slope_ref, mask_ref, bwd_ref, base_ref, cols_ref, store, count, first):
    for row in range(count):
        grad = (
            incoming_ref[:, lane(row)].astype(F32) * slope_ref[:, lane(row + first - 2)]
        ).astype(BF16)
        shifted_rows(base_ref, row, grad)

    def backward(pair, carry):
        make_cols(cols_ref, base_ref, mask_ref, 2 * pair + 1, 2 * pair + first)
        total = incoming_ref[:, lane(2 * pair + 1, 2)].astype(F32) + product(
            bwd_ref[...], cols_ref[...]
        )
        store(pair, total.astype(BF16))
        return carry

    lax.fori_loop(0, (count - 2) // 2, backward, 0)


def middle_kernel(
    count, first, incoming_ref, slope_ref, mask_ref, bwd_ref, grad_in, out_in,
    result_ref, grad_ref, out_ref, base_ref, cols_ref,
):
    def store(pair, value):
        result_ref[:, lane(2 * pair, 2)] = value

    step_rows(
        incoming_ref, slope_ref, mask_ref, bwd_ref, base_ref, cols_ref, store, count, first
    )
    for row in range(8):
        grad_ref[:, lane(row)] = grad_in[:, lane(row)] + base_ref[4, :, lane(row + 5 - first)]
        out_ref[:, lane(row)] = out_in[:, lane(row)] + result_ref[:, lane(row + 4 - first)]


def late_kernel(
    count, first, incoming_ref, slope_ref, mask_ref, bwd_ref, grad_in, out_in,
    centre_ref, left_ref, right_ref, grad_ref, out_ref, base_ref, cols_ref, result_ref,
):
    middle_kernel(
        count, first, incoming_ref, slope_ref, mask_ref, bwd_ref, grad_in, out_in,
        result_ref, grad_ref, out_ref, base_ref, cols_ref,
    )
    rows = [result_ref[:, lane(row)] for row in range(count - 2)]
    for row in range(0, count - 2, 2):
        centre_ref[:, lane(row // 2)] = jnp.concatenate(
            [rows[row][:, 32:96], rows[row + 1][:, 32:96]], 1
        )
    spare = jnp.zeros((C, WIDE - 8 * (count - 2)), BF16)
    left_ref[...] = jnp.concatenate([row[:, 32:40] for row in rows] + [spare], 1)
    right_ref[...] = jnp.concatenate([row[:, 88:96] for row in rows] + [spare], 1)


def last_kernel(
    centre_ref, from_left, from_right, slope_ref, mask_ref, bwd_ref, x_ref, grad_in, out_in,
    out_ref, terms_ref, base_ref, cols_ref, incoming_ref, sums_ref, all_ref,
):
    pad = jnp.zeros((C, 24), BF16)
    for row in range(10):
        at = 64 * row
        incoming_ref[:, lane(row)] = jnp.concatenate(
            [
                pad,
                from_left[:, 8 * row : 8 * row + 8],
                centre_ref[:, at : at + 64],
                from_right[:, 8 * row : 8 * row + 8],
                pad,
            ],
            1,
        )

    def store(pair, value):
        sums_ref[:, lane(2 * pair, 2)] = out_in[:, lane(2 * pair, 2)] + value

    step_rows(incoming_ref, slope_ref, mask_ref, bwd_ref, base_ref, cols_ref, store, 10, 4)
    for pair in range(4):
        first, second = sums_ref[:, lane(2 * pair)], sums_ref[:, lane(2 * pair + 1)]
        out_ref[:, lane(pair)] = jnp.concatenate([first[:, 32:96], second[:, 32:96]], 1)

    where = lax.broadcasted_iota(jnp.int32, (C, WIDE), 1)
    inside = (where >= 32) & (where < 96)
    grads = []
    for row in range(8):
        grad = grad_in[:, lane(row)] + base_ref[4, :, lane(row + 1)]
        grads.append(jnp.where(inside, grad, jnp.zeros_like(grad)))
    grads = jnp.concatenate(grads, 1)
    for row in range(10):
        shifted_rows(base_ref, row, x_ref[:, lane(row)])

    def gather(pair, carry):
        make_cols(all_ref, base_ref, mask_ref, 2 * pair + 1, 2 * pair + 4, 2 * pair)
        return carry

    lax.fori_loop(0, 4, gather, 0)
    for tap in range(TAPS):
        part = lax.dot_general(
            all_ref[C * tap : C * tap + C, :], grads, (((1,), (1,)), ((), ())),
            preferred_element_type=F32,
        )
        terms_ref[C * tap : C * tap + C, :] = part.astype(BF16)
    terms_ref[DEEP:, :] = jnp.zeros((COLS * CHUNK - DEEP, C), BF16)


def groups(devices):
    rows = devices // (2 * ROWS)
    near = [[y * 32 + z * 2 + c for y in range(rows) for c in range(2)] for z in range(ROWS)]
    far = [[y * 32 + z * 2 + c for z in range(ROWS)] for y in range(rows) for c in range(2)]
    return near, far


def body(section_input, top_grad, conv_weight, brick_height):
    devices = lax.axis_size("space")
    section = lax.axis_index("pipe")
    both = ("space", "pipe")

    def between(by_row, by_col, sections):
        pairs = []
        for x in range(ROWS):
            for y in range(COLS):
                if 0 <= x + by_row < ROWS and 0 <= y + by_col < COLS:
                    source = x * COLS + y
                    target = (x + by_row) * COLS + y + by_col
                    for a, b in sections:
                        pairs.append((source * SECTIONS + a, target * SECTIONS + b))
        return pairs

    same = [(s, s) for s in range(SECTIONS)]
    code = jnp.broadcast_to((brick_height + CODE).astype(BF16)[:, None], (16, CELLS))
    own = jnp.concatenate([section_input.reshape(C, CELLS), top_grad.reshape(C, CELLS), code], 0)
    fwd, bwd = call(weight_kernel, [((C, DEEP), BF16)] * 2)(conv_weight[0])
    left = lax.ppermute(own, both, between(0, 1, same))
    right = lax.ppermute(own, both, between(0, -1, same))
    own, up, down = call(
        pack_kernel,
        [((2 * C + 16, 8 * WIDE), BF16), ((C, 10 * WIDE), BF16), ((C, 10 * WIDE), BF16)],
    )(own, left, right)
    before = lax.ppermute(up, both, between(1, 0, same))
    after = lax.ppermute(down, both, between(-1, 0, same))
    active = jnp.where(section == SECTIONS - 1, 1.0, 0.0) * jnp.ones((8, WIDE), F32)

    core = ((C, 8 * WIDE), BF16)
    cols = ((DEEP, 2 * WIDE), BF16)
    result, slope, mask, x_rows, grad, out = call(
        first_kernel,
        [((C, 14 * WIDE), BF16), ((C, 14 * WIDE), F32), ((TAPS, 16, 16 * WIDE), BF16),
         ((C, 10 * WIDE), BF16), core, core],
        [((9, C, 18 * WIDE), BF16), cols, ((8, 18 * WIDE), F32), ((C, 16 * WIDE), F32),
         ((C, 16 * WIDE), F32)],
    )(own, before, after, fwd, bwd, active)
    incoming = lax.ppermute(result, both, between(0, 0, [(3, 2)]))
    result, grad, out = call(
        functools.partial(middle_kernel, 14, 2),
        [((C, 12 * WIDE), BF16), core, core],
        [((9, C, 14 * WIDE), BF16), cols],
    )(incoming, slope, mask, bwd, grad, out)
    incoming = lax.ppermute(result, both, between(0, 0, [(2, 1)]))
    centre, left, right, grad, out = call(
        functools.partial(late_kernel, 12, 3),
        [((C, 5 * WIDE), BF16), ((C, WIDE), BF16), ((C, WIDE), BF16), core, core],
        [((9, C, 12 * WIDE), BF16), cols, ((C, 10 * WIDE), BF16)],
    )(incoming, slope, mask, bwd, grad, out)
    centre = lax.ppermute(centre, both, between(0, 0, [(1, 0)]))
    from_left = lax.ppermute(right, both, between(0, 1, [(1, 0)]))
    from_right = lax.ppermute(left, both, between(0, -1, [(1, 0)]))
    out, terms = call(
        last_kernel,
        [((C, CELLS), BF16), ((COLS * CHUNK, C), BF16)],
        [((9, C, 10 * WIDE), BF16), cols, ((C, 10 * WIDE), BF16), core, ((DEEP, 8 * WIDE), BF16)],
    )(centre, from_left, from_right, slope, mask, bwd, x_rows, grad, out)

    near, far = groups(devices)
    parts = lax.all_to_all(
        terms.reshape(COLS, CHUNK, C), "space", 0, 0, axis_index_groups=near
    )
    part = jnp.sum(parts.astype(F32), 0)
    pieces = lax.all_to_all(
        part.reshape(ROWS, CHUNK // ROWS, C), "space", 0, 0, axis_index_groups=far
    )
    piece = jnp.sum(pieces, 0)
    part = lax.all_gather(piece, "space", axis_index_groups=far).reshape(CHUNK, C)
    whole = lax.all_gather(part.astype(BF16), "space", axis_index_groups=near)
    total = whole.reshape(COLS * CHUNK, C)[:DEEP].astype(F32)
    scale = lax.rsqrt(jnp.sum(total * total) / (DEEP * C) + 1e-06)
    return (out.reshape(1, 1, C, CELLS), (total * scale).reshape(1, TAPS, C, C))


def solution(mesh):
    return jax.shard_map(
        body,
        mesh=mesh,
        in_specs=(
            P("pipe", "space", None, None),
            P("space", None, None),
            P("pipe", None, None, None),
            P("space"),
        ),
        out_specs=(P("pipe", "space", None, None), P("pipe", None, None, None)),
        check_vma=False,
    )
```

time: 946 us -> 207 us (0.22); the launches traced: 928 us -> 207 us
  waiting for transfers between devices: 321 us -> 50.5 us
  local copies, waits for them, and re-layouts: 215 us -> 7.37 us
  starting transfers between devices: 224 us -> 22.2 us
  other arithmetic: 93.3 us -> 2.09 us
  blocking collectives: 0 us -> 83.7 us
  between operations: 46.7 us -> 2.2 us
  Pallas kernels: 0 us -> 38.9 us
  matrix products: 28.7 us -> 0 us
    psum x1 -> x0, waiting for transfers between devices: 307 us -> none  [body(): total = lax.psum(terms, 'space')]
    ppermute x51 -> x9, starting transfers between devices: 224 us -> 22.2 us  [the longest x1 8.79 us: body(): right = lax.ppermute(own, both, between(0, -1, same))]
    reshape x95 -> x2, local copies, waits for them, and re-layouts: 74.9 us -> 1.44 us  [the longest x1 1.43 us: body(): terms.reshape(COLS, CHUNK, C)]
    slice x57 -> x0, local copies, waits for them, and re-layouts: 49.8 us -> none  [the longest x40 31.4 us: take_layer(): return lax.slice_in_dim(block, start, start + 1, axis=axis)]
    all_gather x0 -> x2, blocking collectives: none -> 47.8 us  [the longest x1 24 us: body(): whole = lax.all_gather(part.astype(BF16), 'space', axis_index_groups=near)]
    mul x55 -> x1, other arithmetic: 42.1 us -> 0.07 us  [body(): return (out.reshape(1, 1, C, CELLS), (total * scale).reshape(1, TAPS, C, C))]
    pallas_call x0 -> x6, Pallas kernels: none -> 38.9 us  [the longest x1 13.1 us: body(): call(first_kernel, [((C, 14 * WIDE), BF16), ((C, 14 * WIDE), F32), ((TAPS...]
    ppermute x51 -> x9, waiting for transfers between devices: 14.2 us -> 50.5 us  [the longest x1 23.1 us: body(): from_left = lax.ppermute(right, both, between(0, 1, [(1, 0)]))]
  transfers between devices with their start and end apart: 52 -> 9, of which waited for: 4 -> 4; matrix products, arithmetic and copies ran while one was open for 22% -> 0% of each run, Pallas kernels for 0% -> 1%
where the time goes in v1:
time: 207 us
  blocking collectives  83.7 us (40%)
  waiting for transfers between devices  50.5 us (24%)
  Pallas kernels  38.9 us (19%)
  starting transfers between devices  22.2 us (11%)
  local copies, waits for them, and re-layouts  7.37 us (4%)
  between operations  2.2 us (1%)
  other arithmetic  2.09 us (1%)
    all_gather x1, blocking collectives, body(): whole = lax.all_gather(part.astype(BF16), 'space', axis_index_groups=near)  24 us
    all_gather x1, blocking collectives, body(): lax.all_gather(piece, 'space', axis_index_groups=far).reshape(CHUNK, C)  23.8 us
    ppermute x1, waiting for transfers between devices, body(): from_left = lax.ppermute(right, both, between(0, 1, [(1, 0)]))  23.1 us
    ppermute x1, waiting for transfers between devices, body(): after = lax.ppermute(down, both, between(-1, 0, same))  20.9 us
    all_to_all x1, blocking collectives, body(): lax.all_to_all(part.reshape(ROWS, CHUNK // ROWS, C), 'space', 0, 0, axis_...  18.8 us
    all_to_all x1, blocking collectives, body(): lax.all_to_all(terms.reshape(COLS, CHUNK, C), 'space', 0, 0, axis_index_g...  17.1 us
    pallas_call x1, Pallas kernels, body(): call(first_kernel, [((C, 14 * WIDE), BF16), ((C, 14 * WIDE), F32), ((TAPS...  13.1 us
    ppermute x1, starting transfers between devices, body(): right = lax.ppermute(own, both, between(0, -1, same))  8.79 us
  transfers between devices with their start and end apart: 9, of which 4 were waited for; matrix products, arithmetic and copies ran while one was open for 0% of the time, Pallas kernels for 1%

profile of v1, /device:TPU:1, one launch (start us, length us, event | category | flops | bytes accessed | tf_op | source)
XLA Modules:
  0.0 206.9 jit_solution(5562771557809504527)
XLA Ops:
  1.3 0.1 pad.2.clone
  1.4 1.0 maximum_maximum_fusion.own_ref
  2.4 0.0 copy-start
  2.4 8.8 %collective-permute-start.1 = (bf16[208,512]{1,0:T(8,128)(2,1)S(1)}, bf16[208,512]{1,0:T(8,128)(2,1)S(1)}, u32[]{:S(2)}, u32[]{:S(2)}) collective-permute-start(bf16[208,512]{1,0:T(8,128)(2,1)S(1)} %maximum_maximum_fusion.own_ref), channel_id=1, source_target_pairs={{4,0},{5,1},{6,2},{7,3},{8,4},{9,5},{10,6},{11,7},{12,8},{13,9},{1... | collective-permute-start | bytes 638984 | tf_op jit(solution)/shard_map/ppermute | solution.py:314
  11.2 1.9 collective-permute-start
  13.1 0.0 collective-permute-done.1.right_ref
  13.2 0.0 copy-start.5
  13.2 2.7 %collective-permute-done.left_ref = bf16[208,512]{1,0:T(8,128)(2,1)S(1)} collective-permute-done((bf16[208,512]{1,0:T(8,128)(2,1)S(1)}, bf16[208,512]{1,0:T(8,128)(2,1)S(1)}, u32[]{:S(2)}, u32[]{:S(2)}) %collective-permute-start) | collective-permute-done | bytes 213024 | tf_op jit(solution)/shard_map/ppermute | solution.py:313
  15.9 0.0 copy-done
  15.9 0.0 copy-done.5
  15.9 0.0 copy-start.6
  15.9 0.7 copy-done.6
  16.6 2.5 %shard_map.59 = (bf16[208,1024]{1,0:T(8,128)(2,1)}, bf16[96,1280]{1,0:T(8,128)(2,1)}, bf16[96,1280]{1,0:T(8,128)(2,1)}) custom-call(bf16[208,512]{1,0:T(8,128)(2,1)} %copy-done, bf16[208,512]{1,0:T(8,128)(2,1)} %copy-done.6, bf16[208,512]{1,0:T(8,128)(2,1)} %copy-done.5), custom_call_target="tpu_custom_call" | custom-call | tf_op jit(solution)/shard_map/pallas_call | solution.py:315
  19.1 5.0 %collective-permute-start.2 = (bf16[96,1280]{1,0:T(8,128)(2,1)}, bf16[96,1280]{1,0:T(8,128)(2,1)S(1)}, u32[]{:S(2)}, u32[]{:S(2)}) collective-permute-start(bf16[96,1280]{1,0:T(8,128)(2,1)} %get-tuple-element.24), channel_id=1, source_target_pairs={{0,32},{1,33},{2,34},{3,35},{4,36},{5,37},{6,38},{7,39},{8,40},{9,... | collective-permute-start | bytes 737288 | tf_op jit(solution)/shard_map/ppermute | solution.py:319
  24.0 1.3 collective-permute-start.3
  25.3 2.8 %shard_map.60 = (bf16[96,2592]{1,0:T(8,128)(2,1)}, bf16[96,2592]{1,0:T(8,128)(2,1)}) custom-call(bf16[27,96,96]{2,1,0:T(8,128)(2,1)} %bitcast.12), custom_call_target="tpu_custom_call" | custom-call | tf_op jit(solution)/shard_map/pallas_call | solution.py:312
  28.2 3.8 %collective-permute-done.2.before_ref = bf16[96,1280]{1,0:T(8,128)(2,1)S(1)} collective-permute-done((bf16[96,1280]{1,0:T(8,128)(2,1)}, bf16[96,1280]{1,0:T(8,128)(2,1)S(1)}, u32[]{:S(2)}, u32[]{:S(2)}) %collective-permute-start.2) | collective-permute-done | bytes 245792 | tf_op jit(solution)/shard_map/ppermute | solution.py:319
  31.9 0.0 copy-start.3
  31.9 20.9 %collective-permute-done.3.after_ref = bf16[96,1280]{1,0:T(8,128)(2,1)S(1)} collective-permute-done((bf16[96,1280]{1,0:T(8,128)(2,1)}, bf16[96,1280]{1,0:T(8,128)(2,1)S(1)}, u32[]{:S(2)}, u32[]{:S(2)}) %collective-permute-start.3) | collective-permute-done | bytes 245792 | tf_op jit(solution)/shard_map/ppermute | solution.py:320
  52.8 0.0 copy-start.4
  52.8 0.6 mul.12.active_ref
  53.4 0.0 copy-done.3
  53.4 0.1 copy-done.4
  53.5 13.1 %shard_map.61 = (bf16[96,1792]{1,0:T(8,128)(2,1)}, f32[96,1792]{1,0:T(8,128)}, bf16[27,16,2048]{2,1,0:T(8,128)(2,1)}, bf16[96,1280]{1,0:T(8,128)(2,1)}, bf16[96,...) custom-call(bf16[208,1024]{1,0:T(8,128)(2,1)} %get-tuple-element.23.own_ref, bf16[96,1280]{1,0:T(8,128)(2,1)} %copy-done.3, ...), custom_call_target="tpu_custom_call" | custom-call | tf_op jit(solution)/shard_map/pallas_call | solution.py:325
  66.6 0.7 collective-permute-start.4
  67.3 0.0 collective-permute-done.4.incoming_ref
  67.3 0.0 copy-start.1
  67.3 0.7 copy-done.1
  68.1 6.3 %shard_map.62 = (bf16[96,1536]{1,0:T(8,128)(2,1)}, bf16[96,1024]{1,0:T(8,128)(2,1)}, bf16[96,1024]{1,0:T(8,128)(2,1)}) custom-call(bf16[96,1792]{1,0:T(8,128)(2,1)} %copy-done.1, f32[96,1792]{1,0:T(8,128)} %get-tuple-element.29.slope_ref, bf16[27,16,2048]{2,1,0:T(8,128)(2,1)} %get-tuple-element.30.mask_ref, bf16[96,2592]{1,0:T(8,128)(2,1)} %get-tuple-element.27.bwd_ref, ...), custom_call_target="tpu_custom_call" | custom-call | tf_op jit(solution)/shard_map/pallas_call | solution.py:333
  74.3 0.7 collective-permute-start.5
  75.0 0.0 collective-permute-done.5.incoming_ref
  75.0 0.0 copy-start.2
  75.0 0.7 copy-done.2
  75.7 5.8 %shard_map.63 = (bf16[96,640]{1,0:T(8,128)(2,1)}, bf16[96,128]{1,0:T(8,128)(2,1)}, bf16[96,128]{1,0:T(8,128)(2,1)}, bf16[96,1024]{1,0:T(8,128)(2,1)}, bf16[96,1024]{1,0:T(8,128)(2,1)}) custom-call(bf16[96,1536]{1,0:T(8,128)(2,1)} %copy-done.2, f32[96,1792]{1,0:T(8,128)} %get-tuple-element.29.slope_ref, bf16[27,16,2048]{2,1,0:T(8,128)(2,1)} %get-tuple-element.30.mask_ref, ...), custom_call_target="tpu_custom_call" | custom-call | tf_op jit(solution)/shard_map/pallas_call | solution.py:339
  81.5 1.3 collective-permute-start.6
  82.8 1.3 collective-permute-start.7
  84.1 1.3 collective-permute-start.8
  85.4 23.1 %collective-permute-done.7.from_left = bf16[96,128]{1,0:T(8,128)(2,1)S(1)} collective-permute-done((bf16[96,128]{1,0:T(8,128)(2,1)}, bf16[96,128]{1,0:T(8,128)(2,1)S(1)}, u32[]{:S(2)}, u32[]{:S(2)}) %collective-permute-start.7) | collective-permute-done | bytes 24608 | tf_op jit(solution)/shard_map/ppermute | solution.py:345
  108.4 0.0 copy-start.8
  108.4 0.0 collective-permute-done.8.from_right
  108.5 0.0 copy-start.9
  108.5 0.0 collective-permute-done.6.centre_ref
  108.5 0.0 copy-start.7
  108.5 0.6 copy-done.8
  109.0 0.0 copy-done.9
  109.0 0.1 copy-done.7
  109.1 8.5 %shard_map.64 = (bf16[96,512]{1,0:T(8,128)(2,1)}, bf16[2688,96]{1,0:T(8,128)(2,1)}) custom-call(bf16[96,640]{1,0:T(8,128)(2,1)} %copy-done.7, bf16[96,128]{1,0:T(8,128)(2,1)} %copy-done.8, bf16[96,128]{1,0:T(8,128)(2,1)} %copy-done.9, f32[96,1792]{1,0:T(8,128)} %get-tuple-element.29.slope_ref, bf16[27,16,2048]{2,1,0:T(8,128)(2,1)} %get-tuple-element.30.mask_ref, ...), custom_call_target="tpu_custom_call" | custom-call | tf_op jit(solution)/shard_map/pallas_call | solution.py:347
  117.6 1.4 copy.16
  119.0 17.1 %all_to_all.10 = bf16[8,336,96]{1,2,0:T(8,128)(2,1)S(1)} all-to-all(bf16[8,336,96]{1,2,0:T(8,128)(2,1)S(1)} %copy.16), channel_id=1, replica_groups={{0,4,128,132,256,260,384,388},{8,12,136,140,264,268,392,396},{16,20,144..., dimensions={0} | all-to-all | bytes 1032192 | tf_op jit(solution)/shard_map/all_to_all | solution.py:354
  136.1 0.1 convert_reduce_fusion
  136.2 0.1 copy.17
  136.3 18.8 %all_to_all.11 = f32[16,21,96]{2,1,0:T(8,128)S(1)} all-to-all(f32[16,21,96]{2,1,0:T(8,128)S(1)} %reshape.42), channel_id=1, replica_groups={{0,8,16,24,32,40,48,56,64,72,80,88,96,104,112,120},{4,12,20,28,36,44,52..., dimensions={0} | all-to-all | bytes 258048 | tf_op jit(solution)/shard_map/all_to_all | solution.py:358
  155.1 23.8 %all-gather.2 = bf16[16,21,96]{2,1,0:T(8,128)(2,1)S(1)} all-gather(bf16[1,21,96]{2,1,0:T(8,128)(2,1)S(1)} %bitcast.15), channel_id=2, replica_groups={{0,8,16,24,32,40,48,56,64,72,80,88,96,104,112,120},{4,12,20,28,36,44,52..., dimensions={0}, use_global_device_ids=true | all-gather | bytes 68544 | tf_op jit(solution)/shard_map/all_gather | solution.py:362
  179.0 0.1 copy.18
  179.1 24.0 %all-gather.3 = bf16[8,336,96]{1,2,0:T(8,128)(2,1)S(1)} all-gather(bf16[1,336,96]{1,2,0:T(8,128)(2,1)S(1)} %copy.18), channel_id=3, replica_groups={{0,4,128,132,256,260,384,388},{8,12,136,140,264,268,392,396},{16,20,144..., dimensions={0}, use_global_device_ids=true | all-gather | bytes 580608 | tf_op jit(solution)/shard_map/all_gather | solution.py:363
  203.1 0.2 copy.19
  203.3 0.4 reshape.54
  203.8 0.9 fusion
  205.3 0.1 convert_multiply_fusion
  205.4 1.5 copy.20
  (4 shorter events, 0.1 us)
Async XLA Ops:
  2.4 13.5 %copy-start = (bf16[208,512]{1,0:T(8,128)(2,1)}, bf16[208,512]{1,0:T(8,128)(2,1)S(1)}, u32[]{:S(2)}) copy-start(bf16[208,512]{1,0:T(8,128)(2,1)S(1)} %maximum_maximum_fusion.own_ref) | copy-start | bytes 638980
  2.4 10.7 %collective-permute-start.1 = (bf16[208,512]{1,0:T(8,128)(2,1)S(1)}, bf16[208,512]{1,0:T(8,128)(2,1)S(1)}, u32[]{:S(2)}, u32[]{:S(2)}) collective-permute-start(bf16[208,512]{1,0:T(8,128)(2,1)S(1)} %maximum_maximum_fusion.own_ref), channel_id=1, source_target_pairs={{4,0},{5,1},{6,2},{7,3},{8,4},{9,5},{10,6},{11,7},{12,8},{13,9},{1... | collective-permute-start | bytes 638984 | tf_op jit(solution)/shard_map/ppermute | solution.py:314
  11.2 4.7 %collective-permute-start = (bf16[208,512]{1,0:T(8,128)(2,1)S(1)}, bf16[208,512]{1,0:T(8,128)(2,1)S(1)}, u32[]{:S(2)}, u32[]{:S(2)}) collective-permute-start(bf16[208,512]{1,0:T(8,128)(2,1)S(1)} %maximum_maximum_fusion.own_ref), channel_id=1, source_target_pairs={{0,4},{1,5},{2,6},{3,7},{4,8},{5,9},{6,10},{7,11},{8,12},{9,13},{1... | collective-permute-start | bytes 638984 | tf_op jit(solution)/shard_map/ppermute | solution.py:313
  13.2 2.8 %copy-start.5 = (bf16[208,512]{1,0:T(8,128)(2,1)}, bf16[208,512]{1,0:T(8,128)(2,1)S(1)}, u32[]{:S(2)}) copy-start(bf16[208,512]{1,0:T(8,128)(2,1)S(1)} %collective-permute-done.1.right_ref) | copy-start | bytes 638980
  15.9 0.7 copy-start.6
  19.1 12.9 %collective-permute-start.2 = (bf16[96,1280]{1,0:T(8,128)(2,1)}, bf16[96,1280]{1,0:T(8,128)(2,1)S(1)}, u32[]{:S(2)}, u32[]{:S(2)}) collective-permute-start(bf16[96,1280]{1,0:T(8,128)(2,1)} %get-tuple-element.24), channel_id=1, source_target_pairs={{0,32},{1,33},{2,34},{3,35},{4,36},{5,37},{6,38},{7,39},{8,40},{9,... | collective-permute-start | bytes 737288 | tf_op jit(solution)/shard_map/ppermute | solution.py:319
  24.0 28.8 %collective-permute-start.3 = (bf16[96,1280]{1,0:T(8,128)(2,1)}, bf16[96,1280]{1,0:T(8,128)(2,1)S(1)}, u32[]{:S(2)}, u32[]{:S(2)}) collective-permute-start(bf16[96,1280]{1,0:T(8,128)(2,1)} %get-tuple-element.25), channel_id=1, source_target_pairs={{32,0},{33,1},{34,2},{35,3},{36,4},{37,5},{38,6},{39,7},{40,8},{41... | collective-permute-start | bytes 737288 | tf_op jit(solution)/shard_map/ppermute | solution.py:320
  31.9 21.5 %copy-start.3 = (bf16[96,1280]{1,0:T(8,128)(2,1)}, bf16[96,1280]{1,0:T(8,128)(2,1)S(1)}, u32[]{:S(2)}) copy-start(bf16[96,1280]{1,0:T(8,128)(2,1)S(1)} %collective-permute-done.2.before_ref) | copy-start | bytes 737284
  52.8 0.7 copy-start.4
  66.6 0.7 collective-permute-start.4
  67.3 0.8 copy-start.1
  74.3 0.7 collective-permute-start.5
  75.0 0.7 copy-start.2
  81.5 27.0 %collective-permute-start.6 = (bf16[96,640]{1,0:T(8,128)(2,1)}, bf16[96,640]{1,0:T(8,128)(2,1)S(1)}, u32[]{:S(2)}, u32[]{:S(2)}) collective-permute-start(bf16[96,640]{1,0:T(8,128)(2,1)} %get-tuple-element.36), channel_id=1, source_target_pairs={{1,0},{5,4},{9,8},{13,12},{17,16},{21,20},{25,24},{29,28},{33,32},... | collective-permute-start | bytes 368648 | tf_op jit(solution)/shard_map/ppermute | solution.py:344
  82.8 25.7 %collective-permute-start.7 = (bf16[96,128]{1,0:T(8,128)(2,1)}, bf16[96,128]{1,0:T(8,128)(2,1)S(1)}, u32[]{:S(2)}, u32[]{:S(2)}) collective-permute-start(bf16[96,128]{1,0:T(8,128)(2,1)} %get-tuple-element.37), channel_id=1, source_target_pairs={{1,4},{5,8},{9,12},{13,16},{17,20},{21,24},{25,28},{33,36},{37,40}... | collective-permute-start | bytes 73736 | tf_op jit(solution)/shard_map/ppermute | solution.py:345
  84.1 24.4 %collective-permute-start.8 = (bf16[96,128]{1,0:T(8,128)(2,1)}, bf16[96,128]{1,0:T(8,128)(2,1)S(1)}, u32[]{:S(2)}, u32[]{:S(2)}) collective-permute-start(bf16[96,128]{1,0:T(8,128)(2,1)} %get-tuple-element.38), channel_id=1, source_target_pairs={{5,0},{9,4},{13,8},{17,12},{21,16},{25,20},{29,24},{37,32},{41,36}... | collective-permute-start | bytes 73736 | tf_op jit(solution)/shard_map/ppermute | solution.py:346
  108.4 0.6 copy-start.8
  108.5 0.6 copy-start.9
  108.5 0.7 copy-start.7

commit v2 on v1

--- a/solution.py
+++ b/solution.py
@@ -16,7 +16,7 @@
 DEEP = TAPS * C
 WIDE = 128
 CODE = 8
-CHUNK = 336
+CHUNK = 384
 VMEM_BYTES = 56 * 1024 * 1024
 F32 = jnp.float32
 BF16 = jnp.bfloat16
@@ -78,6 +78,7 @@
 
 
 def pack_kernel(own_ref, left_ref, right_ref, own_out, up_out, down_out):
+    lowest = lax.axis_index("pipe") == 0
     rows = []
     for i in range(8):
         at = 64 * i
@@ -92,46 +93,60 @@
             )
         )
         own_out[:, lane(i)] = rows[i]
-    codes = jnp.concatenate([rows[0][2 * C :]] * (C // 16), 0)
-    for out, first in ((up_out, 3), (down_out, 0)):
-        for n in range(5):
-            out[:, lane(n)] = rows[first + n][:C]
-        for n in range(4):
-            row = first + n + (1 if first else 0)
-            out[:, lane(5 + n)] = rows[row][C : 2 * C]
-        out[:, lane(9)] = codes
-
-
-def first_kernel(
-    own_ref, before_ref, after_ref, fwd_ref, bwd_ref, active_ref,
-    result_ref, slope_ref, mask_ref, x_ref, grad_ref, out_ref,
-    base_ref, cols_ref, code_ref, top_ref, pre_ref,
+    code = jnp.concatenate([rows[0][2 * C :]] * (C // 16), 0)
+    own_code = jnp.concatenate([own_ref[2 * C :, :WIDE]] * (C // 16), 0)
+    where = lax.broadcasted_iota(jnp.int32, (C, WIDE), 1)
+    for out, order, tops in (
+        (up_out, (3, 4, 5, None, 6, 7), (4, 5, 6, 7)),
+        (down_out, (2, 3, 4, None, 0, 1), (0, 1, 2, 3)),
+    ):
+
+        @pl.when(jnp.logical_not(lowest))
+        def _(out=out, order=order):
+            for slot, row in enumerate(order):
+                out[:, lane(slot)] = code if row is None else rows[row][:C]
+
+        @pl.when(lowest)
+        def _(out=out, order=order, tops=tops):
+            tiles = [rows[row][C : 2 * C] for row in tops]
+            out[:, lane(0)] = jnp.where((where < 8) | (where >= 120), code, tiles[0])
+            out[:, lane(1)] = jnp.where(where < 8, own_code, tiles[1])
+            out[:, lane(2)] = tiles[2]
+            out[:, lane(3)] = tiles[3]
+            out[:, lane(4)] = rows[order[4]][:C]
+            out[:, lane(5)] = rows[order[5]][:C]
+
+
+def side_code(side_ref):
+    where = lax.broadcasted_iota(jnp.int32, (8, WIDE), 1)
+    first, second = side_ref[0:8, lane(0)].astype(F32), side_ref[0:8, lane(1)].astype(F32)
+    parts = jnp.where(
+        where < 32, first[:, 0:1], jnp.where(where < 96, second[:, 0:1], first[:, 127:128])
+    )
+    return jnp.where(lax.axis_index("pipe") == 0, parts, side_ref[0:8, lane(3)].astype(F32))
+
+
+def forward_kernel(
+    own_ref, before_ref, after_ref, fwd_ref,
+    slope_ref, mask_ref, x_ref,
+    base_ref, cols_ref, code_ref, pre_ref,
 ):
-    active = active_ref[0:1, 0:1]
     own_code = own_ref[2 * C : 2 * C + 8, :WIDE].astype(F32)
-    before_code = before_ref[0:8, lane(9)].astype(F32)
-    after_code = after_ref[0:8, lane(9)].astype(F32)
+    before_code = side_code(before_ref)
+    after_code = side_code(after_ref)
     for row in range(18):
         code = before_code if row < 5 else own_code if row < 13 else after_code
         code_ref[:, lane(row)] = code
     for row in range(18):
         if row < 5:
-            tile = before_ref[:, lane(row)]
+            tile = before_ref[:, lane((0, 1, 2, 4, 5)[row])]
         elif row < 13:
             tile = own_ref[:C, lane(row - 5)]
         else:
-            tile = after_ref[:, lane(row - 13)]
+            tile = after_ref[:, lane((4, 5, 0, 1, 2)[row - 13])]
         if 4 <= row < 14:
             x_ref[:, lane(row - 4)] = tile
         shifted_rows(base_ref, row, tile)
-    for row in range(1, 17):
-        if row < 5:
-            tile = before_ref[:, lane(4 + row)]
-        elif row < 13:
-            tile = own_ref[C : 2 * C, lane(row - 5)]
-        else:
-            tile = after_ref[:, lane(5 + row - 13)]
-        top_ref[:, lane(row - 1)] = tile.astype(F32) * active
 
     level = lax.broadcasted_iota(jnp.int32, (8, WIDE), 1) % 8
     rise_of = {
@@ -163,29 +178,37 @@
     for row in range(16):
         pre = pre_ref[:, lane(row)]
         sigma = 1.0 / (1.0 + jnp.exp(-pre))
-        slope = sigma * (1.0 + pre * (1.0 - sigma))
-        grad = (top_ref[:, lane(row)] * slope).astype(BF16)
-        if 1 <= row < 15:
-            slope_ref[:, lane(row - 1)] = slope
-        if 4 <= row < 12:
-            grad_ref[:, lane(row - 4)] = grad
-        shifted_rows(base_ref, row, grad)
-
-    def backward(pair, carry):
-        make_cols(cols_ref, base_ref, mask_ref, 2 * pair + 1, 2 * pair + 1)
-        total = top_ref[:, lane(2 * pair + 1, 2)] + product(bwd_ref[...], cols_ref[...])
-        result_ref[:, lane(2 * pair, 2)] = total.astype(BF16)
-        return carry
-
-    lax.fori_loop(0, 7, backward, 0)
+        slope_ref[:, lane(row)] = sigma * (1.0 + pre * (1.0 - sigma))
+
+
+def top_kernel(
+    own_ref, before_ref, after_ref, slope_ref, mask_ref, bwd_ref,
+    result_ref, grad_ref, out_ref,
+    base_ref, cols_ref, top_ref,
+):
+    active = lax.axis_index("pipe") == SECTIONS - 1
+    for row in range(1, 17):
+        if row < 5:
+            tile = before_ref[:, lane(row - 1)]
+        elif row < 13:
+            tile = own_ref[C : 2 * C, lane(row - 5)]
+        else:
+            tile = after_ref[:, lane(row - 13)]
+        top_ref[:, lane(row - 1)] = jnp.where(active, tile, jnp.zeros_like(tile))
+
+    def store(pair, value):
+        result_ref[:, lane(2 * pair, 2)] = value
+
+    step_rows(top_ref, slope_ref, mask_ref, bwd_ref, base_ref, cols_ref, store, 16, 1)
     for row in range(8):
+        grad_ref[:, lane(row)] = base_ref[4, :, lane(row + 4)]
         out_ref[:, lane(row)] = result_ref[:, lane(row + 3)]
 
 
 def step_rows(incoming_ref, slope_ref, mask_ref, bwd_ref, base_ref, cols_ref, store, count, first):
     for row in range(count):
         grad = (
-            incoming_ref[:, lane(row)].astype(F32) * slope_ref[:, lane(row + first - 2)]
+            incoming_ref[:, lane(row)].astype(F32) * slope_ref[:, lane(row + first - 1)]
         ).astype(BF16)
         shifted_rows(base_ref, row, grad)
 
@@ -279,8 +302,16 @@
             all_ref[C * tap : C * tap + C, :], grads, (((1,), (1,)), ((), ())),
             preferred_element_type=F32,
         )
-        terms_ref[C * tap : C * tap + C, :] = part.astype(BF16)
-    terms_ref[DEEP:, :] = jnp.zeros((COLS * CHUNK - DEEP, C), BF16)
+        terms_ref[C * tap : C * tap + C, :] = jnp.concatenate(
+            [part, jnp.zeros((C, WIDE - C), F32)], 1
+        ).astype(BF16)
+    terms_ref[DEEP:, :] = jnp.zeros((COLS * CHUNK - DEEP, WIDE), BF16)
+
+
+def scale_kernel(whole_ref, out_ref):
+    total = whole_ref[:DEEP, :C].astype(F32)
+    mean = jnp.sum(total * total) / (DEEP * C)
+    out_ref[...] = total * lax.rsqrt(mean + 1e-06)
 
 
 def groups(devices):
@@ -292,7 +323,6 @@
 
 def body(section_input, top_grad, conv_weight, brick_height):
     devices = lax.axis_size("space")
-    section = lax.axis_index("pipe")
     both = ("space", "pipe")
 
     def between(by_row, by_col, sections):
@@ -314,21 +344,25 @@
     right = lax.ppermute(own, both, between(0, -1, same))
     own, up, down = call(
         pack_kernel,
-        [((2 * C + 16, 8 * WIDE), BF16), ((C, 10 * WIDE), BF16), ((C, 10 * WIDE), BF16)],
+        [((2 * C + 16, 8 * WIDE), BF16), ((C, 6 * WIDE), BF16), ((C, 6 * WIDE), BF16)],
     )(own, left, right)
     before = lax.ppermute(up, both, between(1, 0, same))
     after = lax.ppermute(down, both, between(-1, 0, same))
-    active = jnp.where(section == SECTIONS - 1, 1.0, 0.0) * jnp.ones((8, WIDE), F32)
+    top_before = lax.ppermute(before, both, between(0, 0, [(0, SECTIONS - 1)]))
+    top_after = lax.ppermute(after, both, between(0, 0, [(0, SECTIONS - 1)]))
 
     core = ((C, 8 * WIDE), BF16)
     cols = ((DEEP, 2 * WIDE), BF16)
-    result, slope, mask, x_rows, grad, out = call(
-        first_kernel,
-        [((C, 14 * WIDE), BF16), ((C, 14 * WIDE), F32), ((TAPS, 16, 16 * WIDE), BF16),
-         ((C, 10 * WIDE), BF16), core, core],
-        [((9, C, 18 * WIDE), BF16), cols, ((8, 18 * WIDE), F32), ((C, 16 * WIDE), F32),
-         ((C, 16 * WIDE), F32)],
-    )(own, before, after, fwd, bwd, active)
+    slope, mask, x_rows = call(
+        forward_kernel,
+        [((C, 16 * WIDE), F32), ((TAPS, 16, 16 * WIDE), BF16), ((C, 10 * WIDE), BF16)],
+        [((9, C, 18 * WIDE), BF16), cols, ((8, 18 * WIDE), F32), ((C, 16 * WIDE), F32)],
+    )(own, before, after, fwd)
+    result, grad, out = call(
+        top_kernel,
+        [((C, 14 * WIDE), BF16), core, core],
+        [((9, C, 16 * WIDE), BF16), cols, ((C, 16 * WIDE), BF16)],
+    )(own, top_before, top_after, slope, mask, bwd)
     incoming = lax.ppermute(result, both, between(0, 0, [(3, 2)]))
     result, grad, out = call(
         functools.partial(middle_kernel, 14, 2),
@@ -346,24 +380,24 @@
     from_right = lax.ppermute(left, both, between(0, -1, [(1, 0)]))
     out, terms = call(
         last_kernel,
-        [((C, CELLS), BF16), ((COLS * CHUNK, C), BF16)],
+        [((C, CELLS), BF16), ((COLS * CHUNK, WIDE), BF16)],
         [((9, C, 10 * WIDE), BF16), cols, ((C, 10 * WIDE), BF16), core, ((DEEP, 8 * WIDE), BF16)],
     )(centre, from_left, from_right, slope, mask, bwd, x_rows, grad, out)
 
     near, far = groups(devices)
     parts = lax.all_to_all(
-        terms.reshape(COLS, CHUNK, C), "space", 0, 0, axis_index_groups=near
-    )
-    part = jnp.sum(parts.astype(F32), 0)
+        terms.reshape(COLS, CHUNK, WIDE), "space", 0, 0, axis_index_groups=near
+    )
+    part = jnp.sum(parts.astype(F32), 0).astype(BF16)
     pieces = lax.all_to_all(
-        part.reshape(ROWS, CHUNK // ROWS, C), "space", 0, 0, axis_index_groups=far
-    )
-    piece = jnp.sum(pieces, 0)
-    part = lax.all_gather(piece, "space", axis_index_groups=far).reshape(CHUNK, C)
-    whole = lax.all_gather(part.astype(BF16), "space", axis_index_groups=near)
-    total = whole.reshape(COLS * CHUNK, C)[:DEEP].astype(F32)
-    scale = lax.rsqrt(jnp.sum(total * total) / (DEEP * C) + 1e-06)
-    return (out.reshape(1, 1, C, CELLS), (total * scale).reshape(1, TAPS, C, C))
+        part.reshape(ROWS, CHUNK // ROWS, WIDE), "space", 0, 0, axis_index_groups=far
+    )
+    piece = jnp.sum(pieces.astype(F32), 0).astype(BF16)
+    copies = jnp.broadcast_to(piece[None], (ROWS,) + piece.shape)
+    part = lax.all_to_all(copies, "space", 0, 0, axis_index_groups=far)
+    whole = lax.all_gather(part.reshape(CHUNK, WIDE), "space", axis_index_groups=near)
+    (weight_grad,) = call(scale_kernel, [((DEEP, C), F32)])(whole.reshape(COLS * CHUNK, WIDE))
+    return (out.reshape(1, 1, C, CELLS), weight_grad.reshape(1, TAPS, C, C))
 
 
 def solution(mesh):

time: 207 us -> 190 us (0.918)
  waiting for transfers between devices: 50.5 us -> 35.2 us
  blocking collectives: 83.7 us -> 69.7 us
  starting transfers between devices: 22.2 us -> 34.1 us
  Pallas kernels: 38.9 us -> 44 us
  local copies, waits for them, and re-layouts: 7.37 us -> 3.57 us
    all_gather x2 -> x1, blocking collectives: 47.8 us -> 17.3 us  [body(): lax.all_gather(part.reshape(CHUNK, WIDE), 'space', axis_index_groups=near)]
    ppermute x1, waiting for transfers between devices: 0.01 us -> 25 us  [body(): from_right = lax.ppermute(left, both, between(0, -1, [(1, 0)]))]
    ppermute x1, waiting for transfers between devices: 23.1 us -> 0.01 us  [body(): from_left = lax.ppermute(right, both, between(0, 1, [(1, 0)]))]
    all_to_all x2 -> x3, blocking collectives: 35.8 us -> 52.4 us  [the longest x1 19.4 us: body(): lax.all_to_all(part.reshape(ROWS, CHUNK // ROWS, WIDE), 'space', 0, 0, ax...]
    ppermute x1, waiting for transfers between devices: 20.9 us -> 4.89 us  [body(): after = lax.ppermute(down, both, between(-1, 0, same))]
    ppermute x0 -> x2, starting transfers between devices: none -> 8.72 us  [the longest x1 4.36 us: body(): top_after = lax.ppermute(after, both, between(0, 0, [(0, SECTIONS - 1)]))]
    pallas_call x3 -> x5, Pallas kernels: 24.1 us -> 29.1 us  [the longest x1 8.57 us: body(): call(last_kernel, [((C, CELLS), BF16), ((COLS * CHUNK, WIDE), BF16)], [((...]
    ppermute x1, starting transfers between devices: 4.96 us -> 8.81 us  [body(): before = lax.ppermute(up, both, between(1, 0, same))]
  transfers between devices with their start and end apart: 9 -> 11, of which waited for: 4 -> 4; matrix products, arithmetic and copies ran while one was open for 0% -> 0% of each run, Pallas kernels for 1% -> 6%
where the time goes in v2:
time: 190 us; the launch traced here: 189 us
  blocking collectives  69.7 us (37%)
  Pallas kernels  44 us (23%)
  waiting for transfers between devices  35.2 us (19%)
  starting transfers between devices  34.1 us (18%)
  local copies, waits for them, and re-layouts  3.57 us (2%)
    ppermute x1, waiting for transfers between devices, body(): from_right = lax.ppermute(left, both, between(0, -1, [(1, 0)]))  25 us
    all_to_all x1, blocking collectives, body(): lax.all_to_all(part.reshape(ROWS, CHUNK // ROWS, WIDE), 'space', 0, 0, ax...  19.4 us
    all_gather x1, blocking collectives, body(): lax.all_gather(part.reshape(CHUNK, WIDE), 'space', axis_index_groups=near)  17.3 us
    all_to_all x1, blocking collectives, body(): lax.all_to_all(terms.reshape(COLS, CHUNK, WIDE), 'space', 0, 0, axis_inde...  16.8 us
    all_to_all x1, blocking collectives, body(): part = lax.all_to_all(copies, 'space', 0, 0, axis_index_groups=far)  16.3 us
    ppermute x1, starting transfers between devices, body(): before = lax.ppermute(up, both, between(1, 0, same))  8.81 us
    pallas_call x1, Pallas kernels, body(): call(last_kernel, [((C, CELLS), BF16), ((COLS * CHUNK, WIDE), BF16)], [((...  8.57 us
    pallas_call x1, Pallas kernels, body(): call(forward_kernel, [((C, 16 * WIDE), F32), ((TAPS, 16, 16 * WIDE), BF16...  8.26 us
  transfers between devices with their start and end apart: 11, of which 4 were waited for; matrix products, arithmetic and copies ran while one was open for 0% of the time, Pallas kernels for 6%

profile of v2, /device:TPU:1, one launch (start us, length us, event | category | flops | bytes accessed | tf_op | source)
XLA Modules:
  0.0 189.3 jit_solution(12181525124810545274)
XLA Ops:
  1.3 0.1 pad.2.clone
  1.4 1.0 maximum_maximum_fusion.own_ref
  2.4 0.0 copy-start
  2.4 4.9 %collective-permute-start = (bf16[208,512]{1,0:T(8,128)(2,1)S(1)}, bf16[208,512]{1,0:T(8,128)(2,1)S(1)}, u32[]{:S(2)}, u32[]{:S(2)}) collective-permute-start(bf16[208,512]{1,0:T(8,128)(2,1)S(1)} %maximum_maximum_fusion.own_ref), channel_id=1, source_target_pairs={{0,4},{1,5},{2,6},{3,7},{4,8},{5,9},{6,10},{7,11},{8,12},{9,13},{1... | collective-permute-start | bytes 638984 | tf_op jit(solution)/shard_map/ppermute | solution.py:343
  7.4 5.2 %collective-permute-start.1 = (bf16[208,512]{1,0:T(8,128)(2,1)S(1)}, bf16[208,512]{1,0:T(8,128)(2,1)S(1)}, u32[]{:S(2)}, u32[]{:S(2)}) collective-permute-start(bf16[208,512]{1,0:T(8,128)(2,1)S(1)} %maximum_maximum_fusion.own_ref), channel_id=1, source_target_pairs={{4,0},{5,1},{6,2},{7,3},{8,4},{9,5},{10,6},{11,7},{12,8},{13,9},{1... | collective-permute-start | bytes 638984 | tf_op jit(solution)/shard_map/ppermute | solution.py:344
  12.5 0.0 collective-permute-done.left_ref
  12.5 0.0 copy-start.3
  12.6 2.0 %collective-permute-done.1.right_ref = bf16[208,512]{1,0:T(8,128)(2,1)S(1)} collective-permute-done((bf16[208,512]{1,0:T(8,128)(2,1)S(1)}, bf16[208,512]{1,0:T(8,128)(2,1)S(1)}, u32[]{:S(2)}, u32[]{:S(2)}) %collective-permute-start.1) | collective-permute-done | bytes 213024 | tf_op jit(solution)/shard_map/ppermute | solution.py:344
  14.5 0.0 copy-done
  14.5 0.0 copy-done.3
  14.5 0.0 copy-start.4
  14.5 0.7 copy-done.4
  15.2 2.5 %shard_map.59 = (bf16[208,1024]{1,0:T(8,128)(2,1)}, bf16[96,768]{1,0:T(8,128)(2,1)}, bf16[96,768]{1,0:T(8,128)(2,1)}) custom-call(bf16[208,512]{1,0:T(8,128)(2,1)} %copy-done, bf16[208,512]{1,0:T(8,128)(2,1)} %copy-done.3, bf16[208,512]{1,0:T(8,128)(2,1)} %copy-done.4), custom_call_target="tpu_custom_call" | custom-call | tf_op jit(solution)/shard_map/pallas_call | solution.py:345
  17.7 8.8 %collective-permute-start.2 = (bf16[96,768]{1,0:T(8,128)(2,1)}, bf16[96,768]{1,0:T(8,128)(2,1)S(1)}, u32[]{:S(2)}, u32[]{:S(2)}) collective-permute-start(bf16[96,768]{1,0:T(8,128)(2,1)} %get-tuple-element.24), channel_id=1, source_target_pairs={{0,32},{1,33},{2,34},{3,35},{4,36},{5,37},{6,38},{7,39},{8,40},{9,... | collective-permute-start | bytes 442376 | tf_op jit(solution)/shard_map/ppermute | solution.py:349
  26.5 1.3 collective-permute-start.4
  27.8 3.4 %collective-permute-done.2.before_ref = bf16[96,768]{1,0:T(8,128)(2,1)S(1)} collective-permute-done((bf16[96,768]{1,0:T(8,128)(2,1)}, bf16[96,768]{1,0:T(8,128)(2,1)S(1)}, u32[]{:S(2)}, u32[]{:S(2)}) %collective-permute-start.2) | collective-permute-done | bytes 147488 | tf_op jit(solution)/shard_map/ppermute | solution.py:349
  31.2 0.0 copy-start.5
  31.2 4.4 %collective-permute-start.3 = (bf16[96,768]{1,0:T(8,128)(2,1)S(1)}, bf16[96,768]{1,0:T(8,128)(2,1)S(1)}, u32[]{:S(2)}, u32[]{:S(2)}) collective-permute-start(bf16[96,768]{1,0:T(8,128)(2,1)S(1)} %collective-permute-done.2.before_ref), channel_id=1, source_target_pairs={{0,3},{4,7},{8,11},{12,15},{16,19},{20,23},{24,27},{28,31},{32,35}... | collective-permute-start | bytes 442376 | tf_op jit(solution)/shard_map/ppermute | solution.py:351
  35.5 4.9 %collective-permute-done.4.after_ref = bf16[96,768]{1,0:T(8,128)(2,1)S(1)} collective-permute-done((bf16[96,768]{1,0:T(8,128)(2,1)}, bf16[96,768]{1,0:T(8,128)(2,1)S(1)}, u32[]{:S(2)}, u32[]{:S(2)}) %collective-permute-start.4) | collective-permute-done | bytes 147488 | tf_op jit(solution)/shard_map/ppermute | solution.py:350
  40.4 0.0 copy-start.6
  40.4 4.4 %collective-permute-start.5 = (bf16[96,768]{1,0:T(8,128)(2,1)S(1)}, bf16[96,768]{1,0:T(8,128)(2,1)S(1)}, u32[]{:S(2)}, u32[]{:S(2)}) collective-permute-start(bf16[96,768]{1,0:T(8,128)(2,1)S(1)} %collective-permute-done.4.after_ref), channel_id=1, source_target_pairs={{0,3},{4,7},{8,11},{12,15},{16,19},{20,23},{24,27},{28,31},{32,35}... | collective-permute-start | bytes 442376 | tf_op jit(solution)/shard_map/ppermute | solution.py:352
  44.8 2.8 %shard_map.60 = (bf16[96,2592]{1,0:T(8,128)(2,1)}, bf16[96,2592]{1,0:T(8,128)(2,1)}) custom-call(bf16[27,96,96]{2,1,0:T(8,128)(2,1)} %bitcast.13), custom_call_target="tpu_custom_call" | custom-call | tf_op jit(solution)/shard_map/pallas_call | solution.py:342
  47.6 0.0 copy-done.5
  47.6 0.0 copy-done.6
  47.6 8.3 %shard_map.61 = (f32[96,2048]{1,0:T(8,128)}, bf16[27,16,2048]{2,1,0:T(8,128)(2,1)}, bf16[96,1280]{1,0:T(8,128)(2,1)}) custom-call(bf16[208,1024]{1,0:T(8,128)(2,1)} %get-tuple-element.23.own_ref, bf16[96,768]{1,0:T(8,128)(2,1)} %copy-done.5, bf16[96,768]{1,0:T(8,128)(2,1)} %copy-done.6, bf16[96,2592]{1,0:T(8,128)(2,1)} %get-tuple-element.26.fwd_ref), custom_call_target="tpu_custom_call" | custom-call | tf_op jit(solution)/shard_map/pallas_call | solution.py:356
  55.9 0.0 collective-permute-done.3.before_ref
  55.9 0.0 copy-start.7
  55.9 0.0 collective-permute-done.5.after_ref
  55.9 0.0 copy-start.8
  55.9 0.6 copy-done.7
  56.5 0.0 copy-done.8
  56.5 7.0 %shard_map.62 = (bf16[96,1792]{1,0:T(8,128)(2,1)}, bf16[96,1024]{1,0:T(8,128)(2,1)}, bf16[96,1024]{1,0:T(8,128)(2,1)}) custom-call(bf16[208,1024]{1,0:T(8,128)(2,1)} %get-tuple-element.23.own_ref, bf16[96,768]{1,0:T(8,128)(2,1)} %copy-done.7, bf16[96,768]{1,0:T(8,128)(2,1)} %copy-done.8, f32[96,2048]{1,0:T(8,128)} %get-tuple-element.27.slope_ref, ...), custom_call_target="tpu_custom_call" | custom-call | tf_op jit(solution)/shard_map/pallas_call | solution.py:361
  63.6 0.7 collective-permute-start.6
  64.3 0.0 collective-permute-done.6.incoming_ref
  64.3 0.0 copy-start.1
  64.3 0.7 copy-done.1
  65.0 6.3 %shard_map.63 = (bf16[96,1536]{1,0:T(8,128)(2,1)}, bf16[96,1024]{1,0:T(8,128)(2,1)}, bf16[96,1024]{1,0:T(8,128)(2,1)}) custom-call(bf16[96,1792]{1,0:T(8,128)(2,1)} %copy-done.1, f32[96,2048]{1,0:T(8,128)} %get-tuple-element.27.slope_ref, bf16[27,16,2048]{2,1,0:T(8,128)(2,1)} %get-tuple-element.28.mask_ref, bf16[96,2592]{1,0:T(8,128)(2,1)} %get-tuple-element.29.bwd_ref, ...), custom_call_target="tpu_custom_call" | custom-call | tf_op jit(solution)/shard_map/pallas_call | solution.py:367
  71.3 0.7 collective-permute-start.7
  72.0 0.0 collective-permute-done.7.incoming_ref
  72.0 0.0 copy-start.2
  72.0 0.7 copy-done.2
  72.7 5.8 %shard_map.64 = (bf16[96,640]{1,0:T(8,128)(2,1)}, bf16[96,128]{1,0:T(8,128)(2,1)}, bf16[96,128]{1,0:T(8,128)(2,1)}, bf16[96,1024]{1,0:T(8,128)(2,1)}, bf16[96,1024]{1,0:T(8,128)(2,1)}) custom-call(bf16[96,1536]{1,0:T(8,128)(2,1)} %copy-done.2, f32[96,2048]{1,0:T(8,128)} %get-tuple-element.27.slope_ref, bf16[27,16,2048]{2,1,0:T(8,128)(2,1)} %get-tuple-element.28.mask_ref, ...), custom_call_target="tpu_custom_call" | custom-call | tf_op jit(solution)/shard_map/pallas_call | solution.py:373
  78.5 1.3 collective-permute-start.8
  79.8 1.3 collective-permute-start.10
  81.1 1.3 collective-permute-start.9
  82.4 25.0 %collective-permute-done.10.from_right = bf16[96,128]{1,0:T(8,128)(2,1)S(1)} collective-permute-done((bf16[96,128]{1,0:T(8,128)(2,1)}, bf16[96,128]{1,0:T(8,128)(2,1)S(1)}, u32[]{:S(2)}, u32[]{:S(2)}) %collective-permute-start.10) | collective-permute-done | bytes 24608 | tf_op jit(solution)/shard_map/ppermute | solution.py:380
  107.4 0.0 copy-start.10
  107.4 0.0 collective-permute-done.9.from_left
  107.4 0.0 copy-start.11
  107.4 0.0 collective-permute-done.8.centre_ref
  107.4 0.0 copy-start.9
  107.4 0.6 copy-done.10
  108.0 0.0 copy-done.11
  108.0 0.1 copy-done.9
  108.1 8.6 %shard_map.65 = (bf16[96,512]{1,0:T(8,128)(2,1)}, bf16[3072,128]{1,0:T(8,128)(2,1)}) custom-call(bf16[96,640]{1,0:T(8,128)(2,1)} %copy-done.9, bf16[96,128]{1,0:T(8,128)(2,1)} %copy-done.11, bf16[96,128]{1,0:T(8,128)(2,1)} %copy-done.10, f32[96,2048]{1,0:T(8,128)} %get-tuple-element.27.slope_ref, bf16[27,16,2048]{2,1,0:T(8,128)(2,1)} %get-tuple-element.28.mask_ref, ...), custom_call_target="tpu_custom_call" | custom-call | tf_op jit(solution)/shard_map/pallas_call | solution.py:381
  116.6 16.8 %all_to_all.15 = bf16[8,384,128]{2,1,0:T(8,128)(2,1)S(1)} all-to-all(bf16[8,384,128]{2,1,0:T(8,128)(2,1)} %bitcast.12), channel_id=1, replica_groups={{0,4,128,132,256,260,384,388},{8,12,136,140,264,268,392,396},{16,20,144..., dimensions={0} | all-to-all | bytes 1572864 | tf_op jit(solution)/shard_map/all_to_all | solution.py:388
  133.4 0.1 reduce_sum.24
  133.5 19.4 %all_to_all.16 = bf16[16,24,128]{2,1,0:T(8,128)(2,1)S(1)} all-to-all(bf16[16,24,128]{2,1,0:T(8,128)(2,1)S(1)} %bitcast.14), channel_id=1, replica_groups={{0,8,16,24,32,40,48,56,64,72,80,88,96,104,112,120},{4,12,20,28,36,44,52..., dimensions={0} | all-to-all | bytes 196608 | tf_op jit(solution)/shard_map/all_to_all | solution.py:392
  152.9 16.3 %all_to_all.17 = bf16[16,24,128]{2,1,0:T(8,128)(2,1)S(1)} all-to-all(bf16[16,24,128]{2,1,0:T(8,128)(2,1)S(1)} %broadcast_in_dim.16), channel_id=1, replica_groups={{0,8,16,24,32,40,48,56,64,72,80,88,96,104,112,120},{4,12,20,28,36,44,52..., dimensions={0} | all-to-all | bytes 196608 | tf_op jit(solution)/shard_map/all_to_all | solution.py:397
  169.2 17.3 %all_gather.3 = bf16[8,384,128]{2,1,0:T(8,128)(2,1)} all-gather(bf16[1,384,128]{2,1,0:T(8,128)(2,1)S(1)} %bitcast.15), channel_id=1, replica_groups={{0,4,128,132,256,260,384,388},{8,12,136,140,264,268,392,396},{16,20,144..., dimensions={0}, use_global_device_ids=true | all-gather | bytes 884736 | tf_op jit(solution)/shard_map/all_gather | solution.py:398
  186.5 2.8 %shard_map.66 = f32[2592,96]{1,0:T(8,128)} custom-call(bf16[3072,128]{1,0:T(8,128)(2,1)} %bitcast.10), custom_call_target="tpu_custom_call" | custom-call | tf_op jit(solution)/shard_map/pallas_call | solution.py:399
  (3 shorter events, 0.0 us)
Async XLA Ops:
  2.4 12.1 %copy-start = (bf16[208,512]{1,0:T(8,128)(2,1)}, bf16[208,512]{1,0:T(8,128)(2,1)S(1)}, u32[]{:S(2)}) copy-start(bf16[208,512]{1,0:T(8,128)(2,1)S(1)} %maximum_maximum_fusion.own_ref) | copy-start | bytes 638980
  2.4 10.1 %collective-permute-start = (bf16[208,512]{1,0:T(8,128)(2,1)S(1)}, bf16[208,512]{1,0:T(8,128)(2,1)S(1)}, u32[]{:S(2)}, u32[]{:S(2)}) collective-permute-start(bf16[208,512]{1,0:T(8,128)(2,1)S(1)} %maximum_maximum_fusion.own_ref), channel_id=1, source_target_pairs={{0,4},{1,5},{2,6},{3,7},{4,8},{5,9},{6,10},{7,11},{8,12},{9,13},{1... | collective-permute-start | bytes 638984 | tf_op jit(solution)/shard_map/ppermute | solution.py:343
  7.4 7.2 %collective-permute-start.1 = (bf16[208,512]{1,0:T(8,128)(2,1)S(1)}, bf16[208,512]{1,0:T(8,128)(2,1)S(1)}, u32[]{:S(2)}, u32[]{:S(2)}) collective-permute-start(bf16[208,512]{1,0:T(8,128)(2,1)S(1)} %maximum_maximum_fusion.own_ref), channel_id=1, source_target_pairs={{4,0},{5,1},{6,2},{7,3},{8,4},{9,5},{10,6},{11,7},{12,8},{13,9},{1... | collective-permute-start | bytes 638984 | tf_op jit(solution)/shard_map/ppermute | solution.py:344
  12.5 2.0 %copy-start.3 = (bf16[208,512]{1,0:T(8,128)(2,1)}, bf16[208,512]{1,0:T(8,128)(2,1)S(1)}, u32[]{:S(2)}) copy-start(bf16[208,512]{1,0:T(8,128)(2,1)S(1)} %collective-permute-done.left_ref) | copy-start | bytes 638980
  14.5 0.7 copy-start.4
  17.7 13.5 %collective-permute-start.2 = (bf16[96,768]{1,0:T(8,128)(2,1)}, bf16[96,768]{1,0:T(8,128)(2,1)S(1)}, u32[]{:S(2)}, u32[]{:S(2)}) collective-permute-start(bf16[96,768]{1,0:T(8,128)(2,1)} %get-tuple-element.24), channel_id=1, source_target_pairs={{0,32},{1,33},{2,34},{3,35},{4,36},{5,37},{6,38},{7,39},{8,40},{9,... | collective-permute-start | bytes 442376 | tf_op jit(solution)/shard_map/ppermute | solution.py:349
  26.5 13.9 %collective-permute-start.4 = (bf16[96,768]{1,0:T(8,128)(2,1)}, bf16[96,768]{1,0:T(8,128)(2,1)S(1)}, u32[]{:S(2)}, u32[]{:S(2)}) collective-permute-start(bf16[96,768]{1,0:T(8,128)(2,1)} %get-tuple-element.25), channel_id=1, source_target_pairs={{32,0},{33,1},{34,2},{35,3},{36,4},{37,5},{38,6},{39,7},{40,8},{41... | collective-permute-start | bytes 442376 | tf_op jit(solution)/shard_map/ppermute | solution.py:350
  31.2 16.4 %copy-start.5 = (bf16[96,768]{1,0:T(8,128)(2,1)}, bf16[96,768]{1,0:T(8,128)(2,1)S(1)}, u32[]{:S(2)}) copy-start(bf16[96,768]{1,0:T(8,128)(2,1)S(1)} %collective-permute-done.2.before_ref) | copy-start | bytes 442372
  31.2 24.7 %collective-permute-start.3 = (bf16[96,768]{1,0:T(8,128)(2,1)S(1)}, bf16[96,768]{1,0:T(8,128)(2,1)S(1)}, u32[]{:S(2)}, u32[]{:S(2)}) collective-permute-start(bf16[96,768]{1,0:T(8,128)(2,1)S(1)} %collective-permute-done.2.before_ref), channel_id=1, source_target_pairs={{0,3},{4,7},{8,11},{12,15},{16,19},{20,23},{24,27},{28,31},{32,35}... | collective-permute-start | bytes 442376 | tf_op jit(solution)/shard_map/ppermute | solution.py:351
  40.4 7.2 %copy-start.6 = (bf16[96,768]{1,0:T(8,128)(2,1)}, bf16[96,768]{1,0:T(8,128)(2,1)S(1)}, u32[]{:S(2)}) copy-start(bf16[96,768]{1,0:T(8,128)(2,1)S(1)} %collective-permute-done.4.after_ref) | copy-start | bytes 442372
  40.4 15.4 %collective-permute-start.5 = (bf16[96,768]{1,0:T(8,128)(2,1)S(1)}, bf16[96,768]{1,0:T(8,128)(2,1)S(1)}, u32[]{:S(2)}, u32[]{:S(2)}) collective-permute-start(bf16[96,768]{1,0:T(8,128)(2,1)S(1)} %collective-permute-done.4.after_ref), channel_id=1, source_target_pairs={{0,3},{4,7},{8,11},{12,15},{16,19},{20,23},{24,27},{28,31},{32,35}... | collective-permute-start | bytes 442376 | tf_op jit(solution)/shard_map/ppermute | solution.py:352
  55.9 0.7 copy-start.7
  55.9 0.7 copy-start.8
  63.6 0.7 collective-permute-start.6
  64.3 0.7 copy-start.1
  71.3 0.7 collective-permute-start.7
  72.0 0.7 copy-start.2
  78.5 28.9 %collective-permute-start.8 = (bf16[96,640]{1,0:T(8,128)(2,1)}, bf16[96,640]{1,0:T(8,128)(2,1)S(1)}, u32[]{:S(2)}, u32[]{:S(2)}) collective-permute-start(bf16[96,640]{1,0:T(8,128)(2,1)} %get-tuple-element.36), channel_id=1, source_target_pairs={{1,0},{5,4},{9,8},{13,12},{17,16},{21,20},{25,24},{29,28},{33,32},... | collective-permute-start | bytes 368648 | tf_op jit(solution)/shard_map/ppermute | solution.py:378
  79.8 27.6 %collective-permute-start.10 = (bf16[96,128]{1,0:T(8,128)(2,1)}, bf16[96,128]{1,0:T(8,128)(2,1)S(1)}, u32[]{:S(2)}, u32[]{:S(2)}) collective-permute-start(bf16[96,128]{1,0:T(8,128)(2,1)} %get-tuple-element.38), channel_id=1, source_target_pairs={{5,0},{9,4},{13,8},{17,12},{21,16},{25,20},{29,24},{37,32},{41,36}... | collective-permute-start | bytes 73736 | tf_op jit(solution)/shard_map/ppermute | solution.py:380
  81.1 26.3 %collective-permute-start.9 = (bf16[96,128]{1,0:T(8,128)(2,1)}, bf16[96,128]{1,0:T(8,128)(2,1)S(1)}, u32[]{:S(2)}, u32[]{:S(2)}) collective-permute-start(bf16[96,128]{1,0:T(8,128)(2,1)} %get-tuple-element.37), channel_id=1, source_target_pairs={{1,4},{5,8},{9,12},{13,16},{17,20},{21,24},{25,28},{33,36},{37,40}... | collective-permute-start | bytes 73736 | tf_op jit(solution)/shard_map/ppermute | solution.py:379
  107.4 0.6 copy-start.10
  107.4 0.6 copy-start.11
  107.4 0.7 copy-start.9

commit v3 on v2

--- a/solution.py
+++ b/solution.py
@@ -16,19 +16,30 @@
 DEEP = TAPS * C
 WIDE = 128
 CODE = 8
-CHUNK = 384
-VMEM_BYTES = 56 * 1024 * 1024
+CHUNK = 256
+VMEM_BYTES = 32 * 1024 * 1024
 F32 = jnp.float32
 BF16 = jnp.bfloat16
 
 
-def call(kernel, outs, scratch=()):
-    return pl.pallas_call(
-        kernel,
-        out_shape=[jax.ShapeDtypeStruct(shape, dtype) for shape, dtype in outs],
-        scratch_shapes=[pltpu.VMEM(shape, dtype) for shape, dtype in scratch],
-        compiler_params=pltpu.CompilerParams(vmem_limit_bytes=VMEM_BYTES),
-    )
+def call(kernel, outs, scratch=(), leave=()):
+    shapes = [
+        jax.ShapeDtypeStruct(shape, dtype) if n in leave else pltpu.VMEM(shape, dtype)
+        for n, (shape, dtype) in enumerate(outs)
+    ]
+
+    def run(*args):
+        inner = pl.pallas_call(
+            kernel,
+            out_shape=shapes,
+            in_specs=[pl.BlockSpec(memory_space=pltpu.VMEM)] * len(args),
+            out_specs=[pl.BlockSpec(memory_space=pltpu.VMEM)] * len(shapes),
+            scratch_shapes=[pltpu.VMEM(shape, dtype) for shape, dtype in scratch],
+            compiler_params=pltpu.CompilerParams(vmem_limit_bytes=VMEM_BYTES),
+        )
+        return inner(*[pltpu.with_memory_space_constraint(arg, pltpu.VMEM) for arg in args])
+
+    return run
 
 
 def lane(row, count=1):
@@ -297,21 +308,53 @@
         return carry
 
     lax.fori_loop(0, 4, gather, 0)
-    for tap in range(TAPS):
-        part = lax.dot_general(
-            all_ref[C * tap : C * tap + C, :], grads, (((1,), (1,)), ((), ())),
-            preferred_element_type=F32,
-        )
-        terms_ref[C * tap : C * tap + C, :] = jnp.concatenate(
-            [part, jnp.zeros((C, WIDE - C), F32)], 1
-        ).astype(BF16)
-    terms_ref[DEEP:, :] = jnp.zeros((COLS * CHUNK - DEEP, WIDE), BF16)
+    for four in range(7):
+        parts = []
+        for tap in range(4 * four, 4 * four + 4):
+            if tap < TAPS:
+                part = lax.dot_general(
+                    all_ref[C * tap : C * tap + C, :], grads, (((1,), (1,)), ((), ())),
+                    preferred_element_type=F32,
+                ).astype(BF16)
+            else:
+                part = jnp.zeros((C, C), BF16)
+            parts.append(part)
+        first, second, third, fourth = parts
+        at = 3 * C * four
+        terms_ref[at : at + C, :] = jnp.concatenate([first, second[:, :32]], 1)
+        terms_ref[at + C : at + 2 * C, :] = jnp.concatenate([second[:, 32:], third[:, :64]], 1)
+        terms_ref[at + 2 * C : at + 3 * C, :] = jnp.concatenate([third[:, 64:], fourth], 1)
+    terms_ref[21 * C :, :] = jnp.zeros((COLS * CHUNK - 21 * C, WIDE), BF16)
+
+
+def sum_kernel(parts_ref, out_ref):
+    total = parts_ref[0].astype(F32)
+    for n in range(1, parts_ref.shape[0]):
+        total = total + parts_ref[n].astype(F32)
+    total = total.astype(BF16)
+    if len(out_ref.shape) == 2:
+        out_ref[...] = total
+    else:
+        for n in range(out_ref.shape[0]):
+            out_ref[n] = total
 
 
 def scale_kernel(whole_ref, out_ref):
-    total = whole_ref[:DEEP, :C].astype(F32)
-    mean = jnp.sum(total * total) / (DEEP * C)
-    out_ref[...] = total * lax.rsqrt(mean + 1e-06)
+    whole = whole_ref[...].astype(F32)
+    scale = lax.rsqrt(jnp.sum(whole * whole) / (DEEP * C) + 1e-06)
+    for four in range(7):
+        at = 3 * C * four
+        first, second, third = (
+            whole_ref[at + n * C : at + n * C + C, :].astype(F32) * scale for n in range(3)
+        )
+        parts = (
+            first[:, :96],
+            jnp.concatenate([first[:, 96:], second[:, :64]], 1),
+            jnp.concatenate([second[:, 64:], third[:, :32]], 1),
+            third[:, 32:],
+        )
+        for n, tap in enumerate(range(4 * four, min(4 * four + 4, TAPS))):
+            out_ref[C * tap : C * tap + C, :] = parts[n]
 
 
 def groups(devices):
@@ -348,6 +391,7 @@
     )(own, left, right)
     before = lax.ppermute(up, both, between(1, 0, same))
     after = lax.ppermute(down, both, between(-1, 0, same))
+    before, after, fwd, bwd = lax.optimization_barrier((before, after, fwd, bwd))
     top_before = lax.ppermute(before, both, between(0, 0, [(0, SECTIONS - 1)]))
     top_after = lax.ppermute(after, both, between(0, 0, [(0, SECTIONS - 1)]))
 
@@ -382,21 +426,21 @@
         last_kernel,
         [((C, CELLS), BF16), ((COLS * CHUNK, WIDE), BF16)],
         [((9, C, 10 * WIDE), BF16), cols, ((C, 10 * WIDE), BF16), core, ((DEEP, 8 * WIDE), BF16)],
+        leave=(0,),
     )(centre, from_left, from_right, slope, mask, bwd, x_rows, grad, out)
 
     near, far = groups(devices)
     parts = lax.all_to_all(
         terms.reshape(COLS, CHUNK, WIDE), "space", 0, 0, axis_index_groups=near
     )
-    part = jnp.sum(parts.astype(F32), 0).astype(BF16)
+    (part,) = call(sum_kernel, [((CHUNK, WIDE), BF16)])(parts)
     pieces = lax.all_to_all(
         part.reshape(ROWS, CHUNK // ROWS, WIDE), "space", 0, 0, axis_index_groups=far
     )
-    piece = jnp.sum(pieces.astype(F32), 0).astype(BF16)
-    copies = jnp.broadcast_to(piece[None], (ROWS,) + piece.shape)
+    (copies,) = call(sum_kernel, [((ROWS, CHUNK // ROWS, WIDE), BF16)])(pieces)
     part = lax.all_to_all(copies, "space", 0, 0, axis_index_groups=far)
     whole = lax.all_gather(part.reshape(CHUNK, WIDE), "space", axis_index_groups=near)
-    (weight_grad,) = call(scale_kernel, [((DEEP, C), F32)])(whole.reshape(COLS * CHUNK, WIDE))
+    (weight_grad,) = call(scale_kernel, [((DEEP, C), F32)], leave=(0,))(whole.reshape(COLS * CHUNK, WIDE))
     return (out.reshape(1, 1, C, CELLS), weight_grad.reshape(1, TAPS, C, C))
 
 

time: 190 us -> 163 us (0.86)
  Pallas kernels: 44 us -> 25.8 us
  blocking collectives: 69.7 us -> 63.7 us
  waiting for transfers between devices: 35.2 us -> 38.6 us
  starting transfers between devices: 34.1 us -> 31.1 us
  local copies, waits for them, and re-layouts: 3.57 us -> 1.16 us
    pallas_call x8 -> x10, Pallas kernels: 44 us -> 25.8 us  [run(): inner(*[pltpu.with_memory_space_constraint(arg, pltpu.VMEM) for arg in ar...]
    ppermute x1, waiting for transfers between devices: 4.89 us -> 9.36 us  [body(): after = lax.ppermute(down, both, between(-1, 0, same))]
    ppermute x1, starting transfers between devices: 4.36 us -> 1.3 us  [body(): top_after = lax.ppermute(after, both, between(0, 0, [(0, SECTIONS - 1)]))]
    all_to_all x1, blocking collectives: 16.8 us -> 13.7 us  [body(): lax.all_to_all(terms.reshape(COLS, CHUNK, WIDE), 'space', 0, 0, axis_inde...]
    unnamed x24 -> x2, local copies, waits for them, and re-layouts: 3.47 us -> 1.09 us
    ppermute x1, waiting for transfers between devices: 3.35 us -> 1.19 us  [body(): before = lax.ppermute(up, both, between(1, 0, same))]
  transfers between devices with their start and end apart: 11 -> 11, of which waited for: 4 -> 4; matrix products, arithmetic and copies ran while one was open for 0% -> 0% of each run, Pallas kernels for 6% -> 4%
where the time goes in v3:
time: 163 us
  blocking collectives  63.7 us (39%)
  waiting for transfers between devices  38.6 us (24%)
  starting transfers between devices  31.1 us (19%)
  Pallas kernels  25.8 us (16%)
    ppermute x1, waiting for transfers between devices, body(): from_right = lax.ppermute(left, both, between(0, -1, [(1, 0)]))  26 us
    pallas_call x10, Pallas kernels, run(): inner(*[pltpu.with_memory_space_constraint(arg, pltpu.VMEM) for arg in ar...  25.8 us
    all_to_all x1, blocking collectives, body(): lax.all_to_all(part.reshape(ROWS, CHUNK // ROWS, WIDE), 'space', 0, 0, ax...  18.9 us
    all_gather x1, blocking collectives, body(): lax.all_gather(part.reshape(CHUNK, WIDE), 'space', axis_index_groups=near)  16.6 us
    all_to_all x1, blocking collectives, body(): part = lax.all_to_all(copies, 'space', 0, 0, axis_index_groups=far)  14.5 us
    all_to_all x1, blocking collectives, body(): lax.all_to_all(terms.reshape(COLS, CHUNK, WIDE), 'space', 0, 0, axis_inde...  13.7 us
    ppermute x1, waiting for transfers between devices, body(): after = lax.ppermute(down, both, between(-1, 0, same))  9.36 us
    ppermute x1, starting transfers between devices, body(): before = lax.ppermute(up, both, between(1, 0, same))  8.82 us
  transfers between devices with their start and end apart: 11, of which 4 were waited for; matrix products, arithmetic and copies ran while one was open for 0% of the time, Pallas kernels for 4%

profile of v3, /device:TPU:1, one launch (start us, length us, event | category | flops | bytes accessed | tf_op | source)
XLA Modules:
  0.0 162.8 jit_solution(1885376033404776940)
XLA Ops:
  1.3 0.1 pad.2.clone
  1.4 1.0 maximum_maximum_fusion.own_ref
  2.4 4.9 %collective-permute-start = (bf16[208,512]{1,0:T(8,128)(2,1)S(1)}, bf16[208,512]{1,0:T(8,128)(2,1)S(1)}, u32[]{:S(2)}, u32[]{:S(2)}) collective-permute-start(bf16[208,512]{1,0:T(8,128)(2,1)S(1)} %maximum_maximum_fusion.own_ref), channel_id=1, source_target_pairs={{0,4},{1,5},{2,6},{3,7},{4,8},{5,9},{6,10},{7,11},{8,12},{9,13},{1... | collective-permute-start | bytes 638984 | tf_op jit(solution)/shard_map/ppermute | solution.py:386
  7.4 5.2 %collective-permute-start.1 = (bf16[208,512]{1,0:T(8,128)(2,1)S(1)}, bf16[208,512]{1,0:T(8,128)(2,1)S(1)}, u32[]{:S(2)}, u32[]{:S(2)}) collective-permute-start(bf16[208,512]{1,0:T(8,128)(2,1)S(1)} %maximum_maximum_fusion.own_ref), channel_id=1, source_target_pairs={{4,0},{5,1},{6,2},{7,3},{8,4},{9,5},{10,6},{11,7},{12,8},{13,9},{1... | collective-permute-start | bytes 638984 | tf_op jit(solution)/shard_map/ppermute | solution.py:387
  12.5 0.0 collective-permute-done.left_ref
  12.5 2.0 %collective-permute-done.1.right_ref = bf16[208,512]{1,0:T(8,128)(2,1)S(1)} collective-permute-done((bf16[208,512]{1,0:T(8,128)(2,1)S(1)}, bf16[208,512]{1,0:T(8,128)(2,1)S(1)}, u32[]{:S(2)}, u32[]{:S(2)}) %collective-permute-start.1) | collective-permute-done | bytes 213024 | tf_op jit(solution)/shard_map/ppermute | solution.py:387
  14.5 0.5 shard_map.59
  15.0 8.8 %collective-permute-start.2 = (bf16[96,768]{1,0:T(8,128)(2,1)S(1)}, bf16[96,768]{1,0:T(8,128)(2,1)S(1)}, u32[]{:S(2)}, u32[]{:S(2)}) collective-permute-start(bf16[96,768]{1,0:T(8,128)(2,1)S(1)} %get-tuple-element.28), channel_id=1, source_target_pairs={{0,32},{1,33},{2,34},{3,35},{4,36},{5,37},{6,38},{7,39},{8,40},{9,... | collective-permute-start | bytes 442376 | tf_op jit(solution)/shard_map/ppermute | solution.py:392
  23.8 1.3 collective-permute-start.3
  25.1 0.0 copy-start
  25.1 1.1 copy-done
  26.2 0.7 shard_map.60
  27.0 1.2 collective-permute-done.2.before_ref
  28.2 9.4 %collective-permute-done.3.after_ref = bf16[96,768]{1,0:T(8,128)(2,1)S(1)} collective-permute-done((bf16[96,768]{1,0:T(8,128)(2,1)S(1)}, bf16[96,768]{1,0:T(8,128)(2,1)S(1)}, u32[]{:S(2)}, u32[]{:S(2)}) %collective-permute-start.3) | collective-permute-done | bytes 147488 | tf_op jit(solution)/shard_map/ppermute | solution.py:393
  37.5 4.4 %collective-permute-start.4 = (bf16[96,768]{1,0:T(8,128)(2,1)S(1)}, bf16[96,768]{1,0:T(8,128)(2,1)S(1)}, u32[]{:S(2)}, u32[]{:S(2)}) collective-permute-start(bf16[96,768]{1,0:T(8,128)(2,1)S(1)} %collective-permute-done.2.before_ref), channel_id=1, source_target_pairs={{0,3},{4,7},{8,11},{12,15},{16,19},{20,23},{24,27},{28,31},{32,35}... | collective-permute-start | bytes 442376 | tf_op jit(solution)/shard_map/ppermute | solution.py:395
  41.9 1.3 collective-permute-start.5
  43.2 6.1 %shard_map.61 = (f32[96,2048]{1,0:T(8,128)S(1)}, bf16[27,16,2048]{2,1,0:T(8,128)(2,1)S(1)}, bf16[96,1280]{1,0:T(8,128)(2,1)S(1)}) custom-call(bf16[208,1024]{1,0:T(8,128)(2,1)S(1)} %get-tuple-element.27.own_ref, bf16[96,768]{1,0:T(8,128)(2,1)S(1)} %collective-permute-done.2.before_ref, bf16[96,768]{1,0:T(8,128)(2,1)S(1)} %collective-permute-done.3.after_ref, ...), custom_call_target="tpu_custom_call" | custom-call | tf_op jit(solution)/shard_map/pallas_call | solution.py:40
  49.3 0.0 collective-permute-done.4.before_ref
  49.4 0.0 collective-permute-done.5.after_ref
  49.4 4.2 %shard_map.62 = (bf16[96,1792]{1,0:T(8,128)(2,1)S(1)}, bf16[96,1024]{1,0:T(8,128)(2,1)S(1)}, bf16[96,1024]{1,0:T(8,128)(2,1)S(1)}) custom-call(bf16[208,1024]{1,0:T(8,128)(2,1)S(1)} %get-tuple-element.27.own_ref, bf16[96,768]{1,0:T(8,128)(2,1)S(1)} %collective-permute-done.4.before_ref, bf16[96,768]{1,0:T(8,128)(2,1)S(1)} %collective-permute-done.5.after_ref, ...), custom_call_target="tpu_custom_call" | custom-call | tf_op jit(solution)/shard_map/pallas_call | solution.py:40
  53.6 0.7 collective-permute-start.6
  54.3 0.0 collective-permute-done.6.incoming_ref
  54.3 3.4 %shard_map.63 = (bf16[96,1536]{1,0:T(8,128)(2,1)S(1)}, bf16[96,1024]{1,0:T(8,128)(2,1)S(1)}, bf16[96,1024]{1,0:T(8,128)(2,1)S(1)}) custom-call(bf16[96,1792]{1,0:T(8,128)(2,1)S(1)} %collective-permute-done.6.incoming_ref, f32[96,2048]{1,0:T(8,128)S(1)} %get-tuple-element.35.slope_ref, bf16[27,16,2048]{2,1,0:T(8,128)(2,1)S(1)} %get-tuple-element.36.mask_ref, ...), custom_call_target="tpu_custom_call" | custom-call | tf_op jit(solution)/shard_map/pallas_call | solution.py:40
  57.7 0.7 collective-permute-start.7
  58.4 0.0 collective-permute-done.7.incoming_ref
  58.4 3.0 %shard_map.64 = (bf16[96,640]{1,0:T(8,128)(2,1)S(1)}, bf16[96,128]{1,0:T(8,128)(2,1)S(1)}, bf16[96,128]{1,0:T(8,128)(2,1)S(1)}, bf16[96,1024]{1,0:T(8,128)(2,1)S(1)}, bf16[96,1024]{1,0:T(8,128)(2,1)S(1)}) custom-call(bf16[96,1536]{1,0:T(8,128)(2,1)S(1)} %collective-permute-done.7.incoming_ref, f32[96,2048]{1,0:T(8,128)S(1)} %get-tuple-element.35.slope_ref, ...), custom_call_target="tpu_custom_call" | custom-call | tf_op jit(solution)/shard_map/pallas_call | solution.py:40
  61.5 1.3 collective-permute-start.8
  62.8 1.3 collective-permute-start.10
  64.1 1.3 collective-permute-start.9
  65.4 26.0 %collective-permute-done.10.from_right = bf16[96,128]{1,0:T(8,128)(2,1)S(1)} collective-permute-done((bf16[96,128]{1,0:T(8,128)(2,1)S(1)}, bf16[96,128]{1,0:T(8,128)(2,1)S(1)}, u32[]{:S(2)}, u32[]{:S(2)}) %collective-permute-start.10) | collective-permute-done | bytes 24608 | tf_op jit(solution)/shard_map/ppermute | solution.py:424
  91.4 0.0 collective-permute-done.9.from_left
  91.4 0.0 collective-permute-done.8.centre_ref
  91.4 5.7 %shard_map.65 = (bf16[96,512]{1,0:T(8,128)(2,1)}, bf16[2048,128]{1,0:T(8,128)(2,1)S(1)}) custom-call(bf16[96,640]{1,0:T(8,128)(2,1)S(1)} %collective-permute-done.8.centre_ref, bf16[96,128]{1,0:T(8,128)(2,1)S(1)} %collective-permute-done.9.from_left, bf16[96,128]{1,0:T(8,128)(2,1)S(1)} %collective-permute-done.10.from_right, ...), custom_call_target="tpu_custom_call" | custom-call | tf_op jit(solution)/shard_map/pallas_call | solution.py:40
  97.1 13.7 %all_to_all.15.parts_ref = bf16[8,256,128]{2,1,0:T(8,128)(2,1)S(1)} all-to-all(bf16[8,256,128]{2,1,0:T(8,128)(2,1)S(1)} %bitcast.12), channel_id=1, replica_groups={{0,4,128,132,256,260,384,388},{8,12,136,140,264,268,392,396},{16,20,144..., dimensions={0} | all-to-all | bytes 1048576 | tf_op jit(solution)/shard_map/all_to_all | solution.py:433
  110.8 0.1 shard_map.66
  110.9 18.9 %all_to_all.16.parts_ref = bf16[16,16,128]{2,1,0:T(8,128)(2,1)S(1)} all-to-all(bf16[16,16,128]{2,1,0:T(8,128)(2,1)S(1)} %bitcast.13), channel_id=1, replica_groups={{0,8,16,24,32,40,48,56,64,72,80,88,96,104,112,120},{4,12,20,28,36,44,52..., dimensions={0} | all-to-all | bytes 131072 | tf_op jit(solution)/shard_map/all_to_all | solution.py:437
  129.8 14.5 %all_to_all.17 = bf16[16,16,128]{2,1,0:T(8,128)(2,1)S(1)} all-to-all(bf16[16,16,128]{2,1,0:T(8,128)(2,1)S(1)} %shard_map.67), channel_id=1, replica_groups={{0,8,16,24,32,40,48,56,64,72,80,88,96,104,112,120},{4,12,20,28,36,44,52..., dimensions={0} | all-to-all | bytes 131072 | tf_op jit(solution)/shard_map/all_to_all | solution.py:441
  144.2 16.6 %all_gather.3 = bf16[8,256,128]{2,1,0:T(8,128)(2,1)S(1)} all-gather(bf16[1,256,128]{2,1,0:T(8,128)(2,1)S(1)} %bitcast.15), channel_id=1, replica_groups={{0,4,128,132,256,260,384,388},{8,12,136,140,264,268,392,396},{16,20,144..., dimensions={0}, use_global_device_ids=true | all-gather | bytes 589824 | tf_op jit(solution)/shard_map/all_gather | solution.py:442
  160.8 2.0 %shard_map.68 = f32[2592,96]{1,0:T(8,128)} custom-call(bf16[2048,128]{1,0:T(8,128)(2,1)S(1)} %bitcast.10), custom_call_target="tpu_custom_call" | custom-call | tf_op jit(solution)/shard_map/pallas_call | solution.py:40
  (2 shorter events, 0.0 us)
Async XLA Ops:
  2.4 10.1 %collective-permute-start = (bf16[208,512]{1,0:T(8,128)(2,1)S(1)}, bf16[208,512]{1,0:T(8,128)(2,1)S(1)}, u32[]{:S(2)}, u32[]{:S(2)}) collective-permute-start(bf16[208,512]{1,0:T(8,128)(2,1)S(1)} %maximum_maximum_fusion.own_ref), channel_id=1, source_target_pairs={{0,4},{1,5},{2,6},{3,7},{4,8},{5,9},{6,10},{7,11},{8,12},{9,13},{1... | collective-permute-start | bytes 638984 | tf_op jit(solution)/shard_map/ppermute | solution.py:386
  7.4 7.2 %collective-permute-start.1 = (bf16[208,512]{1,0:T(8,128)(2,1)S(1)}, bf16[208,512]{1,0:T(8,128)(2,1)S(1)}, u32[]{:S(2)}, u32[]{:S(2)}) collective-permute-start(bf16[208,512]{1,0:T(8,128)(2,1)S(1)} %maximum_maximum_fusion.own_ref), channel_id=1, source_target_pairs={{4,0},{5,1},{6,2},{7,3},{8,4},{9,5},{10,6},{11,7},{12,8},{13,9},{1... | collective-permute-start | bytes 638984 | tf_op jit(solution)/shard_map/ppermute | solution.py:387
  15.0 13.2 %collective-permute-start.2 = (bf16[96,768]{1,0:T(8,128)(2,1)S(1)}, bf16[96,768]{1,0:T(8,128)(2,1)S(1)}, u32[]{:S(2)}, u32[]{:S(2)}) collective-permute-start(bf16[96,768]{1,0:T(8,128)(2,1)S(1)} %get-tuple-element.28), channel_id=1, source_target_pairs={{0,32},{1,33},{2,34},{3,35},{4,36},{5,37},{6,38},{7,39},{8,40},{9,... | collective-permute-start | bytes 442376 | tf_op jit(solution)/shard_map/ppermute | solution.py:392
  23.8 13.7 %collective-permute-start.3 = (bf16[96,768]{1,0:T(8,128)(2,1)S(1)}, bf16[96,768]{1,0:T(8,128)(2,1)S(1)}, u32[]{:S(2)}, u32[]{:S(2)}) collective-permute-start(bf16[96,768]{1,0:T(8,128)(2,1)S(1)} %get-tuple-element.29), channel_id=1, source_target_pairs={{32,0},{33,1},{34,2},{35,3},{36,4},{37,5},{38,6},{39,7},{40,8},{41... | collective-permute-start | bytes 442376 | tf_op jit(solution)/shard_map/ppermute | solution.py:393
  25.1 1.1 copy-start
  37.5 11.8 %collective-permute-start.4 = (bf16[96,768]{1,0:T(8,128)(2,1)S(1)}, bf16[96,768]{1,0:T(8,128)(2,1)S(1)}, u32[]{:S(2)}, u32[]{:S(2)}) collective-permute-start(bf16[96,768]{1,0:T(8,128)(2,1)S(1)} %collective-permute-done.2.before_ref), channel_id=1, source_target_pairs={{0,3},{4,7},{8,11},{12,15},{16,19},{20,23},{24,27},{28,31},{32,35}... | collective-permute-start | bytes 442376 | tf_op jit(solution)/shard_map/ppermute | solution.py:395
  41.9 7.5 %collective-permute-start.5 = (bf16[96,768]{1,0:T(8,128)(2,1)S(1)}, bf16[96,768]{1,0:T(8,128)(2,1)S(1)}, u32[]{:S(2)}, u32[]{:S(2)}) collective-permute-start(bf16[96,768]{1,0:T(8,128)(2,1)S(1)} %collective-permute-done.3.after_ref), channel_id=1, source_target_pairs={{0,3},{4,7},{8,11},{12,15},{16,19},{20,23},{24,27},{28,31},{32,35}... | collective-permute-start | bytes 442376 | tf_op jit(solution)/shard_map/ppermute | solution.py:396
  53.6 0.7 collective-permute-start.6
  57.7 0.7 collective-permute-start.7
  61.5 29.9 %collective-permute-start.8 = (bf16[96,640]{1,0:T(8,128)(2,1)S(1)}, bf16[96,640]{1,0:T(8,128)(2,1)S(1)}, u32[]{:S(2)}, u32[]{:S(2)}) collective-permute-start(bf16[96,640]{1,0:T(8,128)(2,1)S(1)} %get-tuple-element.44), channel_id=1, source_target_pairs={{1,0},{5,4},{9,8},{13,12},{17,16},{21,20},{25,24},{29,28},{33,32},... | collective-permute-start | bytes 368648 | tf_op jit(solution)/shard_map/ppermute | solution.py:422
  62.8 28.6 %collective-permute-start.10 = (bf16[96,128]{1,0:T(8,128)(2,1)S(1)}, bf16[96,128]{1,0:T(8,128)(2,1)S(1)}, u32[]{:S(2)}, u32[]{:S(2)}) collective-permute-start(bf16[96,128]{1,0:T(8,128)(2,1)S(1)} %get-tuple-element.46), channel_id=1, source_target_pairs={{5,0},{9,4},{13,8},{17,12},{21,16},{25,20},{29,24},{37,32},{41,36}... | collective-permute-start | bytes 73736 | tf_op jit(solution)/shard_map/ppermute | solution.py:424
  64.1 27.3 %collective-permute-start.9 = (bf16[96,128]{1,0:T(8,128)(2,1)S(1)}, bf16[96,128]{1,0:T(8,128)(2,1)S(1)}, u32[]{:S(2)}, u32[]{:S(2)}) collective-permute-start(bf16[96,128]{1,0:T(8,128)(2,1)S(1)} %get-tuple-element.45), channel_id=1, source_target_pairs={{1,4},{5,8},{9,12},{13,16},{17,20},{21,24},{25,28},{33,36},{37,40}... | collective-permute-start | bytes 73736 | tf_op jit(solution)/shard_map/ppermute | solution.py:423

commit v4 on v3

--- a/solution.py
+++ b/solution.py
@@ -32,12 +32,21 @@
         inner = pl.pallas_call(
             kernel,
             out_shape=shapes,
-            in_specs=[pl.BlockSpec(memory_space=pltpu.VMEM)] * len(args),
+            in_specs=[
+                pl.BlockSpec(memory_space=pltpu.SMEM if arg.dtype == jnp.int32 else pltpu.VMEM)
+                for arg in args
+            ],
             out_specs=[pl.BlockSpec(memory_space=pltpu.VMEM)] * len(shapes),
             scratch_shapes=[pltpu.VMEM(shape, dtype) for shape, dtype in scratch],
             compiler_params=pltpu.CompilerParams(vmem_limit_bytes=VMEM_BYTES),
         )
-        return inner(*[pltpu.with_memory_space_constraint(arg, pltpu.VMEM) for arg in args])
+        return inner(
+            *[
+                arg if arg.dtype == jnp.int32
+                else pltpu.with_memory_space_constraint(arg, pltpu.VMEM)
+                for arg in args
+            ]
+        )
 
     return run
 
@@ -88,75 +97,148 @@
         bwd_ref[:, C * q : C * q + C] = w_ref[TAPS - 1 - q]
 
 
-def pack_kernel(own_ref, left_ref, right_ref, own_out, up_out, down_out):
+def code_of(height_ref, shape):
+    return jnp.full(shape, (height_ref[0] + CODE).astype(F32), F32)
+
+
+def rows_kernel(x_ref, top_ref, height_ref, up_ref, down_ref, x_out, top_out):
     lowest = lax.axis_index("pipe") == 0
-    rows = []
-    for i in range(8):
-        at = 64 * i
-        rows.append(
-            jnp.concatenate(
+    code = code_of(height_ref, (16, 3 * WIDE)).astype(BF16)
+    spare = jnp.zeros((C, 64), BF16)
+    up_ref[C:, :] = code
+    down_ref[C:, :] = code
+    up_ref[:C, :WIDE] = x_ref[:, 384:512]
+    down_ref[:C, :WIDE] = x_ref[:, 0:128]
+    x_out[...] = x_ref[...]
+    top_out[...] = top_ref[...]
+
+    @pl.when(lowest)
+    def _():
+        up_ref[:C, WIDE:] = top_ref[:, 256:512]
+        down_ref[:C, WIDE:] = top_ref[:, 0:256]
+
+    @pl.when(jnp.logical_not(lowest))
+    def _():
+        up_ref[:C, WIDE:] = jnp.concatenate([x_ref[:, 192:384], spare], 1)
+        down_ref[:C, WIDE:] = jnp.concatenate([x_ref[:, 128:320], spare], 1)
+
+
+def x_layer(x_ref, before_ref, after_ref, row):
+    if row < 5:
+        at = 64 * (row - 3) if row >= 3 else WIDE + 64 * row
+        return before_ref[:C, at : at + 64]
+    if row < 13:
+        return x_ref[:, 64 * (row - 5) : 64 * (row - 5) + 64]
+    at = 64 * (row - 13) if row < 15 else WIDE + 64 * (row - 15)
+    return after_ref[:C, at : at + 64]
+
+
+def top_layer(top_ref, before_ref, after_ref, row):
+    if row < 5:
+        return before_ref[:C, WIDE + 64 * (row - 1) : WIDE + 64 * row]
+    if row < 13:
+        return top_ref[:, 64 * (row - 5) : 64 * (row - 5) + 64]
+    return after_ref[:C, WIDE + 64 * (row - 13) : WIDE + 64 * (row - 12)]
+
+
+def join(parts):
+    return jnp.concatenate(parts, 1)
+
+
+def cols_kernel(x_ref, top_ref, height_ref, before_ref, after_ref, right_ref, left_ref):
+    lowest = lax.axis_index("pipe") == 0
+    codes = join(
+        [before_ref[C:, :WIDE], code_of(height_ref, (16, WIDE)).astype(BF16), after_ref[C:, :WIDE]]
+    )
+    for out, start in ((right_ref, 32), (left_ref, 0)):
+
+        def piece(layer, start=start):
+            return layer[:, start : start + 32]
+
+        out[C:, : 3 * WIDE] = codes
+        out[C:, 3 * WIDE :] = jnp.zeros((16, 4 * WIDE), BF16)
+        for four in range(3):
+            rows = range(3 + 4 * four, 7 + 4 * four)
+            out[:C, lane(four)] = join(
+                [piece(x_layer(x_ref, before_ref, after_ref, row)) for row in rows]
+            )
+
+        @pl.when(lowest)
+        def _(out=out, piece=piece):
+            for four in range(4):
+                rows = range(1 + 4 * four, 5 + 4 * four)
+                out[:C, lane(3 + four)] = join(
+                    [piece(top_layer(top_ref, before_ref, after_ref, row)) for row in rows]
+                )
+
+        @pl.when(jnp.logical_not(lowest))
+        def _(out=out, piece=piece):
+            outer = [
+                piece(x_layer(x_ref, before_ref, after_ref, row)) for row in (0, 1, 2, 15, 16, 17)
+            ]
+            out[:C, lane(3)] = join(outer[:4])
+            out[:C, lane(4)] = join(outer[4:] + [jnp.zeros((C, 64), BF16)])
+            out[:C, lane(5, 2)] = jnp.zeros((C, 2 * WIDE), BF16)
+
+
+def x_side(side_ref, row):
+    if 3 <= row < 15:
+        at = 32 * (row - 3)
+    else:
+        at = 3 * WIDE + 32 * (row if row < 3 else row - 12)
+    return side_ref[:C, at : at + 32]
+
+
+def top_side(side_ref, row):
+    return side_ref[:C, 3 * WIDE + 32 * (row - 1) : 3 * WIDE + 32 * row]
+
+
+def halo_kernel(before_ref, after_ref, left_ref, right_ref, halo_ref):
+    @pl.when(lax.axis_index("pipe") == 0)
+    def _():
+        for n, row in enumerate((1, 2, 3, 4, 13, 14, 15, 16)):
+            middle = top_layer(None, before_ref, after_ref, row)
+            halo_ref[:, lane(n)] = join([top_side(left_ref, row), middle, top_side(right_ref, row)])
+        for pair in range(4):
+            first, second = 5 + 2 * pair, 6 + 2 * pair
+            halo_ref[:, lane(8 + pair)] = join(
                 [
-                    left_ref[:, at + 32 : at + 64],
-                    own_ref[:, at : at + 64],
-                    right_ref[:, at : at + 32],
-                ],
-                1,
+                    top_side(left_ref, first),
+                    top_side(right_ref, first),
+                    top_side(left_ref, second),
+                    top_side(right_ref, second),
+                ]
             )
-        )
-        own_out[:, lane(i)] = rows[i]
-    code = jnp.concatenate([rows[0][2 * C :]] * (C // 16), 0)
-    own_code = jnp.concatenate([own_ref[2 * C :, :WIDE]] * (C // 16), 0)
-    where = lax.broadcasted_iota(jnp.int32, (C, WIDE), 1)
-    for out, order, tops in (
-        (up_out, (3, 4, 5, None, 6, 7), (4, 5, 6, 7)),
-        (down_out, (2, 3, 4, None, 0, 1), (0, 1, 2, 3)),
-    ):
-
-        @pl.when(jnp.logical_not(lowest))
-        def _(out=out, order=order):
-            for slot, row in enumerate(order):
-                out[:, lane(slot)] = code if row is None else rows[row][:C]
-
-        @pl.when(lowest)
-        def _(out=out, order=order, tops=tops):
-            tiles = [rows[row][C : 2 * C] for row in tops]
-            out[:, lane(0)] = jnp.where((where < 8) | (where >= 120), code, tiles[0])
-            out[:, lane(1)] = jnp.where(where < 8, own_code, tiles[1])
-            out[:, lane(2)] = tiles[2]
-            out[:, lane(3)] = tiles[3]
-            out[:, lane(4)] = rows[order[4]][:C]
-            out[:, lane(5)] = rows[order[5]][:C]
-
-
-def side_code(side_ref):
-    where = lax.broadcasted_iota(jnp.int32, (8, WIDE), 1)
-    first, second = side_ref[0:8, lane(0)].astype(F32), side_ref[0:8, lane(1)].astype(F32)
-    parts = jnp.where(
-        where < 32, first[:, 0:1], jnp.where(where < 96, second[:, 0:1], first[:, 127:128])
-    )
-    return jnp.where(lax.axis_index("pipe") == 0, parts, side_ref[0:8, lane(3)].astype(F32))
 
 
 def forward_kernel(
-    own_ref, before_ref, after_ref, fwd_ref,
-    slope_ref, mask_ref, x_ref,
+    x_ref, height_ref, before_ref, after_ref, left_ref, right_ref, fwd_ref,
+    slope_ref, mask_ref, rows_ref,
     base_ref, cols_ref, code_ref, pre_ref,
 ):
-    own_code = own_ref[2 * C : 2 * C + 8, :WIDE].astype(F32)
-    before_code = side_code(before_ref)
-    after_code = side_code(after_ref)
+    where = lax.broadcasted_iota(jnp.int32, (8, WIDE), 1)
+    middle = (
+        before_ref[C : C + 8, :WIDE].astype(F32),
+        code_of(height_ref, (8, WIDE)),
+        after_ref[C : C + 8, :WIDE].astype(F32),
+    )
+    codes = []
+    for n in range(3):
+        left = left_ref[C : C + 8, lane(n)].astype(F32)
+        right = right_ref[C : C + 8, lane(n)].astype(F32)
+        codes.append(jnp.where(where < 32, left, jnp.where(where < 96, middle[n], right)))
     for row in range(18):
-        code = before_code if row < 5 else own_code if row < 13 else after_code
-        code_ref[:, lane(row)] = code
+        code_ref[:, lane(row)] = codes[0 if row < 5 else 1 if row < 13 else 2]
     for row in range(18):
-        if row < 5:
-            tile = before_ref[:, lane((0, 1, 2, 4, 5)[row])]
-        elif row < 13:
-            tile = own_ref[:C, lane(row - 5)]
-        else:
-            tile = after_ref[:, lane((4, 5, 0, 1, 2)[row - 13])]
+        tile = join(
+            [
+                x_side(left_ref, row),
+                x_layer(x_ref, before_ref, after_ref, row),
+                x_side(right_ref, row),
+            ]
+        )
         if 4 <= row < 14:
-            x_ref[:, lane(row - 4)] = tile
+            rows_ref[:, lane(row - 4)] = tile
         shifted_rows(base_ref, row, tile)
 
     level = lax.broadcasted_iota(jnp.int32, (8, WIDE), 1) % 8
@@ -193,18 +275,20 @@
 
 
 def top_kernel(
-    own_ref, before_ref, after_ref, slope_ref, mask_ref, bwd_ref,
+    own_ref, halo_ref, slope_ref, mask_ref, bwd_ref,
     result_ref, grad_ref, out_ref,
     base_ref, cols_ref, top_ref,
 ):
     active = lax.axis_index("pipe") == SECTIONS - 1
     for row in range(1, 17):
         if row < 5:
-            tile = before_ref[:, lane(row - 1)]
+            tile = halo_ref[:, lane(row - 1)]
         elif row < 13:
-            tile = own_ref[C : 2 * C, lane(row - 5)]
+            at = 8 * WIDE + 64 * (row - 5)
+            middle = own_ref[:, 64 * (row - 5) : 64 * (row - 5) + 64]
+            tile = join([halo_ref[:, at : at + 32], middle, halo_ref[:, at + 32 : at + 64]])
         else:
-            tile = after_ref[:, lane(row - 13)]
+            tile = halo_ref[:, lane(row - 9)]
         top_ref[:, lane(row - 1)] = jnp.where(active, tile, jnp.zeros_like(tile))
 
     def store(pair, value):
@@ -380,20 +464,22 @@
         return pairs
 
     same = [(s, s) for s in range(SECTIONS)]
-    code = jnp.broadcast_to((brick_height + CODE).astype(BF16)[:, None], (16, CELLS))
-    own = jnp.concatenate([section_input.reshape(C, CELLS), top_grad.reshape(C, CELLS), code], 0)
+    x = section_input.reshape(C, CELLS)
+    top = top_grad.reshape(C, CELLS)
     fwd, bwd = call(weight_kernel, [((C, DEEP), BF16)] * 2)(conv_weight[0])
-    left = lax.ppermute(own, both, between(0, 1, same))
-    right = lax.ppermute(own, both, between(0, -1, same))
-    own, up, down = call(
-        pack_kernel,
-        [((2 * C + 16, 8 * WIDE), BF16), ((C, 6 * WIDE), BF16), ((C, 6 * WIDE), BF16)],
-    )(own, left, right)
+    up, down, x, top = call(
+        rows_kernel, [((C + 16, 3 * WIDE), BF16)] * 2 + [((C, CELLS), BF16)] * 2
+    )(x, top, brick_height)
     before = lax.ppermute(up, both, between(1, 0, same))
     after = lax.ppermute(down, both, between(-1, 0, same))
     before, after, fwd, bwd = lax.optimization_barrier((before, after, fwd, bwd))
-    top_before = lax.ppermute(before, both, between(0, 0, [(0, SECTIONS - 1)]))
-    top_after = lax.ppermute(after, both, between(0, 0, [(0, SECTIONS - 1)]))
+    to_right, to_left = call(cols_kernel, [((C + 16, 7 * WIDE), BF16)] * 2)(
+        x, top, brick_height, before, after
+    )
+    left = lax.ppermute(to_right, both, between(0, 1, same))
+    right = lax.ppermute(to_left, both, between(0, -1, same))
+    (halo,) = call(halo_kernel, [((C, 12 * WIDE), BF16)])(before, after, left, right)
+    halo = lax.ppermute(halo, both, between(0, 0, [(0, SECTIONS - 1)]))
 
     core = ((C, 8 * WIDE), BF16)
     cols = ((DEEP, 2 * WIDE), BF16)
@@ -401,12 +487,12 @@
         forward_kernel,
         [((C, 16 * WIDE), F32), ((TAPS, 16, 16 * WIDE), BF16), ((C, 10 * WIDE), BF16)],
         [((9, C, 18 * WIDE), BF16), cols, ((8, 18 * WIDE), F32), ((C, 16 * WIDE), F32)],
-    )(own, before, after, fwd)
+    )(x, brick_height, before, after, left, right, fwd)
     result, grad, out = call(
         top_kernel,
         [((C, 14 * WIDE), BF16), core, core],
         [((9, C, 16 * WIDE), BF16), cols, ((C, 16 * WIDE), BF16)],
-    )(own, top_before, top_after, slope, mask, bwd)
+    )(top, halo, slope, mask, bwd)
     incoming = lax.ppermute(result, both, between(0, 0, [(3, 2)]))
     result, grad, out = call(
         functools.partial(middle_kernel, 14, 2),

time: 163 us -> 161 us (0.988)
  starting transfers between devices: 31.1 us -> 24.8 us
  Pallas kernels: 25.8 us -> 27.6 us
  local copies, waits for them, and re-layouts: 1.16 us -> 2.86 us
    ppermute x1, waiting for transfers between devices: 26 us -> 9.69 us  [body(): from_right = lax.ppermute(left, both, between(0, -1, [(1, 0)]))]
    ppermute x1, waiting for transfers between devices: 0.01 us -> 11.4 us  [body(): from_left = lax.ppermute(right, both, between(0, 1, [(1, 0)]))]
    ppermute x4 -> x3, starting transfers between devices: 15.7 us -> 8.44 us  [the longest x1 4.11 us: body(): halo = lax.ppermute(halo, both, between(0, 0, [(0, SECTIONS - 1)]))]
    ppermute x1, waiting for transfers between devices: 9.36 us -> 13.7 us  [body(): after = lax.ppermute(down, both, between(-1, 0, same))]
    ppermute x4 -> x3, waiting for transfers between devices: 2 us -> 4.94 us  [the longest x1 4.4 us: body(): right = lax.ppermute(to_left, both, between(0, -1, same))]
    pallas_call x10 -> x12, Pallas kernels: 25.8 us -> 27.6 us  [run(): inner(*[arg if arg.dtype == jnp.int32 else pltpu.with_memory_space_constr...]
    unnamed x2 -> x6, local copies, waits for them, and re-layouts: 1.09 us -> 2.86 us
  transfers between devices with their start and end apart: 11 -> 10, of which waited for: 4 -> 5; matrix products, arithmetic and copies ran while one was open for 0% -> 0% of each run, Pallas kernels for 4% -> 5%
where the time goes in v4:
time: 161 us; the launch traced here: 160 us
  blocking collectives  63.9 us (40%)
  waiting for transfers between devices  39.7 us (25%)
  Pallas kernels  27.6 us (17%)
  starting transfers between devices  24.8 us (15%)
  local copies, waits for them, and re-layouts  2.86 us (2%)
    pallas_call x12, Pallas kernels, run(): inner(*[arg if arg.dtype == jnp.int32 else pltpu.with_memory_space_constr...  27.6 us
    all_to_all x1, blocking collectives, body(): lax.all_to_all(part.reshape(ROWS, CHUNK // ROWS, WIDE), 'space', 0, 0, ax...  19 us
    all_gather x1, blocking collectives, body(): lax.all_gather(part.reshape(CHUNK, WIDE), 'space', axis_index_groups=near)  16.6 us
    all_to_all x1, blocking collectives, body(): part = lax.all_to_all(copies, 'space', 0, 0, axis_index_groups=far)  14.5 us
    all_to_all x1, blocking collectives, body(): lax.all_to_all(terms.reshape(COLS, CHUNK, WIDE), 'space', 0, 0, axis_inde...  13.8 us
    ppermute x1, waiting for transfers between devices, body(): after = lax.ppermute(down, both, between(-1, 0, same))  13.7 us
    ppermute x1, waiting for transfers between devices, body(): from_left = lax.ppermute(right, both, between(0, 1, [(1, 0)]))  11.4 us
    ppermute x1, waiting for transfers between devices, body(): from_right = lax.ppermute(left, both, between(0, -1, [(1, 0)]))  9.69 us
  transfers between devices with their start and end apart: 10, of which 5 were waited for; matrix products, arithmetic and copies ran while one was open for 0% of the time, Pallas kernels for 5%

profile of v4, /device:TPU:1, one launch (start us, length us, event | category | flops | bytes accessed | tf_op | source)
XLA Modules:
  0.0 160.4 jit_solution(15988583355992100243)
XLA Ops:
  1.3 0.0 copy-start.1
  1.3 0.9 copy-done.1
  2.2 0.0 copy-start.2
  2.2 0.9 copy-done.2
  3.1 9.6 %collective-permute-start = (bf16[112,384]{1,0:T(8,128)(2,1)S(1)}, bf16[112,384]{1,0:T(8,128)(2,1)S(1)}, u32[]{:S(2)}, u32[]{:S(2)}) collective-permute-start(bf16[112,384]{1,0:T(8,128)(2,1)S(1)} %get-tuple-element.31), channel_id=1, source_target_pairs={{0,32},{1,33},{2,34},{3,35},{4,36},{5,37},{6,38},{7,39},{8,40},{9,... | collective-permute-start | bytes 258056 | tf_op jit(solution)/shard_map/ppermute | solution.py:473
  12.8 1.3 collective-permute-start.1
  14.1 0.0 copy-start
  14.1 1.1 copy-done
  15.2 0.7 shard_map.60
  15.9 0.0 collective-permute-done.before_ref
  15.9 13.7 %collective-permute-done.1.after_ref = bf16[112,384]{1,0:T(8,128)(2,1)S(1)} collective-permute-done((bf16[112,384]{1,0:T(8,128)(2,1)S(1)}, bf16[112,384]{1,0:T(8,128)(2,1)S(1)}, u32[]{:S(2)}, u32[]{:S(2)}) %collective-permute-start.1) | collective-permute-done | bytes 86048 | tf_op jit(solution)/shard_map/ppermute | solution.py:474
  29.6 0.5 shard_map.61
  30.1 2.3 %collective-permute-start.2 = (bf16[112,896]{1,0:T(8,128)(2,1)S(1)}, bf16[112,896]{1,0:T(8,128)(2,1)S(1)}, u32[]{:S(2)}, u32[]{:S(2)}) collective-permute-start(bf16[112,896]{1,0:T(8,128)(2,1)S(1)} %get-tuple-element.38), channel_id=1, source_target_pairs={{0,4},{1,5},{2,6},{3,7},{4,8},{5,9},{6,10},{7,11},{8,12},{9,13},{1... | collective-permute-start | bytes 602120 | tf_op jit(solution)/shard_map/ppermute | solution.py:479
  32.4 2.1 %collective-permute-start.3 = (bf16[112,896]{1,0:T(8,128)(2,1)S(1)}, bf16[112,896]{1,0:T(8,128)(2,1)S(1)}, u32[]{:S(2)}, u32[]{:S(2)}) collective-permute-start(bf16[112,896]{1,0:T(8,128)(2,1)S(1)} %get-tuple-element.39), channel_id=1, source_target_pairs={{4,0},{5,1},{6,2},{7,3},{8,4},{9,5},{10,6},{11,7},{12,8},{13,9},{1... | collective-permute-start | bytes 602120 | tf_op jit(solution)/shard_map/ppermute | solution.py:480
  34.5 0.5 collective-permute-done.2.left_ref
  35.0 4.4 %collective-permute-done.3.right_ref = bf16[112,896]{1,0:T(8,128)(2,1)S(1)} collective-permute-done((bf16[112,896]{1,0:T(8,128)(2,1)S(1)}, bf16[112,896]{1,0:T(8,128)(2,1)S(1)}, u32[]{:S(2)}, u32[]{:S(2)}) %collective-permute-start.3) | collective-permute-done | bytes 200736 | tf_op jit(solution)/shard_map/ppermute | solution.py:480
  39.4 0.3 shard_map.62
  39.7 4.1 %collective-permute-start.4 = (bf16[96,1536]{1,0:T(8,128)(2,1)S(1)}, bf16[96,1536]{1,0:T(8,128)(2,1)S(1)}, u32[]{:S(2)}, u32[]{:S(2)}) collective-permute-start(bf16[96,1536]{1,0:T(8,128)(2,1)S(1)} %shard_map.62), channel_id=1, source_target_pairs={{0,3},{4,7},{8,11},{12,15},{16,19},{20,23},{24,27},{28,31},{32,35}... | collective-permute-start | bytes 884744 | tf_op jit(solution)/shard_map/ppermute | solution.py:482
  43.8 7.5 %shard_map.63 = (f32[96,2048]{1,0:T(8,128)S(1)}, bf16[27,16,2048]{2,1,0:T(8,128)(2,1)S(1)}, bf16[96,1280]{1,0:T(8,128)(2,1)S(1)}) custom-call(bf16[96,512]{1,0:T(8,128)(2,1)S(1)} %get-tuple-element.37.x_ref, s32[1]{0:T(128)S(6)} %copy.6.height_ref, bf16[112,384]{1,0:T(8,128)(2,1)S(1)} %collective-permute-done.before_ref, ...), custom_call_target="tpu_custom_call" | custom-call | tf_op jit(solution)/shard_map/pallas_call | solution.py:43
  51.4 0.0 collective-permute-done.4.halo_ref
  51.4 4.2 %shard_map.64 = (bf16[96,1792]{1,0:T(8,128)(2,1)S(1)}, bf16[96,1024]{1,0:T(8,128)(2,1)S(1)}, bf16[96,1024]{1,0:T(8,128)(2,1)S(1)}) custom-call(bf16[96,512]{1,0:T(8,128)(2,1)S(1)} %get-tuple-element.30.top_ref.own_ref, bf16[96,1536]{1,0:T(8,128)(2,1)S(1)} %collective-permute-done.4.halo_ref, f32[96,2048]{1,0:T(8,128)S(1)} %get-tuple-element.41.slope_ref, ...), custom_call_target="tpu_custom_call" | custom-call | tf_op jit(solution)/shard_map/pallas_call | solution.py:43
  55.6 0.7 collective-permute-start.5
  56.3 0.0 collective-permute-done.5.incoming_ref
  56.3 3.4 %shard_map.65 = (bf16[96,1536]{1,0:T(8,128)(2,1)S(1)}, bf16[96,1024]{1,0:T(8,128)(2,1)S(1)}, bf16[96,1024]{1,0:T(8,128)(2,1)S(1)}) custom-call(bf16[96,1792]{1,0:T(8,128)(2,1)S(1)} %collective-permute-done.5.incoming_ref, f32[96,2048]{1,0:T(8,128)S(1)} %get-tuple-element.41.slope_ref, bf16[27,16,2048]{2,1,0:T(8,128)(2,1)S(1)} %get-tuple-element.42.mask_ref, ...), custom_call_target="tpu_custom_call" | custom-call | tf_op jit(solution)/shard_map/pallas_call | solution.py:43
  59.8 0.7 collective-permute-start.6
  60.4 0.0 collective-permute-done.6.incoming_ref
  60.5 3.0 %shard_map.66 = (bf16[96,640]{1,0:T(8,128)(2,1)S(1)}, bf16[96,128]{1,0:T(8,128)(2,1)S(1)}, bf16[96,128]{1,0:T(8,128)(2,1)S(1)}, bf16[96,1024]{1,0:T(8,128)(2,1)S(1)}, bf16[96,1024]{1,0:T(8,128)(2,1)S(1)}) custom-call(bf16[96,1536]{1,0:T(8,128)(2,1)S(1)} %collective-permute-done.6.incoming_ref, f32[96,2048]{1,0:T(8,128)S(1)} %get-tuple-element.41.slope_ref, ...), custom_call_target="tpu_custom_call" | custom-call | tf_op jit(solution)/shard_map/pallas_call | solution.py:43
  63.5 1.3 collective-permute-start.7
  64.8 1.3 collective-permute-start.8
  66.1 1.5 collective-permute-start.9
  67.6 11.4 %collective-permute-done.8.from_left = bf16[96,128]{1,0:T(8,128)(2,1)S(1)} collective-permute-done((bf16[96,128]{1,0:T(8,128)(2,1)S(1)}, bf16[96,128]{1,0:T(8,128)(2,1)S(1)}, u32[]{:S(2)}, u32[]{:S(2)}) %collective-permute-start.8) | collective-permute-done | bytes 24608 | tf_op jit(solution)/shard_map/ppermute | solution.py:509
  78.9 9.7 %collective-permute-done.9.from_right = bf16[96,128]{1,0:T(8,128)(2,1)S(1)} collective-permute-done((bf16[96,128]{1,0:T(8,128)(2,1)S(1)}, bf16[96,128]{1,0:T(8,128)(2,1)S(1)}, u32[]{:S(2)}, u32[]{:S(2)}) %collective-permute-start.9) | collective-permute-done | bytes 24608 | tf_op jit(solution)/shard_map/ppermute | solution.py:510
  88.6 0.0 collective-permute-done.7.centre_ref
  88.6 5.7 %shard_map.67 = (bf16[96,512]{1,0:T(8,128)(2,1)}, bf16[2048,128]{1,0:T(8,128)(2,1)S(1)}) custom-call(bf16[96,640]{1,0:T(8,128)(2,1)S(1)} %collective-permute-done.7.centre_ref, bf16[96,128]{1,0:T(8,128)(2,1)S(1)} %collective-permute-done.8.from_left, bf16[96,128]{1,0:T(8,128)(2,1)S(1)} %collective-permute-done.9.from_right, ...), custom_call_target="tpu_custom_call" | custom-call | tf_op jit(solution)/shard_map/pallas_call | solution.py:43
  94.4 13.8 %all_to_all.15.parts_ref = bf16[8,256,128]{2,1,0:T(8,128)(2,1)S(1)} all-to-all(bf16[8,256,128]{2,1,0:T(8,128)(2,1)S(1)} %bitcast.11), channel_id=1, replica_groups={{0,4,128,132,256,260,384,388},{8,12,136,140,264,268,392,396},{16,20,144..., dimensions={0} | all-to-all | bytes 1048576 | tf_op jit(solution)/shard_map/all_to_all | solution.py:519
  108.2 0.1 shard_map.68
  108.3 19.0 %all_to_all.16.parts_ref = bf16[16,16,128]{2,1,0:T(8,128)(2,1)S(1)} all-to-all(bf16[16,16,128]{2,1,0:T(8,128)(2,1)S(1)} %bitcast.12), channel_id=1, replica_groups={{0,8,16,24,32,40,48,56,64,72,80,88,96,104,112,120},{4,12,20,28,36,44,52..., dimensions={0} | all-to-all | bytes 131072 | tf_op jit(solution)/shard_map/all_to_all | solution.py:523
  127.3 14.5 %all_to_all.17 = bf16[16,16,128]{2,1,0:T(8,128)(2,1)S(1)} all-to-all(bf16[16,16,128]{2,1,0:T(8,128)(2,1)S(1)} %shard_map.69), channel_id=1, replica_groups={{0,8,16,24,32,40,48,56,64,72,80,88,96,104,112,120},{4,12,20,28,36,44,52..., dimensions={0} | all-to-all | bytes 131072 | tf_op jit(solution)/shard_map/all_to_all | solution.py:527
  141.8 16.6 %all_gather.3 = bf16[8,256,128]{2,1,0:T(8,128)(2,1)S(1)} all-gather(bf16[1,256,128]{2,1,0:T(8,128)(2,1)S(1)} %bitcast.16), channel_id=1, replica_groups={{0,4,128,132,256,260,384,388},{8,12,136,140,264,268,392,396},{16,20,144..., dimensions={0}, use_global_device_ids=true | all-gather | bytes 589824 | tf_op jit(solution)/shard_map/all_gather | solution.py:528
  158.4 2.0 %shard_map.70 = f32[2592,96]{1,0:T(8,128)} custom-call(bf16[2048,128]{1,0:T(8,128)(2,1)S(1)} %bitcast.9), custom_call_target="tpu_custom_call" | custom-call | tf_op jit(solution)/shard_map/pallas_call | solution.py:43
  (2 shorter events, 0.1 us)
Async XLA Ops:
  1.3 0.9 copy-start.1
  2.2 0.9 copy-start.2
  3.1 12.8 %collective-permute-start = (bf16[112,384]{1,0:T(8,128)(2,1)S(1)}, bf16[112,384]{1,0:T(8,128)(2,1)S(1)}, u32[]{:S(2)}, u32[]{:S(2)}) collective-permute-start(bf16[112,384]{1,0:T(8,128)(2,1)S(1)} %get-tuple-element.31), channel_id=1, source_target_pairs={{0,32},{1,33},{2,34},{3,35},{4,36},{5,37},{6,38},{7,39},{8,40},{9,... | collective-permute-start | bytes 258056 | tf_op jit(solution)/shard_map/ppermute | solution.py:473
  12.8 16.9 %collective-permute-start.1 = (bf16[112,384]{1,0:T(8,128)(2,1)S(1)}, bf16[112,384]{1,0:T(8,128)(2,1)S(1)}, u32[]{:S(2)}, u32[]{:S(2)}) collective-permute-start(bf16[112,384]{1,0:T(8,128)(2,1)S(1)} %get-tuple-element.32), channel_id=1, source_target_pairs={{32,0},{33,1},{34,2},{35,3},{36,4},{37,5},{38,6},{39,7},{40,8},{41... | collective-permute-start | bytes 258056 | tf_op jit(solution)/shard_map/ppermute | solution.py:474
  14.1 1.1 copy-start
  30.1 4.9 %collective-permute-start.2 = (bf16[112,896]{1,0:T(8,128)(2,1)S(1)}, bf16[112,896]{1,0:T(8,128)(2,1)S(1)}, u32[]{:S(2)}, u32[]{:S(2)}) collective-permute-start(bf16[112,896]{1,0:T(8,128)(2,1)S(1)} %get-tuple-element.38), channel_id=1, source_target_pairs={{0,4},{1,5},{2,6},{3,7},{4,8},{5,9},{6,10},{7,11},{8,12},{9,13},{1... | collective-permute-start | bytes 602120 | tf_op jit(solution)/shard_map/ppermute | solution.py:479
  32.4 7.0 %collective-permute-start.3 = (bf16[112,896]{1,0:T(8,128)(2,1)S(1)}, bf16[112,896]{1,0:T(8,128)(2,1)S(1)}, u32[]{:S(2)}, u32[]{:S(2)}) collective-permute-start(bf16[112,896]{1,0:T(8,128)(2,1)S(1)} %get-tuple-element.39), channel_id=1, source_target_pairs={{4,0},{5,1},{6,2},{7,3},{8,4},{9,5},{10,6},{11,7},{12,8},{13,9},{1... | collective-permute-start | bytes 602120 | tf_op jit(solution)/shard_map/ppermute | solution.py:480
  39.7 11.6 %collective-permute-start.4 = (bf16[96,1536]{1,0:T(8,128)(2,1)S(1)}, bf16[96,1536]{1,0:T(8,128)(2,1)S(1)}, u32[]{:S(2)}, u32[]{:S(2)}) collective-permute-start(bf16[96,1536]{1,0:T(8,128)(2,1)S(1)} %shard_map.62), channel_id=1, source_target_pairs={{0,3},{4,7},{8,11},{12,15},{16,19},{20,23},{24,27},{28,31},{32,35}... | collective-permute-start | bytes 884744 | tf_op jit(solution)/shard_map/ppermute | solution.py:482
  55.6 0.7 collective-permute-start.5
  59.8 0.7 collective-permute-start.6
  63.5 25.1 %collective-permute-start.7 = (bf16[96,640]{1,0:T(8,128)(2,1)S(1)}, bf16[96,640]{1,0:T(8,128)(2,1)S(1)}, u32[]{:S(2)}, u32[]{:S(2)}) collective-permute-start(bf16[96,640]{1,0:T(8,128)(2,1)S(1)} %get-tuple-element.50), channel_id=1, source_target_pairs={{1,0},{5,4},{9,8},{13,12},{17,16},{21,20},{25,24},{29,28},{33,32},... | collective-permute-start | bytes 368648 | tf_op jit(solution)/shard_map/ppermute | solution.py:508
  64.8 14.1 %collective-permute-start.8 = (bf16[96,128]{1,0:T(8,128)(2,1)S(1)}, bf16[96,128]{1,0:T(8,128)(2,1)S(1)}, u32[]{:S(2)}, u32[]{:S(2)}) collective-permute-start(bf16[96,128]{1,0:T(8,128)(2,1)S(1)} %get-tuple-element.51), channel_id=1, source_target_pairs={{1,4},{5,8},{9,12},{13,16},{17,20},{21,24},{25,28},{33,36},{37,40}... | collective-permute-start | bytes 73736 | tf_op jit(solution)/shard_map/ppermute | solution.py:509
  66.1 22.5 %collective-permute-start.9 = (bf16[96,128]{1,0:T(8,128)(2,1)S(1)}, bf16[96,128]{1,0:T(8,128)(2,1)S(1)}, u32[]{:S(2)}, u32[]{:S(2)}) collective-permute-start(bf16[96,128]{1,0:T(8,128)(2,1)S(1)} %get-tuple-element.52), channel_id=1, source_target_pairs={{5,0},{9,4},{13,8},{17,12},{21,16},{25,20},{29,24},{37,32},{41,36}... | collective-permute-start | bytes 73736 | tf_op jit(solution)/shard_map/ppermute | solution.py:510

commit v5 on v4

--- a/solution.py
+++ b/solution.py
@@ -22,7 +22,7 @@
 BF16 = jnp.bfloat16
 
 
-def call(kernel, outs, scratch=(), leave=()):
+def call(kernel, outs, scratch=(), leave=(), bring=True):
     shapes = [
         jax.ShapeDtypeStruct(shape, dtype) if n in leave else pltpu.VMEM(shape, dtype)
         for n, (shape, dtype) in enumerate(outs)
@@ -42,7 +42,7 @@
         )
         return inner(
             *[
-                arg if arg.dtype == jnp.int32
+                arg if arg.dtype == jnp.int32 or not bring
                 else pltpu.with_memory_space_constraint(arg, pltpu.VMEM)
                 for arg in args
             ]
@@ -63,16 +63,17 @@
     return pltpu.roll(value, by, 1) if by else value
 
 
-def shifted_rows(base_ref, row, tile):
+def shifted_rows(base_ref, row, tile, low=None, high=None):
     level = lax.broadcasted_iota(jnp.int32, (C, WIDE), 1) % 8
-    for oy in (-1, 0, 1):
+    for oy, source in ((-1, low), (0, None), (1, high)):
+        source = tile if source is None else source
         for oz in (-1, 0, 1):
             if oz == 0:
-                moved = turn(tile, -8 * oy)
+                moved = turn(source, -8 * oy)
             elif oz > 0:
-                moved = jnp.where(level < 7, turn(tile, -8 * oy - 1), turn(tile, -8 * oy + 7))
+                moved = jnp.where(level < 7, turn(source, -8 * oy - 1), turn(source, -8 * oy + 7))
             else:
-                moved = jnp.where(level > 0, turn(tile, -8 * oy + 1), turn(tile, -8 * oy - 7))
+                moved = jnp.where(level > 0, turn(source, -8 * oy + 1), turn(source, -8 * oy - 7))
             base_ref[3 * (oy + 1) + oz + 1, :, lane(row)] = moved
 
 
@@ -150,7 +151,7 @@
     codes = join(
         [before_ref[C:, :WIDE], code_of(height_ref, (16, WIDE)).astype(BF16), after_ref[C:, :WIDE]]
     )
-    for out, start in ((right_ref, 32), (left_ref, 0)):
+    for out, start, fifth in ((right_ref, 32, 24), (left_ref, 0, 32)):
 
         def piece(layer, start=start):
             return layer[:, start : start + 32]
@@ -172,13 +173,18 @@
                 )
 
         @pl.when(jnp.logical_not(lowest))
-        def _(out=out, piece=piece):
+        def _(out=out, piece=piece, fifth=fifth):
             outer = [
                 piece(x_layer(x_ref, before_ref, after_ref, row)) for row in (0, 1, 2, 15, 16, 17)
             ]
             out[:C, lane(3)] = join(outer[:4])
             out[:C, lane(4)] = join(outer[4:] + [jnp.zeros((C, 64), BF16)])
-            out[:C, lane(5, 2)] = jnp.zeros((C, 2 * WIDE), BF16)
+            more = [
+                x_layer(x_ref, before_ref, after_ref, row)[:, fifth : fifth + 8]
+                for row in range(18)
+            ]
+            out[:C, lane(5)] = join(more[:16])
+            out[:C, lane(6)] = join(more[16:] + [jnp.zeros((C, 112), BF16)])
 
 
 def x_side(side_ref, row):
@@ -239,7 +245,10 @@
         )
         if 4 <= row < 14:
             rows_ref[:, lane(row - 4)] = tile
-        shifted_rows(base_ref, row, tile)
+        at = 5 * WIDE + 8 * row
+        low = join([tile[:, :120], left_ref[:C, at : at + 8]])
+        high = join([right_ref[:C, at : at + 8], tile[:, 8:]])
+        shifted_rows(base_ref, row, tile, low, high)
 
     level = lax.broadcasted_iota(jnp.int32, (8, WIDE), 1) % 8
     rise_of = {
@@ -248,19 +257,24 @@
         1: jnp.where(level == 7, 1.0, 0.0),
     }
 
-    def masks(row, carry):
-        here = code_ref[:, lane(row + 1)]
+    for rows in ((0, 1, 2), (3,), (4,), (5, 6, 7, 8, 9, 10), (11,), (12,), (13, 14, 15)):
+        here = code_ref[:, lane(rows[0] + 1)]
         for ox in (-1, 0, 1):
-            near = code_ref[:, lane(row + 1 + ox)]
+            near = code_ref[:, lane(rows[0] + 1 + ox)]
             for oy in (-1, 0, 1):
-                rise = turn(near, -8 * oy) - here
+                if oy < 0:
+                    source = jnp.where(where >= 120, near[:, 0:1], near)
+                elif oy > 0:
+                    source = jnp.where(where < 8, near[:, 127:128], near)
+                else:
+                    source = near
+                rise = turn(source, -8 * oy) - here
                 for oz in (-1, 0, 1):
                     keep = jnp.where(rise == rise_of[oz], 1.0, 0.0)
+                    keep = jnp.concatenate([keep, keep], 0).astype(BF16)
                     tap = 9 * (ox + 1) + 3 * (oy + 1) + oz + 1
-                    mask_ref[tap, :, lane(row)] = jnp.concatenate([keep, keep], 0).astype(BF16)
-        return carry
-
-    lax.fori_loop(0, 16, masks, 0)
+                    for row in rows:
+                        mask_ref[tap, :, lane(row)] = keep
 
     def forward(pair, carry):
         make_cols(cols_ref, base_ref, mask_ref, 2 * pair + 1, 2 * pair)
@@ -333,65 +347,35 @@
         out_ref[:, lane(row)] = out_in[:, lane(row)] + result_ref[:, lane(row + 4 - first)]
 
 
-def late_kernel(
-    count, first, incoming_ref, slope_ref, mask_ref, bwd_ref, grad_in, out_in,
-    centre_ref, left_ref, right_ref, grad_ref, out_ref, base_ref, cols_ref, result_ref,
-):
-    middle_kernel(
-        count, first, incoming_ref, slope_ref, mask_ref, bwd_ref, grad_in, out_in,
-        result_ref, grad_ref, out_ref, base_ref, cols_ref,
-    )
-    rows = [result_ref[:, lane(row)] for row in range(count - 2)]
-    for row in range(0, count - 2, 2):
-        centre_ref[:, lane(row // 2)] = jnp.concatenate(
-            [rows[row][:, 32:96], rows[row + 1][:, 32:96]], 1
-        )
-    spare = jnp.zeros((C, WIDE - 8 * (count - 2)), BF16)
-    left_ref[...] = jnp.concatenate([row[:, 32:40] for row in rows] + [spare], 1)
-    right_ref[...] = jnp.concatenate([row[:, 88:96] for row in rows] + [spare], 1)
-
-
-def last_kernel(
-    centre_ref, from_left, from_right, slope_ref, mask_ref, bwd_ref, x_ref, grad_in, out_in,
-    out_ref, terms_ref, base_ref, cols_ref, incoming_ref, sums_ref, all_ref,
-):
-    pad = jnp.zeros((C, 24), BF16)
+def halves(first, second):
+    where = lax.broadcasted_iota(jnp.int32, first.shape, 1)
+    return jnp.where(where < 64, turn(first, -32), turn(second, 32))
+
+
+def gather_kernel(x_ref, mask_ref, all_ref, base_ref):
     for row in range(10):
-        at = 64 * row
-        incoming_ref[:, lane(row)] = jnp.concatenate(
-            [
-                pad,
-                from_left[:, 8 * row : 8 * row + 8],
-                centre_ref[:, at : at + 64],
-                from_right[:, 8 * row : 8 * row + 8],
-                pad,
-            ],
-            1,
-        )
-
-    def store(pair, value):
-        sums_ref[:, lane(2 * pair, 2)] = out_in[:, lane(2 * pair, 2)] + value
-
-    step_rows(incoming_ref, slope_ref, mask_ref, bwd_ref, base_ref, cols_ref, store, 10, 4)
-    for pair in range(4):
-        first, second = sums_ref[:, lane(2 * pair)], sums_ref[:, lane(2 * pair + 1)]
-        out_ref[:, lane(pair)] = jnp.concatenate([first[:, 32:96], second[:, 32:96]], 1)
-
-    where = lax.broadcasted_iota(jnp.int32, (C, WIDE), 1)
-    inside = (where >= 32) & (where < 96)
+        shifted_rows(base_ref, row, x_ref[:, lane(row)])
+
+    def one(pair, carry):
+        for tap in range(TAPS):
+            ox, j = tap // 9 - 1, tap % 9
+            tiles = []
+            for n in range(2):
+                tile = base_ref[j, :, lane(2 * pair + 1 + n + ox)].reshape(C // 16, 16, WIDE)
+                kept = tile * mask_ref[tap, :, lane(2 * pair + 4 + n)][None]
+                tiles.append(kept.reshape(C, WIDE))
+            all_ref[C * tap : C * tap + C, lane(pair)] = halves(*tiles)
+        return carry
+
+    lax.fori_loop(0, 4, one, 0)
+
+
+def terms_kernel(incoming_ref, slope_ref, grad_in, all_ref, terms_ref):
     grads = []
     for row in range(8):
-        grad = grad_in[:, lane(row)] + base_ref[4, :, lane(row + 1)]
-        grads.append(jnp.where(inside, grad, jnp.zeros_like(grad)))
-    grads = jnp.concatenate(grads, 1)
-    for row in range(10):
-        shifted_rows(base_ref, row, x_ref[:, lane(row)])
-
-    def gather(pair, carry):
-        make_cols(all_ref, base_ref, mask_ref, 2 * pair + 1, 2 * pair + 4, 2 * pair)
-        return carry
-
-    lax.fori_loop(0, 4, gather, 0)
+        grad = incoming_ref[:, lane(row + 1)].astype(F32) * slope_ref[:, lane(row + 4)]
+        grads.append(grad_in[:, lane(row)] + grad.astype(BF16))
+    grads = join([halves(grads[2 * pair], grads[2 * pair + 1]) for pair in range(4)])
     for four in range(7):
         parts = []
         for tap in range(4 * four, 4 * four + 4):
@@ -411,6 +395,16 @@
     terms_ref[21 * C :, :] = jnp.zeros((COLS * CHUNK - 21 * C, WIDE), BF16)
 
 
+def last_kernel(
+    incoming_ref, slope_ref, mask_ref, bwd_ref, out_in, out_ref, base_ref, cols_ref
+):
+    def store(pair, value):
+        total = out_in[:, lane(2 * pair, 2)] + value
+        out_ref[:, lane(pair)] = halves(total[:, :WIDE], total[:, WIDE:])
+
+    step_rows(incoming_ref, slope_ref, mask_ref, bwd_ref, base_ref, cols_ref, store, 10, 4)
+
+
 def sum_kernel(parts_ref, out_ref):
     total = parts_ref[0].astype(F32)
     for n in range(1, parts_ref.shape[0]):
@@ -468,7 +462,7 @@
     top = top_grad.reshape(C, CELLS)
     fwd, bwd = call(weight_kernel, [((C, DEEP), BF16)] * 2)(conv_weight[0])
     up, down, x, top = call(
-        rows_kernel, [((C + 16, 3 * WIDE), BF16)] * 2 + [((C, CELLS), BF16)] * 2
+        rows_kernel, [((C + 16, 3 * WIDE), BF16)] * 2 + [((C, CELLS), BF16)] * 2, bring=False
     )(x, top, brick_height)
     before = lax.ppermute(up, both, between(1, 0, same))
     after = lax.ppermute(down, both, between(-1, 0, same))
@@ -500,25 +494,26 @@
         [((9, C, 14 * WIDE), BF16), cols],
     )(incoming, slope, mask, bwd, grad, out)
     incoming = lax.ppermute(result, both, between(0, 0, [(2, 1)]))
-    centre, left, right, grad, out = call(
-        functools.partial(late_kernel, 12, 3),
-        [((C, 5 * WIDE), BF16), ((C, WIDE), BF16), ((C, WIDE), BF16), core, core],
-        [((9, C, 12 * WIDE), BF16), cols, ((C, 10 * WIDE), BF16)],
+    result, grad, out = call(
+        functools.partial(middle_kernel, 12, 3),
+        [((C, 10 * WIDE), BF16), core, core],
+        [((9, C, 12 * WIDE), BF16), cols],
     )(incoming, slope, mask, bwd, grad, out)
-    centre = lax.ppermute(centre, both, between(0, 0, [(1, 0)]))
-    from_left = lax.ppermute(right, both, between(0, 1, [(1, 0)]))
-    from_right = lax.ppermute(left, both, between(0, -1, [(1, 0)]))
-    out, terms = call(
-        last_kernel,
-        [((C, CELLS), BF16), ((COLS * CHUNK, WIDE), BF16)],
-        [((9, C, 10 * WIDE), BF16), cols, ((C, 10 * WIDE), BF16), core, ((DEEP, 8 * WIDE), BF16)],
-        leave=(0,),
-    )(centre, from_left, from_right, slope, mask, bwd, x_rows, grad, out)
+    incoming = lax.ppermute(result, both, between(0, 0, [(1, 0)]))
+    x_rows, _ = lax.optimization_barrier((x_rows, result))
+    (x_cols,) = call(gather_kernel, [((DEEP, CELLS), BF16)], [((9, C, 10 * WIDE), BF16)])(
+        x_rows, mask
+    )
+    (terms,) = call(terms_kernel, [((COLS * CHUNK, WIDE), BF16)])(incoming, slope, grad, x_cols)
 
     near, far = groups(devices)
     parts = lax.all_to_all(
         terms.reshape(COLS, CHUNK, WIDE), "space", 0, 0, axis_index_groups=near
     )
+    parts, out = lax.optimization_barrier((parts, out))
+    (out,) = call(
+        last_kernel, [((C, CELLS), BF16)], [((9, C, 10 * WIDE), BF16), cols], leave=(0,)
+    )(incoming, slope, mask, bwd, out)
     (part,) = call(sum_kernel, [((CHUNK, WIDE), BF16)])(parts)
     pieces = lax.all_to_all(
         part.reshape(ROWS, CHUNK // ROWS, WIDE), "space", 0, 0, axis_index_groups=far

time: 161 us -> 160 us (level)
  blocking collectives: 63.9 us -> 56.6 us
  waiting for transfers between devices: 39.7 us -> 44.1 us
    all_to_all x1 -> x0, blocking collectives: 14.5 us -> none  [body(): part = lax.all_to_all(copies, 'space', 0, 0, axis_index_groups=far)]
    all_to_all x0 -> x1, waiting for transfers between devices: none -> 8.48 us  [body(): part = lax.all_to_all(copies, 'space', 0, 0, axis_index_groups=far)]
    all_to_all x1, blocking collectives: 19 us -> 26.1 us  [body(): lax.all_to_all(part.reshape(ROWS, CHUNK // ROWS, WIDE), 'space', 0, 0, ax...]
    all_to_all x0 -> x1, starting transfers between devices: none -> 4.16 us  [body(): part = lax.all_to_all(copies, 'space', 0, 0, axis_index_groups=far)]
    ppermute x3 -> x1, waiting for transfers between devices: 21.1 us -> 17 us  [body(): incoming = lax.ppermute(result, both, between(0, 0, [(1, 0)]))]
    ppermute x3 -> x1, starting transfers between devices: 4.06 us -> 1.29 us  [body(): incoming = lax.ppermute(result, both, between(0, 0, [(1, 0)]))]
    pallas_call x12 -> x14, Pallas kernels: 27.6 us -> 28.4 us  [run(): inner(*[arg if arg.dtype == jnp.int32 or not bring else pltpu.with_memory...]
  transfers between devices with their start and end apart: 10 -> 9, of which waited for: 5 -> 5; matrix products, arithmetic and copies ran while one was open for 0% -> 0% of each run, Pallas kernels for 5% -> 8%
where the time goes in v5:
time: 160 us
  blocking collectives  56.6 us (35%)
  waiting for transfers between devices  44.1 us (28%)
  Pallas kernels  28.4 us (18%)
  starting transfers between devices  26.4 us (16%)
  local copies, waits for them, and re-layouts  2.86 us (2%)
    pallas_call x14, Pallas kernels, run(): inner(*[arg if arg.dtype == jnp.int32 or not bring else pltpu.with_memory...  28.4 us
    all_to_all x1, blocking collectives, body(): lax.all_to_all(part.reshape(ROWS, CHUNK // ROWS, WIDE), 'space', 0, 0, ax...  26.1 us
    ppermute x1, waiting for transfers between devices, body(): incoming = lax.ppermute(result, both, between(0, 0, [(1, 0)]))  17 us
    all_gather x1, blocking collectives, body(): lax.all_gather(part.reshape(CHUNK, WIDE), 'space', axis_index_groups=near)  16.7 us
    all_to_all x1, blocking collectives, body(): lax.all_to_all(terms.reshape(COLS, CHUNK, WIDE), 'space', 0, 0, axis_inde...  13.8 us
    ppermute x1, waiting for transfers between devices, body(): after = lax.ppermute(down, both, between(-1, 0, same))  13.7 us
    ppermute x1, starting transfers between devices, body(): before = lax.ppermute(up, both, between(1, 0, same))  9.65 us
    all_to_all x1, waiting for transfers between devices, body(): part = lax.all_to_all(copies, 'space', 0, 0, axis_index_groups=far)  8.48 us
  transfers between devices with their start and end apart: 9, of which 5 were waited for; matrix products, arithmetic and copies ran while one was open for 0% of the time, Pallas kernels for 8%

profile of v5, /device:TPU:1, one launch (start us, length us, event | category | flops | bytes accessed | tf_op | source)
XLA Modules:
  0.0 159.8 jit_solution(9032702910790894343)
XLA Ops:
  1.3 0.0 copy-start.1
  1.3 0.9 copy-done.1
  2.2 0.0 copy-start.2
  2.2 0.9 copy-done.2
  3.1 9.6 %collective-permute-start = (bf16[112,384]{1,0:T(8,128)(2,1)S(1)}, bf16[112,384]{1,0:T(8,128)(2,1)S(1)}, u32[]{:S(2)}, u32[]{:S(2)}) collective-permute-start(bf16[112,384]{1,0:T(8,128)(2,1)S(1)} %get-tuple-element.30), channel_id=1, source_target_pairs={{0,32},{1,33},{2,34},{3,35},{4,36},{5,37},{6,38},{7,39},{8,40},{9,... | collective-permute-start | bytes 258056 | tf_op jit(solution)/shard_map/ppermute | solution.py:467
  12.8 1.3 collective-permute-start.1
  14.1 0.0 copy-start
  14.1 1.1 copy-done
  15.2 0.7 shard_map.60
  15.9 0.0 collective-permute-done.before_ref
  15.9 13.7 %collective-permute-done.1.after_ref = bf16[112,384]{1,0:T(8,128)(2,1)S(1)} collective-permute-done((bf16[112,384]{1,0:T(8,128)(2,1)S(1)}, bf16[112,384]{1,0:T(8,128)(2,1)S(1)}, u32[]{:S(2)}, u32[]{:S(2)}) %collective-permute-start.1) | collective-permute-done | bytes 86048 | tf_op jit(solution)/shard_map/ppermute | solution.py:468
  29.6 0.5 shard_map.61
  30.2 2.3 %collective-permute-start.2 = (bf16[112,896]{1,0:T(8,128)(2,1)S(1)}, bf16[112,896]{1,0:T(8,128)(2,1)S(1)}, u32[]{:S(2)}, u32[]{:S(2)}) collective-permute-start(bf16[112,896]{1,0:T(8,128)(2,1)S(1)} %get-tuple-element.37), channel_id=1, source_target_pairs={{0,4},{1,5},{2,6},{3,7},{4,8},{5,9},{6,10},{7,11},{8,12},{9,13},{1... | collective-permute-start | bytes 602120 | tf_op jit(solution)/shard_map/ppermute | solution.py:473
  32.4 2.1 %collective-permute-start.3 = (bf16[112,896]{1,0:T(8,128)(2,1)S(1)}, bf16[112,896]{1,0:T(8,128)(2,1)S(1)}, u32[]{:S(2)}, u32[]{:S(2)}) collective-permute-start(bf16[112,896]{1,0:T(8,128)(2,1)S(1)} %get-tuple-element.38), channel_id=1, source_target_pairs={{4,0},{5,1},{6,2},{7,3},{8,4},{9,5},{10,6},{11,7},{12,8},{13,9},{1... | collective-permute-start | bytes 602120 | tf_op jit(solution)/shard_map/ppermute | solution.py:474
  34.5 0.5 collective-permute-done.2.left_ref
  35.1 4.4 %collective-permute-done.3.right_ref = bf16[112,896]{1,0:T(8,128)(2,1)S(1)} collective-permute-done((bf16[112,896]{1,0:T(8,128)(2,1)S(1)}, bf16[112,896]{1,0:T(8,128)(2,1)S(1)}, u32[]{:S(2)}, u32[]{:S(2)}) %collective-permute-start.3) | collective-permute-done | bytes 200736 | tf_op jit(solution)/shard_map/ppermute | solution.py:474
  39.4 0.3 shard_map.62
  39.7 4.3 %collective-permute-start.4 = (bf16[96,1536]{1,0:T(8,128)(2,1)S(1)}, bf16[96,1536]{1,0:T(8,128)(2,1)S(1)}, u32[]{:S(2)}, u32[]{:S(2)}) collective-permute-start(bf16[96,1536]{1,0:T(8,128)(2,1)S(1)} %shard_map.62), channel_id=1, source_target_pairs={{0,3},{4,7},{8,11},{12,15},{16,19},{20,23},{24,27},{28,31},{32,35}... | collective-permute-start | bytes 884744 | tf_op jit(solution)/shard_map/ppermute | solution.py:476
  44.1 6.9 %shard_map.63 = (f32[96,2048]{1,0:T(8,128)S(1)}, bf16[27,16,2048]{2,1,0:T(8,128)(2,1)S(1)}, bf16[96,1280]{1,0:T(8,128)(2,1)S(1)}) custom-call(bf16[96,512]{1,0:T(8,128)(2,1)S(1)} %get-tuple-element.36.x_ref, s32[1]{0:T(128)S(6)} %copy.6.height_ref, bf16[112,384]{1,0:T(8,128)(2,1)S(1)} %collective-permute-done.before_ref, ...), custom_call_target="tpu_custom_call" | custom-call | tf_op jit(solution)/shard_map/pallas_call | solution.py:43
  51.0 0.0 collective-permute-done.4.halo_ref
  51.0 4.2 %shard_map.64 = (bf16[96,1792]{1,0:T(8,128)(2,1)S(1)}, bf16[96,1024]{1,0:T(8,128)(2,1)S(1)}, bf16[96,1024]{1,0:T(8,128)(2,1)S(1)}) custom-call(bf16[96,512]{1,0:T(8,128)(2,1)S(1)} %get-tuple-element.29.top_ref.own_ref, bf16[96,1536]{1,0:T(8,128)(2,1)S(1)} %collective-permute-done.4.halo_ref, f32[96,2048]{1,0:T(8,128)S(1)} %get-tuple-element.40.slope_ref, ...), custom_call_target="tpu_custom_call" | custom-call | tf_op jit(solution)/shard_map/pallas_call | solution.py:43
  55.2 0.7 collective-permute-start.5
  55.9 0.0 collective-permute-done.5.incoming_ref
  55.9 3.4 %shard_map.65 = (bf16[96,1536]{1,0:T(8,128)(2,1)S(1)}, bf16[96,1024]{1,0:T(8,128)(2,1)S(1)}, bf16[96,1024]{1,0:T(8,128)(2,1)S(1)}) custom-call(bf16[96,1792]{1,0:T(8,128)(2,1)S(1)} %collective-permute-done.5.incoming_ref, f32[96,2048]{1,0:T(8,128)S(1)} %get-tuple-element.40.slope_ref, bf16[27,16,2048]{2,1,0:T(8,128)(2,1)S(1)} %get-tuple-element.41.mask_ref, ...), custom_call_target="tpu_custom_call" | custom-call | tf_op jit(solution)/shard_map/pallas_call | solution.py:43
  59.3 0.7 collective-permute-start.6
  60.0 0.0 collective-permute-done.6.incoming_ref
  60.0 2.9 %shard_map.66 = (bf16[96,1280]{1,0:T(8,128)(2,1)S(1)}, bf16[96,1024]{1,0:T(8,128)(2,1)S(1)}, bf16[96,1024]{1,0:T(8,128)(2,1)S(1)}) custom-call(bf16[96,1536]{1,0:T(8,128)(2,1)S(1)} %collective-permute-done.6.incoming_ref, f32[96,2048]{1,0:T(8,128)S(1)} %get-tuple-element.40.slope_ref, bf16[27,16,2048]{2,1,0:T(8,128)(2,1)S(1)} %get-tuple-element.41.mask_ref, ...), custom_call_target="tpu_custom_call" | custom-call | tf_op jit(solution)/shard_map/pallas_call | solution.py:43
  62.9 1.3 collective-permute-start.7
  64.2 2.4 %shard_map.67.all_ref = bf16[2592,512]{1,0:T(8,128)(2,1)S(1)} custom-call(bf16[96,1280]{1,0:T(8,128)(2,1)S(1)} %get-tuple-element.52.x_ref, bf16[27,16,2048]{2,1,0:T(8,128)(2,1)S(1)} %get-tuple-element.41.mask_ref), custom_call_target="tpu_custom_call" | custom-call | tf_op jit(solution)/shard_map/pallas_call | solution.py:43
  66.6 17.0 %collective-permute-done.7.incoming_ref = bf16[96,1280]{1,0:T(8,128)(2,1)S(1)} collective-permute-done((bf16[96,1280]{1,0:T(8,128)(2,1)S(1)}, bf16[96,1280]{1,0:T(8,128)(2,1)S(1)}, u32[]{:S(2)}, u32[]{:S(2)}) %collective-permute-start.7) | collective-permute-done | bytes 245792 | tf_op jit(solution)/shard_map/ppermute | solution.py:502
  83.5 1.0 shard_map.68
  84.6 13.8 %all_to_all.15.parts_ref = bf16[8,256,128]{2,1,0:T(8,128)(2,1)S(1)} all-to-all(bf16[8,256,128]{2,1,0:T(8,128)(2,1)S(1)} %bitcast.9), channel_id=1, replica_groups={{0,4,128,132,256,260,384,388},{8,12,136,140,264,268,392,396},{16,20,144..., dimensions={0} | all-to-all | bytes 1048576 | tf_op jit(solution)/shard_map/all_to_all | solution.py:510
  98.4 0.1 shard_map.70
  98.5 26.1 %all_to_all.16.parts_ref = bf16[16,16,128]{2,1,0:T(8,128)(2,1)S(1)} all-to-all(bf16[16,16,128]{2,1,0:T(8,128)(2,1)S(1)} %bitcast.12), channel_id=1, replica_groups={{0,8,16,24,32,40,48,56,64,72,80,88,96,104,112,120},{4,12,20,28,36,44,52..., dimensions={0} | all-to-all | bytes 131072 | tf_op jit(solution)/shard_map/all_to_all | solution.py:518
  124.5 0.7 shard_map.71
  125.2 4.2 %all-to-all-start.2 = ((bf16[16,16,128]{2,1,0:T(8,128)(2,1)}), bf16[16,16,128]{2,1,0:T(8,128)(2,1)}, u32[]{:S(2)}, u32[]{:S(2)}) async-start(bf16[16,16,128]{2,1,0:T(8,128)(2,1)} %shard_map.71), calls=%async_computation.2 | async-start | bytes 131072 | tf_op jit(solution)/shard_map/all_to_all | solution.py:522
  129.3 3.3 %shard_map.69 = bf16[96,512]{1,0:T(8,128)(2,1)} custom-call(bf16[96,1280]{1,0:T(8,128)(2,1)S(1)} %collective-permute-done.7.incoming_ref, f32[96,2048]{1,0:T(8,128)S(1)} %get-tuple-element.40.slope_ref, bf16[27,16,2048]{2,1,0:T(8,128)(2,1)S(1)} %get-tuple-element.41.mask_ref, bf16[96,2592]{1,0:T(8,128)(2,1)S(1)} %get-tuple-element.42.bwd_ref, ...), custom_call_target="tpu_custom_call" | custom-call | tf_op jit(solution)/shard_map/pallas_call | solution.py:43
  132.6 8.5 %all-to-all-done.2 = bf16[16,16,128]{2,1,0:T(8,128)(2,1)} async-done(((bf16[16,16,128]{2,1,0:T(8,128)(2,1)}), bf16[16,16,128]{2,1,0:T(8,128)(2,1)}, u32[]{:S(2)}, u32[]{:S(2)}) %all-to-all-start.2) | async-done | bytes 65568 | tf_op jit(solution)/shard_map/all_to_all | solution.py:522
  141.1 16.7 %all_gather.3 = bf16[8,256,128]{2,1,0:T(8,128)(2,1)S(1)} all-gather(bf16[1,256,128]{2,1,0:T(8,128)(2,1)} %bitcast.6), channel_id=1, replica_groups={{0,4,128,132,256,260,384,388},{8,12,136,140,264,268,392,396},{16,20,144..., dimensions={0}, use_global_device_ids=true | all-gather | bytes 589824 | tf_op jit(solution)/shard_map/all_gather | solution.py:523
  157.8 2.0 %shard_map.72 = f32[2592,96]{1,0:T(8,128)} custom-call(bf16[2048,128]{1,0:T(8,128)(2,1)S(1)} %bitcast.10), custom_call_target="tpu_custom_call" | custom-call | tf_op jit(solution)/shard_map/pallas_call | solution.py:43
  (1 shorter events, 0.0 us)
Async XLA Ops:
  1.3 0.9 copy-start.1
  2.2 0.9 copy-start.2
  3.1 12.8 %collective-permute-start = (bf16[112,384]{1,0:T(8,128)(2,1)S(1)}, bf16[112,384]{1,0:T(8,128)(2,1)S(1)}, u32[]{:S(2)}, u32[]{:S(2)}) collective-permute-start(bf16[112,384]{1,0:T(8,128)(2,1)S(1)} %get-tuple-element.30), channel_id=1, source_target_pairs={{0,32},{1,33},{2,34},{3,35},{4,36},{5,37},{6,38},{7,39},{8,40},{9,... | collective-permute-start | bytes 258056 | tf_op jit(solution)/shard_map/ppermute | solution.py:467
  12.8 16.9 %collective-permute-start.1 = (bf16[112,384]{1,0:T(8,128)(2,1)S(1)}, bf16[112,384]{1,0:T(8,128)(2,1)S(1)}, u32[]{:S(2)}, u32[]{:S(2)}) collective-permute-start(bf16[112,384]{1,0:T(8,128)(2,1)S(1)} %get-tuple-element.31), channel_id=1, source_target_pairs={{32,0},{33,1},{34,2},{35,3},{36,4},{37,5},{38,6},{39,7},{40,8},{41... | collective-permute-start | bytes 258056 | tf_op jit(solution)/shard_map/ppermute | solution.py:468
  14.1 1.1 copy-start
  30.2 4.9 %collective-permute-start.2 = (bf16[112,896]{1,0:T(8,128)(2,1)S(1)}, bf16[112,896]{1,0:T(8,128)(2,1)S(1)}, u32[]{:S(2)}, u32[]{:S(2)}) collective-permute-start(bf16[112,896]{1,0:T(8,128)(2,1)S(1)} %get-tuple-element.37), channel_id=1, source_target_pairs={{0,4},{1,5},{2,6},{3,7},{4,8},{5,9},{6,10},{7,11},{8,12},{9,13},{1... | collective-permute-start | bytes 602120 | tf_op jit(solution)/shard_map/ppermute | solution.py:473
  32.4 7.0 %collective-permute-start.3 = (bf16[112,896]{1,0:T(8,128)(2,1)S(1)}, bf16[112,896]{1,0:T(8,128)(2,1)S(1)}, u32[]{:S(2)}, u32[]{:S(2)}) collective-permute-start(bf16[112,896]{1,0:T(8,128)(2,1)S(1)} %get-tuple-element.38), channel_id=1, source_target_pairs={{4,0},{5,1},{6,2},{7,3},{8,4},{9,5},{10,6},{11,7},{12,8},{13,9},{1... | collective-permute-start | bytes 602120 | tf_op jit(solution)/shard_map/ppermute | solution.py:474
  39.7 11.3 %collective-permute-start.4 = (bf16[96,1536]{1,0:T(8,128)(2,1)S(1)}, bf16[96,1536]{1,0:T(8,128)(2,1)S(1)}, u32[]{:S(2)}, u32[]{:S(2)}) collective-permute-start(bf16[96,1536]{1,0:T(8,128)(2,1)S(1)} %shard_map.62), channel_id=1, source_target_pairs={{0,3},{4,7},{8,11},{12,15},{16,19},{20,23},{24,27},{28,31},{32,35}... | collective-permute-start | bytes 884744 | tf_op jit(solution)/shard_map/ppermute | solution.py:476
  55.2 0.7 collective-permute-start.5
  59.3 0.7 collective-permute-start.6
  62.9 20.6 %collective-permute-start.7 = (bf16[96,1280]{1,0:T(8,128)(2,1)S(1)}, bf16[96,1280]{1,0:T(8,128)(2,1)S(1)}, u32[]{:S(2)}, u32[]{:S(2)}) collective-permute-start(bf16[96,1280]{1,0:T(8,128)(2,1)S(1)} %get-tuple-element.49), channel_id=1, source_target_pairs={{1,0},{5,4},{9,8},{13,12},{17,16},{21,20},{25,24},{29,28},{33,32},... | collective-permute-start | bytes 737288 | tf_op jit(solution)/shard_map/ppermute | solution.py:502
  125.2 15.9 %all-to-all-start.2 = ((bf16[16,16,128]{2,1,0:T(8,128)(2,1)}), bf16[16,16,128]{2,1,0:T(8,128)(2,1)}, u32[]{:S(2)}, u32[]{:S(2)}) async-start(bf16[16,16,128]{2,1,0:T(8,128)(2,1)} %shard_map.71), calls=%async_computation.2 | async-start | bytes 131072 | tf_op jit(solution)/shard_map/all_to_all | solution.py:522

commit v6 on v5

--- a/solution.py
+++ b/solution.py
@@ -16,7 +16,9 @@
 DEEP = TAPS * C
 WIDE = 128
 CODE = 8
-CHUNK = 256
+NEAR = 16
+FAR = 8
+CHUNK = 128
 VMEM_BYTES = 32 * 1024 * 1024
 F32 = jnp.float32
 BF16 = jnp.bfloat16
@@ -33,17 +35,22 @@
             kernel,
             out_shape=shapes,
             in_specs=[
-                pl.BlockSpec(memory_space=pltpu.SMEM if arg.dtype == jnp.int32 else pltpu.VMEM)
+                pl.BlockSpec(
+                    memory_space=pltpu.SMEM if arg.dtype == jnp.int32
+                    else pltpu.VMEM if bring else pl.ANY
+                )
                 for arg in args
             ],
             out_specs=[pl.BlockSpec(memory_space=pltpu.VMEM)] * len(shapes),
-            scratch_shapes=[pltpu.VMEM(shape, dtype) for shape, dtype in scratch],
+            scratch_shapes=[
+                pltpu.VMEM(*item) if isinstance(item, tuple) else item for item in scratch
+            ],
             compiler_params=pltpu.CompilerParams(vmem_limit_bytes=VMEM_BYTES),
         )
         return inner(
             *[
-                arg if arg.dtype == jnp.int32 or not bring
-                else pltpu.with_memory_space_constraint(arg, pltpu.VMEM)
+                arg if arg.dtype == jnp.int32
+                else pltpu.with_memory_space_constraint(arg, pltpu.VMEM if bring else pltpu.HBM)
                 for arg in args
             ]
         )
@@ -102,7 +109,13 @@
     return jnp.full(shape, (height_ref[0] + CODE).astype(F32), F32)
 
 
-def rows_kernel(x_ref, top_ref, height_ref, up_ref, down_ref, x_out, top_out):
+def rows_kernel(x_hbm, top_hbm, height_ref, up_ref, down_ref, x_ref, top_ref, sems):
+    x_copy = pltpu.make_async_copy(x_hbm, x_ref, sems.at[0])
+    top_copy = pltpu.make_async_copy(top_hbm, top_ref, sems.at[1])
+    x_copy.start()
+    top_copy.start()
+    x_copy.wait()
+    top_copy.wait()
     lowest = lax.axis_index("pipe") == 0
     code = code_of(height_ref, (16, 3 * WIDE)).astype(BF16)
     spare = jnp.zeros((C, 64), BF16)
@@ -110,8 +123,6 @@
     down_ref[C:, :] = code
     up_ref[:C, :WIDE] = x_ref[:, 384:512]
     down_ref[:C, :WIDE] = x_ref[:, 0:128]
-    x_out[...] = x_ref[...]
-    top_out[...] = top_ref[...]
 
     @pl.when(lowest)
     def _():
@@ -332,19 +343,32 @@
     lax.fori_loop(0, (count - 2) // 2, backward, 0)
 
 
+def spread(packed_ref, width, row):
+    spare = jnp.zeros((C, (WIDE - width) // 2), BF16)
+    return join([spare, packed_ref[:, width * row : width * row + width], spare])
+
+
 def middle_kernel(
-    count, first, incoming_ref, slope_ref, mask_ref, bwd_ref, grad_in, out_in,
-    result_ref, grad_ref, out_ref, base_ref, cols_ref,
+    count, first, width_in, width_out, incoming_ref, slope_ref, mask_ref, bwd_ref, grad_in, out_in,
+    result_ref, grad_ref, out_ref, base_ref, cols_ref, rows_ref, full_ref,
 ):
+    for row in range(count):
+        rows_ref[:, lane(row)] = (
+            incoming_ref[:, lane(row)] if width_in == WIDE else spread(incoming_ref, width_in, row)
+        )
+
     def store(pair, value):
-        result_ref[:, lane(2 * pair, 2)] = value
-
-    step_rows(
-        incoming_ref, slope_ref, mask_ref, bwd_ref, base_ref, cols_ref, store, count, first
-    )
+        full_ref[:, lane(2 * pair, 2)] = value
+
+    step_rows(rows_ref, slope_ref, mask_ref, bwd_ref, base_ref, cols_ref, store, count, first)
+    skip = (WIDE - width_out) // 2
+    rows = [full_ref[:, lane(row)] for row in range(count - 2)]
+    packed = [row[:, skip : skip + width_out] for row in rows]
+    spare = result_ref.shape[1] - width_out * (count - 2)
+    result_ref[...] = join(packed + [jnp.zeros((C, spare), BF16)] if spare else packed)
     for row in range(8):
         grad_ref[:, lane(row)] = grad_in[:, lane(row)] + base_ref[4, :, lane(row + 5 - first)]
-        out_ref[:, lane(row)] = out_in[:, lane(row)] + result_ref[:, lane(row + 4 - first)]
+        out_ref[:, lane(row)] = out_in[:, lane(row)] + rows[row + 4 - first]
 
 
 def halves(first, second):
@@ -370,7 +394,9 @@
     lax.fori_loop(0, 4, one, 0)
 
 
-def terms_kernel(incoming_ref, slope_ref, grad_in, all_ref, terms_ref):
+def terms_kernel(packed_ref, slope_ref, grad_in, all_ref, terms_ref, incoming_ref):
+    for row in range(10):
+        incoming_ref[:, lane(row)] = spread(packed_ref, 80, row)
     grads = []
     for row in range(8):
         grad = incoming_ref[:, lane(row + 1)].astype(F32) * slope_ref[:, lane(row + 4)]
@@ -392,7 +418,7 @@
         terms_ref[at : at + C, :] = jnp.concatenate([first, second[:, :32]], 1)
         terms_ref[at + C : at + 2 * C, :] = jnp.concatenate([second[:, 32:], third[:, :64]], 1)
         terms_ref[at + 2 * C : at + 3 * C, :] = jnp.concatenate([third[:, 64:], fourth], 1)
-    terms_ref[21 * C :, :] = jnp.zeros((COLS * CHUNK - 21 * C, WIDE), BF16)
+    terms_ref[21 * C :, :] = jnp.zeros((NEAR * CHUNK - 21 * C, WIDE), BF16)
 
 
 def last_kernel(
@@ -410,11 +436,8 @@
     for n in range(1, parts_ref.shape[0]):
         total = total + parts_ref[n].astype(F32)
     total = total.astype(BF16)
-    if len(out_ref.shape) == 2:
-        out_ref[...] = total
-    else:
-        for n in range(out_ref.shape[0]):
-            out_ref[n] = total
+    for n in range(out_ref.shape[0]):
+        out_ref[n] = total
 
 
 def scale_kernel(whole_ref, out_ref):
@@ -435,15 +458,17 @@
             out_ref[C * tap : C * tap + C, :] = parts[n]
 
 
-def groups(devices):
-    rows = devices // (2 * ROWS)
-    near = [[y * 32 + z * 2 + c for y in range(rows) for c in range(2)] for z in range(ROWS)]
-    far = [[y * 32 + z * 2 + c for z in range(ROWS)] for y in range(rows) for c in range(2)]
+def groups():
+    def device(y, high, low, core):
+        return y * 32 + (2 * high + low) * 2 + core
+
+    kinds = [(y, low, core) for y in range(4) for low in range(2) for core in range(2)]
+    near = [[device(y, high, low, core) for y, low, core in kinds] for high in range(FAR)]
+    far = [[device(y, high, low, core) for high in range(FAR)] for y, low, core in kinds]
     return near, far
 
 
 def body(section_input, top_grad, conv_weight, brick_height):
-    devices = lax.axis_size("space")
     both = ("space", "pipe")
 
     def between(by_row, by_col, sections):
@@ -462,7 +487,10 @@
     top = top_grad.reshape(C, CELLS)
     fwd, bwd = call(weight_kernel, [((C, DEEP), BF16)] * 2)(conv_weight[0])
     up, down, x, top = call(
-        rows_kernel, [((C + 16, 3 * WIDE), BF16)] * 2 + [((C, CELLS), BF16)] * 2, bring=False
+        rows_kernel,
+        [((C + 16, 3 * WIDE), BF16)] * 2 + [((C, CELLS), BF16)] * 2,
+        [pltpu.SemaphoreType.DMA((2,))],
+        bring=False,
     )(x, top, brick_height)
     before = lax.ppermute(up, both, between(1, 0, same))
     after = lax.ppermute(down, both, between(-1, 0, same))
@@ -489,39 +517,40 @@
     )(top, halo, slope, mask, bwd)
     incoming = lax.ppermute(result, both, between(0, 0, [(3, 2)]))
     result, grad, out = call(
-        functools.partial(middle_kernel, 14, 2),
-        [((C, 12 * WIDE), BF16), core, core],
-        [((9, C, 14 * WIDE), BF16), cols],
+        functools.partial(middle_kernel, 14, 2, WIDE, 96),
+        [((C, 12 * 96), BF16), core, core],
+        [((9, C, 14 * WIDE), BF16), cols, ((C, 14 * WIDE), BF16), ((C, 12 * WIDE), BF16)],
     )(incoming, slope, mask, bwd, grad, out)
     incoming = lax.ppermute(result, both, between(0, 0, [(2, 1)]))
     result, grad, out = call(
-        functools.partial(middle_kernel, 12, 3),
-        [((C, 10 * WIDE), BF16), core, core],
-        [((9, C, 12 * WIDE), BF16), cols],
+        functools.partial(middle_kernel, 12, 3, 96, 80),
+        [((C, 7 * WIDE), BF16), core, core],
+        [((9, C, 12 * WIDE), BF16), cols, ((C, 12 * WIDE), BF16), ((C, 10 * WIDE), BF16)],
     )(incoming, slope, mask, bwd, grad, out)
     incoming = lax.ppermute(result, both, between(0, 0, [(1, 0)]))
     x_rows, _ = lax.optimization_barrier((x_rows, result))
     (x_cols,) = call(gather_kernel, [((DEEP, CELLS), BF16)], [((9, C, 10 * WIDE), BF16)])(
         x_rows, mask
     )
-    (terms,) = call(terms_kernel, [((COLS * CHUNK, WIDE), BF16)])(incoming, slope, grad, x_cols)
-
-    near, far = groups(devices)
+    terms, incoming = call(
+        terms_kernel, [((NEAR * CHUNK, WIDE), BF16), ((C, 10 * WIDE), BF16)]
+    )(incoming, slope, grad, x_cols)
+
+    near, far = groups()
     parts = lax.all_to_all(
-        terms.reshape(COLS, CHUNK, WIDE), "space", 0, 0, axis_index_groups=near
+        terms.reshape(NEAR, CHUNK, WIDE), "space", 0, 0, axis_index_groups=near
     )
     parts, out = lax.optimization_barrier((parts, out))
     (out,) = call(
         last_kernel, [((C, CELLS), BF16)], [((9, C, 10 * WIDE), BF16), cols], leave=(0,)
     )(incoming, slope, mask, bwd, out)
-    (part,) = call(sum_kernel, [((CHUNK, WIDE), BF16)])(parts)
-    pieces = lax.all_to_all(
-        part.reshape(ROWS, CHUNK // ROWS, WIDE), "space", 0, 0, axis_index_groups=far
-    )
-    (copies,) = call(sum_kernel, [((ROWS, CHUNK // ROWS, WIDE), BF16)])(pieces)
-    part = lax.all_to_all(copies, "space", 0, 0, axis_index_groups=far)
-    whole = lax.all_gather(part.reshape(CHUNK, WIDE), "space", axis_index_groups=near)
-    (weight_grad,) = call(scale_kernel, [((DEEP, C), F32)], leave=(0,))(whole.reshape(COLS * CHUNK, WIDE))
+    (copies,) = call(sum_kernel, [((FAR, CHUNK, WIDE), BF16)])(parts)
+    parts = lax.all_to_all(copies, "space", 0, 0, axis_index_groups=far)
+    (copies,) = call(sum_kernel, [((NEAR, CHUNK, WIDE), BF16)])(parts)
+    whole = lax.all_to_all(copies, "space", 0, 0, axis_index_groups=near)
+    (weight_grad,) = call(scale_kernel, [((DEEP, C), F32)], leave=(0,))(
+        whole.reshape(NEAR * CHUNK, WIDE)
+    )
     return (out.reshape(1, 1, C, CELLS), weight_grad.reshape(1, TAPS, C, C))
 
 

time: 160 us -> 151 us (0.944)
  blocking collectives: 56.6 us -> 45.2 us
  starting transfers between devices: 26.4 us -> 32.3 us
  waiting for transfers between devices: 44.1 us -> 39.2 us
  Pallas kernels: 28.4 us -> 30.2 us
    all_gather x1 -> x0, blocking collectives: 16.7 us -> none  [body(): lax.all_gather(part.reshape(CHUNK, WIDE), 'space', axis_index_groups=near)]
    all_to_all x1, starting transfers between devices: 4.16 us -> 10 us  [body(): whole = lax.all_to_all(copies, 'space', 0, 0, axis_index_groups=near)]
    all_to_all x2, blocking collectives: 39.9 us -> 45.2 us  [the longest x1 24.7 us: body(): parts = lax.all_to_all(copies, 'space', 0, 0, axis_index_groups=far)]
    ppermute x1, waiting for transfers between devices: 17 us -> 13.8 us  [body(): incoming = lax.ppermute(result, both, between(0, 0, [(1, 0)]))]
    pallas_call x14, Pallas kernels: 28.4 us -> 30.2 us  [run(): inner(*[arg if arg.dtype == jnp.int32 else pltpu.with_memory_space_constr...]
    all_to_all x1, waiting for transfers between devices: 8.48 us -> 6.74 us  [body(): whole = lax.all_to_all(copies, 'space', 0, 0, axis_index_groups=near)]
  transfers between devices with their start and end apart: 9 -> 9, of which waited for: 5 -> 5; matrix products, arithmetic and copies ran while one was open for 0% -> 0% of each run, Pallas kernels for 8% -> 9%
where the time goes in v6:
time: 151 us; the launch traced here: 150 us
  blocking collectives  45.2 us (30%)
  waiting for transfers between devices  39.2 us (26%)
  starting transfers between devices  32.3 us (21%)
  Pallas kernels  30.2 us (20%)
  local copies, waits for them, and re-layouts  1.87 us (1%)
    pallas_call x14, Pallas kernels, run(): inner(*[arg if arg.dtype == jnp.int32 else pltpu.with_memory_space_constr...  30.2 us
    all_to_all x1, blocking collectives, body(): parts = lax.all_to_all(copies, 'space', 0, 0, axis_index_groups=far)  24.7 us
    all_to_all x1, blocking collectives, body(): lax.all_to_all(terms.reshape(NEAR, CHUNK, WIDE), 'space', 0, 0, axis_inde...  20.5 us
    ppermute x1, waiting for transfers between devices, body(): incoming = lax.ppermute(result, both, between(0, 0, [(1, 0)]))  13.8 us
    ppermute x1, waiting for transfers between devices, body(): after = lax.ppermute(down, both, between(-1, 0, same))  13.7 us
    all_to_all x1, starting transfers between devices, body(): whole = lax.all_to_all(copies, 'space', 0, 0, axis_index_groups=near)  10 us
    ppermute x1, starting transfers between devices, body(): before = lax.ppermute(up, both, between(1, 0, same))  9.65 us
    all_to_all x1, waiting for transfers between devices, body(): whole = lax.all_to_all(copies, 'space', 0, 0, axis_index_groups=near)  6.74 us
  transfers between devices with their start and end apart: 9, of which 5 were waited for; matrix products, arithmetic and copies ran while one was open for 0% of the time, Pallas kernels for 9%

profile of v6, /device:TPU:1, one launch (start us, length us, event | category | flops | bytes accessed | tf_op | source)
XLA Modules:
  0.0 150.2 jit_solution(8420561832649406865)
XLA Ops:
  1.3 1.0 shard_map.59
  2.3 9.6 %collective-permute-start = (bf16[112,384]{1,0:T(8,128)(2,1)S(1)}, bf16[112,384]{1,0:T(8,128)(2,1)S(1)}, u32[]{:S(2)}, u32[]{:S(2)}) collective-permute-start(bf16[112,384]{1,0:T(8,128)(2,1)S(1)} %get-tuple-element.32), channel_id=1, source_target_pairs={{0,32},{1,33},{2,34},{3,35},{4,36},{5,37},{6,38},{7,39},{8,40},{9,... | collective-permute-start | bytes 258056 | tf_op jit(solution)/shard_map/ppermute | solution.py:495
  11.9 1.3 collective-permute-start.1
  13.2 0.0 copy-start.1
  13.2 1.1 copy-done.1
  14.3 0.7 shard_map.60
  15.1 0.0 collective-permute-done.before_ref
  15.1 13.7 %collective-permute-done.1.after_ref = bf16[112,384]{1,0:T(8,128)(2,1)S(1)} collective-permute-done((bf16[112,384]{1,0:T(8,128)(2,1)S(1)}, bf16[112,384]{1,0:T(8,128)(2,1)S(1)}, u32[]{:S(2)}, u32[]{:S(2)}) %collective-permute-start.1) | collective-permute-done | bytes 86048 | tf_op jit(solution)/shard_map/ppermute | solution.py:496
  28.8 0.5 shard_map.61
  29.3 2.3 %collective-permute-start.2 = (bf16[112,896]{1,0:T(8,128)(2,1)S(1)}, bf16[112,896]{1,0:T(8,128)(2,1)S(1)}, u32[]{:S(2)}, u32[]{:S(2)}) collective-permute-start(bf16[112,896]{1,0:T(8,128)(2,1)S(1)} %get-tuple-element.39), channel_id=1, source_target_pairs={{0,4},{1,5},{2,6},{3,7},{4,8},{5,9},{6,10},{7,11},{8,12},{9,13},{1... | collective-permute-start | bytes 602120 | tf_op jit(solution)/shard_map/ppermute | solution.py:501
  31.6 2.1 %collective-permute-start.3 = (bf16[112,896]{1,0:T(8,128)(2,1)S(1)}, bf16[112,896]{1,0:T(8,128)(2,1)S(1)}, u32[]{:S(2)}, u32[]{:S(2)}) collective-permute-start(bf16[112,896]{1,0:T(8,128)(2,1)S(1)} %get-tuple-element.40), channel_id=1, source_target_pairs={{4,0},{5,1},{6,2},{7,3},{8,4},{9,5},{10,6},{11,7},{12,8},{13,9},{1... | collective-permute-start | bytes 602120 | tf_op jit(solution)/shard_map/ppermute | solution.py:502
  33.7 0.5 collective-permute-done.2.left_ref
  34.2 4.4 %collective-permute-done.3.right_ref = bf16[112,896]{1,0:T(8,128)(2,1)S(1)} collective-permute-done((bf16[112,896]{1,0:T(8,128)(2,1)S(1)}, bf16[112,896]{1,0:T(8,128)(2,1)S(1)}, u32[]{:S(2)}, u32[]{:S(2)}) %collective-permute-start.3) | collective-permute-done | bytes 200736 | tf_op jit(solution)/shard_map/ppermute | solution.py:502
  38.6 0.3 shard_map.62
  38.9 4.3 %collective-permute-start.4 = (bf16[96,1536]{1,0:T(8,128)(2,1)S(1)}, bf16[96,1536]{1,0:T(8,128)(2,1)S(1)}, u32[]{:S(2)}, u32[]{:S(2)}) collective-permute-start(bf16[96,1536]{1,0:T(8,128)(2,1)S(1)} %shard_map.62), channel_id=1, source_target_pairs={{0,3},{4,7},{8,11},{12,15},{16,19},{20,23},{24,27},{28,31},{32,35}... | collective-permute-start | bytes 884744 | tf_op jit(solution)/shard_map/ppermute | solution.py:504
  43.2 6.9 %shard_map.63 = (f32[96,2048]{1,0:T(8,128)S(1)}, bf16[27,16,2048]{2,1,0:T(8,128)(2,1)S(1)}, bf16[96,1280]{1,0:T(8,128)(2,1)S(1)}) custom-call(bf16[96,512]{1,0:T(8,128)(2,1)S(1)} %get-tuple-element.38.x_ref, s32[1]{0:T(128)S(6)} %copy.6.height_ref, bf16[112,384]{1,0:T(8,128)(2,1)S(1)} %collective-permute-done.before_ref, ...), custom_call_target="tpu_custom_call" | custom-call | tf_op jit(solution)/shard_map/pallas_call | solution.py:50
  50.1 0.0 collective-permute-done.4.halo_ref
  50.1 4.2 %shard_map.64 = (bf16[96,1792]{1,0:T(8,128)(2,1)S(1)}, bf16[96,1024]{1,0:T(8,128)(2,1)S(1)}, bf16[96,1024]{1,0:T(8,128)(2,1)S(1)}) custom-call(bf16[96,512]{1,0:T(8,128)(2,1)S(1)} %get-tuple-element.31.top_ref.own_ref, bf16[96,1536]{1,0:T(8,128)(2,1)S(1)} %collective-permute-done.4.halo_ref, f32[96,2048]{1,0:T(8,128)S(1)} %get-tuple-element.42.slope_ref, ...), custom_call_target="tpu_custom_call" | custom-call | tf_op jit(solution)/shard_map/pallas_call | solution.py:50
  54.4 0.7 collective-permute-start.5
  55.1 0.0 collective-permute-done.5.incoming_ref
  55.1 3.5 %shard_map.65 = (bf16[96,1152]{1,0:T(8,128)(2,1)S(1)}, bf16[96,1024]{1,0:T(8,128)(2,1)S(1)}, bf16[96,1024]{1,0:T(8,128)(2,1)S(1)}) custom-call(bf16[96,1792]{1,0:T(8,128)(2,1)S(1)} %collective-permute-done.5.incoming_ref, f32[96,2048]{1,0:T(8,128)S(1)} %get-tuple-element.42.slope_ref, bf16[27,16,2048]{2,1,0:T(8,128)(2,1)S(1)} %get-tuple-element.43.mask_ref, ...), custom_call_target="tpu_custom_call" | custom-call | tf_op jit(solution)/shard_map/pallas_call | solution.py:50
  58.6 0.7 collective-permute-start.6
  59.3 0.0 collective-permute-done.6.incoming_ref
  59.3 3.1 %shard_map.66 = (bf16[96,896]{1,0:T(8,128)(2,1)S(1)}, bf16[96,1024]{1,0:T(8,128)(2,1)S(1)}, bf16[96,1024]{1,0:T(8,128)(2,1)S(1)}) custom-call(bf16[96,1152]{1,0:T(8,128)(2,1)S(1)} %collective-permute-done.6.incoming_ref, f32[96,2048]{1,0:T(8,128)S(1)} %get-tuple-element.42.slope_ref, bf16[27,16,2048]{2,1,0:T(8,128)(2,1)S(1)} %get-tuple-element.43.mask_ref, ...), custom_call_target="tpu_custom_call" | custom-call | tf_op jit(solution)/shard_map/pallas_call | solution.py:50
  62.4 1.3 collective-permute-start.7
  63.7 2.4 %shard_map.67.all_ref = bf16[2592,512]{1,0:T(8,128)(2,1)S(1)} custom-call(bf16[96,1280]{1,0:T(8,128)(2,1)S(1)} %get-tuple-element.54.x_ref, bf16[27,16,2048]{2,1,0:T(8,128)(2,1)S(1)} %get-tuple-element.43.mask_ref), custom_call_target="tpu_custom_call" | custom-call | tf_op jit(solution)/shard_map/pallas_call | solution.py:50
  66.1 13.8 %collective-permute-done.7.packed_ref = bf16[96,896]{1,0:T(8,128)(2,1)S(1)} collective-permute-done((bf16[96,896]{1,0:T(8,128)(2,1)S(1)}, bf16[96,896]{1,0:T(8,128)(2,1)S(1)}, u32[]{:S(2)}, u32[]{:S(2)}) %collective-permute-start.7) | collective-permute-done | bytes 172064 | tf_op jit(solution)/shard_map/ppermute | solution.py:530
  79.9 1.1 shard_map.68
  81.0 20.5 %all_to_all.15.parts_ref = bf16[16,128,128]{2,1,0:T(8,128)(2,1)S(1)} all-to-all(bf16[16,128,128]{2,1,0:T(8,128)(2,1)S(1)} %bitcast.8), channel_id=1, replica_groups={{0,4,8,12,128,132,136,140,256,260,264,268,384,388,392,396},{16,20,24,28..., dimensions={0} | all-to-all | bytes 1048576 | tf_op jit(solution)/shard_map/all_to_all | solution.py:540
  101.5 0.1 shard_map.70
  101.6 24.7 %all_to_all.16.parts_ref = bf16[8,128,128]{2,1,0:T(8,128)(2,1)S(1)} all-to-all(bf16[8,128,128]{2,1,0:T(8,128)(2,1)S(1)} %shard_map.70), channel_id=1, replica_groups={{0,16,32,48,64,80,96,112},{4,20,36,52,68,84,100,116},{8,24,40,56,72,88,..., dimensions={0} | all-to-all | bytes 524288 | tf_op jit(solution)/shard_map/all_to_all | solution.py:548
  126.3 0.1 shard_map.71
  126.4 0.0 copy-start
  126.4 0.8 copy-done
  127.2 10.0 %all-to-all-start.2 = ((bf16[16,128,128]{2,1,0:T(8,128)(2,1)}), bf16[16,128,128]{2,1,0:T(8,128)(2,1)}, u32[]{:S(2)}, u32[]{:S(2)}) async-start(bf16[16,128,128]{2,1,0:T(8,128)(2,1)} %copy-done), calls=%async_computation.2 | async-start | bytes 1048576 | tf_op jit(solution)/shard_map/all_to_all | solution.py:550
  137.2 3.2 %shard_map.69 = bf16[96,512]{1,0:T(8,128)(2,1)} custom-call(bf16[96,1280]{1,0:T(8,128)(2,1)S(1)} %get-tuple-element.55.incoming_ref, f32[96,2048]{1,0:T(8,128)S(1)} %get-tuple-element.42.slope_ref, bf16[27,16,2048]{2,1,0:T(8,128)(2,1)S(1)} %get-tuple-element.43.mask_ref, bf16[96,2592]{1,0:T(8,128)(2,1)S(1)} %get-tuple-element.44.bwd_ref, ...), custom_call_target="tpu_custom_call" | custom-call | tf_op jit(solution)/shard_map/pallas_call | solution.py:50
  140.5 6.7 %all-to-all-done.2 = bf16[16,128,128]{2,1,0:T(8,128)(2,1)} async-done(((bf16[16,128,128]{2,1,0:T(8,128)(2,1)}), bf16[16,128,128]{2,1,0:T(8,128)(2,1)}, u32[]{:S(2)}, u32[]{:S(2)}) %all-to-all-start.2) | async-done | bytes 524320 | tf_op jit(solution)/shard_map/all_to_all | solution.py:550
  147.2 3.0 %shard_map.72 = f32[2592,96]{1,0:T(8,128)} custom-call(bf16[2048,128]{1,0:T(8,128)(2,1)} %bitcast.5.whole_ref), custom_call_target="tpu_custom_call" | custom-call | tf_op jit(solution)/shard_map/pallas_call | solution.py:50
Async XLA Ops:
  2.3 12.8 %collective-permute-start = (bf16[112,384]{1,0:T(8,128)(2,1)S(1)}, bf16[112,384]{1,0:T(8,128)(2,1)S(1)}, u32[]{:S(2)}, u32[]{:S(2)}) collective-permute-start(bf16[112,384]{1,0:T(8,128)(2,1)S(1)} %get-tuple-element.32), channel_id=1, source_target_pairs={{0,32},{1,33},{2,34},{3,35},{4,36},{5,37},{6,38},{7,39},{8,40},{9,... | collective-permute-start | bytes 258056 | tf_op jit(solution)/shard_map/ppermute | solution.py:495
  11.9 16.9 %collective-permute-start.1 = (bf16[112,384]{1,0:T(8,128)(2,1)S(1)}, bf16[112,384]{1,0:T(8,128)(2,1)S(1)}, u32[]{:S(2)}, u32[]{:S(2)}) collective-permute-start(bf16[112,384]{1,0:T(8,128)(2,1)S(1)} %get-tuple-element.33), channel_id=1, source_target_pairs={{32,0},{33,1},{34,2},{35,3},{36,4},{37,5},{38,6},{39,7},{40,8},{41... | collective-permute-start | bytes 258056 | tf_op jit(solution)/shard_map/ppermute | solution.py:496
  13.2 1.1 copy-start.1
  29.3 4.9 %collective-permute-start.2 = (bf16[112,896]{1,0:T(8,128)(2,1)S(1)}, bf16[112,896]{1,0:T(8,128)(2,1)S(1)}, u32[]{:S(2)}, u32[]{:S(2)}) collective-permute-start(bf16[112,896]{1,0:T(8,128)(2,1)S(1)} %get-tuple-element.39), channel_id=1, source_target_pairs={{0,4},{1,5},{2,6},{3,7},{4,8},{5,9},{6,10},{7,11},{8,12},{9,13},{1... | collective-permute-start | bytes 602120 | tf_op jit(solution)/shard_map/ppermute | solution.py:501
  31.6 7.0 %collective-permute-start.3 = (bf16[112,896]{1,0:T(8,128)(2,1)S(1)}, bf16[112,896]{1,0:T(8,128)(2,1)S(1)}, u32[]{:S(2)}, u32[]{:S(2)}) collective-permute-start(bf16[112,896]{1,0:T(8,128)(2,1)S(1)} %get-tuple-element.40), channel_id=1, source_target_pairs={{4,0},{5,1},{6,2},{7,3},{8,4},{9,5},{10,6},{11,7},{12,8},{13,9},{1... | collective-permute-start | bytes 602120 | tf_op jit(solution)/shard_map/ppermute | solution.py:502
  38.9 11.3 %collective-permute-start.4 = (bf16[96,1536]{1,0:T(8,128)(2,1)S(1)}, bf16[96,1536]{1,0:T(8,128)(2,1)S(1)}, u32[]{:S(2)}, u32[]{:S(2)}) collective-permute-start(bf16[96,1536]{1,0:T(8,128)(2,1)S(1)} %shard_map.62), channel_id=1, source_target_pairs={{0,3},{4,7},{8,11},{12,15},{16,19},{20,23},{24,27},{28,31},{32,35}... | collective-permute-start | bytes 884744 | tf_op jit(solution)/shard_map/ppermute | solution.py:504
  54.4 0.7 collective-permute-start.5
  58.6 0.7 collective-permute-start.6
  62.4 17.5 %collective-permute-start.7 = (bf16[96,896]{1,0:T(8,128)(2,1)S(1)}, bf16[96,896]{1,0:T(8,128)(2,1)S(1)}, u32[]{:S(2)}, u32[]{:S(2)}) collective-permute-start(bf16[96,896]{1,0:T(8,128)(2,1)S(1)} %get-tuple-element.51), channel_id=1, source_target_pairs={{1,0},{5,4},{9,8},{13,12},{17,16},{21,20},{25,24},{29,28},{33,32},... | collective-permute-start | bytes 516104 | tf_op jit(solution)/shard_map/ppermute | solution.py:530
  126.4 0.8 copy-start
  127.2 20.0 %all-to-all-start.2 = ((bf16[16,128,128]{2,1,0:T(8,128)(2,1)}), bf16[16,128,128]{2,1,0:T(8,128)(2,1)}, u32[]{:S(2)}, u32[]{:S(2)}) async-start(bf16[16,128,128]{2,1,0:T(8,128)(2,1)} %copy-done), calls=%async_computation.2 | async-start | bytes 1048576 | tf_op jit(solution)/shard_map/all_to_all | solution.py:550

commit v7 on v6

--- a/solution.py
+++ b/solution.py
@@ -105,6 +105,9 @@
         bwd_ref[:, C * q : C * q + C] = w_ref[TAPS - 1 - q]
 
 
+OUTER = (1, 2, 3, 4, 13, 14, 15, 16)
+
+
 def code_of(height_ref, shape):
     return jnp.full(shape, (height_ref[0] + CODE).astype(F32), F32)
 
@@ -145,11 +148,9 @@
     return after_ref[:C, at : at + 64]
 
 
-def top_layer(top_ref, before_ref, after_ref, row):
+def top_layer(before_ref, after_ref, row):
     if row < 5:
         return before_ref[:C, WIDE + 64 * (row - 1) : WIDE + 64 * row]
-    if row < 13:
-        return top_ref[:, 64 * (row - 5) : 64 * (row - 5) + 64]
     return after_ref[:C, WIDE + 64 * (row - 13) : WIDE + 64 * (row - 12)]
 
 
@@ -168,7 +169,7 @@
             return layer[:, start : start + 32]
 
         out[C:, : 3 * WIDE] = codes
-        out[C:, 3 * WIDE :] = jnp.zeros((16, 4 * WIDE), BF16)
+        out[C:, 3 * WIDE :] = jnp.zeros((16, 5 * WIDE), BF16)
         for four in range(3):
             rows = range(3 + 4 * four, 7 + 4 * four)
             out[:C, lane(four)] = join(
@@ -177,25 +178,26 @@
 
         @pl.when(lowest)
         def _(out=out, piece=piece):
-            for four in range(4):
-                rows = range(1 + 4 * four, 5 + 4 * four)
-                out[:C, lane(3 + four)] = join(
-                    [piece(top_layer(top_ref, before_ref, after_ref, row)) for row in rows]
-                )
+            tops = [piece(top_layer(before_ref, after_ref, row)) for row in OUTER]
+            out[:C, lane(3)] = join(tops[:4])
+            out[:C, lane(4)] = join(tops[4:])
+            out[:C, lane(5, 3)] = jnp.zeros((C, 3 * WIDE), BF16)
 
         @pl.when(jnp.logical_not(lowest))
         def _(out=out, piece=piece, fifth=fifth):
             outer = [
                 piece(x_layer(x_ref, before_ref, after_ref, row)) for row in (0, 1, 2, 15, 16, 17)
             ]
-            out[:C, lane(3)] = join(outer[:4])
-            out[:C, lane(4)] = join(outer[4:] + [jnp.zeros((C, 64), BF16)])
             more = [
                 x_layer(x_ref, before_ref, after_ref, row)[:, fifth : fifth + 8]
                 for row in range(18)
             ]
-            out[:C, lane(5)] = join(more[:16])
-            out[:C, lane(6)] = join(more[16:] + [jnp.zeros((C, 112), BF16)])
+            tops = [piece(top_ref[:, 64 * n : 64 * n + 64]) for n in range(8)]
+            out[:C, lane(3)] = join(outer[:4])
+            out[:C, lane(4)] = join(outer[4:] + more[:8])
+            out[:C, lane(5)] = join(more[8:] + [jnp.zeros((C, 48), BF16)])
+            out[:C, lane(6)] = join(tops[:4])
+            out[:C, lane(7)] = join(tops[4:])
 
 
 def x_side(side_ref, row):
@@ -206,26 +208,14 @@
     return side_ref[:C, at : at + 32]
 
 
-def top_side(side_ref, row):
-    return side_ref[:C, 3 * WIDE + 32 * (row - 1) : 3 * WIDE + 32 * row]
-
-
 def halo_kernel(before_ref, after_ref, left_ref, right_ref, halo_ref):
     @pl.when(lax.axis_index("pipe") == 0)
     def _():
-        for n, row in enumerate((1, 2, 3, 4, 13, 14, 15, 16)):
-            middle = top_layer(None, before_ref, after_ref, row)
-            halo_ref[:, lane(n)] = join([top_side(left_ref, row), middle, top_side(right_ref, row)])
-        for pair in range(4):
-            first, second = 5 + 2 * pair, 6 + 2 * pair
-            halo_ref[:, lane(8 + pair)] = join(
-                [
-                    top_side(left_ref, first),
-                    top_side(right_ref, first),
-                    top_side(left_ref, second),
-                    top_side(right_ref, second),
-                ]
-            )
+        for n, row in enumerate(OUTER):
+            at = 3 * WIDE + 32 * n
+            middle = top_layer(before_ref, after_ref, row)
+            sides = left_ref[:C, at : at + 32], right_ref[:C, at : at + 32]
+            halo_ref[:, lane(n)] = join([sides[0], middle, sides[1]])
 
 
 def forward_kernel(
@@ -256,7 +246,7 @@
         )
         if 4 <= row < 14:
             rows_ref[:, lane(row - 4)] = tile
-        at = 5 * WIDE + 8 * row
+        at = 4 * WIDE + 64 + 8 * row
         low = join([tile[:, :120], left_ref[:C, at : at + 8]])
         high = join([right_ref[:C, at : at + 8], tile[:, 8:]])
         shifted_rows(base_ref, row, tile, low, high)
@@ -299,30 +289,19 @@
         slope_ref[:, lane(row)] = sigma * (1.0 + pre * (1.0 - sigma))
 
 
-def top_kernel(
-    own_ref, halo_ref, slope_ref, mask_ref, bwd_ref,
-    result_ref, grad_ref, out_ref,
-    base_ref, cols_ref, top_ref,
-):
-    active = lax.axis_index("pipe") == SECTIONS - 1
-    for row in range(1, 17):
-        if row < 5:
-            tile = halo_ref[:, lane(row - 1)]
-        elif row < 13:
-            at = 8 * WIDE + 64 * (row - 5)
-            middle = own_ref[:, 64 * (row - 5) : 64 * (row - 5) + 64]
-            tile = join([halo_ref[:, at : at + 32], middle, halo_ref[:, at + 32 : at + 64]])
-        else:
-            tile = halo_ref[:, lane(row - 9)]
-        top_ref[:, lane(row - 1)] = jnp.where(active, tile, jnp.zeros_like(tile))
-
-    def store(pair, value):
-        result_ref[:, lane(2 * pair, 2)] = value
-
-    step_rows(top_ref, slope_ref, mask_ref, bwd_ref, base_ref, cols_ref, store, 16, 1)
-    for row in range(8):
-        grad_ref[:, lane(row)] = base_ref[4, :, lane(row + 4)]
-        out_ref[:, lane(row)] = result_ref[:, lane(row + 3)]
+def top_row(top_ref, halo_ref, left_ref, right_ref, row):
+    if 5 <= row < 13:
+        at, side = 64 * (row - 5), 6 * WIDE + 32 * (row - 5)
+        tile = join(
+            [
+                left_ref[:C, side : side + 32],
+                top_ref[:, at : at + 64],
+                right_ref[:C, side : side + 32],
+            ]
+        )
+    else:
+        tile = halo_ref[:, lane(OUTER.index(row))]
+    return jnp.where(lax.axis_index("pipe") == SECTIONS - 1, tile, jnp.zeros_like(tile))
 
 
 def step_rows(incoming_ref, slope_ref, mask_ref, bwd_ref, base_ref, cols_ref, store, count, first):
@@ -348,27 +327,86 @@
     return join([spare, packed_ref[:, width * row : width * row + width], spare])
 
 
-def middle_kernel(
-    count, first, width_in, width_out, incoming_ref, slope_ref, mask_ref, bwd_ref, grad_in, out_in,
-    result_ref, grad_ref, out_ref, base_ref, cols_ref, rows_ref, full_ref,
-):
-    for row in range(count):
-        rows_ref[:, lane(row)] = (
-            incoming_ref[:, lane(row)] if width_in == WIDE else spread(incoming_ref, width_in, row)
-        )
+def pieces_row(pieces, row):
+    for ref, first, count, width in pieces:
+        if first <= row < first + count:
+            if width == WIDE:
+                return ref[:, lane(row - first)]
+            return spread(ref, width, row - first)
+
+
+def step_part(row_of, low, count, width, result_ref, slope_ref, mask_ref, bwd_ref, scratch):
+    base_ref, cols_ref, rows_ref, full_ref = scratch
+    for n in range(count + 2):
+        rows_ref[:, lane(n)] = row_of(low - 1 + n)
 
     def store(pair, value):
         full_ref[:, lane(2 * pair, 2)] = value
 
-    step_rows(rows_ref, slope_ref, mask_ref, bwd_ref, base_ref, cols_ref, store, count, first)
-    skip = (WIDE - width_out) // 2
-    rows = [full_ref[:, lane(row)] for row in range(count - 2)]
-    packed = [row[:, skip : skip + width_out] for row in rows]
-    spare = result_ref.shape[1] - width_out * (count - 2)
+    step_rows(
+        rows_ref, slope_ref, mask_ref, bwd_ref, base_ref, cols_ref, store, count + 2, low - 1
+    )
+    skip = (WIDE - width) // 2
+    packed = [full_ref[:, lane(n)][:, skip : skip + width] for n in range(count)]
+    spare = result_ref.shape[1] - width * count
     result_ref[...] = join(packed + [jnp.zeros((C, spare), BF16)] if spare else packed)
-    for row in range(8):
-        grad_ref[:, lane(row)] = grad_in[:, lane(row)] + base_ref[4, :, lane(row + 5 - first)]
-        out_ref[:, lane(row)] = out_in[:, lane(row)] + rows[row + 4 - first]
+
+
+def keep_own(row_of, result_of, slope_ref, grad_in, out_in, grad_ref, out_ref):
+    for n in range(8):
+        grad = (row_of(n + 5).astype(F32) * slope_ref[:, lane(n + 4)]).astype(BF16)
+        out = result_of(n + 5)
+        if grad_in is not None:
+            grad, out = grad + grad_in[:, lane(n)], out + out_in[:, lane(n)]
+        grad_ref[:, lane(n)] = grad
+        out_ref[:, lane(n)] = out
+
+
+def top_first_kernel(
+    top_ref, halo_ref, left_ref, right_ref, slope_ref, mask_ref, bwd_ref, result_ref, *scratch
+):
+    def row_of(row):
+        return top_row(top_ref, halo_ref, left_ref, right_ref, row)
+
+    step_part(row_of, 2, 8, WIDE, result_ref, slope_ref, mask_ref, bwd_ref, scratch)
+
+
+def top_second_kernel(
+    top_ref, halo_ref, left_ref, right_ref, slope_ref, mask_ref, bwd_ref, earlier_ref,
+    result_ref, grad_ref, out_ref, *scratch,
+):
+    def row_of(row):
+        return top_row(top_ref, halo_ref, left_ref, right_ref, row)
+
+    def result_of(row):
+        return pieces_row(((earlier_ref, 2, 8, WIDE), (result_ref, 10, 6, WIDE)), row)
+
+    step_part(row_of, 10, 6, WIDE, result_ref, slope_ref, mask_ref, bwd_ref, scratch)
+    keep_own(row_of, result_of, slope_ref, None, None, grad_ref, out_ref)
+
+
+def first_kernel(piece, low, count, width, piece_ref, slope_ref, mask_ref, bwd_ref, result_ref,
+                 *scratch):
+    def row_of(row):
+        return pieces_row(((piece_ref,) + piece,), row)
+
+    step_part(row_of, low, count, width, result_ref, slope_ref, mask_ref, bwd_ref, scratch)
+
+
+def second_kernel(
+    pieces, early, low, count, width,
+    first_ref, second_ref, slope_ref, mask_ref, bwd_ref, earlier_ref, grad_in, out_in,
+    result_ref, grad_ref, out_ref, *scratch,
+):
+    def row_of(row):
+        return pieces_row(((first_ref,) + pieces[0], (second_ref,) + pieces[1]), row)
+
+    def result_of(row):
+        later = (result_ref, low, count, width)
+        return pieces_row(((earlier_ref, early, low - early, width), later), row)
+
+    step_part(row_of, low, count, width, result_ref, slope_ref, mask_ref, bwd_ref, scratch)
+    keep_own(row_of, result_of, slope_ref, grad_in, out_in, grad_ref, out_ref)
 
 
 def halves(first, second):
@@ -394,9 +432,13 @@
     lax.fori_loop(0, 4, one, 0)
 
 
-def terms_kernel(packed_ref, slope_ref, grad_in, all_ref, terms_ref, incoming_ref):
+def terms_kernel(
+    first_ref, second_ref, slope_ref, grad_in, all_ref, terms_ref, incoming_ref
+):
     for row in range(10):
-        incoming_ref[:, lane(row)] = spread(packed_ref, 80, row)
+        incoming_ref[:, lane(row)] = pieces_row(
+            ((first_ref, 4, 4, 80), (second_ref, 8, 6, 80)), row + 4
+        )
     grads = []
     for row in range(8):
         grad = incoming_ref[:, lane(row + 1)].astype(F32) * slope_ref[:, lane(row + 4)]
@@ -495,12 +537,12 @@
     before = lax.ppermute(up, both, between(1, 0, same))
     after = lax.ppermute(down, both, between(-1, 0, same))
     before, after, fwd, bwd = lax.optimization_barrier((before, after, fwd, bwd))
-    to_right, to_left = call(cols_kernel, [((C + 16, 7 * WIDE), BF16)] * 2)(
+    to_right, to_left = call(cols_kernel, [((C + 16, 8 * WIDE), BF16)] * 2)(
         x, top, brick_height, before, after
     )
     left = lax.ppermute(to_right, both, between(0, 1, same))
     right = lax.ppermute(to_left, both, between(0, -1, same))
-    (halo,) = call(halo_kernel, [((C, 12 * WIDE), BF16)])(before, after, left, right)
+    (halo,) = call(halo_kernel, [((C, 8 * WIDE), BF16)])(before, after, left, right)
     halo = lax.ppermute(halo, both, between(0, 0, [(0, SECTIONS - 1)]))
 
     core = ((C, 8 * WIDE), BF16)
@@ -510,31 +552,55 @@
         [((C, 16 * WIDE), F32), ((TAPS, 16, 16 * WIDE), BF16), ((C, 10 * WIDE), BF16)],
         [((9, C, 18 * WIDE), BF16), cols, ((8, 18 * WIDE), F32), ((C, 16 * WIDE), F32)],
     )(x, brick_height, before, after, left, right, fwd)
+    def scratch(count):
+        return [
+            ((9, C, (count + 2) * WIDE), BF16), cols, ((C, (count + 2) * WIDE), BF16),
+            ((C, count * WIDE), BF16),
+        ]
+
+    def hand_on(value, source):
+        return lax.ppermute(value, both, between(0, 0, [(source, source - 1)]))
+
+    tops = (top, halo, left, right, slope, mask, bwd)
+    (result,) = call(top_first_kernel, [((C, 8 * WIDE), BF16)], scratch(8))(*tops)
+    first = hand_on(result, 3)
     result, grad, out = call(
-        top_kernel,
-        [((C, 14 * WIDE), BF16), core, core],
-        [((9, C, 16 * WIDE), BF16), cols, ((C, 16 * WIDE), BF16)],
-    )(top, halo, slope, mask, bwd)
-    incoming = lax.ppermute(result, both, between(0, 0, [(3, 2)]))
+        top_second_kernel, [((C, 6 * WIDE), BF16), core, core], scratch(6)
+    )(*tops, result)
+    second = hand_on(result, 3)
+
+    pieces = (2, 8, WIDE), (10, 6, WIDE)
+    (result,) = call(
+        functools.partial(first_kernel, pieces[0], 3, 6, 96), [((C, 5 * WIDE), BF16)], scratch(6)
+    )(first, slope, mask, bwd)
+    next_first = hand_on(result, 2)
     result, grad, out = call(
-        functools.partial(middle_kernel, 14, 2, WIDE, 96),
-        [((C, 12 * 96), BF16), core, core],
-        [((9, C, 14 * WIDE), BF16), cols, ((C, 14 * WIDE), BF16), ((C, 12 * WIDE), BF16)],
-    )(incoming, slope, mask, bwd, grad, out)
-    incoming = lax.ppermute(result, both, between(0, 0, [(2, 1)]))
+        functools.partial(second_kernel, pieces, 3, 9, 6, 96),
+        [((C, 5 * WIDE), BF16), core, core],
+        scratch(6),
+    )(first, second, slope, mask, bwd, result, grad, out)
+    next_second = hand_on(result, 2)
+    first, second = next_first, next_second
+
+    pieces = (3, 6, 96), (9, 6, 96)
+    (result,) = call(
+        functools.partial(first_kernel, pieces[0], 4, 4, 80), [((C, 3 * WIDE), BF16)], scratch(4)
+    )(first, slope, mask, bwd)
+    next_first = hand_on(result, 1)
     result, grad, out = call(
-        functools.partial(middle_kernel, 12, 3, 96, 80),
-        [((C, 7 * WIDE), BF16), core, core],
-        [((9, C, 12 * WIDE), BF16), cols, ((C, 12 * WIDE), BF16), ((C, 10 * WIDE), BF16)],
-    )(incoming, slope, mask, bwd, grad, out)
-    incoming = lax.ppermute(result, both, between(0, 0, [(1, 0)]))
+        functools.partial(second_kernel, pieces, 4, 8, 6, 80),
+        [((C, 4 * WIDE), BF16), core, core],
+        scratch(6),
+    )(first, second, slope, mask, bwd, result, grad, out)
+    next_second = hand_on(result, 1)
+    first, second = next_first, next_second
     x_rows, _ = lax.optimization_barrier((x_rows, result))
     (x_cols,) = call(gather_kernel, [((DEEP, CELLS), BF16)], [((9, C, 10 * WIDE), BF16)])(
         x_rows, mask
     )
     terms, incoming = call(
         terms_kernel, [((NEAR * CHUNK, WIDE), BF16), ((C, 10 * WIDE), BF16)]
-    )(incoming, slope, grad, x_cols)
+    )(first, second, slope, grad, x_cols)
 
     near, far = groups()
     parts = lax.all_to_all(

time: 151 us -> 144 us (0.954)
  waiting for transfers between devices: 39.2 us -> 30.5 us
  blocking collectives: 45.2 us -> 41.9 us
  starting transfers between devices: 32.3 us -> 35.3 us
  Pallas kernels: 30.2 us -> 31.9 us
    ppermute x3 -> x6, waiting for transfers between devices: 13.8 us -> 4.8 us  [hand_on(): return lax.ppermute(value, both, between(0, 0, [(source, source - 1)]))]
    ppermute x3 -> x6, starting transfers between devices: 2.65 us -> 5.44 us  [hand_on(): return lax.ppermute(value, both, between(0, 0, [(source, source - 1)]))]
    all_to_all x1, blocking collectives: 20.5 us -> 17.9 us  [body(): lax.all_to_all(terms.reshape(NEAR, CHUNK, WIDE), 'space', 0, 0, axis_inde...]
    pallas_call x14 -> x17, Pallas kernels: 30.2 us -> 31.9 us  [run(): inner(*[arg if arg.dtype == jnp.int32 else pltpu.with_memory_space_constr...]
  transfers between devices with their start and end apart: 9 -> 12, of which waited for: 5 -> 5; matrix products, arithmetic and copies ran while one was open for 0% -> 0% of each run, Pallas kernels for 9% -> 15%
where the time goes in v7:
time: 144 us; the launch traced here: 143 us
  blocking collectives  41.9 us (29%)
  starting transfers between devices  35.3 us (25%)
  Pallas kernels  31.9 us (22%)
  waiting for transfers between devices  30.5 us (21%)
  local copies, waits for them, and re-layouts  1.87 us (1%)
  between operations  1.54 us (1%)
    pallas_call x17, Pallas kernels, run(): inner(*[arg if arg.dtype == jnp.int32 else pltpu.with_memory_space_constr...  31.9 us
    all_to_all x1, blocking collectives, body(): parts = lax.all_to_all(copies, 'space', 0, 0, axis_index_groups=far)  24 us
    all_to_all x1, blocking collectives, body(): lax.all_to_all(terms.reshape(NEAR, CHUNK, WIDE), 'space', 0, 0, axis_inde...  17.9 us
    ppermute x1, waiting for transfers between devices, body(): after = lax.ppermute(down, both, between(-1, 0, same))  13.7 us
    all_to_all x1, starting transfers between devices, body(): whole = lax.all_to_all(copies, 'space', 0, 0, axis_index_groups=near)  10 us
    ppermute x1, starting transfers between devices, body(): before = lax.ppermute(up, both, between(1, 0, same))  9.65 us
    all_to_all x1, waiting for transfers between devices, body(): whole = lax.all_to_all(copies, 'space', 0, 0, axis_index_groups=near)  6.74 us
    ppermute x6, starting transfers between devices, hand_on(): return lax.ppermute(value, both, between(0, 0, [(source, source - 1)]))  5.44 us
  transfers between devices with their start and end apart: 12, of which 5 were waited for; matrix products, arithmetic and copies ran while one was open for 0% of the time, Pallas kernels for 15%

profile of v7, /device:TPU:1, one launch (start us, length us, event | category | flops | bytes accessed | tf_op | source)
XLA Modules:
  0.0 143.0 jit_solution(17577916656391874996)
XLA Ops:
  1.3 1.0 shard_map.59
  2.3 9.6 %collective-permute-start = (bf16[112,384]{1,0:T(8,128)(2,1)S(1)}, bf16[112,384]{1,0:T(8,128)(2,1)S(1)}, u32[]{:S(2)}, u32[]{:S(2)}) collective-permute-start(bf16[112,384]{1,0:T(8,128)(2,1)S(1)} %get-tuple-element.32), channel_id=1, source_target_pairs={{0,32},{1,33},{2,34},{3,35},{4,36},{5,37},{6,38},{7,39},{8,40},{9,... | collective-permute-start | bytes 258056 | tf_op jit(solution)/shard_map/ppermute | solution.py:537
  11.9 1.3 collective-permute-start.1
  13.2 0.0 copy-start.1
  13.2 1.1 copy-done.1
  14.3 0.7 shard_map.60
  15.1 0.0 collective-permute-done.before_ref
  15.1 13.7 %collective-permute-done.1.after_ref = bf16[112,384]{1,0:T(8,128)(2,1)S(1)} collective-permute-done((bf16[112,384]{1,0:T(8,128)(2,1)S(1)}, bf16[112,384]{1,0:T(8,128)(2,1)S(1)}, u32[]{:S(2)}, u32[]{:S(2)}) %collective-permute-start.1) | collective-permute-done | bytes 86048 | tf_op jit(solution)/shard_map/ppermute | solution.py:538
  28.8 0.5 shard_map.61
  29.2 2.3 %collective-permute-start.2 = (bf16[112,1024]{1,0:T(8,128)(2,1)S(1)}, bf16[112,1024]{1,0:T(8,128)(2,1)S(1)}, u32[]{:S(2)}, u32[]{:S(2)}) collective-permute-start(bf16[112,1024]{1,0:T(8,128)(2,1)S(1)} %get-tuple-element.39), channel_id=1, source_target_pairs={{0,4},{1,5},{2,6},{3,7},{4,8},{5,9},{6,10},{7,11},{8,12},{9,13},{1... | collective-permute-start | bytes 688136 | tf_op jit(solution)/shard_map/ppermute | solution.py:543
  31.5 2.1 %collective-permute-start.3 = (bf16[112,1024]{1,0:T(8,128)(2,1)S(1)}, bf16[112,1024]{1,0:T(8,128)(2,1)S(1)}, u32[]{:S(2)}, u32[]{:S(2)}) collective-permute-start(bf16[112,1024]{1,0:T(8,128)(2,1)S(1)} %get-tuple-element.40), channel_id=1, source_target_pairs={{4,0},{5,1},{6,2},{7,3},{8,4},{9,5},{10,6},{11,7},{12,8},{13,9},{1... | collective-permute-start | bytes 688136 | tf_op jit(solution)/shard_map/ppermute | solution.py:544
  33.6 0.9 collective-permute-done.2.left_ref
  34.4 4.4 %collective-permute-done.3.right_ref = bf16[112,1024]{1,0:T(8,128)(2,1)S(1)} collective-permute-done((bf16[112,1024]{1,0:T(8,128)(2,1)S(1)}, bf16[112,1024]{1,0:T(8,128)(2,1)S(1)}, u32[]{:S(2)}, u32[]{:S(2)}) %collective-permute-start.3) | collective-permute-done | bytes 229408 | tf_op jit(solution)/shard_map/ppermute | solution.py:544
  38.8 0.2 shard_map.62
  39.0 4.5 %collective-permute-start.4 = (bf16[96,1024]{1,0:T(8,128)(2,1)S(1)}, bf16[96,1024]{1,0:T(8,128)(2,1)S(1)}, u32[]{:S(2)}, u32[]{:S(2)}) collective-permute-start(bf16[96,1024]{1,0:T(8,128)(2,1)S(1)} %shard_map.62), channel_id=1, source_target_pairs={{0,3},{4,7},{8,11},{12,15},{16,19},{20,23},{24,27},{28,31},{32,35}... | collective-permute-start | bytes 589832 | tf_op jit(solution)/shard_map/ppermute | solution.py:546
  43.6 7.0 %shard_map.63 = (f32[96,2048]{1,0:T(8,128)S(1)}, bf16[27,16,2048]{2,1,0:T(8,128)(2,1)S(1)}, bf16[96,1280]{1,0:T(8,128)(2,1)S(1)}) custom-call(bf16[96,512]{1,0:T(8,128)(2,1)S(1)} %get-tuple-element.38.x_ref, s32[1]{0:T(128)S(6)} %copy.6.height_ref, bf16[112,384]{1,0:T(8,128)(2,1)S(1)} %collective-permute-done.before_ref, ...), custom_call_target="tpu_custom_call" | custom-call | tf_op jit(solution)/shard_map/pallas_call | solution.py:50
  50.6 0.0 collective-permute-done.4.halo_ref
  50.6 2.4 %shard_map.64.earlier_ref = bf16[96,1024]{1,0:T(8,128)(2,1)S(1)} custom-call(bf16[96,512]{1,0:T(8,128)(2,1)S(1)} %get-tuple-element.31.top_ref, bf16[96,1024]{1,0:T(8,128)(2,1)S(1)} %collective-permute-done.4.halo_ref, bf16[112,1024]{1,0:T(8,128)(2,1)S(1)} %collective-permute-done.2.left_ref, bf16[112,1024]{1,0:T(8,128)(2,1)S(1)} %collective-permute-done.3.right_ref, ...), custom_call_target="tpu_custom_call" | custom-call | tf_op jit(solution)/shard_map/pallas_call | solution.py:50
  53.0 0.7 collective-permute-start.5
  53.7 2.2 %shard_map.67 = (bf16[96,768]{1,0:T(8,128)(2,1)S(1)}, bf16[96,1024]{1,0:T(8,128)(2,1)S(1)}, bf16[96,1024]{1,0:T(8,128)(2,1)S(1)}) custom-call(bf16[96,512]{1,0:T(8,128)(2,1)S(1)} %get-tuple-element.31.top_ref, bf16[96,1024]{1,0:T(8,128)(2,1)S(1)} %collective-permute-done.4.halo_ref, bf16[112,1024]{1,0:T(8,128)(2,1)S(1)} %collective-permute-done.2.left_ref, ...), custom_call_target="tpu_custom_call" | custom-call | tf_op jit(solution)/shard_map/pallas_call | solution.py:50
  55.9 0.7 collective-permute-start.8
  56.6 0.0 collective-permute-done.5.piece_ref.first_ref
  56.6 2.1 %shard_map.65.earlier_ref = bf16[96,640]{1,0:T(8,128)(2,1)S(1)} custom-call(bf16[96,1024]{1,0:T(8,128)(2,1)S(1)} %collective-permute-done.5.piece_ref.first_ref, f32[96,2048]{1,0:T(8,128)S(1)} %get-tuple-element.42.slope_ref, bf16[27,16,2048]{2,1,0:T(8,128)(2,1)S(1)} %get-tuple-element.43.mask_ref, bf16[96,2592]{1,0:T(8,128)(2,1)S(1)} %get-tuple-element.44.bwd_ref), custom_call_target="tpu_custom_call" | custom-call | tf_op jit(solution)/shard_map/pallas_call | solution.py:50
  58.6 0.7 collective-permute-start.6
  59.3 0.0 collective-permute-done.8.second_ref
  59.3 2.2 %shard_map.68 = (bf16[96,640]{1,0:T(8,128)(2,1)S(1)}, bf16[96,1024]{1,0:T(8,128)(2,1)S(1)}, bf16[96,1024]{1,0:T(8,128)(2,1)S(1)}) custom-call(bf16[96,1024]{1,0:T(8,128)(2,1)S(1)} %collective-permute-done.5.piece_ref.first_ref, bf16[96,768]{1,0:T(8,128)(2,1)S(1)} %collective-permute-done.8.second_ref, f32[96,2048]{1,0:T(8,128)S(1)} %get-tuple-element.42.slope_ref, ...), custom_call_target="tpu_custom_call" | custom-call | tf_op jit(solution)/shard_map/pallas_call | solution.py:50
  61.6 0.7 collective-permute-start.9
  62.2 0.0 collective-permute-done.6.piece_ref.first_ref
  62.2 1.4 %shard_map.66.earlier_ref = bf16[96,384]{1,0:T(8,128)(2,1)S(1)} custom-call(bf16[96,640]{1,0:T(8,128)(2,1)S(1)} %collective-permute-done.6.piece_ref.first_ref, f32[96,2048]{1,0:T(8,128)S(1)} %get-tuple-element.42.slope_ref, bf16[27,16,2048]{2,1,0:T(8,128)(2,1)S(1)} %get-tuple-element.43.mask_ref, bf16[96,2592]{1,0:T(8,128)(2,1)S(1)} %get-tuple-element.44.bwd_ref), custom_call_target="tpu_custom_call" | custom-call | tf_op jit(solution)/shard_map/pallas_call | solution.py:50
  63.7 0.0 collective-permute-done.9.second_ref
  63.7 2.3 %shard_map.69 = (bf16[96,512]{1,0:T(8,128)(2,1)S(1)}, bf16[96,1024]{1,0:T(8,128)(2,1)S(1)}, bf16[96,1024]{1,0:T(8,128)(2,1)S(1)}) custom-call(bf16[96,640]{1,0:T(8,128)(2,1)S(1)} %collective-permute-done.6.piece_ref.first_ref, bf16[96,640]{1,0:T(8,128)(2,1)S(1)} %collective-permute-done.9.second_ref, f32[96,2048]{1,0:T(8,128)S(1)} %get-tuple-element.42.slope_ref, ...), custom_call_target="tpu_custom_call" | custom-call | tf_op jit(solution)/shard_map/pallas_call | solution.py:50
  66.0 1.3 collective-permute-start.10
  67.3 1.5 %collective-permute-start.7 = (bf16[96,384]{1,0:T(8,128)(2,1)S(1)}, bf16[96,384]{1,0:T(8,128)(2,1)S(1)}, u32[]{:S(2)}, u32[]{:S(2)}) collective-permute-start(bf16[96,384]{1,0:T(8,128)(2,1)S(1)} %shard_map.66.earlier_ref), channel_id=1, source_target_pairs={{1,0},{5,4},{9,8},{13,12},{17,16},{21,20},{25,24},{29,28},{33,32},... | collective-permute-start | bytes 221192 | tf_op jit(solution)/shard_map/ppermute | solution.py:562
  68.8 2.4 %shard_map.70.all_ref = bf16[2592,512]{1,0:T(8,128)(2,1)S(1)} custom-call(bf16[96,1280]{1,0:T(8,128)(2,1)S(1)} %get-tuple-element.54.x_ref, bf16[27,16,2048]{2,1,0:T(8,128)(2,1)S(1)} %get-tuple-element.43.mask_ref), custom_call_target="tpu_custom_call" | custom-call | tf_op jit(solution)/shard_map/pallas_call | solution.py:50
  71.2 4.8 %collective-permute-done.7.first_ref = bf16[96,384]{1,0:T(8,128)(2,1)S(1)} collective-permute-done((bf16[96,384]{1,0:T(8,128)(2,1)S(1)}, bf16[96,384]{1,0:T(8,128)(2,1)S(1)}, u32[]{:S(2)}, u32[]{:S(2)}) %collective-permute-start.7) | collective-permute-done | bytes 73760 | tf_op jit(solution)/shard_map/ppermute | solution.py:562
  76.0 0.0 collective-permute-done.10.second_ref
  76.0 1.2 shard_map.71
  77.1 17.9 %all_to_all.15.parts_ref = bf16[16,128,128]{2,1,0:T(8,128)(2,1)S(1)} all-to-all(bf16[16,128,128]{2,1,0:T(8,128)(2,1)S(1)} %bitcast.8), channel_id=1, replica_groups={{0,4,8,12,128,132,136,140,256,260,264,268,384,388,392,396},{16,20,24,28..., dimensions={0} | all-to-all | bytes 1048576 | tf_op jit(solution)/shard_map/all_to_all | solution.py:606
  95.0 0.1 shard_map.73
  95.1 24.0 %all_to_all.16.parts_ref = bf16[8,128,128]{2,1,0:T(8,128)(2,1)S(1)} all-to-all(bf16[8,128,128]{2,1,0:T(8,128)(2,1)S(1)} %shard_map.73), channel_id=1, replica_groups={{0,16,32,48,64,80,96,112},{4,20,36,52,68,84,100,116},{8,24,40,56,72,88,..., dimensions={0} | all-to-all | bytes 524288 | tf_op jit(solution)/shard_map/all_to_all | solution.py:614
  119.1 0.1 shard_map.74
  119.2 0.0 copy-start
  119.2 0.8 copy-done
  120.0 10.0 %all-to-all-start.2 = ((bf16[16,128,128]{2,1,0:T(8,128)(2,1)}), bf16[16,128,128]{2,1,0:T(8,128)(2,1)}, u32[]{:S(2)}, u32[]{:S(2)}) async-start(bf16[16,128,128]{2,1,0:T(8,128)(2,1)} %copy-done), calls=%async_computation.2 | async-start | bytes 1048576 | tf_op jit(solution)/shard_map/all_to_all | solution.py:616
  130.0 3.2 %shard_map.72 = bf16[96,512]{1,0:T(8,128)(2,1)} custom-call(bf16[96,1280]{1,0:T(8,128)(2,1)S(1)} %get-tuple-element.55.incoming_ref, f32[96,2048]{1,0:T(8,128)S(1)} %get-tuple-element.42.slope_ref, bf16[27,16,2048]{2,1,0:T(8,128)(2,1)S(1)} %get-tuple-element.43.mask_ref, bf16[96,2592]{1,0:T(8,128)(2,1)S(1)} %get-tuple-element.44.bwd_ref, ...), custom_call_target="tpu_custom_call" | custom-call | tf_op jit(solution)/shard_map/pallas_call | solution.py:50
  133.3 6.7 %all-to-all-done.2 = bf16[16,128,128]{2,1,0:T(8,128)(2,1)} async-done(((bf16[16,128,128]{2,1,0:T(8,128)(2,1)}), bf16[16,128,128]{2,1,0:T(8,128)(2,1)}, u32[]{:S(2)}, u32[]{:S(2)}) %all-to-all-start.2) | async-done | bytes 524320 | tf_op jit(solution)/shard_map/all_to_all | solution.py:616
  140.0 3.0 %shard_map.75 = f32[2592,96]{1,0:T(8,128)} custom-call(bf16[2048,128]{1,0:T(8,128)(2,1)} %bitcast.5.whole_ref), custom_call_target="tpu_custom_call" | custom-call | tf_op jit(solution)/shard_map/pallas_call | solution.py:50
Async XLA Ops:
  2.3 12.8 %collective-permute-start = (bf16[112,384]{1,0:T(8,128)(2,1)S(1)}, bf16[112,384]{1,0:T(8,128)(2,1)S(1)}, u32[]{:S(2)}, u32[]{:S(2)}) collective-permute-start(bf16[112,384]{1,0:T(8,128)(2,1)S(1)} %get-tuple-element.32), channel_id=1, source_target_pairs={{0,32},{1,33},{2,34},{3,35},{4,36},{5,37},{6,38},{7,39},{8,40},{9,... | collective-permute-start | bytes 258056 | tf_op jit(solution)/shard_map/ppermute | solution.py:537
  11.9 16.9 %collective-permute-start.1 = (bf16[112,384]{1,0:T(8,128)(2,1)S(1)}, bf16[112,384]{1,0:T(8,128)(2,1)S(1)}, u32[]{:S(2)}, u32[]{:S(2)}) collective-permute-start(bf16[112,384]{1,0:T(8,128)(2,1)S(1)} %get-tuple-element.33), channel_id=1, source_target_pairs={{32,0},{33,1},{34,2},{35,3},{36,4},{37,5},{38,6},{39,7},{40,8},{41... | collective-permute-start | bytes 258056 | tf_op jit(solution)/shard_map/ppermute | solution.py:538
  13.2 1.1 copy-start.1
  29.2 5.2 %collective-permute-start.2 = (bf16[112,1024]{1,0:T(8,128)(2,1)S(1)}, bf16[112,1024]{1,0:T(8,128)(2,1)S(1)}, u32[]{:S(2)}, u32[]{:S(2)}) collective-permute-start(bf16[112,1024]{1,0:T(8,128)(2,1)S(1)} %get-tuple-element.39), channel_id=1, source_target_pairs={{0,4},{1,5},{2,6},{3,7},{4,8},{5,9},{6,10},{7,11},{8,12},{9,13},{1... | collective-permute-start | bytes 688136 | tf_op jit(solution)/shard_map/ppermute | solution.py:543
  31.5 7.3 %collective-permute-start.3 = (bf16[112,1024]{1,0:T(8,128)(2,1)S(1)}, bf16[112,1024]{1,0:T(8,128)(2,1)S(1)}, u32[]{:S(2)}, u32[]{:S(2)}) collective-permute-start(bf16[112,1024]{1,0:T(8,128)(2,1)S(1)} %get-tuple-element.40), channel_id=1, source_target_pairs={{4,0},{5,1},{6,2},{7,3},{8,4},{9,5},{10,6},{11,7},{12,8},{13,9},{1... | collective-permute-start | bytes 688136 | tf_op jit(solution)/shard_map/ppermute | solution.py:544
  39.0 11.5 %collective-permute-start.4 = (bf16[96,1024]{1,0:T(8,128)(2,1)S(1)}, bf16[96,1024]{1,0:T(8,128)(2,1)S(1)}, u32[]{:S(2)}, u32[]{:S(2)}) collective-permute-start(bf16[96,1024]{1,0:T(8,128)(2,1)S(1)} %shard_map.62), channel_id=1, source_target_pairs={{0,3},{4,7},{8,11},{12,15},{16,19},{20,23},{24,27},{28,31},{32,35}... | collective-permute-start | bytes 589832 | tf_op jit(solution)/shard_map/ppermute | solution.py:546
  53.0 3.6 %collective-permute-start.5 = (bf16[96,1024]{1,0:T(8,128)(2,1)S(1)}, bf16[96,1024]{1,0:T(8,128)(2,1)S(1)}, u32[]{:S(2)}, u32[]{:S(2)}) collective-permute-start(bf16[96,1024]{1,0:T(8,128)(2,1)S(1)} %shard_map.64.earlier_ref), channel_id=1, source_target_pairs={{3,2},{7,6},{11,10},{15,14},{19,18},{23,22},{27,26},{31,30},{35,34... | collective-permute-start | bytes 589832 | tf_op jit(solution)/shard_map/ppermute | solution.py:562
  55.9 3.4 %collective-permute-start.8 = (bf16[96,768]{1,0:T(8,128)(2,1)S(1)}, bf16[96,768]{1,0:T(8,128)(2,1)S(1)}, u32[]{:S(2)}, u32[]{:S(2)}) collective-permute-start(bf16[96,768]{1,0:T(8,128)(2,1)S(1)} %get-tuple-element.45), channel_id=1, source_target_pairs={{3,2},{7,6},{11,10},{15,14},{19,18},{23,22},{27,26},{31,30},{35,34... | collective-permute-start | bytes 442376 | tf_op jit(solution)/shard_map/ppermute | solution.py:562
  58.6 3.6 %collective-permute-start.6 = (bf16[96,640]{1,0:T(8,128)(2,1)S(1)}, bf16[96,640]{1,0:T(8,128)(2,1)S(1)}, u32[]{:S(2)}, u32[]{:S(2)}) collective-permute-start(bf16[96,640]{1,0:T(8,128)(2,1)S(1)} %shard_map.65.earlier_ref), channel_id=1, source_target_pairs={{2,1},{6,5},{10,9},{14,13},{18,17},{22,21},{26,25},{30,29},{34,33}... | collective-permute-start | bytes 368648 | tf_op jit(solution)/shard_map/ppermute | solution.py:562
  61.6 2.1 %collective-permute-start.9 = (bf16[96,640]{1,0:T(8,128)(2,1)S(1)}, bf16[96,640]{1,0:T(8,128)(2,1)S(1)}, u32[]{:S(2)}, u32[]{:S(2)}) collective-permute-start(bf16[96,640]{1,0:T(8,128)(2,1)S(1)} %get-tuple-element.48), channel_id=1, source_target_pairs={{2,1},{6,5},{10,9},{14,13},{18,17},{22,21},{26,25},{30,29},{34,33}... | collective-permute-start | bytes 368648 | tf_op jit(solution)/shard_map/ppermute | solution.py:562
  66.0 10.0 %collective-permute-start.10 = (bf16[96,512]{1,0:T(8,128)(2,1)S(1)}, bf16[96,512]{1,0:T(8,128)(2,1)S(1)}, u32[]{:S(2)}, u32[]{:S(2)}) collective-permute-start(bf16[96,512]{1,0:T(8,128)(2,1)S(1)} %get-tuple-element.51), channel_id=1, source_target_pairs={{1,0},{5,4},{9,8},{13,12},{17,16},{21,20},{25,24},{29,28},{33,32},... | collective-permute-start | bytes 294920 | tf_op jit(solution)/shard_map/ppermute | solution.py:562
  67.3 8.7 %collective-permute-start.7 = (bf16[96,384]{1,0:T(8,128)(2,1)S(1)}, bf16[96,384]{1,0:T(8,128)(2,1)S(1)}, u32[]{:S(2)}, u32[]{:S(2)}) collective-permute-start(bf16[96,384]{1,0:T(8,128)(2,1)S(1)} %shard_map.66.earlier_ref), channel_id=1, source_target_pairs={{1,0},{5,4},{9,8},{13,12},{17,16},{21,20},{25,24},{29,28},{33,32},... | collective-permute-start | bytes 221192 | tf_op jit(solution)/shard_map/ppermute | solution.py:562
  119.2 0.8 copy-start
  120.0 20.0 %all-to-all-start.2 = ((bf16[16,128,128]{2,1,0:T(8,128)(2,1)}), bf16[16,128,128]{2,1,0:T(8,128)(2,1)}, u32[]{:S(2)}, u32[]{:S(2)}) async-start(bf16[16,128,128]{2,1,0:T(8,128)(2,1)} %copy-done), calls=%async_computation.2 | async-start | bytes 1048576 | tf_op jit(solution)/shard_map/all_to_all | solution.py:616

commit v8 on v7

--- a/solution.py
+++ b/solution.py
@@ -487,9 +487,7 @@
     scale = lax.rsqrt(jnp.sum(whole * whole) / (DEEP * C) + 1e-06)
     for four in range(7):
         at = 3 * C * four
-        first, second, third = (
-            whole_ref[at + n * C : at + n * C + C, :].astype(F32) * scale for n in range(3)
-        )
+        first, second, third = (whole_ref[at + n * C : at + n * C + C, :] for n in range(3))
         parts = (
             first[:, :96],
             jnp.concatenate([first[:, 96:], second[:, :64]], 1),
@@ -497,7 +495,7 @@
             third[:, 32:],
         )
         for n, tap in enumerate(range(4 * four, min(4 * four + 4, TAPS))):
-            out_ref[C * tap : C * tap + C, :] = parts[n]
+            out_ref[C * tap : C * tap + C, :] = parts[n].astype(F32) * scale
 
 
 def groups():
@@ -612,6 +610,7 @@
     )(incoming, slope, mask, bwd, out)
     (copies,) = call(sum_kernel, [((FAR, CHUNK, WIDE), BF16)])(parts)
     parts = lax.all_to_all(copies, "space", 0, 0, axis_index_groups=far)
+    parts, out = lax.optimization_barrier((parts, out))
     (copies,) = call(sum_kernel, [((NEAR, CHUNK, WIDE), BF16)])(parts)
     whole = lax.all_to_all(copies, "space", 0, 0, axis_index_groups=near)
     (weight_grad,) = call(scale_kernel, [((DEEP, C), F32)], leave=(0,))(

time: 144 us -> 141 us (0.979)
  blocking collectives: 41.9 us -> 36.3 us
  waiting for transfers between devices: 30.5 us -> 36.1 us
  starting transfers between devices: 35.3 us -> 32.9 us
    all_to_all x1, waiting for transfers between devices: 6.74 us -> 12.4 us  [body(): parts = lax.all_to_all(copies, 'space', 0, 0, axis_index_groups=far)]
    all_to_all x1, blocking collectives: 24 us -> 18.4 us  [body(): whole = lax.all_to_all(copies, 'space', 0, 0, axis_index_groups=near)]
    all_to_all x1, starting transfers between devices: 10 us -> 7.64 us  [body(): parts = lax.all_to_all(copies, 'space', 0, 0, axis_index_groups=far)]
where the time goes in v8:
time: 141 us; the launch traced here: 140 us
  blocking collectives  36.3 us (26%)
  waiting for transfers between devices  36.1 us (26%)
  starting transfers between devices  32.9 us (23%)
  Pallas kernels  30.6 us (22%)
  local copies, waits for them, and re-layouts  2.73 us (2%)
  between operations  1.55 us (1%)
    pallas_call x17, Pallas kernels, run(): inner(*[arg if arg.dtype == jnp.int32 else pltpu.with_memory_space_constr...  30.6 us
    all_to_all x1, blocking collectives, body(): whole = lax.all_to_all(copies, 'space', 0, 0, axis_index_groups=near)  18.4 us
    all_to_all x1, blocking collectives, body(): lax.all_to_all(terms.reshape(NEAR, CHUNK, WIDE), 'space', 0, 0, axis_inde...  17.9 us
    ppermute x1, waiting for transfers between devices, body(): after = lax.ppermute(down, both, between(-1, 0, same))  13.7 us
    all_to_all x1, waiting for transfers between devices, body(): parts = lax.all_to_all(copies, 'space', 0, 0, axis_index_groups=far)  12.4 us
    ppermute x1, starting transfers between devices, body(): before = lax.ppermute(up, both, between(1, 0, same))  9.65 us
    all_to_all x1, starting transfers between devices, body(): parts = lax.all_to_all(copies, 'space', 0, 0, axis_index_groups=far)  7.64 us
    ppermute x6, starting transfers between devices, hand_on(): return lax.ppermute(value, both, between(0, 0, [(source, source - 1)]))  5.44 us
  transfers between devices with their start and end apart: 12, of which 5 were waited for; matrix products, arithmetic and copies ran while one was open for 0% of the time, Pallas kernels for 15%

profile of v8, /device:TPU:1, one launch (start us, length us, event | category | flops | bytes accessed | tf_op | source)
XLA Modules:
  0.0 140.3 jit_solution(17018560445275798843)
XLA Ops:
  1.3 1.0 shard_map.59
  2.3 9.6 %collective-permute-start = (bf16[112,384]{1,0:T(8,128)(2,1)S(1)}, bf16[112,384]{1,0:T(8,128)(2,1)S(1)}, u32[]{:S(2)}, u32[]{:S(2)}) collective-permute-start(bf16[112,384]{1,0:T(8,128)(2,1)S(1)} %get-tuple-element.34), channel_id=1, source_target_pairs={{0,32},{1,33},{2,34},{3,35},{4,36},{5,37},{6,38},{7,39},{8,40},{9,... | collective-permute-start | bytes 258056 | tf_op jit(solution)/shard_map/ppermute | solution.py:535
  11.9 1.3 collective-permute-start.1
  13.2 0.0 copy-start.1
  13.2 1.1 copy-done.1
  14.3 0.7 shard_map.60
  15.1 0.0 collective-permute-done.before_ref
  15.1 13.7 %collective-permute-done.1.after_ref = bf16[112,384]{1,0:T(8,128)(2,1)S(1)} collective-permute-done((bf16[112,384]{1,0:T(8,128)(2,1)S(1)}, bf16[112,384]{1,0:T(8,128)(2,1)S(1)}, u32[]{:S(2)}, u32[]{:S(2)}) %collective-permute-start.1) | collective-permute-done | bytes 86048 | tf_op jit(solution)/shard_map/ppermute | solution.py:536
  28.8 0.5 shard_map.61
  29.2 2.3 %collective-permute-start.2 = (bf16[112,1024]{1,0:T(8,128)(2,1)S(1)}, bf16[112,1024]{1,0:T(8,128)(2,1)S(1)}, u32[]{:S(2)}, u32[]{:S(2)}) collective-permute-start(bf16[112,1024]{1,0:T(8,128)(2,1)S(1)} %get-tuple-element.41), channel_id=1, source_target_pairs={{0,4},{1,5},{2,6},{3,7},{4,8},{5,9},{6,10},{7,11},{8,12},{9,13},{1... | collective-permute-start | bytes 688136 | tf_op jit(solution)/shard_map/ppermute | solution.py:541
  31.5 2.1 %collective-permute-start.3 = (bf16[112,1024]{1,0:T(8,128)(2,1)S(1)}, bf16[112,1024]{1,0:T(8,128)(2,1)S(1)}, u32[]{:S(2)}, u32[]{:S(2)}) collective-permute-start(bf16[112,1024]{1,0:T(8,128)(2,1)S(1)} %get-tuple-element.42), channel_id=1, source_target_pairs={{4,0},{5,1},{6,2},{7,3},{8,4},{9,5},{10,6},{11,7},{12,8},{13,9},{1... | collective-permute-start | bytes 688136 | tf_op jit(solution)/shard_map/ppermute | solution.py:542
  33.6 0.9 collective-permute-done.2.left_ref
  34.4 4.4 %collective-permute-done.3.right_ref = bf16[112,1024]{1,0:T(8,128)(2,1)S(1)} collective-permute-done((bf16[112,1024]{1,0:T(8,128)(2,1)S(1)}, bf16[112,1024]{1,0:T(8,128)(2,1)S(1)}, u32[]{:S(2)}, u32[]{:S(2)}) %collective-permute-start.3) | collective-permute-done | bytes 229408 | tf_op jit(solution)/shard_map/ppermute | solution.py:542
  38.8 0.2 shard_map.62
  39.0 4.5 %collective-permute-start.4 = (bf16[96,1024]{1,0:T(8,128)(2,1)S(1)}, bf16[96,1024]{1,0:T(8,128)(2,1)S(1)}, u32[]{:S(2)}, u32[]{:S(2)}) collective-permute-start(bf16[96,1024]{1,0:T(8,128)(2,1)S(1)} %shard_map.62), channel_id=1, source_target_pairs={{0,3},{4,7},{8,11},{12,15},{16,19},{20,23},{24,27},{28,31},{32,35}... | collective-permute-start | bytes 589832 | tf_op jit(solution)/shard_map/ppermute | solution.py:544
  43.6 7.0 %shard_map.63 = (f32[96,2048]{1,0:T(8,128)S(1)}, bf16[27,16,2048]{2,1,0:T(8,128)(2,1)S(1)}, bf16[96,1280]{1,0:T(8,128)(2,1)S(1)}) custom-call(bf16[96,512]{1,0:T(8,128)(2,1)S(1)} %get-tuple-element.40.x_ref, s32[1]{0:T(128)S(6)} %copy.6.height_ref, bf16[112,384]{1,0:T(8,128)(2,1)S(1)} %collective-permute-done.before_ref, ...), custom_call_target="tpu_custom_call" | custom-call | tf_op jit(solution)/shard_map/pallas_call | solution.py:50
  50.6 0.0 collective-permute-done.4.halo_ref
  50.6 2.4 %shard_map.64.earlier_ref = bf16[96,1024]{1,0:T(8,128)(2,1)S(1)} custom-call(bf16[96,512]{1,0:T(8,128)(2,1)S(1)} %get-tuple-element.33.top_ref, bf16[96,1024]{1,0:T(8,128)(2,1)S(1)} %collective-permute-done.4.halo_ref, bf16[112,1024]{1,0:T(8,128)(2,1)S(1)} %collective-permute-done.2.left_ref, bf16[112,1024]{1,0:T(8,128)(2,1)S(1)} %collective-permute-done.3.right_ref, ...), custom_call_target="tpu_custom_call" | custom-call | tf_op jit(solution)/shard_map/pallas_call | solution.py:50
  53.0 0.7 collective-permute-start.5
  53.7 2.2 %shard_map.67 = (bf16[96,768]{1,0:T(8,128)(2,1)S(1)}, bf16[96,1024]{1,0:T(8,128)(2,1)S(1)}, bf16[96,1024]{1,0:T(8,128)(2,1)S(1)}) custom-call(bf16[96,512]{1,0:T(8,128)(2,1)S(1)} %get-tuple-element.33.top_ref, bf16[96,1024]{1,0:T(8,128)(2,1)S(1)} %collective-permute-done.4.halo_ref, bf16[112,1024]{1,0:T(8,128)(2,1)S(1)} %collective-permute-done.2.left_ref, ...), custom_call_target="tpu_custom_call" | custom-call | tf_op jit(solution)/shard_map/pallas_call | solution.py:50
  55.9 0.7 collective-permute-start.8
  56.6 0.0 collective-permute-done.5.piece_ref.first_ref
  56.6 2.1 %shard_map.65.earlier_ref = bf16[96,640]{1,0:T(8,128)(2,1)S(1)} custom-call(bf16[96,1024]{1,0:T(8,128)(2,1)S(1)} %collective-permute-done.5.piece_ref.first_ref, f32[96,2048]{1,0:T(8,128)S(1)} %get-tuple-element.44.slope_ref, bf16[27,16,2048]{2,1,0:T(8,128)(2,1)S(1)} %get-tuple-element.45.mask_ref, bf16[96,2592]{1,0:T(8,128)(2,1)S(1)} %get-tuple-element.46.bwd_ref), custom_call_target="tpu_custom_call" | custom-call | tf_op jit(solution)/shard_map/pallas_call | solution.py:50
  58.6 0.7 collective-permute-start.6
  59.3 0.0 collective-permute-done.8.second_ref
  59.3 2.2 %shard_map.68 = (bf16[96,640]{1,0:T(8,128)(2,1)S(1)}, bf16[96,1024]{1,0:T(8,128)(2,1)S(1)}, bf16[96,1024]{1,0:T(8,128)(2,1)S(1)}) custom-call(bf16[96,1024]{1,0:T(8,128)(2,1)S(1)} %collective-permute-done.5.piece_ref.first_ref, bf16[96,768]{1,0:T(8,128)(2,1)S(1)} %collective-permute-done.8.second_ref, f32[96,2048]{1,0:T(8,128)S(1)} %get-tuple-element.44.slope_ref, ...), custom_call_target="tpu_custom_call" | custom-call | tf_op jit(solution)/shard_map/pallas_call | solution.py:50
  61.6 0.7 collective-permute-start.9
  62.2 0.0 collective-permute-done.6.piece_ref.first_ref
  62.2 1.4 %shard_map.66.earlier_ref = bf16[96,384]{1,0:T(8,128)(2,1)S(1)} custom-call(bf16[96,640]{1,0:T(8,128)(2,1)S(1)} %collective-permute-done.6.piece_ref.first_ref, f32[96,2048]{1,0:T(8,128)S(1)} %get-tuple-element.44.slope_ref, bf16[27,16,2048]{2,1,0:T(8,128)(2,1)S(1)} %get-tuple-element.45.mask_ref, bf16[96,2592]{1,0:T(8,128)(2,1)S(1)} %get-tuple-element.46.bwd_ref), custom_call_target="tpu_custom_call" | custom-call | tf_op jit(solution)/shard_map/pallas_call | solution.py:50
  63.7 0.0 collective-permute-done.9.second_ref
  63.7 2.3 %shard_map.69 = (bf16[96,512]{1,0:T(8,128)(2,1)S(1)}, bf16[96,1024]{1,0:T(8,128)(2,1)S(1)}, bf16[96,1024]{1,0:T(8,128)(2,1)S(1)}) custom-call(bf16[96,640]{1,0:T(8,128)(2,1)S(1)} %collective-permute-done.6.piece_ref.first_ref, bf16[96,640]{1,0:T(8,128)(2,1)S(1)} %collective-permute-done.9.second_ref, f32[96,2048]{1,0:T(8,128)S(1)} %get-tuple-element.44.slope_ref, ...), custom_call_target="tpu_custom_call" | custom-call | tf_op jit(solution)/shard_map/pallas_call | solution.py:50
  66.0 1.3 collective-permute-start.10
  67.3 1.5 %collective-permute-start.7 = (bf16[96,384]{1,0:T(8,128)(2,1)S(1)}, bf16[96,384]{1,0:T(8,128)(2,1)S(1)}, u32[]{:S(2)}, u32[]{:S(2)}) collective-permute-start(bf16[96,384]{1,0:T(8,128)(2,1)S(1)} %shard_map.66.earlier_ref), channel_id=1, source_target_pairs={{1,0},{5,4},{9,8},{13,12},{17,16},{21,20},{25,24},{29,28},{33,32},... | collective-permute-start | bytes 221192 | tf_op jit(solution)/shard_map/ppermute | solution.py:560
  68.8 2.4 %shard_map.70.all_ref = bf16[2592,512]{1,0:T(8,128)(2,1)S(1)} custom-call(bf16[96,1280]{1,0:T(8,128)(2,1)S(1)} %get-tuple-element.56.x_ref, bf16[27,16,2048]{2,1,0:T(8,128)(2,1)S(1)} %get-tuple-element.45.mask_ref), custom_call_target="tpu_custom_call" | custom-call | tf_op jit(solution)/shard_map/pallas_call | solution.py:50
  71.2 4.8 %collective-permute-done.7.first_ref = bf16[96,384]{1,0:T(8,128)(2,1)S(1)} collective-permute-done((bf16[96,384]{1,0:T(8,128)(2,1)S(1)}, bf16[96,384]{1,0:T(8,128)(2,1)S(1)}, u32[]{:S(2)}, u32[]{:S(2)}) %collective-permute-start.7) | collective-permute-done | bytes 73760 | tf_op jit(solution)/shard_map/ppermute | solution.py:560
  76.0 0.0 collective-permute-done.10.second_ref
  76.0 1.2 shard_map.71
  77.1 0.0 copy-start.2
  77.1 17.9 %all_to_all.15.parts_ref = bf16[16,128,128]{2,1,0:T(8,128)(2,1)S(1)} all-to-all(bf16[16,128,128]{2,1,0:T(8,128)(2,1)S(1)} %bitcast.9), channel_id=1, replica_groups={{0,4,8,12,128,132,136,140,256,260,264,268,384,388,392,396},{16,20,24,28..., dimensions={0} | all-to-all | bytes 1048576 | tf_op jit(solution)/shard_map/all_to_all | solution.py:604
  95.0 0.0 copy-done.2
  95.0 0.1 shard_map.72
  95.1 0.0 copy-start
  95.1 0.7 copy-done
  95.8 7.6 %all-to-all-start.1 = ((bf16[8,128,128]{2,1,0:T(8,128)(2,1)}), bf16[8,128,128]{2,1,0:T(8,128)(2,1)S(1)}, u32[]{:S(2)}, u32[]{:S(2)}) async-start(bf16[8,128,128]{2,1,0:T(8,128)(2,1)} %copy-done), calls=%async_computation.1 | async-start | bytes 524288 | tf_op jit(solution)/shard_map/all_to_all | solution.py:612
  103.5 0.0 copy-start.3
  103.5 0.9 copy-done.3
  104.4 3.2 %shard_map.73 = bf16[96,512]{1,0:T(8,128)(2,1)} custom-call(bf16[96,1280]{1,0:T(8,128)(2,1)S(1)} %copy-done.3, f32[96,2048]{1,0:T(8,128)S(1)} %get-tuple-element.44.slope_ref, bf16[27,16,2048]{2,1,0:T(8,128)(2,1)S(1)} %get-tuple-element.45.mask_ref, bf16[96,2592]{1,0:T(8,128)(2,1)S(1)} %get-tuple-element.46.bwd_ref, ...), custom_call_target="tpu_custom_call" | custom-call | tf_op jit(solution)/shard_map/pallas_call | solution.py:50
  107.6 12.4 %all-to-all-done.1.parts_ref = bf16[8,128,128]{2,1,0:T(8,128)(2,1)S(1)} async-done(((bf16[8,128,128]{2,1,0:T(8,128)(2,1)}), bf16[8,128,128]{2,1,0:T(8,128)(2,1)S(1)}, u32[]{:S(2)}, u32[]{:S(2)}) %all-to-all-start.1) | async-done | bytes 262176 | tf_op jit(solution)/shard_map/all_to_all | solution.py:612
  120.0 0.1 shard_map.74
  120.1 18.4 %all_to_all.16 = bf16[16,128,128]{2,1,0:T(8,128)(2,1)S(1)} all-to-all(bf16[16,128,128]{2,1,0:T(8,128)(2,1)S(1)} %shard_map.74), channel_id=1, replica_groups={{0,4,8,12,128,132,136,140,256,260,264,268,384,388,392,396},{16,20,24,28..., dimensions={0} | all-to-all | bytes 1048576 | tf_op jit(solution)/shard_map/all_to_all | solution.py:615
  138.5 1.8 %shard_map.75 = f32[2592,96]{1,0:T(8,128)} custom-call(bf16[2048,128]{1,0:T(8,128)(2,1)S(1)} %bitcast.7), custom_call_target="tpu_custom_call" | custom-call | tf_op jit(solution)/shard_map/pallas_call | solution.py:50
Async XLA Ops:
  2.3 12.8 %collective-permute-start = (bf16[112,384]{1,0:T(8,128)(2,1)S(1)}, bf16[112,384]{1,0:T(8,128)(2,1)S(1)}, u32[]{:S(2)}, u32[]{:S(2)}) collective-permute-start(bf16[112,384]{1,0:T(8,128)(2,1)S(1)} %get-tuple-element.34), channel_id=1, source_target_pairs={{0,32},{1,33},{2,34},{3,35},{4,36},{5,37},{6,38},{7,39},{8,40},{9,... | collective-permute-start | bytes 258056 | tf_op jit(solution)/shard_map/ppermute | solution.py:535
  11.9 16.9 %collective-permute-start.1 = (bf16[112,384]{1,0:T(8,128)(2,1)S(1)}, bf16[112,384]{1,0:T(8,128)(2,1)S(1)}, u32[]{:S(2)}, u32[]{:S(2)}) collective-permute-start(bf16[112,384]{1,0:T(8,128)(2,1)S(1)} %get-tuple-element.35), channel_id=1, source_target_pairs={{32,0},{33,1},{34,2},{35,3},{36,4},{37,5},{38,6},{39,7},{40,8},{41... | collective-permute-start | bytes 258056 | tf_op jit(solution)/shard_map/ppermute | solution.py:536
  13.2 1.1 copy-start.1
  29.2 5.2 %collective-permute-start.2 = (bf16[112,1024]{1,0:T(8,128)(2,1)S(1)}, bf16[112,1024]{1,0:T(8,128)(2,1)S(1)}, u32[]{:S(2)}, u32[]{:S(2)}) collective-permute-start(bf16[112,1024]{1,0:T(8,128)(2,1)S(1)} %get-tuple-element.41), channel_id=1, source_target_pairs={{0,4},{1,5},{2,6},{3,7},{4,8},{5,9},{6,10},{7,11},{8,12},{9,13},{1... | collective-permute-start | bytes 688136 | tf_op jit(solution)/shard_map/ppermute | solution.py:541
  31.5 7.3 %collective-permute-start.3 = (bf16[112,1024]{1,0:T(8,128)(2,1)S(1)}, bf16[112,1024]{1,0:T(8,128)(2,1)S(1)}, u32[]{:S(2)}, u32[]{:S(2)}) collective-permute-start(bf16[112,1024]{1,0:T(8,128)(2,1)S(1)} %get-tuple-element.42), channel_id=1, source_target_pairs={{4,0},{5,1},{6,2},{7,3},{8,4},{9,5},{10,6},{11,7},{12,8},{13,9},{1... | collective-permute-start | bytes 688136 | tf_op jit(solution)/shard_map/ppermute | solution.py:542
  39.0 11.5 %collective-permute-start.4 = (bf16[96,1024]{1,0:T(8,128)(2,1)S(1)}, bf16[96,1024]{1,0:T(8,128)(2,1)S(1)}, u32[]{:S(2)}, u32[]{:S(2)}) collective-permute-start(bf16[96,1024]{1,0:T(8,128)(2,1)S(1)} %shard_map.62), channel_id=1, source_target_pairs={{0,3},{4,7},{8,11},{12,15},{16,19},{20,23},{24,27},{28,31},{32,35}... | collective-permute-start | bytes 589832 | tf_op jit(solution)/shard_map/ppermute | solution.py:544
  53.0 3.6 %collective-permute-start.5 = (bf16[96,1024]{1,0:T(8,128)(2,1)S(1)}, bf16[96,1024]{1,0:T(8,128)(2,1)S(1)}, u32[]{:S(2)}, u32[]{:S(2)}) collective-permute-start(bf16[96,1024]{1,0:T(8,128)(2,1)S(1)} %shard_map.64.earlier_ref), channel_id=1, source_target_pairs={{3,2},{7,6},{11,10},{15,14},{19,18},{23,22},{27,26},{31,30},{35,34... | collective-permute-start | bytes 589832 | tf_op jit(solution)/shard_map/ppermute | solution.py:560
  55.9 3.4 %collective-permute-start.8 = (bf16[96,768]{1,0:T(8,128)(2,1)S(1)}, bf16[96,768]{1,0:T(8,128)(2,1)S(1)}, u32[]{:S(2)}, u32[]{:S(2)}) collective-permute-start(bf16[96,768]{1,0:T(8,128)(2,1)S(1)} %get-tuple-element.47), channel_id=1, source_target_pairs={{3,2},{7,6},{11,10},{15,14},{19,18},{23,22},{27,26},{31,30},{35,34... | collective-permute-start | bytes 442376 | tf_op jit(solution)/shard_map/ppermute | solution.py:560
  58.6 3.6 %collective-permute-start.6 = (bf16[96,640]{1,0:T(8,128)(2,1)S(1)}, bf16[96,640]{1,0:T(8,128)(2,1)S(1)}, u32[]{:S(2)}, u32[]{:S(2)}) collective-permute-start(bf16[96,640]{1,0:T(8,128)(2,1)S(1)} %shard_map.65.earlier_ref), channel_id=1, source_target_pairs={{2,1},{6,5},{10,9},{14,13},{18,17},{22,21},{26,25},{30,29},{34,33}... | collective-permute-start | bytes 368648 | tf_op jit(solution)/shard_map/ppermute | solution.py:560
  61.6 2.1 %collective-permute-start.9 = (bf16[96,640]{1,0:T(8,128)(2,1)S(1)}, bf16[96,640]{1,0:T(8,128)(2,1)S(1)}, u32[]{:S(2)}, u32[]{:S(2)}) collective-permute-start(bf16[96,640]{1,0:T(8,128)(2,1)S(1)} %get-tuple-element.50), channel_id=1, source_target_pairs={{2,1},{6,5},{10,9},{14,13},{18,17},{22,21},{26,25},{30,29},{34,33}... | collective-permute-start | bytes 368648 | tf_op jit(solution)/shard_map/ppermute | solution.py:560
  66.0 10.0 %collective-permute-start.10 = (bf16[96,512]{1,0:T(8,128)(2,1)S(1)}, bf16[96,512]{1,0:T(8,128)(2,1)S(1)}, u32[]{:S(2)}, u32[]{:S(2)}) collective-permute-start(bf16[96,512]{1,0:T(8,128)(2,1)S(1)} %get-tuple-element.53), channel_id=1, source_target_pairs={{1,0},{5,4},{9,8},{13,12},{17,16},{21,20},{25,24},{29,28},{33,32},... | collective-permute-start | bytes 294920 | tf_op jit(solution)/shard_map/ppermute | solution.py:560
  67.3 8.7 %collective-permute-start.7 = (bf16[96,384]{1,0:T(8,128)(2,1)S(1)}, bf16[96,384]{1,0:T(8,128)(2,1)S(1)}, u32[]{:S(2)}, u32[]{:S(2)}) collective-permute-start(bf16[96,384]{1,0:T(8,128)(2,1)S(1)} %shard_map.66.earlier_ref), channel_id=1, source_target_pairs={{1,0},{5,4},{9,8},{13,12},{17,16},{21,20},{25,24},{29,28},{33,32},... | collective-permute-start | bytes 221192 | tf_op jit(solution)/shard_map/ppermute | solution.py:560
  77.1 17.9 %copy-start.2 = (bf16[96,1280]{1,0:T(8,128)(2,1)}, bf16[96,1280]{1,0:T(8,128)(2,1)S(1)}, u32[]{:S(2)}) copy-start(bf16[96,1280]{1,0:T(8,128)(2,1)S(1)} %get-tuple-element.60.incoming_ref) | copy-start | bytes 737284
  95.1 0.7 copy-start
  95.8 24.2 %all-to-all-start.1 = ((bf16[8,128,128]{2,1,0:T(8,128)(2,1)}), bf16[8,128,128]{2,1,0:T(8,128)(2,1)S(1)}, u32[]{:S(2)}, u32[]{:S(2)}) async-start(bf16[8,128,128]{2,1,0:T(8,128)(2,1)} %copy-done), calls=%async_computation.1 | async-start | bytes 524288 | tf_op jit(solution)/shard_map/all_to_all | solution.py:612
  103.5 0.9 copy-start.3

commit v9 on v8

--- a/solution.py
+++ b/solution.py
@@ -72,8 +72,17 @@
 
 def shifted_rows(base_ref, row, tile, low=None, high=None):
     level = lax.broadcasted_iota(jnp.int32, (C, WIDE), 1) % 8
-    for oy, source in ((-1, low), (0, None), (1, high)):
-        source = tile if source is None else source
+    if low is None:
+        along = (
+            jnp.where(level > 0, turn(tile, 1), turn(tile, -7)),
+            tile,
+            jnp.where(level < 7, turn(tile, -1), turn(tile, 7)),
+        )
+        for oy in (-1, 0, 1):
+            for n in range(3):
+                base_ref[3 * (oy + 1) + n, :, lane(row)] = turn(along[n], -8 * oy)
+        return
+    for oy, source in ((-1, low), (0, tile), (1, high)):
         for oz in (-1, 0, 1):
             if oz == 0:
                 moved = turn(source, -8 * oy)
@@ -327,6 +336,11 @@
     return join([spare, packed_ref[:, width * row : width * row + width], spare])
 
 
+TOP_PIECES = (2, 8, WIDE), (10, 6, WIDE)
+MIDDLE_PIECES = (3, 6, 96), (9, 6, 96)
+LATE_PIECES = (4, 4, 80), (8, 6, 80)
+
+
 def pieces_row(pieces, row):
     for ref, first, count, width in pieces:
         if first <= row < first + count:
@@ -352,61 +366,24 @@
     result_ref[...] = join(packed + [jnp.zeros((C, spare), BF16)] if spare else packed)
 
 
-def keep_own(row_of, result_of, slope_ref, grad_in, out_in, grad_ref, out_ref):
-    for n in range(8):
-        grad = (row_of(n + 5).astype(F32) * slope_ref[:, lane(n + 4)]).astype(BF16)
-        out = result_of(n + 5)
-        if grad_in is not None:
-            grad, out = grad + grad_in[:, lane(n)], out + out_in[:, lane(n)]
-        grad_ref[:, lane(n)] = grad
-        out_ref[:, lane(n)] = out
-
-
-def top_first_kernel(
-    top_ref, halo_ref, left_ref, right_ref, slope_ref, mask_ref, bwd_ref, result_ref, *scratch
+def top_kernel(
+    low, count, top_ref, halo_ref, left_ref, right_ref, slope_ref, mask_ref, bwd_ref,
+    result_ref, *scratch,
 ):
     def row_of(row):
         return top_row(top_ref, halo_ref, left_ref, right_ref, row)
 
-    step_part(row_of, 2, 8, WIDE, result_ref, slope_ref, mask_ref, bwd_ref, scratch)
-
-
-def top_second_kernel(
-    top_ref, halo_ref, left_ref, right_ref, slope_ref, mask_ref, bwd_ref, earlier_ref,
-    result_ref, grad_ref, out_ref, *scratch,
-):
+    step_part(row_of, low, count, WIDE, result_ref, slope_ref, mask_ref, bwd_ref, scratch)
+
+
+def middle_kernel(pieces, low, count, width, *refs):
+    given, refs = refs[: len(pieces)], refs[len(pieces) :]
+    slope_ref, mask_ref, bwd_ref, result_ref, *scratch = refs
+
     def row_of(row):
-        return top_row(top_ref, halo_ref, left_ref, right_ref, row)
-
-    def result_of(row):
-        return pieces_row(((earlier_ref, 2, 8, WIDE), (result_ref, 10, 6, WIDE)), row)
-
-    step_part(row_of, 10, 6, WIDE, result_ref, slope_ref, mask_ref, bwd_ref, scratch)
-    keep_own(row_of, result_of, slope_ref, None, None, grad_ref, out_ref)
-
-
-def first_kernel(piece, low, count, width, piece_ref, slope_ref, mask_ref, bwd_ref, result_ref,
-                 *scratch):
-    def row_of(row):
-        return pieces_row(((piece_ref,) + piece,), row)
+        return pieces_row([(ref,) + piece for ref, piece in zip(given, pieces)], row)
 
     step_part(row_of, low, count, width, result_ref, slope_ref, mask_ref, bwd_ref, scratch)
-
-
-def second_kernel(
-    pieces, early, low, count, width,
-    first_ref, second_ref, slope_ref, mask_ref, bwd_ref, earlier_ref, grad_in, out_in,
-    result_ref, grad_ref, out_ref, *scratch,
-):
-    def row_of(row):
-        return pieces_row(((first_ref,) + pieces[0], (second_ref,) + pieces[1]), row)
-
-    def result_of(row):
-        later = (result_ref, low, count, width)
-        return pieces_row(((earlier_ref, early, low - early, width), later), row)
-
-    step_part(row_of, low, count, width, result_ref, slope_ref, mask_ref, bwd_ref, scratch)
-    keep_own(row_of, result_of, slope_ref, grad_in, out_in, grad_ref, out_ref)
 
 
 def halves(first, second):
@@ -414,7 +391,25 @@
     return jnp.where(where < 64, turn(first, -32), turn(second, 32))
 
 
-def gather_kernel(x_ref, mask_ref, all_ref, base_ref):
+def gather_kernel(
+    top_ref, halo_ref, left_ref, right_ref, slope_ref, mask_ref, x_ref, *refs
+):
+    kinds = TOP_PIECES + MIDDLE_PIECES + LATE_PIECES
+    pieces = [(ref,) + piece for ref, piece in zip(refs[:6], kinds)]
+    incoming = [(ref,) + piece for ref, piece in zip(refs[6:10], TOP_PIECES + MIDDLE_PIECES)]
+    all_ref, grad_ref, out_ref, base_ref = refs[10:]
+    for n in range(8):
+        row = n + 5
+        scale = slope_ref[:, lane(n + 4)]
+        tiles = (
+            top_row(top_ref, halo_ref, left_ref, right_ref, row),
+            pieces_row(incoming[:2], row),
+            pieces_row(incoming[2:], row),
+        )
+        grads = [(tile.astype(F32) * scale).astype(BF16) for tile in tiles]
+        grad_ref[:, lane(n)] = grads[0] + grads[1] + grads[2]
+        outs = [pieces_row(pieces[at : at + 2], row) for at in (0, 2, 4)]
+        out_ref[:, lane(n)] = outs[0] + outs[1] + outs[2]
     for row in range(10):
         shifted_rows(base_ref, row, x_ref[:, lane(row)])
 
@@ -437,7 +432,7 @@
 ):
     for row in range(10):
         incoming_ref[:, lane(row)] = pieces_row(
-            ((first_ref, 4, 4, 80), (second_ref, 8, 6, 80)), row + 4
+            ((first_ref,) + LATE_PIECES[0], (second_ref,) + LATE_PIECES[1]), row + 4
         )
     grads = []
     for row in range(8):
@@ -559,42 +554,47 @@
     def hand_on(value, source):
         return lax.ppermute(value, both, between(0, 0, [(source, source - 1)]))
 
-    tops = (top, halo, left, right, slope, mask, bwd)
-    (result,) = call(top_first_kernel, [((C, 8 * WIDE), BF16)], scratch(8))(*tops)
-    first = hand_on(result, 3)
-    result, grad, out = call(
-        top_second_kernel, [((C, 6 * WIDE), BF16), core, core], scratch(6)
-    )(*tops, result)
-    second = hand_on(result, 3)
-
-    pieces = (2, 8, WIDE), (10, 6, WIDE)
-    (result,) = call(
-        functools.partial(first_kernel, pieces[0], 3, 6, 96), [((C, 5 * WIDE), BF16)], scratch(6)
-    )(first, slope, mask, bwd)
-    next_first = hand_on(result, 2)
-    result, grad, out = call(
-        functools.partial(second_kernel, pieces, 3, 9, 6, 96),
-        [((C, 5 * WIDE), BF16), core, core],
-        scratch(6),
-    )(first, second, slope, mask, bwd, result, grad, out)
-    next_second = hand_on(result, 2)
-    first, second = next_first, next_second
-
-    pieces = (3, 6, 96), (9, 6, 96)
-    (result,) = call(
-        functools.partial(first_kernel, pieces[0], 4, 4, 80), [((C, 3 * WIDE), BF16)], scratch(4)
-    )(first, slope, mask, bwd)
-    next_first = hand_on(result, 1)
-    result, grad, out = call(
-        functools.partial(second_kernel, pieces, 4, 8, 6, 80),
-        [((C, 4 * WIDE), BF16), core, core],
-        scratch(6),
-    )(first, second, slope, mask, bwd, result, grad, out)
-    next_second = hand_on(result, 1)
-    first, second = next_first, next_second
-    x_rows, _ = lax.optimization_barrier((x_rows, result))
-    (x_cols,) = call(gather_kernel, [((DEEP, CELLS), BF16)], [((9, C, 10 * WIDE), BF16)])(
-        x_rows, mask
+    def behind(kernel, count):
+        return lambda *refs: kernel(*refs[:count], *refs[count + 1 :])
+
+    def parts_of(kernels, args, pieces, source):
+        made = []
+        for kernel, given, (low, count, width) in zip(kernels, args, pieces):
+            if made:
+                kernel, given = behind(kernel, len(given)), given + (made[0][0],)
+            lanes = -(-count * width // WIDE) * WIDE
+            (result,) = call(kernel, [((C, lanes), BF16)], scratch(count))(*given)
+            made.append((result, hand_on(result, source)))
+        return [result for result, _ in made], [moved for _, moved in made]
+
+    def middle(given, pieces, low, count, width):
+        return functools.partial(middle_kernel, pieces[:given], low, count, width)
+
+    rest = (slope, mask, bwd)
+    tops, moved = parts_of(
+        [functools.partial(top_kernel, low, count) for low, count, _ in TOP_PIECES],
+        [(top, halo, left, right) + rest] * 2,
+        TOP_PIECES,
+        3,
+    )
+    middles, moved_on = parts_of(
+        [middle(n + 1, TOP_PIECES, *MIDDLE_PIECES[n]) for n in range(2)],
+        [tuple(moved[: n + 1]) + rest for n in range(2)],
+        MIDDLE_PIECES,
+        2,
+    )
+    lates, (first, second) = parts_of(
+        [middle(n + 1, MIDDLE_PIECES, *LATE_PIECES[n]) for n in range(2)],
+        [tuple(moved_on[: n + 1]) + rest for n in range(2)],
+        LATE_PIECES,
+        1,
+    )
+    x_rows, result = lax.optimization_barrier((x_rows, lates[1]))
+    x_cols, grad, out = call(
+        gather_kernel, [((DEEP, CELLS), BF16), core, core], [((9, C, 10 * WIDE), BF16)]
+    )(
+        top, halo, left, right, slope, mask, x_rows,
+        *tops, *middles, lates[0], result, *moved, *moved_on,
     )
     terms, incoming = call(
         terms_kernel, [((NEAR * CHUNK, WIDE), BF16), ((C, 10 * WIDE), BF16)]

time: 141 us -> 142 us (level)
  waiting for transfers between devices: 36.1 us -> 32.9 us
  Pallas kernels: 30.6 us -> 33.5 us
  local copies, waits for them, and re-layouts: 2.73 us -> 4.32 us
    pallas_call x17, Pallas kernels: 30.6 us -> 33.5 us  [run(): inner(*[arg if arg.dtype == jnp.int32 else pltpu.with_memory_space_constr...]
    ppermute x6, waiting for transfers between devices: 4.81 us -> 3.01 us  [hand_on(): return lax.ppermute(value, both, between(0, 0, [(source, source - 1)]))]
    unnamed x8 -> x12, local copies, waits for them, and re-layouts: 2.73 us -> 4.32 us
  transfers between devices with their start and end apart: 12 -> 12, of which waited for: 5 -> 5; matrix products, arithmetic and copies ran while one was open for 0% -> 0% of each run, Pallas kernels for 15% -> 17%
where the time goes in v9:
time: 142 us
  blocking collectives  36.2 us (25%)
  Pallas kernels  33.5 us (24%)
  starting transfers between devices  33 us (23%)
  waiting for transfers between devices  32.9 us (23%)
  local copies, waits for them, and re-layouts  4.32 us (3%)
  between operations  1.56 us (1%)
    pallas_call x17, Pallas kernels, run(): inner(*[arg if arg.dtype == jnp.int32 else pltpu.with_memory_space_constr...  33.5 us
    all_to_all x1, blocking collectives, body(): whole = lax.all_to_all(copies, 'space', 0, 0, axis_index_groups=near)  18.4 us
    all_to_all x1, blocking collectives, body(): lax.all_to_all(terms.reshape(NEAR, CHUNK, WIDE), 'space', 0, 0, axis_inde...  17.8 us
    ppermute x1, waiting for transfers between devices, body(): after = lax.ppermute(down, both, between(-1, 0, same))  13.7 us
    all_to_all x1, waiting for transfers between devices, body(): parts = lax.all_to_all(copies, 'space', 0, 0, axis_index_groups=far)  11 us
    ppermute x1, starting transfers between devices, body(): before = lax.ppermute(up, both, between(1, 0, same))  9.65 us
    all_to_all x1, starting transfers between devices, body(): parts = lax.all_to_all(copies, 'space', 0, 0, axis_index_groups=far)  7.77 us
    ppermute x6, starting transfers between devices, hand_on(): return lax.ppermute(value, both, between(0, 0, [(source, source - 1)]))  5.44 us
  transfers between devices with their start and end apart: 12, of which 5 were waited for; matrix products, arithmetic and copies ran while one was open for 0% of the time, Pallas kernels for 17%

profile of v9, /device:TPU:1, one launch (start us, length us, event | category | flops | bytes accessed | tf_op | source)
XLA Modules:
  0.0 141.6 jit_solution(2300471365862233094)
XLA Ops:
  1.3 1.0 shard_map.59
  2.3 9.6 %collective-permute-start = (bf16[112,384]{1,0:T(8,128)(2,1)S(1)}, bf16[112,384]{1,0:T(8,128)(2,1)S(1)}, u32[]{:S(2)}, u32[]{:S(2)}) collective-permute-start(bf16[112,384]{1,0:T(8,128)(2,1)S(1)} %get-tuple-element.29), channel_id=1, source_target_pairs={{0,32},{1,33},{2,34},{3,35},{4,36},{5,37},{6,38},{7,39},{8,40},{9,... | collective-permute-start | bytes 258056 | tf_op jit(solution)/shard_map/ppermute | solution.py:530
  11.9 1.3 collective-permute-start.1
  13.2 0.0 copy-start.1
  13.2 1.1 copy-done.1
  14.3 0.7 shard_map.60
  15.1 0.0 collective-permute-done.before_ref
  15.1 13.7 %collective-permute-done.1.after_ref = bf16[112,384]{1,0:T(8,128)(2,1)S(1)} collective-permute-done((bf16[112,384]{1,0:T(8,128)(2,1)S(1)}, bf16[112,384]{1,0:T(8,128)(2,1)S(1)}, u32[]{:S(2)}, u32[]{:S(2)}) %collective-permute-start.1) | collective-permute-done | bytes 86048 | tf_op jit(solution)/shard_map/ppermute | solution.py:531
  28.8 0.5 shard_map.61
  29.2 2.3 %collective-permute-start.2 = (bf16[112,1024]{1,0:T(8,128)(2,1)S(1)}, bf16[112,1024]{1,0:T(8,128)(2,1)S(1)}, u32[]{:S(2)}, u32[]{:S(2)}) collective-permute-start(bf16[112,1024]{1,0:T(8,128)(2,1)S(1)} %get-tuple-element.36), channel_id=1, source_target_pairs={{0,4},{1,5},{2,6},{3,7},{4,8},{5,9},{6,10},{7,11},{8,12},{9,13},{1... | collective-permute-start | bytes 688136 | tf_op jit(solution)/shard_map/ppermute | solution.py:536
  31.5 2.1 %collective-permute-start.3 = (bf16[112,1024]{1,0:T(8,128)(2,1)S(1)}, bf16[112,1024]{1,0:T(8,128)(2,1)S(1)}, u32[]{:S(2)}, u32[]{:S(2)}) collective-permute-start(bf16[112,1024]{1,0:T(8,128)(2,1)S(1)} %get-tuple-element.37), channel_id=1, source_target_pairs={{4,0},{5,1},{6,2},{7,3},{8,4},{9,5},{10,6},{11,7},{12,8},{13,9},{1... | collective-permute-start | bytes 688136 | tf_op jit(solution)/shard_map/ppermute | solution.py:537
  33.6 0.9 collective-permute-done.2.left_ref.refs_2_
  34.4 4.4 %collective-permute-done.3.right_ref.refs_3_ = bf16[112,1024]{1,0:T(8,128)(2,1)S(1)} collective-permute-done((bf16[112,1024]{1,0:T(8,128)(2,1)S(1)}, bf16[112,1024]{1,0:T(8,128)(2,1)S(1)}, u32[]{:S(2)}, u32[]{:S(2)}) %collective-permute-start.3) | collective-permute-done | bytes 229408 | tf_op jit(solution)/shard_map/ppermute | solution.py:537
  38.8 0.2 shard_map.62
  39.0 4.5 %collective-permute-start.4 = (bf16[96,1024]{1,0:T(8,128)(2,1)S(1)}, bf16[96,1024]{1,0:T(8,128)(2,1)S(1)}, u32[]{:S(2)}, u32[]{:S(2)}) collective-permute-start(bf16[96,1024]{1,0:T(8,128)(2,1)S(1)} %shard_map.62), channel_id=1, source_target_pairs={{0,3},{4,7},{8,11},{12,15},{16,19},{20,23},{24,27},{28,31},{32,35}... | collective-permute-start | bytes 589832 | tf_op jit(solution)/shard_map/ppermute | solution.py:539
  43.6 7.0 %shard_map.63 = (f32[96,2048]{1,0:T(8,128)S(1)}, bf16[27,16,2048]{2,1,0:T(8,128)(2,1)S(1)}, bf16[96,1280]{1,0:T(8,128)(2,1)S(1)}) custom-call(bf16[96,512]{1,0:T(8,128)(2,1)S(1)} %get-tuple-element.35.x_ref, s32[1]{0:T(128)S(6)} %copy.6.height_ref, bf16[112,384]{1,0:T(8,128)(2,1)S(1)} %collective-permute-done.before_ref, ...), custom_call_target="tpu_custom_call" | custom-call | tf_op jit(solution)/shard_map/pallas_call | solution.py:50
  50.6 0.0 collective-permute-done.4.halo_ref.refs_1_
  50.6 2.9 %shard_map.64.refs_7_.refs_0_ = bf16[96,1024]{1,0:T(8,128)(2,1)S(1)} custom-call(bf16[96,512]{1,0:T(8,128)(2,1)S(1)} %get-tuple-element.28.top_ref.refs_0_, bf16[96,1024]{1,0:T(8,128)(2,1)S(1)} %collective-permute-done.4.halo_ref.refs_1_, bf16[112,1024]{1,0:T(8,128)(2,1)S(1)} %collective-permute-done.2.left_ref.refs_2_, ...), custom_call_target="tpu_custom_call" | custom-call | tf_op jit(solution)/shard_map/pallas_call | solution.py:50
  53.5 0.7 collective-permute-start.5
  54.2 2.3 %shard_map.67.refs_1_ = bf16[96,768]{1,0:T(8,128)(2,1)S(1)} custom-call(bf16[96,512]{1,0:T(8,128)(2,1)S(1)} %get-tuple-element.28.top_ref.refs_0_, bf16[96,1024]{1,0:T(8,128)(2,1)S(1)} %collective-permute-done.4.halo_ref.refs_1_, bf16[112,1024]{1,0:T(8,128)(2,1)S(1)} %collective-permute-done.2.left_ref.refs_2_, ...), custom_call_target="tpu_custom_call" | custom-call | tf_op jit(solution)/shard_map/pallas_call | solution.py:50
  56.5 0.7 collective-permute-start.8
  57.2 0.0 collective-permute-done.5.refs_0_.refs_6_
  57.2 2.4 %shard_map.65.refs_5_.refs_2_ = bf16[96,640]{1,0:T(8,128)(2,1)S(1)} custom-call(bf16[96,1024]{1,0:T(8,128)(2,1)S(1)} %collective-permute-done.5.refs_0_.refs_6_, f32[96,2048]{1,0:T(8,128)S(1)} %get-tuple-element.39.slope_ref.refs_1_.refs_4_.refs_2_, bf16[27,16,2048]{2,1,0:T(8,128)(2,1)S(1)} %get-tuple-element.40.mask_ref.refs_2_.refs_5_.refs_3_, ...), custom_call_target="tpu_custom_call" | custom-call | tf_op jit(solution)/shard_map/pallas_call | solution.py:50
  59.6 0.7 collective-permute-start.6
  60.2 0.0 collective-permute-done.8.refs_1_.refs_7_
  60.3 2.4 %shard_map.68.refs_3_ = bf16[96,640]{1,0:T(8,128)(2,1)S(1)} custom-call(bf16[96,1024]{1,0:T(8,128)(2,1)S(1)} %collective-permute-done.5.refs_0_.refs_6_, bf16[96,768]{1,0:T(8,128)(2,1)S(1)} %collective-permute-done.8.refs_1_.refs_7_, f32[96,2048]{1,0:T(8,128)S(1)} %get-tuple-element.39.slope_ref.refs_1_.refs_4_.refs_2_, ...), custom_call_target="tpu_custom_call" | custom-call | tf_op jit(solution)/shard_map/pallas_call | solution.py:50
  62.7 0.7 collective-permute-start.9
  63.3 0.0 collective-permute-done.6.refs_0_.refs_8_
  63.4 1.7 %shard_map.66.refs_5_.refs_4_ = bf16[96,384]{1,0:T(8,128)(2,1)S(1)} custom-call(bf16[96,640]{1,0:T(8,128)(2,1)S(1)} %collective-permute-done.6.refs_0_.refs_8_, f32[96,2048]{1,0:T(8,128)S(1)} %get-tuple-element.39.slope_ref.refs_1_.refs_4_.refs_2_, bf16[27,16,2048]{2,1,0:T(8,128)(2,1)S(1)} %get-tuple-element.40.mask_ref.refs_2_.refs_5_.refs_3_, ...), custom_call_target="tpu_custom_call" | custom-call | tf_op jit(solution)/shard_map/pallas_call | solution.py:50
  65.0 0.0 collective-permute-done.9.refs_1_.refs_9_
  65.0 2.5 %shard_map.69.refs_5_ = bf16[96,512]{1,0:T(8,128)(2,1)S(1)} custom-call(bf16[96,640]{1,0:T(8,128)(2,1)S(1)} %collective-permute-done.6.refs_0_.refs_8_, bf16[96,640]{1,0:T(8,128)(2,1)S(1)} %collective-permute-done.9.refs_1_.refs_9_, f32[96,2048]{1,0:T(8,128)S(1)} %get-tuple-element.39.slope_ref.refs_1_.refs_4_.refs_2_, ...), custom_call_target="tpu_custom_call" | custom-call | tf_op jit(solution)/shard_map/pallas_call | solution.py:50
  67.5 1.5 %collective-permute-start.10 = (bf16[96,512]{1,0:T(8,128)(2,1)S(1)}, bf16[96,512]{1,0:T(8,128)(2,1)S(1)}, u32[]{:S(2)}, u32[]{:S(2)}) collective-permute-start(bf16[96,512]{1,0:T(8,128)(2,1)S(1)} %shard_map.69.refs_5_), channel_id=1, source_target_pairs={{1,0},{5,4},{9,8},{13,12},{17,16},{21,20},{25,24},{29,28},{33,32},... | collective-permute-start | bytes 294920 | tf_op jit(solution)/shard_map/ppermute | solution.py:555
  69.0 1.3 collective-permute-start.7
  70.3 3.2 %shard_map.70 = (bf16[2592,512]{1,0:T(8,128)(2,1)S(1)}, bf16[96,1024]{1,0:T(8,128)(2,1)S(1)}, bf16[96,1024]{1,0:T(8,128)(2,1)S(1)}) custom-call(bf16[96,512]{1,0:T(8,128)(2,1)S(1)} %get-tuple-element.28.top_ref.refs_0_, bf16[96,1024]{1,0:T(8,128)(2,1)S(1)} %collective-permute-done.4.halo_ref.refs_1_, ...), custom_call_target="tpu_custom_call" | custom-call | tf_op jit(solution)/shard_map/pallas_call | solution.py:50
  73.6 0.0 copy-start.4
  73.6 0.7 copy-done.4
  74.2 3.0 %collective-permute-done.7.first_ref = bf16[96,384]{1,0:T(8,128)(2,1)S(1)} collective-permute-done((bf16[96,384]{1,0:T(8,128)(2,1)S(1)}, bf16[96,384]{1,0:T(8,128)(2,1)S(1)}, u32[]{:S(2)}, u32[]{:S(2)}) %collective-permute-start.7) | collective-permute-done | bytes 73760 | tf_op jit(solution)/shard_map/ppermute | solution.py:555
  77.2 0.0 collective-permute-done.10.second_ref
  77.2 1.2 shard_map.71
  78.4 0.0 copy-start.2
  78.4 17.8 %all_to_all.15.parts_ref = bf16[16,128,128]{2,1,0:T(8,128)(2,1)S(1)} all-to-all(bf16[16,128,128]{2,1,0:T(8,128)(2,1)S(1)} %bitcast.9), channel_id=1, replica_groups={{0,4,8,12,128,132,136,140,256,260,264,268,384,388,392,396},{16,20,24,28..., dimensions={0} | all-to-all | bytes 1048576 | tf_op jit(solution)/shard_map/all_to_all | solution.py:604
  96.3 0.0 copy-done.2
  96.3 0.1 shard_map.72
  96.3 0.0 copy-start
  96.3 0.7 copy-done
  97.0 7.8 %all-to-all-start.1 = ((bf16[8,128,128]{2,1,0:T(8,128)(2,1)}), bf16[8,128,128]{2,1,0:T(8,128)(2,1)S(1)}, u32[]{:S(2)}, u32[]{:S(2)}) async-start(bf16[8,128,128]{2,1,0:T(8,128)(2,1)} %copy-done), calls=%async_computation.1 | async-start | bytes 524288 | tf_op jit(solution)/shard_map/all_to_all | solution.py:612
  104.8 0.0 copy-start.3
  104.8 0.9 copy-done.3
  105.8 0.0 copy-start.5
  105.8 0.9 copy-done.5
  106.7 3.7 %shard_map.73 = bf16[96,512]{1,0:T(8,128)(2,1)} custom-call(bf16[96,1280]{1,0:T(8,128)(2,1)S(1)} %copy-done.3, f32[96,2048]{1,0:T(8,128)S(1)} %get-tuple-element.39.slope_ref.refs_1_.refs_4_.refs_2_, bf16[27,16,2048]{2,1,0:T(8,128)(2,1)S(1)} %get-tuple-element.40.mask_ref.refs_2_.refs_5_.refs_3_, ...), custom_call_target="tpu_custom_call" | custom-call | tf_op jit(solution)/shard_map/pallas_call | solution.py:50
  110.4 11.0 %all-to-all-done.1.parts_ref = bf16[8,128,128]{2,1,0:T(8,128)(2,1)S(1)} async-done(((bf16[8,128,128]{2,1,0:T(8,128)(2,1)}), bf16[8,128,128]{2,1,0:T(8,128)(2,1)S(1)}, u32[]{:S(2)}, u32[]{:S(2)}) %all-to-all-start.1) | async-done | bytes 262176 | tf_op jit(solution)/shard_map/all_to_all | solution.py:612
  121.4 0.1 shard_map.74
  121.4 18.4 %all_to_all.16 = bf16[16,128,128]{2,1,0:T(8,128)(2,1)S(1)} all-to-all(bf16[16,128,128]{2,1,0:T(8,128)(2,1)S(1)} %shard_map.74), channel_id=1, replica_groups={{0,4,8,12,128,132,136,140,256,260,264,268,384,388,392,396},{16,20,24,28..., dimensions={0} | all-to-all | bytes 1048576 | tf_op jit(solution)/shard_map/all_to_all | solution.py:615
  139.8 1.8 %shard_map.75 = f32[2592,96]{1,0:T(8,128)} custom-call(bf16[2048,128]{1,0:T(8,128)(2,1)S(1)} %bitcast.7), custom_call_target="tpu_custom_call" | custom-call | tf_op jit(solution)/shard_map/pallas_call | solution.py:50
Async XLA Ops:
  2.3 12.8 %collective-permute-start = (bf16[112,384]{1,0:T(8,128)(2,1)S(1)}, bf16[112,384]{1,0:T(8,128)(2,1)S(1)}, u32[]{:S(2)}, u32[]{:S(2)}) collective-permute-start(bf16[112,384]{1,0:T(8,128)(2,1)S(1)} %get-tuple-element.29), channel_id=1, source_target_pairs={{0,32},{1,33},{2,34},{3,35},{4,36},{5,37},{6,38},{7,39},{8,40},{9,... | collective-permute-start | bytes 258056 | tf_op jit(solution)/shard_map/ppermute | solution.py:530
  11.9 16.9 %collective-permute-start.1 = (bf16[112,384]{1,0:T(8,128)(2,1)S(1)}, bf16[112,384]{1,0:T(8,128)(2,1)S(1)}, u32[]{:S(2)}, u32[]{:S(2)}) collective-permute-start(bf16[112,384]{1,0:T(8,128)(2,1)S(1)} %get-tuple-element.30), channel_id=1, source_target_pairs={{32,0},{33,1},{34,2},{35,3},{36,4},{37,5},{38,6},{39,7},{40,8},{41... | collective-permute-start | bytes 258056 | tf_op jit(solution)/shard_map/ppermute | solution.py:531
  13.2 1.1 copy-start.1
  29.2 5.2 %collective-permute-start.2 = (bf16[112,1024]{1,0:T(8,128)(2,1)S(1)}, bf16[112,1024]{1,0:T(8,128)(2,1)S(1)}, u32[]{:S(2)}, u32[]{:S(2)}) collective-permute-start(bf16[112,1024]{1,0:T(8,128)(2,1)S(1)} %get-tuple-element.36), channel_id=1, source_target_pairs={{0,4},{1,5},{2,6},{3,7},{4,8},{5,9},{6,10},{7,11},{8,12},{9,13},{1... | collective-permute-start | bytes 688136 | tf_op jit(solution)/shard_map/ppermute | solution.py:536
  31.5 7.3 %collective-permute-start.3 = (bf16[112,1024]{1,0:T(8,128)(2,1)S(1)}, bf16[112,1024]{1,0:T(8,128)(2,1)S(1)}, u32[]{:S(2)}, u32[]{:S(2)}) collective-permute-start(bf16[112,1024]{1,0:T(8,128)(2,1)S(1)} %get-tuple-element.37), channel_id=1, source_target_pairs={{4,0},{5,1},{6,2},{7,3},{8,4},{9,5},{10,6},{11,7},{12,8},{13,9},{1... | collective-permute-start | bytes 688136 | tf_op jit(solution)/shard_map/ppermute | solution.py:537
  39.0 11.5 %collective-permute-start.4 = (bf16[96,1024]{1,0:T(8,128)(2,1)S(1)}, bf16[96,1024]{1,0:T(8,128)(2,1)S(1)}, u32[]{:S(2)}, u32[]{:S(2)}) collective-permute-start(bf16[96,1024]{1,0:T(8,128)(2,1)S(1)} %shard_map.62), channel_id=1, source_target_pairs={{0,3},{4,7},{8,11},{12,15},{16,19},{20,23},{24,27},{28,31},{32,35}... | collective-permute-start | bytes 589832 | tf_op jit(solution)/shard_map/ppermute | solution.py:539
  53.5 3.7 %collective-permute-start.5 = (bf16[96,1024]{1,0:T(8,128)(2,1)S(1)}, bf16[96,1024]{1,0:T(8,128)(2,1)S(1)}, u32[]{:S(2)}, u32[]{:S(2)}) collective-permute-start(bf16[96,1024]{1,0:T(8,128)(2,1)S(1)} %shard_map.64.refs_7_.refs_0_), channel_id=1, source_target_pairs={{3,2},{7,6},{11,10},{15,14},{19,18},{23,22},{27,26},{31,30},{35,34... | collective-permute-start | bytes 589832 | tf_op jit(solution)/shard_map/ppermute | solution.py:555
  56.5 3.7 %collective-permute-start.8 = (bf16[96,768]{1,0:T(8,128)(2,1)S(1)}, bf16[96,768]{1,0:T(8,128)(2,1)S(1)}, u32[]{:S(2)}, u32[]{:S(2)}) collective-permute-start(bf16[96,768]{1,0:T(8,128)(2,1)S(1)} %shard_map.67.refs_1_), channel_id=1, source_target_pairs={{3,2},{7,6},{11,10},{15,14},{19,18},{23,22},{27,26},{31,30},{35,34... | collective-permute-start | bytes 442376 | tf_op jit(solution)/shard_map/ppermute | solution.py:555
  59.6 3.8 %collective-permute-start.6 = (bf16[96,640]{1,0:T(8,128)(2,1)S(1)}, bf16[96,640]{1,0:T(8,128)(2,1)S(1)}, u32[]{:S(2)}, u32[]{:S(2)}) collective-permute-start(bf16[96,640]{1,0:T(8,128)(2,1)S(1)} %shard_map.65.refs_5_.refs_2_), channel_id=1, source_target_pairs={{2,1},{6,5},{10,9},{14,13},{18,17},{22,21},{26,25},{30,29},{34,33}... | collective-permute-start | bytes 368648 | tf_op jit(solution)/shard_map/ppermute | solution.py:555
  62.7 2.4 %collective-permute-start.9 = (bf16[96,640]{1,0:T(8,128)(2,1)S(1)}, bf16[96,640]{1,0:T(8,128)(2,1)S(1)}, u32[]{:S(2)}, u32[]{:S(2)}) collective-permute-start(bf16[96,640]{1,0:T(8,128)(2,1)S(1)} %shard_map.68.refs_3_), channel_id=1, source_target_pairs={{2,1},{6,5},{10,9},{14,13},{18,17},{22,21},{26,25},{30,29},{34,33}... | collective-permute-start | bytes 368648 | tf_op jit(solution)/shard_map/ppermute | solution.py:555
  67.5 9.7 %collective-permute-start.10 = (bf16[96,512]{1,0:T(8,128)(2,1)S(1)}, bf16[96,512]{1,0:T(8,128)(2,1)S(1)}, u32[]{:S(2)}, u32[]{:S(2)}) collective-permute-start(bf16[96,512]{1,0:T(8,128)(2,1)S(1)} %shard_map.69.refs_5_), channel_id=1, source_target_pairs={{1,0},{5,4},{9,8},{13,12},{17,16},{21,20},{25,24},{29,28},{33,32},... | collective-permute-start | bytes 294920 | tf_op jit(solution)/shard_map/ppermute | solution.py:555
  69.0 8.2 %collective-permute-start.7 = (bf16[96,384]{1,0:T(8,128)(2,1)S(1)}, bf16[96,384]{1,0:T(8,128)(2,1)S(1)}, u32[]{:S(2)}, u32[]{:S(2)}) collective-permute-start(bf16[96,384]{1,0:T(8,128)(2,1)S(1)} %shard_map.66.refs_5_.refs_4_), channel_id=1, source_target_pairs={{1,0},{5,4},{9,8},{13,12},{17,16},{21,20},{25,24},{29,28},{33,32},... | collective-permute-start | bytes 221192 | tf_op jit(solution)/shard_map/ppermute | solution.py:555
  73.6 0.7 copy-start.4
  78.4 17.9 %copy-start.2 = (bf16[96,1280]{1,0:T(8,128)(2,1)}, bf16[96,1280]{1,0:T(8,128)(2,1)S(1)}, u32[]{:S(2)}) copy-start(bf16[96,1280]{1,0:T(8,128)(2,1)S(1)} %get-tuple-element.50.incoming_ref) | copy-start | bytes 737284
  96.3 0.7 copy-start
  97.0 24.3 %all-to-all-start.1 = ((bf16[8,128,128]{2,1,0:T(8,128)(2,1)}), bf16[8,128,128]{2,1,0:T(8,128)(2,1)S(1)}, u32[]{:S(2)}, u32[]{:S(2)}) async-start(bf16[8,128,128]{2,1,0:T(8,128)(2,1)} %copy-done), calls=%async_computation.1 | async-start | bytes 524288 | tf_op jit(solution)/shard_map/all_to_all | solution.py:612
  104.8 0.9 copy-start.3
  105.8 0.9 copy-start.5

commit v10 on v9

--- a/solution.py
+++ b/solution.py
@@ -72,17 +72,8 @@
 
 def shifted_rows(base_ref, row, tile, low=None, high=None):
     level = lax.broadcasted_iota(jnp.int32, (C, WIDE), 1) % 8
-    if low is None:
-        along = (
-            jnp.where(level > 0, turn(tile, 1), turn(tile, -7)),
-            tile,
-            jnp.where(level < 7, turn(tile, -1), turn(tile, 7)),
-        )
-        for oy in (-1, 0, 1):
-            for n in range(3):
-                base_ref[3 * (oy + 1) + n, :, lane(row)] = turn(along[n], -8 * oy)
-        return
-    for oy, source in ((-1, low), (0, tile), (1, high)):
+    for oy, source in ((-1, low), (0, None), (1, high)):
+        source = tile if source is None else source
         for oz in (-1, 0, 1):
             if oz == 0:
                 moved = turn(source, -8 * oy)

time: 142 us -> 141 us (level)
  Pallas kernels: 33.5 us -> 30.5 us
  waiting for transfers between devices: 32.9 us -> 34.4 us
    pallas_call x17, Pallas kernels: 33.5 us -> 30.5 us  [run(): inner(*[arg if arg.dtype == jnp.int32 else pltpu.with_memory_space_constr...]
  transfers between devices with their start and end apart: 12 -> 12, of which waited for: 5 -> 5; matrix products, arithmetic and copies ran while one was open for 0% -> 0% of each run, Pallas kernels for 17% -> 15%
where the time goes in v10:
time: 141 us; the launch traced here: 140 us
  blocking collectives  36.4 us (26%)
  waiting for transfers between devices  34.4 us (24%)
  starting transfers between devices  32.7 us (23%)
  Pallas kernels  30.5 us (22%)
  local copies, waits for them, and re-layouts  4.32 us (3%)
  between operations  1.56 us (1%)
    pallas_call x17, Pallas kernels, run(): inner(*[arg if arg.dtype == jnp.int32 else pltpu.with_memory_space_constr...  30.5 us
    all_to_all x1, blocking collectives, body(): whole = lax.all_to_all(copies, 'space', 0, 0, axis_index_groups=near)  18.4 us
    all_to_all x1, blocking collectives, body(): lax.all_to_all(terms.reshape(NEAR, CHUNK, WIDE), 'space', 0, 0, axis_inde...  18 us
    ppermute x1, waiting for transfers between devices, body(): after = lax.ppermute(down, both, between(-1, 0, same))  13.7 us
    all_to_all x1, waiting for transfers between devices, body(): parts = lax.all_to_all(copies, 'space', 0, 0, axis_index_groups=far)  11.4 us
    ppermute x1, starting transfers between devices, body(): before = lax.ppermute(up, both, between(1, 0, same))  9.65 us
    all_to_all x1, starting transfers between devices, body(): parts = lax.all_to_all(copies, 'space', 0, 0, axis_index_groups=far)  7.45 us
    ppermute x6, starting transfers between devices, hand_on(): return lax.ppermute(value, both, between(0, 0, [(source, source - 1)]))  5.44 us
  transfers between devices with their start and end apart: 12, of which 5 were waited for; matrix products, arithmetic and copies ran while one was open for 0% of the time, Pallas kernels for 15%

profile of v10, /device:TPU:1, one launch (start us, length us, event | category | flops | bytes accessed | tf_op | source)
XLA Modules:
  0.0 139.9 jit_solution(8985430305288532982)
XLA Ops:
  1.3 1.0 shard_map.59
  2.3 9.6 %collective-permute-start = (bf16[112,384]{1,0:T(8,128)(2,1)S(1)}, bf16[112,384]{1,0:T(8,128)(2,1)S(1)}, u32[]{:S(2)}, u32[]{:S(2)}) collective-permute-start(bf16[112,384]{1,0:T(8,128)(2,1)S(1)} %get-tuple-element.29), channel_id=1, source_target_pairs={{0,32},{1,33},{2,34},{3,35},{4,36},{5,37},{6,38},{7,39},{8,40},{9,... | collective-permute-start | bytes 258056 | tf_op jit(solution)/shard_map/ppermute | solution.py:521
  11.9 1.3 collective-permute-start.1
  13.2 0.0 copy-start.1
  13.2 1.1 copy-done.1
  14.3 0.7 shard_map.60
  15.1 0.0 collective-permute-done.before_ref
  15.1 13.7 %collective-permute-done.1.after_ref = bf16[112,384]{1,0:T(8,128)(2,1)S(1)} collective-permute-done((bf16[112,384]{1,0:T(8,128)(2,1)S(1)}, bf16[112,384]{1,0:T(8,128)(2,1)S(1)}, u32[]{:S(2)}, u32[]{:S(2)}) %collective-permute-start.1) | collective-permute-done | bytes 86048 | tf_op jit(solution)/shard_map/ppermute | solution.py:522
  28.8 0.5 shard_map.61
  29.2 2.3 %collective-permute-start.2 = (bf16[112,1024]{1,0:T(8,128)(2,1)S(1)}, bf16[112,1024]{1,0:T(8,128)(2,1)S(1)}, u32[]{:S(2)}, u32[]{:S(2)}) collective-permute-start(bf16[112,1024]{1,0:T(8,128)(2,1)S(1)} %get-tuple-element.36), channel_id=1, source_target_pairs={{0,4},{1,5},{2,6},{3,7},{4,8},{5,9},{6,10},{7,11},{8,12},{9,13},{1... | collective-permute-start | bytes 688136 | tf_op jit(solution)/shard_map/ppermute | solution.py:527
  31.5 2.1 %collective-permute-start.3 = (bf16[112,1024]{1,0:T(8,128)(2,1)S(1)}, bf16[112,1024]{1,0:T(8,128)(2,1)S(1)}, u32[]{:S(2)}, u32[]{:S(2)}) collective-permute-start(bf16[112,1024]{1,0:T(8,128)(2,1)S(1)} %get-tuple-element.37), channel_id=1, source_target_pairs={{4,0},{5,1},{6,2},{7,3},{8,4},{9,5},{10,6},{11,7},{12,8},{13,9},{1... | collective-permute-start | bytes 688136 | tf_op jit(solution)/shard_map/ppermute | solution.py:528
  33.6 0.9 collective-permute-done.2.left_ref.refs_2_
  34.4 4.4 %collective-permute-done.3.right_ref.refs_3_ = bf16[112,1024]{1,0:T(8,128)(2,1)S(1)} collective-permute-done((bf16[112,1024]{1,0:T(8,128)(2,1)S(1)}, bf16[112,1024]{1,0:T(8,128)(2,1)S(1)}, u32[]{:S(2)}, u32[]{:S(2)}) %collective-permute-start.3) | collective-permute-done | bytes 229408 | tf_op jit(solution)/shard_map/ppermute | solution.py:528
  38.8 0.2 shard_map.62
  39.0 4.5 %collective-permute-start.4 = (bf16[96,1024]{1,0:T(8,128)(2,1)S(1)}, bf16[96,1024]{1,0:T(8,128)(2,1)S(1)}, u32[]{:S(2)}, u32[]{:S(2)}) collective-permute-start(bf16[96,1024]{1,0:T(8,128)(2,1)S(1)} %shard_map.62), channel_id=1, source_target_pairs={{0,3},{4,7},{8,11},{12,15},{16,19},{20,23},{24,27},{28,31},{32,35}... | collective-permute-start | bytes 589832 | tf_op jit(solution)/shard_map/ppermute | solution.py:530
  43.6 7.0 %shard_map.63 = (f32[96,2048]{1,0:T(8,128)S(1)}, bf16[27,16,2048]{2,1,0:T(8,128)(2,1)S(1)}, bf16[96,1280]{1,0:T(8,128)(2,1)S(1)}) custom-call(bf16[96,512]{1,0:T(8,128)(2,1)S(1)} %get-tuple-element.35.x_ref, s32[1]{0:T(128)S(6)} %copy.6.height_ref, bf16[112,384]{1,0:T(8,128)(2,1)S(1)} %collective-permute-done.before_ref, ...), custom_call_target="tpu_custom_call" | custom-call | tf_op jit(solution)/shard_map/pallas_call | solution.py:50
  50.6 0.0 collective-permute-done.4.halo_ref.refs_1_
  50.6 2.4 %shard_map.64.refs_7_.refs_0_ = bf16[96,1024]{1,0:T(8,128)(2,1)S(1)} custom-call(bf16[96,512]{1,0:T(8,128)(2,1)S(1)} %get-tuple-element.28.top_ref.refs_0_, bf16[96,1024]{1,0:T(8,128)(2,1)S(1)} %collective-permute-done.4.halo_ref.refs_1_, bf16[112,1024]{1,0:T(8,128)(2,1)S(1)} %collective-permute-done.2.left_ref.refs_2_, ...), custom_call_target="tpu_custom_call" | custom-call | tf_op jit(solution)/shard_map/pallas_call | solution.py:50
  53.0 0.7 collective-permute-start.5
  53.7 2.0 %shard_map.67.refs_1_ = bf16[96,768]{1,0:T(8,128)(2,1)S(1)} custom-call(bf16[96,512]{1,0:T(8,128)(2,1)S(1)} %get-tuple-element.28.top_ref.refs_0_, bf16[96,1024]{1,0:T(8,128)(2,1)S(1)} %collective-permute-done.4.halo_ref.refs_1_, bf16[112,1024]{1,0:T(8,128)(2,1)S(1)} %collective-permute-done.2.left_ref.refs_2_, ...), custom_call_target="tpu_custom_call" | custom-call | tf_op jit(solution)/shard_map/pallas_call | solution.py:50
  55.7 0.7 collective-permute-start.8
  56.4 0.0 collective-permute-done.5.refs_0_.refs_6_
  56.4 2.1 %shard_map.65.refs_5_.refs_2_ = bf16[96,640]{1,0:T(8,128)(2,1)S(1)} custom-call(bf16[96,1024]{1,0:T(8,128)(2,1)S(1)} %collective-permute-done.5.refs_0_.refs_6_, f32[96,2048]{1,0:T(8,128)S(1)} %get-tuple-element.39.slope_ref.refs_1_.refs_4_.refs_2_, bf16[27,16,2048]{2,1,0:T(8,128)(2,1)S(1)} %get-tuple-element.40.mask_ref.refs_2_.refs_5_.refs_3_, ...), custom_call_target="tpu_custom_call" | custom-call | tf_op jit(solution)/shard_map/pallas_call | solution.py:50
  58.4 0.7 collective-permute-start.6
  59.1 0.0 collective-permute-done.8.refs_1_.refs_7_
  59.1 2.1 %shard_map.68.refs_3_ = bf16[96,640]{1,0:T(8,128)(2,1)S(1)} custom-call(bf16[96,1024]{1,0:T(8,128)(2,1)S(1)} %collective-permute-done.5.refs_0_.refs_6_, bf16[96,768]{1,0:T(8,128)(2,1)S(1)} %collective-permute-done.8.refs_1_.refs_7_, f32[96,2048]{1,0:T(8,128)S(1)} %get-tuple-element.39.slope_ref.refs_1_.refs_4_.refs_2_, ...), custom_call_target="tpu_custom_call" | custom-call | tf_op jit(solution)/shard_map/pallas_call | solution.py:50
  61.2 0.7 collective-permute-start.9
  61.9 0.0 collective-permute-done.6.refs_0_.refs_8_
  61.9 1.4 %shard_map.66.refs_5_.refs_4_ = bf16[96,384]{1,0:T(8,128)(2,1)S(1)} custom-call(bf16[96,640]{1,0:T(8,128)(2,1)S(1)} %collective-permute-done.6.refs_0_.refs_8_, f32[96,2048]{1,0:T(8,128)S(1)} %get-tuple-element.39.slope_ref.refs_1_.refs_4_.refs_2_, bf16[27,16,2048]{2,1,0:T(8,128)(2,1)S(1)} %get-tuple-element.40.mask_ref.refs_2_.refs_5_.refs_3_, ...), custom_call_target="tpu_custom_call" | custom-call | tf_op jit(solution)/shard_map/pallas_call | solution.py:50
  63.3 0.0 collective-permute-done.9.refs_1_.refs_9_
  63.4 2.1 %shard_map.69.refs_5_ = bf16[96,512]{1,0:T(8,128)(2,1)S(1)} custom-call(bf16[96,640]{1,0:T(8,128)(2,1)S(1)} %collective-permute-done.6.refs_0_.refs_8_, bf16[96,640]{1,0:T(8,128)(2,1)S(1)} %collective-permute-done.9.refs_1_.refs_9_, f32[96,2048]{1,0:T(8,128)S(1)} %get-tuple-element.39.slope_ref.refs_1_.refs_4_.refs_2_, ...), custom_call_target="tpu_custom_call" | custom-call | tf_op jit(solution)/shard_map/pallas_call | solution.py:50
  65.5 1.3 collective-permute-start.10
  66.8 1.5 %collective-permute-start.7 = (bf16[96,384]{1,0:T(8,128)(2,1)S(1)}, bf16[96,384]{1,0:T(8,128)(2,1)S(1)}, u32[]{:S(2)}, u32[]{:S(2)}) collective-permute-start(bf16[96,384]{1,0:T(8,128)(2,1)S(1)} %shard_map.66.refs_5_.refs_4_), channel_id=1, source_target_pairs={{1,0},{5,4},{9,8},{13,12},{17,16},{21,20},{25,24},{29,28},{33,32},... | collective-permute-start | bytes 221192 | tf_op jit(solution)/shard_map/ppermute | solution.py:546
  68.3 2.8 %shard_map.70 = (bf16[2592,512]{1,0:T(8,128)(2,1)S(1)}, bf16[96,1024]{1,0:T(8,128)(2,1)S(1)}, bf16[96,1024]{1,0:T(8,128)(2,1)S(1)}) custom-call(bf16[96,512]{1,0:T(8,128)(2,1)S(1)} %get-tuple-element.28.top_ref.refs_0_, bf16[96,1024]{1,0:T(8,128)(2,1)S(1)} %collective-permute-done.4.halo_ref.refs_1_, ...), custom_call_target="tpu_custom_call" | custom-call | tf_op jit(solution)/shard_map/pallas_call | solution.py:50
  71.0 0.0 copy-start.4
  71.0 0.7 copy-done.4
  71.7 4.0 %collective-permute-done.7.first_ref = bf16[96,384]{1,0:T(8,128)(2,1)S(1)} collective-permute-done((bf16[96,384]{1,0:T(8,128)(2,1)S(1)}, bf16[96,384]{1,0:T(8,128)(2,1)S(1)}, u32[]{:S(2)}, u32[]{:S(2)}) %collective-permute-start.7) | collective-permute-done | bytes 73760 | tf_op jit(solution)/shard_map/ppermute | solution.py:546
  75.7 0.0 collective-permute-done.10.second_ref
  75.7 1.2 shard_map.71
  76.8 0.0 copy-start.2
  76.9 18.0 %all_to_all.15.parts_ref = bf16[16,128,128]{2,1,0:T(8,128)(2,1)S(1)} all-to-all(bf16[16,128,128]{2,1,0:T(8,128)(2,1)S(1)} %bitcast.9), channel_id=1, replica_groups={{0,4,8,12,128,132,136,140,256,260,264,268,384,388,392,396},{16,20,24,28..., dimensions={0} | all-to-all | bytes 1048576 | tf_op jit(solution)/shard_map/all_to_all | solution.py:595
  94.9 0.0 copy-done.2
  94.9 0.1 shard_map.72
  95.0 0.0 copy-start
  95.0 0.7 copy-done
  95.7 7.4 %all-to-all-start.1 = ((bf16[8,128,128]{2,1,0:T(8,128)(2,1)}), bf16[8,128,128]{2,1,0:T(8,128)(2,1)S(1)}, u32[]{:S(2)}, u32[]{:S(2)}) async-start(bf16[8,128,128]{2,1,0:T(8,128)(2,1)} %copy-done), calls=%async_computation.1 | async-start | bytes 524288 | tf_op jit(solution)/shard_map/all_to_all | solution.py:603
  103.1 0.0 copy-start.3
  103.1 0.9 copy-done.3
  104.1 0.0 copy-start.5
  104.1 0.9 copy-done.5
  105.0 3.2 %shard_map.73 = bf16[96,512]{1,0:T(8,128)(2,1)} custom-call(bf16[96,1280]{1,0:T(8,128)(2,1)S(1)} %copy-done.3, f32[96,2048]{1,0:T(8,128)S(1)} %get-tuple-element.39.slope_ref.refs_1_.refs_4_.refs_2_, bf16[27,16,2048]{2,1,0:T(8,128)(2,1)S(1)} %get-tuple-element.40.mask_ref.refs_2_.refs_5_.refs_3_, ...), custom_call_target="tpu_custom_call" | custom-call | tf_op jit(solution)/shard_map/pallas_call | solution.py:50
  108.3 11.4 %all-to-all-done.1.parts_ref = bf16[8,128,128]{2,1,0:T(8,128)(2,1)S(1)} async-done(((bf16[8,128,128]{2,1,0:T(8,128)(2,1)}), bf16[8,128,128]{2,1,0:T(8,128)(2,1)S(1)}, u32[]{:S(2)}, u32[]{:S(2)}) %all-to-all-start.1) | async-done | bytes 262176 | tf_op jit(solution)/shard_map/all_to_all | solution.py:603
  119.7 0.1 shard_map.74
  119.8 18.4 %all_to_all.16 = bf16[16,128,128]{2,1,0:T(8,128)(2,1)S(1)} all-to-all(bf16[16,128,128]{2,1,0:T(8,128)(2,1)S(1)} %shard_map.74), channel_id=1, replica_groups={{0,4,8,12,128,132,136,140,256,260,264,268,384,388,392,396},{16,20,24,28..., dimensions={0} | all-to-all | bytes 1048576 | tf_op jit(solution)/shard_map/all_to_all | solution.py:606
  138.2 1.8 %shard_map.75 = f32[2592,96]{1,0:T(8,128)} custom-call(bf16[2048,128]{1,0:T(8,128)(2,1)S(1)} %bitcast.7), custom_call_target="tpu_custom_call" | custom-call | tf_op jit(solution)/shard_map/pallas_call | solution.py:50
Async XLA Ops:
  2.3 12.8 %collective-permute-start = (bf16[112,384]{1,0:T(8,128)(2,1)S(1)}, bf16[112,384]{1,0:T(8,128)(2,1)S(1)}, u32[]{:S(2)}, u32[]{:S(2)}) collective-permute-start(bf16[112,384]{1,0:T(8,128)(2,1)S(1)} %get-tuple-element.29), channel_id=1, source_target_pairs={{0,32},{1,33},{2,34},{3,35},{4,36},{5,37},{6,38},{7,39},{8,40},{9,... | collective-permute-start | bytes 258056 | tf_op jit(solution)/shard_map/ppermute | solution.py:521
  11.9 16.9 %collective-permute-start.1 = (bf16[112,384]{1,0:T(8,128)(2,1)S(1)}, bf16[112,384]{1,0:T(8,128)(2,1)S(1)}, u32[]{:S(2)}, u32[]{:S(2)}) collective-permute-start(bf16[112,384]{1,0:T(8,128)(2,1)S(1)} %get-tuple-element.30), channel_id=1, source_target_pairs={{32,0},{33,1},{34,2},{35,3},{36,4},{37,5},{38,6},{39,7},{40,8},{41... | collective-permute-start | bytes 258056 | tf_op jit(solution)/shard_map/ppermute | solution.py:522
  13.2 1.1 copy-start.1
  29.2 5.2 %collective-permute-start.2 = (bf16[112,1024]{1,0:T(8,128)(2,1)S(1)}, bf16[112,1024]{1,0:T(8,128)(2,1)S(1)}, u32[]{:S(2)}, u32[]{:S(2)}) collective-permute-start(bf16[112,1024]{1,0:T(8,128)(2,1)S(1)} %get-tuple-element.36), channel_id=1, source_target_pairs={{0,4},{1,5},{2,6},{3,7},{4,8},{5,9},{6,10},{7,11},{8,12},{9,13},{1... | collective-permute-start | bytes 688136 | tf_op jit(solution)/shard_map/ppermute | solution.py:527
  31.5 7.3 %collective-permute-start.3 = (bf16[112,1024]{1,0:T(8,128)(2,1)S(1)}, bf16[112,1024]{1,0:T(8,128)(2,1)S(1)}, u32[]{:S(2)}, u32[]{:S(2)}) collective-permute-start(bf16[112,1024]{1,0:T(8,128)(2,1)S(1)} %get-tuple-element.37), channel_id=1, source_target_pairs={{4,0},{5,1},{6,2},{7,3},{8,4},{9,5},{10,6},{11,7},{12,8},{13,9},{1... | collective-permute-start | bytes 688136 | tf_op jit(solution)/shard_map/ppermute | solution.py:528
  39.0 11.5 %collective-permute-start.4 = (bf16[96,1024]{1,0:T(8,128)(2,1)S(1)}, bf16[96,1024]{1,0:T(8,128)(2,1)S(1)}, u32[]{:S(2)}, u32[]{:S(2)}) collective-permute-start(bf16[96,1024]{1,0:T(8,128)(2,1)S(1)} %shard_map.62), channel_id=1, source_target_pairs={{0,3},{4,7},{8,11},{12,15},{16,19},{20,23},{24,27},{28,31},{32,35}... | collective-permute-start | bytes 589832 | tf_op jit(solution)/shard_map/ppermute | solution.py:530
  53.0 3.4 %collective-permute-start.5 = (bf16[96,1024]{1,0:T(8,128)(2,1)S(1)}, bf16[96,1024]{1,0:T(8,128)(2,1)S(1)}, u32[]{:S(2)}, u32[]{:S(2)}) collective-permute-start(bf16[96,1024]{1,0:T(8,128)(2,1)S(1)} %shard_map.64.refs_7_.refs_0_), channel_id=1, source_target_pairs={{3,2},{7,6},{11,10},{15,14},{19,18},{23,22},{27,26},{31,30},{35,34... | collective-permute-start | bytes 589832 | tf_op jit(solution)/shard_map/ppermute | solution.py:546
  55.7 3.4 %collective-permute-start.8 = (bf16[96,768]{1,0:T(8,128)(2,1)S(1)}, bf16[96,768]{1,0:T(8,128)(2,1)S(1)}, u32[]{:S(2)}, u32[]{:S(2)}) collective-permute-start(bf16[96,768]{1,0:T(8,128)(2,1)S(1)} %shard_map.67.refs_1_), channel_id=1, source_target_pairs={{3,2},{7,6},{11,10},{15,14},{19,18},{23,22},{27,26},{31,30},{35,34... | collective-permute-start | bytes 442376 | tf_op jit(solution)/shard_map/ppermute | solution.py:546
  58.4 3.4 %collective-permute-start.6 = (bf16[96,640]{1,0:T(8,128)(2,1)S(1)}, bf16[96,640]{1,0:T(8,128)(2,1)S(1)}, u32[]{:S(2)}, u32[]{:S(2)}) collective-permute-start(bf16[96,640]{1,0:T(8,128)(2,1)S(1)} %shard_map.65.refs_5_.refs_2_), channel_id=1, source_target_pairs={{2,1},{6,5},{10,9},{14,13},{18,17},{22,21},{26,25},{30,29},{34,33}... | collective-permute-start | bytes 368648 | tf_op jit(solution)/shard_map/ppermute | solution.py:546
  61.2 2.1 %collective-permute-start.9 = (bf16[96,640]{1,0:T(8,128)(2,1)S(1)}, bf16[96,640]{1,0:T(8,128)(2,1)S(1)}, u32[]{:S(2)}, u32[]{:S(2)}) collective-permute-start(bf16[96,640]{1,0:T(8,128)(2,1)S(1)} %shard_map.68.refs_3_), channel_id=1, source_target_pairs={{2,1},{6,5},{10,9},{14,13},{18,17},{22,21},{26,25},{30,29},{34,33}... | collective-permute-start | bytes 368648 | tf_op jit(solution)/shard_map/ppermute | solution.py:546
  65.5 10.2 %collective-permute-start.10 = (bf16[96,512]{1,0:T(8,128)(2,1)S(1)}, bf16[96,512]{1,0:T(8,128)(2,1)S(1)}, u32[]{:S(2)}, u32[]{:S(2)}) collective-permute-start(bf16[96,512]{1,0:T(8,128)(2,1)S(1)} %shard_map.69.refs_5_), channel_id=1, source_target_pairs={{1,0},{5,4},{9,8},{13,12},{17,16},{21,20},{25,24},{29,28},{33,32},... | collective-permute-start | bytes 294920 | tf_op jit(solution)/shard_map/ppermute | solution.py:546
  66.8 8.9 %collective-permute-start.7 = (bf16[96,384]{1,0:T(8,128)(2,1)S(1)}, bf16[96,384]{1,0:T(8,128)(2,1)S(1)}, u32[]{:S(2)}, u32[]{:S(2)}) collective-permute-start(bf16[96,384]{1,0:T(8,128)(2,1)S(1)} %shard_map.66.refs_5_.refs_4_), channel_id=1, source_target_pairs={{1,0},{5,4},{9,8},{13,12},{17,16},{21,20},{25,24},{29,28},{33,32},... | collective-permute-start | bytes 221192 | tf_op jit(solution)/shard_map/ppermute | solution.py:546
  71.0 0.7 copy-start.4
  76.8 18.1 %copy-start.2 = (bf16[96,1280]{1,0:T(8,128)(2,1)}, bf16[96,1280]{1,0:T(8,128)(2,1)S(1)}, u32[]{:S(2)}) copy-start(bf16[96,1280]{1,0:T(8,128)(2,1)S(1)} %get-tuple-element.50.incoming_ref) | copy-start | bytes 737284
  95.0 0.7 copy-start
  95.7 24.0 %all-to-all-start.1 = ((bf16[8,128,128]{2,1,0:T(8,128)(2,1)}), bf16[8,128,128]{2,1,0:T(8,128)(2,1)S(1)}, u32[]{:S(2)}, u32[]{:S(2)}) async-start(bf16[8,128,128]{2,1,0:T(8,128)(2,1)} %copy-done), calls=%async_computation.1 | async-start | bytes 524288 | tf_op jit(solution)/shard_map/all_to_all | solution.py:603
  103.1 0.9 copy-start.3
  104.1 0.9 copy-start.5

commit v11 on v10

--- a/solution.py
+++ b/solution.py
@@ -277,12 +277,9 @@
                     for row in rows:
                         mask_ref[tap, :, lane(row)] = keep
 
-    def forward(pair, carry):
-        make_cols(cols_ref, base_ref, mask_ref, 2 * pair + 1, 2 * pair)
-        pre_ref[:, lane(2 * pair, 2)] = product(fwd_ref[...], cols_ref[...])
-        return carry
-
-    lax.fori_loop(0, 8, forward, 0)
+    for pair in range(8):
+        make_cols(cols_ref, base_ref, mask_ref, 2 * pair + 1, 2 * pair, 2 * pair)
+    pre_ref[...] = product(fwd_ref[...], cols_ref[...])
     for row in range(16):
         pre = pre_ref[:, lane(row)]
         sigma = 1.0 / (1.0 + jnp.exp(-pre))
@@ -311,15 +308,12 @@
         ).astype(BF16)
         shifted_rows(base_ref, row, grad)
 
-    def backward(pair, carry):
-        make_cols(cols_ref, base_ref, mask_ref, 2 * pair + 1, 2 * pair + first)
-        total = incoming_ref[:, lane(2 * pair + 1, 2)].astype(F32) + product(
-            bwd_ref[...], cols_ref[...]
-        )
-        store(pair, total.astype(BF16))
-        return carry
-
-    lax.fori_loop(0, (count - 2) // 2, backward, 0)
+    for pair in range((count - 2) // 2):
+        make_cols(cols_ref, base_ref, mask_ref, 2 * pair + 1, 2 * pair + first, 2 * pair)
+    rows = lane(1, count - 2)
+    total = incoming_ref[:, rows].astype(F32) + product(bwd_ref[...], cols_ref[...])
+    for pair in range((count - 2) // 2):
+        store(pair, total[:, 2 * pair * WIDE : 2 * (pair + 1) * WIDE].astype(BF16))
 
 
 def spread(packed_ref, width, row):
@@ -530,15 +524,16 @@
     halo = lax.ppermute(halo, both, between(0, 0, [(0, SECTIONS - 1)]))
 
     core = ((C, 8 * WIDE), BF16)
-    cols = ((DEEP, 2 * WIDE), BF16)
     slope, mask, x_rows = call(
         forward_kernel,
         [((C, 16 * WIDE), F32), ((TAPS, 16, 16 * WIDE), BF16), ((C, 10 * WIDE), BF16)],
-        [((9, C, 18 * WIDE), BF16), cols, ((8, 18 * WIDE), F32), ((C, 16 * WIDE), F32)],
+        [((9, C, 18 * WIDE), BF16), ((DEEP, 16 * WIDE), BF16), ((8, 18 * WIDE), F32),
+         ((C, 16 * WIDE), F32)],
     )(x, brick_height, before, after, left, right, fwd)
     def scratch(count):
         return [
-            ((9, C, (count + 2) * WIDE), BF16), cols, ((C, (count + 2) * WIDE), BF16),
+            ((9, C, (count + 2) * WIDE), BF16), ((DEEP, count * WIDE), BF16),
+            ((C, (count + 2) * WIDE), BF16),
             ((C, count * WIDE), BF16),
         ]
 
@@ -597,7 +592,10 @@
     )
     parts, out = lax.optimization_barrier((parts, out))
     (out,) = call(
-        last_kernel, [((C, CELLS), BF16)], [((9, C, 10 * WIDE), BF16), cols], leave=(0,)
+        last_kernel,
+        [((C, CELLS), BF16)],
+        [((9, C, 10 * WIDE), BF16), ((DEEP, 8 * WIDE), BF16)],
+        leave=(0,),
     )(incoming, slope, mask, bwd, out)
     (copies,) = call(sum_kernel, [((FAR, CHUNK, WIDE), BF16)])(parts)
     parts = lax.all_to_all(copies, "space", 0, 0, axis_index_groups=far)

time: 141 us -> 138 us (0.979)
  Pallas kernels: 30.5 us -> 22.6 us
  waiting for transfers between devices: 34.4 us -> 38.6 us
    pallas_call x17, Pallas kernels: 30.5 us -> 22.6 us  [run(): inner(*[arg if arg.dtype == jnp.int32 else pltpu.with_memory_space_constr...]
    ppermute x6, waiting for transfers between devices: 3.99 us -> 7.12 us  [hand_on(): return lax.ppermute(value, both, between(0, 0, [(source, source - 1)]))]
  transfers between devices with their start and end apart: 12 -> 12, of which waited for: 5 -> 5; matrix products, arithmetic and copies ran while one was open for 0% -> 0% of each run, Pallas kernels for 15% -> 11%
where the time goes in v11:
time: 138 us; the launch traced here: 137 us
  waiting for transfers between devices  38.6 us (28%)
  blocking collectives  37 us (27%)
  starting transfers between devices  32.9 us (24%)
  Pallas kernels  22.6 us (16%)
  local copies, waits for them, and re-layouts  4.32 us (3%)
  between operations  1.55 us (1%)
    pallas_call x17, Pallas kernels, run(): inner(*[arg if arg.dtype == jnp.int32 else pltpu.with_memory_space_constr...  22.6 us
    all_to_all x1, blocking collectives, body(): lax.all_to_all(terms.reshape(NEAR, CHUNK, WIDE), 'space', 0, 0, axis_inde...  18.6 us
    all_to_all x1, blocking collectives, body(): whole = lax.all_to_all(copies, 'space', 0, 0, axis_index_groups=near)  18.4 us
    ppermute x1, waiting for transfers between devices, body(): after = lax.ppermute(down, both, between(-1, 0, same))  13.7 us
    all_to_all x1, waiting for transfers between devices, body(): parts = lax.all_to_all(copies, 'space', 0, 0, axis_index_groups=far)  12.6 us
    ppermute x1, starting transfers between devices, body(): before = lax.ppermute(up, both, between(1, 0, same))  9.65 us
    all_to_all x1, starting transfers between devices, body(): parts = lax.all_to_all(copies, 'space', 0, 0, axis_index_groups=far)  7.69 us
    ppermute x6, waiting for transfers between devices, hand_on(): return lax.ppermute(value, both, between(0, 0, [(source, source - 1)]))  7.12 us
  transfers between devices with their start and end apart: 12, of which 5 were waited for; matrix products, arithmetic and copies ran while one was open for 0% of the time, Pallas kernels for 11%

profile of v11, /device:TPU:1, one launch (start us, length us, event | category | flops | bytes accessed | tf_op | source)
XLA Modules:
  0.0 137.1 jit_solution(7929674045640351131)
XLA Ops:
  1.3 1.0 shard_map.59
  2.3 9.6 %collective-permute-start = (bf16[112,384]{1,0:T(8,128)(2,1)S(1)}, bf16[112,384]{1,0:T(8,128)(2,1)S(1)}, u32[]{:S(2)}, u32[]{:S(2)}) collective-permute-start(bf16[112,384]{1,0:T(8,128)(2,1)S(1)} %get-tuple-element.29), channel_id=1, source_target_pairs={{0,32},{1,33},{2,34},{3,35},{4,36},{5,37},{6,38},{7,39},{8,40},{9,... | collective-permute-start | bytes 258056 | tf_op jit(solution)/shard_map/ppermute | solution.py:515
  11.9 1.3 collective-permute-start.1
  13.2 0.0 copy-start.1
  13.2 1.1 copy-done.1
  14.3 0.7 shard_map.60
  15.1 0.0 collective-permute-done.before_ref
  15.1 13.7 %collective-permute-done.1.after_ref = bf16[112,384]{1,0:T(8,128)(2,1)S(1)} collective-permute-done((bf16[112,384]{1,0:T(8,128)(2,1)S(1)}, bf16[112,384]{1,0:T(8,128)(2,1)S(1)}, u32[]{:S(2)}, u32[]{:S(2)}) %collective-permute-start.1) | collective-permute-done | bytes 86048 | tf_op jit(solution)/shard_map/ppermute | solution.py:516
  28.8 0.5 shard_map.61
  29.2 2.3 %collective-permute-start.2 = (bf16[112,1024]{1,0:T(8,128)(2,1)S(1)}, bf16[112,1024]{1,0:T(8,128)(2,1)S(1)}, u32[]{:S(2)}, u32[]{:S(2)}) collective-permute-start(bf16[112,1024]{1,0:T(8,128)(2,1)S(1)} %get-tuple-element.36), channel_id=1, source_target_pairs={{0,4},{1,5},{2,6},{3,7},{4,8},{5,9},{6,10},{7,11},{8,12},{9,13},{1... | collective-permute-start | bytes 688136 | tf_op jit(solution)/shard_map/ppermute | solution.py:521
  31.5 2.1 %collective-permute-start.3 = (bf16[112,1024]{1,0:T(8,128)(2,1)S(1)}, bf16[112,1024]{1,0:T(8,128)(2,1)S(1)}, u32[]{:S(2)}, u32[]{:S(2)}) collective-permute-start(bf16[112,1024]{1,0:T(8,128)(2,1)S(1)} %get-tuple-element.37), channel_id=1, source_target_pairs={{4,0},{5,1},{6,2},{7,3},{8,4},{9,5},{10,6},{11,7},{12,8},{13,9},{1... | collective-permute-start | bytes 688136 | tf_op jit(solution)/shard_map/ppermute | solution.py:522
  33.6 0.9 collective-permute-done.2.left_ref.refs_2_
  34.4 4.4 %collective-permute-done.3.right_ref.refs_3_ = bf16[112,1024]{1,0:T(8,128)(2,1)S(1)} collective-permute-done((bf16[112,1024]{1,0:T(8,128)(2,1)S(1)}, bf16[112,1024]{1,0:T(8,128)(2,1)S(1)}, u32[]{:S(2)}, u32[]{:S(2)}) %collective-permute-start.3) | collective-permute-done | bytes 229408 | tf_op jit(solution)/shard_map/ppermute | solution.py:522
  38.8 0.2 shard_map.62
  39.0 4.5 %collective-permute-start.4 = (bf16[96,1024]{1,0:T(8,128)(2,1)S(1)}, bf16[96,1024]{1,0:T(8,128)(2,1)S(1)}, u32[]{:S(2)}, u32[]{:S(2)}) collective-permute-start(bf16[96,1024]{1,0:T(8,128)(2,1)S(1)} %shard_map.62), channel_id=1, source_target_pairs={{0,3},{4,7},{8,11},{12,15},{16,19},{20,23},{24,27},{28,31},{32,35}... | collective-permute-start | bytes 589832 | tf_op jit(solution)/shard_map/ppermute | solution.py:524
  43.6 4.3 %shard_map.63 = (f32[96,2048]{1,0:T(8,128)S(1)}, bf16[27,16,2048]{2,1,0:T(8,128)(2,1)S(1)}, bf16[96,1280]{1,0:T(8,128)(2,1)S(1)}) custom-call(bf16[96,512]{1,0:T(8,128)(2,1)S(1)} %get-tuple-element.35.x_ref, s32[1]{0:T(128)S(6)} %copy.6.height_ref, bf16[112,384]{1,0:T(8,128)(2,1)S(1)} %collective-permute-done.before_ref, ...), custom_call_target="tpu_custom_call" | custom-call | tf_op jit(solution)/shard_map/pallas_call | solution.py:50
  47.9 0.0 collective-permute-done.4.halo_ref.refs_1_
  47.9 1.6 %shard_map.64.refs_7_.refs_0_ = bf16[96,1024]{1,0:T(8,128)(2,1)S(1)} custom-call(bf16[96,512]{1,0:T(8,128)(2,1)S(1)} %get-tuple-element.28.top_ref.refs_0_, bf16[96,1024]{1,0:T(8,128)(2,1)S(1)} %collective-permute-done.4.halo_ref.refs_1_, bf16[112,1024]{1,0:T(8,128)(2,1)S(1)} %collective-permute-done.2.left_ref.refs_2_, ...), custom_call_target="tpu_custom_call" | custom-call | tf_op jit(solution)/shard_map/pallas_call | solution.py:50
  49.6 0.7 collective-permute-start.5
  50.3 1.3 shard_map.67.refs_1_
  51.6 0.7 collective-permute-start.8
  52.2 0.0 collective-permute-done.5.refs_0_.refs_6_
  52.2 1.3 shard_map.65.refs_5_.refs_2_
  53.5 0.7 collective-permute-start.6
  54.2 0.0 collective-permute-done.8.refs_1_.refs_7_
  54.2 1.3 shard_map.68.refs_3_
  55.5 0.7 collective-permute-start.9
  56.1 0.0 collective-permute-done.6.refs_0_.refs_8_
  56.1 1.1 shard_map.66.refs_5_.refs_4_
  57.3 0.0 collective-permute-done.9.refs_1_.refs_9_
  57.3 1.4 %shard_map.69.refs_5_ = bf16[96,512]{1,0:T(8,128)(2,1)S(1)} custom-call(bf16[96,640]{1,0:T(8,128)(2,1)S(1)} %collective-permute-done.6.refs_0_.refs_8_, bf16[96,640]{1,0:T(8,128)(2,1)S(1)} %collective-permute-done.9.refs_1_.refs_9_, f32[96,2048]{1,0:T(8,128)S(1)} %get-tuple-element.39.slope_ref.refs_1_.refs_4_.refs_2_, ...), custom_call_target="tpu_custom_call" | custom-call | tf_op jit(solution)/shard_map/pallas_call | solution.py:50
  58.7 1.3 collective-permute-start.10
  60.0 1.5 %collective-permute-start.7 = (bf16[96,384]{1,0:T(8,128)(2,1)S(1)}, bf16[96,384]{1,0:T(8,128)(2,1)S(1)}, u32[]{:S(2)}, u32[]{:S(2)}) collective-permute-start(bf16[96,384]{1,0:T(8,128)(2,1)S(1)} %shard_map.66.refs_5_.refs_4_), channel_id=1, source_target_pairs={{1,0},{5,4},{9,8},{13,12},{17,16},{21,20},{25,24},{29,28},{33,32},... | collective-permute-start | bytes 221192 | tf_op jit(solution)/shard_map/ppermute | solution.py:541
  61.5 2.8 %shard_map.70 = (bf16[2592,512]{1,0:T(8,128)(2,1)S(1)}, bf16[96,1024]{1,0:T(8,128)(2,1)S(1)}, bf16[96,1024]{1,0:T(8,128)(2,1)S(1)}) custom-call(bf16[96,512]{1,0:T(8,128)(2,1)S(1)} %get-tuple-element.28.top_ref.refs_0_, bf16[96,1024]{1,0:T(8,128)(2,1)S(1)} %collective-permute-done.4.halo_ref.refs_1_, ...), custom_call_target="tpu_custom_call" | custom-call | tf_op jit(solution)/shard_map/pallas_call | solution.py:50
  64.3 0.0 copy-start.4
  64.3 0.7 copy-done.4
  64.9 7.1 %collective-permute-done.7.first_ref = bf16[96,384]{1,0:T(8,128)(2,1)S(1)} collective-permute-done((bf16[96,384]{1,0:T(8,128)(2,1)S(1)}, bf16[96,384]{1,0:T(8,128)(2,1)S(1)}, u32[]{:S(2)}, u32[]{:S(2)}) %collective-permute-start.7) | collective-permute-done | bytes 73760 | tf_op jit(solution)/shard_map/ppermute | solution.py:541
  72.0 0.0 collective-permute-done.10.second_ref
  72.0 1.2 shard_map.71
  73.2 0.0 copy-start.2
  73.2 18.6 %all_to_all.15.parts_ref = bf16[16,128,128]{2,1,0:T(8,128)(2,1)S(1)} all-to-all(bf16[16,128,128]{2,1,0:T(8,128)(2,1)S(1)} %bitcast.9), channel_id=1, replica_groups={{0,4,8,12,128,132,136,140,256,260,264,268,384,388,392,396},{16,20,24,28..., dimensions={0} | all-to-all | bytes 1048576 | tf_op jit(solution)/shard_map/all_to_all | solution.py:590
  91.9 0.0 copy-done.2
  91.9 0.1 shard_map.72
  91.9 0.0 copy-start
  91.9 0.7 copy-done
  92.6 7.7 %all-to-all-start.1 = ((bf16[8,128,128]{2,1,0:T(8,128)(2,1)}), bf16[8,128,128]{2,1,0:T(8,128)(2,1)S(1)}, u32[]{:S(2)}, u32[]{:S(2)}) async-start(bf16[8,128,128]{2,1,0:T(8,128)(2,1)} %copy-done), calls=%async_computation.1 | async-start | bytes 524288 | tf_op jit(solution)/shard_map/all_to_all | solution.py:601
  100.3 0.0 copy-start.3
  100.3 0.9 copy-done.3
  101.3 0.0 copy-start.5
  101.3 0.9 copy-done.5
  102.2 2.1 %shard_map.73 = bf16[96,512]{1,0:T(8,128)(2,1)} custom-call(bf16[96,1280]{1,0:T(8,128)(2,1)S(1)} %copy-done.3, f32[96,2048]{1,0:T(8,128)S(1)} %get-tuple-element.39.slope_ref.refs_1_.refs_4_.refs_2_, bf16[27,16,2048]{2,1,0:T(8,128)(2,1)S(1)} %get-tuple-element.40.mask_ref.refs_2_.refs_5_.refs_3_, ...), custom_call_target="tpu_custom_call" | custom-call | tf_op jit(solution)/shard_map/pallas_call | solution.py:50
  104.3 12.6 %all-to-all-done.1.parts_ref = bf16[8,128,128]{2,1,0:T(8,128)(2,1)S(1)} async-done(((bf16[8,128,128]{2,1,0:T(8,128)(2,1)}), bf16[8,128,128]{2,1,0:T(8,128)(2,1)S(1)}, u32[]{:S(2)}, u32[]{:S(2)}) %all-to-all-start.1) | async-done | bytes 262176 | tf_op jit(solution)/shard_map/all_to_all | solution.py:601
  116.9 0.1 shard_map.74
  117.0 18.4 %all_to_all.16 = bf16[16,128,128]{2,1,0:T(8,128)(2,1)S(1)} all-to-all(bf16[16,128,128]{2,1,0:T(8,128)(2,1)S(1)} %shard_map.74), channel_id=1, replica_groups={{0,4,8,12,128,132,136,140,256,260,264,268,384,388,392,396},{16,20,24,28..., dimensions={0} | all-to-all | bytes 1048576 | tf_op jit(solution)/shard_map/all_to_all | solution.py:604
  135.4 1.8 %shard_map.75 = f32[2592,96]{1,0:T(8,128)} custom-call(bf16[2048,128]{1,0:T(8,128)(2,1)S(1)} %bitcast.7), custom_call_target="tpu_custom_call" | custom-call | tf_op jit(solution)/shard_map/pallas_call | solution.py:50
Async XLA Ops:
  2.3 12.8 %collective-permute-start = (bf16[112,384]{1,0:T(8,128)(2,1)S(1)}, bf16[112,384]{1,0:T(8,128)(2,1)S(1)}, u32[]{:S(2)}, u32[]{:S(2)}) collective-permute-start(bf16[112,384]{1,0:T(8,128)(2,1)S(1)} %get-tuple-element.29), channel_id=1, source_target_pairs={{0,32},{1,33},{2,34},{3,35},{4,36},{5,37},{6,38},{7,39},{8,40},{9,... | collective-permute-start | bytes 258056 | tf_op jit(solution)/shard_map/ppermute | solution.py:515
  11.9 16.9 %collective-permute-start.1 = (bf16[112,384]{1,0:T(8,128)(2,1)S(1)}, bf16[112,384]{1,0:T(8,128)(2,1)S(1)}, u32[]{:S(2)}, u32[]{:S(2)}) collective-permute-start(bf16[112,384]{1,0:T(8,128)(2,1)S(1)} %get-tuple-element.30), channel_id=1, source_target_pairs={{32,0},{33,1},{34,2},{35,3},{36,4},{37,5},{38,6},{39,7},{40,8},{41... | collective-permute-start | bytes 258056 | tf_op jit(solution)/shard_map/ppermute | solution.py:516
  13.2 1.1 copy-start.1
  29.2 5.2 %collective-permute-start.2 = (bf16[112,1024]{1,0:T(8,128)(2,1)S(1)}, bf16[112,1024]{1,0:T(8,128)(2,1)S(1)}, u32[]{:S(2)}, u32[]{:S(2)}) collective-permute-start(bf16[112,1024]{1,0:T(8,128)(2,1)S(1)} %get-tuple-element.36), channel_id=1, source_target_pairs={{0,4},{1,5},{2,6},{3,7},{4,8},{5,9},{6,10},{7,11},{8,12},{9,13},{1... | collective-permute-start | bytes 688136 | tf_op jit(solution)/shard_map/ppermute | solution.py:521
  31.5 7.3 %collective-permute-start.3 = (bf16[112,1024]{1,0:T(8,128)(2,1)S(1)}, bf16[112,1024]{1,0:T(8,128)(2,1)S(1)}, u32[]{:S(2)}, u32[]{:S(2)}) collective-permute-start(bf16[112,1024]{1,0:T(8,128)(2,1)S(1)} %get-tuple-element.37), channel_id=1, source_target_pairs={{4,0},{5,1},{6,2},{7,3},{8,4},{9,5},{10,6},{11,7},{12,8},{13,9},{1... | collective-permute-start | bytes 688136 | tf_op jit(solution)/shard_map/ppermute | solution.py:522
  39.0 8.9 %collective-permute-start.4 = (bf16[96,1024]{1,0:T(8,128)(2,1)S(1)}, bf16[96,1024]{1,0:T(8,128)(2,1)S(1)}, u32[]{:S(2)}, u32[]{:S(2)}) collective-permute-start(bf16[96,1024]{1,0:T(8,128)(2,1)S(1)} %shard_map.62), channel_id=1, source_target_pairs={{0,3},{4,7},{8,11},{12,15},{16,19},{20,23},{24,27},{28,31},{32,35}... | collective-permute-start | bytes 589832 | tf_op jit(solution)/shard_map/ppermute | solution.py:524
  49.6 2.7 %collective-permute-start.5 = (bf16[96,1024]{1,0:T(8,128)(2,1)S(1)}, bf16[96,1024]{1,0:T(8,128)(2,1)S(1)}, u32[]{:S(2)}, u32[]{:S(2)}) collective-permute-start(bf16[96,1024]{1,0:T(8,128)(2,1)S(1)} %shard_map.64.refs_7_.refs_0_), channel_id=1, source_target_pairs={{3,2},{7,6},{11,10},{15,14},{19,18},{23,22},{27,26},{31,30},{35,34... | collective-permute-start | bytes 589832 | tf_op jit(solution)/shard_map/ppermute | solution.py:541
  51.6 2.6 %collective-permute-start.8 = (bf16[96,768]{1,0:T(8,128)(2,1)S(1)}, bf16[96,768]{1,0:T(8,128)(2,1)S(1)}, u32[]{:S(2)}, u32[]{:S(2)}) collective-permute-start(bf16[96,768]{1,0:T(8,128)(2,1)S(1)} %shard_map.67.refs_1_), channel_id=1, source_target_pairs={{3,2},{7,6},{11,10},{15,14},{19,18},{23,22},{27,26},{31,30},{35,34... | collective-permute-start | bytes 442376 | tf_op jit(solution)/shard_map/ppermute | solution.py:541
  53.5 2.6 %collective-permute-start.6 = (bf16[96,640]{1,0:T(8,128)(2,1)S(1)}, bf16[96,640]{1,0:T(8,128)(2,1)S(1)}, u32[]{:S(2)}, u32[]{:S(2)}) collective-permute-start(bf16[96,640]{1,0:T(8,128)(2,1)S(1)} %shard_map.65.refs_5_.refs_2_), channel_id=1, source_target_pairs={{2,1},{6,5},{10,9},{14,13},{18,17},{22,21},{26,25},{30,29},{34,33}... | collective-permute-start | bytes 368648 | tf_op jit(solution)/shard_map/ppermute | solution.py:541
  55.5 1.8 %collective-permute-start.9 = (bf16[96,640]{1,0:T(8,128)(2,1)S(1)}, bf16[96,640]{1,0:T(8,128)(2,1)S(1)}, u32[]{:S(2)}, u32[]{:S(2)}) collective-permute-start(bf16[96,640]{1,0:T(8,128)(2,1)S(1)} %shard_map.68.refs_3_), channel_id=1, source_target_pairs={{2,1},{6,5},{10,9},{14,13},{18,17},{22,21},{26,25},{30,29},{34,33}... | collective-permute-start | bytes 368648 | tf_op jit(solution)/shard_map/ppermute | solution.py:541
  58.7 13.3 %collective-permute-start.10 = (bf16[96,512]{1,0:T(8,128)(2,1)S(1)}, bf16[96,512]{1,0:T(8,128)(2,1)S(1)}, u32[]{:S(2)}, u32[]{:S(2)}) collective-permute-start(bf16[96,512]{1,0:T(8,128)(2,1)S(1)} %shard_map.69.refs_5_), channel_id=1, source_target_pairs={{1,0},{5,4},{9,8},{13,12},{17,16},{21,20},{25,24},{29,28},{33,32},... | collective-permute-start | bytes 294920 | tf_op jit(solution)/shard_map/ppermute | solution.py:541
  60.0 12.0 %collective-permute-start.7 = (bf16[96,384]{1,0:T(8,128)(2,1)S(1)}, bf16[96,384]{1,0:T(8,128)(2,1)S(1)}, u32[]{:S(2)}, u32[]{:S(2)}) collective-permute-start(bf16[96,384]{1,0:T(8,128)(2,1)S(1)} %shard_map.66.refs_5_.refs_4_), channel_id=1, source_target_pairs={{1,0},{5,4},{9,8},{13,12},{17,16},{21,20},{25,24},{29,28},{33,32},... | collective-permute-start | bytes 221192 | tf_op jit(solution)/shard_map/ppermute | solution.py:541
  64.3 0.7 copy-start.4
  73.2 18.7 %copy-start.2 = (bf16[96,1280]{1,0:T(8,128)(2,1)}, bf16[96,1280]{1,0:T(8,128)(2,1)S(1)}, u32[]{:S(2)}) copy-start(bf16[96,1280]{1,0:T(8,128)(2,1)S(1)} %get-tuple-element.50.incoming_ref) | copy-start | bytes 737284
  91.9 0.7 copy-start
  92.6 24.3 %all-to-all-start.1 = ((bf16[8,128,128]{2,1,0:T(8,128)(2,1)}), bf16[8,128,128]{2,1,0:T(8,128)(2,1)S(1)}, u32[]{:S(2)}, u32[]{:S(2)}) async-start(bf16[8,128,128]{2,1,0:T(8,128)(2,1)} %copy-done), calls=%async_computation.1 | async-start | bytes 524288 | tf_op jit(solution)/shard_map/all_to_all | solution.py:601
  100.3 0.9 copy-start.3
  101.3 0.9 copy-start.5

commit v12 on v11

--- a/solution.py
+++ b/solution.py
@@ -208,14 +208,15 @@
     return side_ref[:C, at : at + 32]
 
 
-def halo_kernel(before_ref, after_ref, left_ref, right_ref, halo_ref):
+def halo_kernel(before_ref, after_ref, left_ref, right_ref, first_ref, second_ref):
     @pl.when(lax.axis_index("pipe") == 0)
     def _():
         for n, row in enumerate(OUTER):
             at = 3 * WIDE + 32 * n
             middle = top_layer(before_ref, after_ref, row)
             sides = left_ref[:C, at : at + 32], right_ref[:C, at : at + 32]
-            halo_ref[:, lane(n)] = join([sides[0], middle, sides[1]])
+            halo_ref = first_ref if n < 4 else second_ref
+            halo_ref[:, lane(n % 4)] = join([sides[0], middle, sides[1]])
 
 
 def forward_kernel(
@@ -297,7 +298,7 @@
             ]
         )
     else:
-        tile = halo_ref[:, lane(OUTER.index(row))]
+        tile = halo_ref[:, lane((row - 1) % 12)]
     return jnp.where(lax.axis_index("pipe") == SECTIONS - 1, tile, jnp.zeros_like(tile))
 
 
@@ -520,8 +521,8 @@
     )
     left = lax.ppermute(to_right, both, between(0, 1, same))
     right = lax.ppermute(to_left, both, between(0, -1, same))
-    (halo,) = call(halo_kernel, [((C, 8 * WIDE), BF16)])(before, after, left, right)
-    halo = lax.ppermute(halo, both, between(0, 0, [(0, SECTIONS - 1)]))
+    halos = call(halo_kernel, [((C, 4 * WIDE), BF16)] * 2)(before, after, left, right)
+    halos = [lax.ppermute(halo, both, between(0, 0, [(0, SECTIONS - 1)])) for halo in halos]
 
     core = ((C, 8 * WIDE), BF16)
     slope, mask, x_rows = call(
@@ -559,7 +560,7 @@
     rest = (slope, mask, bwd)
     tops, moved = parts_of(
         [functools.partial(top_kernel, low, count) for low, count, _ in TOP_PIECES],
-        [(top, halo, left, right) + rest] * 2,
+        [(top, halo, left, right) + rest for halo in halos],
         TOP_PIECES,
         3,
     )
@@ -579,7 +580,7 @@
     x_cols, grad, out = call(
         gather_kernel, [((DEEP, CELLS), BF16), core, core], [((9, C, 10 * WIDE), BF16)]
     )(
-        top, halo, left, right, slope, mask, x_rows,
+        top, halos[0], left, right, slope, mask, x_rows,
         *tops, *middles, lates[0], result, *moved, *moved_on,
     )
     terms, incoming = call(

time: 138 us -> 136 us (0.986)
  waiting for transfers between devices: 38.6 us -> 36.5 us
    ppermute x6, waiting for transfers between devices: 7.12 us -> 4.93 us  [hand_on(): return lax.ppermute(value, both, between(0, 0, [(source, source - 1)]))]
    ppermute x1 -> x2, starting transfers between devices: 4.54 us -> 5.83 us  [body(): lax.ppermute(halo, both, between(0, 0, [(0, SECTIONS - 1)]))]
  transfers between devices with their start and end apart: 12 -> 13, of which waited for: 5 -> 5; matrix products, arithmetic and copies ran while one was open for 0% -> 0% of each run, Pallas kernels for 11% -> 12%
where the time goes in v12:
time: 136 us
  waiting for transfers between devices  36.5 us (27%)
  blocking collectives  36.1 us (27%)
  starting transfers between devices  33.9 us (25%)
  Pallas kernels  22.6 us (17%)
  local copies, waits for them, and re-layouts  5 us (4%)
  between operations  1.57 us (1%)
    pallas_call x17, Pallas kernels, run(): inner(*[arg if arg.dtype == jnp.int32 else pltpu.with_memory_space_constr...  22.6 us
    all_to_all x1, blocking collectives, body(): whole = lax.all_to_all(copies, 'space', 0, 0, axis_index_groups=near)  18.4 us
    all_to_all x1, blocking collectives, body(): lax.all_to_all(terms.reshape(NEAR, CHUNK, WIDE), 'space', 0, 0, axis_inde...  17.7 us
    ppermute x1, waiting for transfers between devices, body(): after = lax.ppermute(down, both, between(-1, 0, same))  13.7 us
    all_to_all x1, waiting for transfers between devices, body(): parts = lax.all_to_all(copies, 'space', 0, 0, axis_index_groups=far)  12.6 us
    ppermute x1, starting transfers between devices, body(): before = lax.ppermute(up, both, between(1, 0, same))  9.65 us
    all_to_all x1, starting transfers between devices, body(): parts = lax.all_to_all(copies, 'space', 0, 0, axis_index_groups=far)  7.39 us
    ppermute x2, starting transfers between devices, body(): lax.ppermute(halo, both, between(0, 0, [(0, SECTIONS - 1)]))  5.83 us
  transfers between devices with their start and end apart: 13, of which 5 were waited for; matrix products, arithmetic and copies ran while one was open for 0% of the time, Pallas kernels for 12%

profile of v12, /device:TPU:1, one launch (start us, length us, event | category | flops | bytes accessed | tf_op | source)
XLA Modules:
  0.0 135.7 jit_solution(6987942548138652929)
XLA Ops:
  1.3 1.0 shard_map.59
  2.3 9.6 %collective-permute-start = (bf16[112,384]{1,0:T(8,128)(2,1)S(1)}, bf16[112,384]{1,0:T(8,128)(2,1)S(1)}, u32[]{:S(2)}, u32[]{:S(2)}) collective-permute-start(bf16[112,384]{1,0:T(8,128)(2,1)S(1)} %get-tuple-element.31), channel_id=1, source_target_pairs={{0,32},{1,33},{2,34},{3,35},{4,36},{5,37},{6,38},{7,39},{8,40},{9,... | collective-permute-start | bytes 258056 | tf_op jit(solution)/shard_map/ppermute | solution.py:516
  11.9 1.3 collective-permute-start.1
  13.2 0.0 copy-start.1
  13.2 1.1 copy-done.1
  14.3 0.7 shard_map.60
  15.1 0.0 collective-permute-done.before_ref
  15.1 13.7 %collective-permute-done.1.after_ref = bf16[112,384]{1,0:T(8,128)(2,1)S(1)} collective-permute-done((bf16[112,384]{1,0:T(8,128)(2,1)S(1)}, bf16[112,384]{1,0:T(8,128)(2,1)S(1)}, u32[]{:S(2)}, u32[]{:S(2)}) %collective-permute-start.1) | collective-permute-done | bytes 86048 | tf_op jit(solution)/shard_map/ppermute | solution.py:517
  28.8 0.5 shard_map.61
  29.2 2.3 %collective-permute-start.2 = (bf16[112,1024]{1,0:T(8,128)(2,1)S(1)}, bf16[112,1024]{1,0:T(8,128)(2,1)S(1)}, u32[]{:S(2)}, u32[]{:S(2)}) collective-permute-start(bf16[112,1024]{1,0:T(8,128)(2,1)S(1)} %get-tuple-element.38), channel_id=1, source_target_pairs={{0,4},{1,5},{2,6},{3,7},{4,8},{5,9},{6,10},{7,11},{8,12},{9,13},{1... | collective-permute-start | bytes 688136 | tf_op jit(solution)/shard_map/ppermute | solution.py:522
  31.5 2.1 %collective-permute-start.3 = (bf16[112,1024]{1,0:T(8,128)(2,1)S(1)}, bf16[112,1024]{1,0:T(8,128)(2,1)S(1)}, u32[]{:S(2)}, u32[]{:S(2)}) collective-permute-start(bf16[112,1024]{1,0:T(8,128)(2,1)S(1)} %get-tuple-element.39), channel_id=1, source_target_pairs={{4,0},{5,1},{6,2},{7,3},{8,4},{9,5},{10,6},{11,7},{12,8},{13,9},{1... | collective-permute-start | bytes 688136 | tf_op jit(solution)/shard_map/ppermute | solution.py:523
  33.6 0.9 collective-permute-done.2.left_ref.refs_2_
  34.4 4.4 %collective-permute-done.3.right_ref.refs_3_ = bf16[112,1024]{1,0:T(8,128)(2,1)S(1)} collective-permute-done((bf16[112,1024]{1,0:T(8,128)(2,1)S(1)}, bf16[112,1024]{1,0:T(8,128)(2,1)S(1)}, u32[]{:S(2)}, u32[]{:S(2)}) %collective-permute-start.3) | collective-permute-done | bytes 229408 | tf_op jit(solution)/shard_map/ppermute | solution.py:523
  38.8 0.2 shard_map.62
  39.0 4.5 %collective-permute-start.4 = (bf16[96,512]{1,0:T(8,128)(2,1)S(1)}, bf16[96,512]{1,0:T(8,128)(2,1)S(1)}, u32[]{:S(2)}, u32[]{:S(2)}) collective-permute-start(bf16[96,512]{1,0:T(8,128)(2,1)S(1)} %get-tuple-element.40), channel_id=1, source_target_pairs={{0,3},{4,7},{8,11},{12,15},{16,19},{20,23},{24,27},{28,31},{32,35}... | collective-permute-start | bytes 294920 | tf_op jit(solution)/shard_map/ppermute | solution.py:525
  43.6 1.3 collective-permute-start.8
  44.9 4.3 %shard_map.63 = (f32[96,2048]{1,0:T(8,128)S(1)}, bf16[27,16,2048]{2,1,0:T(8,128)(2,1)S(1)}, bf16[96,1280]{1,0:T(8,128)(2,1)S(1)}) custom-call(bf16[96,512]{1,0:T(8,128)(2,1)S(1)} %get-tuple-element.37.x_ref, s32[1]{0:T(128)S(6)} %copy.6.height_ref, bf16[112,384]{1,0:T(8,128)(2,1)S(1)} %collective-permute-done.before_ref, ...), custom_call_target="tpu_custom_call" | custom-call | tf_op jit(solution)/shard_map/pallas_call | solution.py:50
  49.2 0.0 collective-permute-done.4.halo_ref
  49.2 1.6 %shard_map.64.refs_7_.refs_0_ = bf16[96,1024]{1,0:T(8,128)(2,1)S(1)} custom-call(bf16[96,512]{1,0:T(8,128)(2,1)S(1)} %get-tuple-element.30.top_ref.refs_0_, bf16[96,512]{1,0:T(8,128)(2,1)S(1)} %collective-permute-done.4.halo_ref, bf16[112,1024]{1,0:T(8,128)(2,1)S(1)} %collective-permute-done.2.left_ref.refs_2_, ...), custom_call_target="tpu_custom_call" | custom-call | tf_op jit(solution)/shard_map/pallas_call | solution.py:50
  50.9 0.7 collective-permute-start.5
  51.6 0.0 collective-permute-done.8.refs_1_
  51.6 1.3 shard_map.67.refs_1_
  52.9 0.7 collective-permute-start.9
  53.5 0.0 collective-permute-done.5.refs_0_.refs_6_
  53.6 1.3 shard_map.65.refs_5_.refs_2_
  54.8 0.7 collective-permute-start.6
  55.5 0.0 collective-permute-done.9.refs_1_.refs_7_
  55.5 1.2 shard_map.68.refs_3_
  56.8 0.7 collective-permute-start.10
  57.4 0.0 collective-permute-done.6.refs_0_.refs_8_
  57.5 1.1 shard_map.66.refs_5_.refs_4_
  58.6 0.0 collective-permute-done.10.refs_1_.refs_9_
  58.6 1.4 %shard_map.69.refs_5_ = bf16[96,512]{1,0:T(8,128)(2,1)S(1)} custom-call(bf16[96,640]{1,0:T(8,128)(2,1)S(1)} %collective-permute-done.6.refs_0_.refs_8_, bf16[96,640]{1,0:T(8,128)(2,1)S(1)} %collective-permute-done.10.refs_1_.refs_9_, f32[96,2048]{1,0:T(8,128)S(1)} %get-tuple-element.42.slope_ref.refs_1_.refs_4_.refs_2_, ...), custom_call_target="tpu_custom_call" | custom-call | tf_op jit(solution)/shard_map/pallas_call | solution.py:50
  60.0 1.3 collective-permute-start.11
  61.3 1.5 %collective-permute-start.7 = (bf16[96,384]{1,0:T(8,128)(2,1)S(1)}, bf16[96,384]{1,0:T(8,128)(2,1)S(1)}, u32[]{:S(2)}, u32[]{:S(2)}) collective-permute-start(bf16[96,384]{1,0:T(8,128)(2,1)S(1)} %shard_map.66.refs_5_.refs_4_), channel_id=1, source_target_pairs={{1,0},{5,4},{9,8},{13,12},{17,16},{21,20},{25,24},{29,28},{33,32},... | collective-permute-start | bytes 221192 | tf_op jit(solution)/shard_map/ppermute | solution.py:542
  62.8 2.8 %shard_map.70 = (bf16[2592,512]{1,0:T(8,128)(2,1)S(1)}, bf16[96,1024]{1,0:T(8,128)(2,1)S(1)}, bf16[96,1024]{1,0:T(8,128)(2,1)S(1)}) custom-call(bf16[96,512]{1,0:T(8,128)(2,1)S(1)} %get-tuple-element.30.top_ref.refs_0_, bf16[96,512]{1,0:T(8,128)(2,1)S(1)} %collective-permute-done.4.halo_ref, bf16[112,1024]{1,0:T(8,128)(2,1)S(1)} %collective-permute-done.2.left_ref.refs_2_, ...), custom_call_target="tpu_custom_call" | custom-call | tf_op jit(solution)/shard_map/pallas_call | solution.py:50
  65.6 0.0 copy-start.4
  65.6 0.7 copy-done.4
  66.2 4.9 %collective-permute-done.7.first_ref = bf16[96,384]{1,0:T(8,128)(2,1)S(1)} collective-permute-done((bf16[96,384]{1,0:T(8,128)(2,1)S(1)}, bf16[96,384]{1,0:T(8,128)(2,1)S(1)}, u32[]{:S(2)}, u32[]{:S(2)}) %collective-permute-start.7) | collective-permute-done | bytes 73760 | tf_op jit(solution)/shard_map/ppermute | solution.py:542
  71.2 0.0 collective-permute-done.11.second_ref
  71.2 1.2 shard_map.71
  72.3 0.0 copy-start.2
  72.3 0.7 copy-done.2
  73.0 17.7 %all_to_all.15.parts_ref = bf16[16,128,128]{2,1,0:T(8,128)(2,1)S(1)} all-to-all(bf16[16,128,128]{2,1,0:T(8,128)(2,1)S(1)} %bitcast.9), channel_id=1, replica_groups={{0,4,8,12,128,132,136,140,256,260,264,268,384,388,392,396},{16,20,24,28..., dimensions={0} | all-to-all | bytes 1048576 | tf_op jit(solution)/shard_map/all_to_all | solution.py:591
  90.7 0.1 shard_map.72
  90.8 0.0 copy-start
  90.8 0.7 copy-done
  91.5 7.4 %all-to-all-start.1 = ((bf16[8,128,128]{2,1,0:T(8,128)(2,1)}), bf16[8,128,128]{2,1,0:T(8,128)(2,1)S(1)}, u32[]{:S(2)}, u32[]{:S(2)}) async-start(bf16[8,128,128]{2,1,0:T(8,128)(2,1)} %copy-done), calls=%async_computation.1 | async-start | bytes 524288 | tf_op jit(solution)/shard_map/all_to_all | solution.py:602
  98.9 0.0 copy-start.3
  98.9 0.9 copy-done.3
  99.8 0.0 copy-start.5
  99.8 0.9 copy-done.5
  100.8 2.1 %shard_map.73 = bf16[96,512]{1,0:T(8,128)(2,1)} custom-call(bf16[96,1280]{1,0:T(8,128)(2,1)S(1)} %copy-done.3, f32[96,2048]{1,0:T(8,128)S(1)} %get-tuple-element.42.slope_ref.refs_1_.refs_4_.refs_2_, bf16[27,16,2048]{2,1,0:T(8,128)(2,1)S(1)} %get-tuple-element.43.mask_ref.refs_2_.refs_5_.refs_3_, ...), custom_call_target="tpu_custom_call" | custom-call | tf_op jit(solution)/shard_map/pallas_call | solution.py:50
  102.9 12.6 %all-to-all-done.1.parts_ref = bf16[8,128,128]{2,1,0:T(8,128)(2,1)S(1)} async-done(((bf16[8,128,128]{2,1,0:T(8,128)(2,1)}), bf16[8,128,128]{2,1,0:T(8,128)(2,1)S(1)}, u32[]{:S(2)}, u32[]{:S(2)}) %all-to-all-start.1) | async-done | bytes 262176 | tf_op jit(solution)/shard_map/all_to_all | solution.py:602
  115.5 0.1 shard_map.74
  115.5 18.4 %all_to_all.16 = bf16[16,128,128]{2,1,0:T(8,128)(2,1)S(1)} all-to-all(bf16[16,128,128]{2,1,0:T(8,128)(2,1)S(1)} %shard_map.74), channel_id=1, replica_groups={{0,4,8,12,128,132,136,140,256,260,264,268,384,388,392,396},{16,20,24,28..., dimensions={0} | all-to-all | bytes 1048576 | tf_op jit(solution)/shard_map/all_to_all | solution.py:605
  133.9 1.8 %shard_map.75 = f32[2592,96]{1,0:T(8,128)} custom-call(bf16[2048,128]{1,0:T(8,128)(2,1)S(1)} %bitcast.7), custom_call_target="tpu_custom_call" | custom-call | tf_op jit(solution)/shard_map/pallas_call | solution.py:50
Async XLA Ops:
  2.3 12.8 %collective-permute-start = (bf16[112,384]{1,0:T(8,128)(2,1)S(1)}, bf16[112,384]{1,0:T(8,128)(2,1)S(1)}, u32[]{:S(2)}, u32[]{:S(2)}) collective-permute-start(bf16[112,384]{1,0:T(8,128)(2,1)S(1)} %get-tuple-element.31), channel_id=1, source_target_pairs={{0,32},{1,33},{2,34},{3,35},{4,36},{5,37},{6,38},{7,39},{8,40},{9,... | collective-permute-start | bytes 258056 | tf_op jit(solution)/shard_map/ppermute | solution.py:516
  11.9 16.9 %collective-permute-start.1 = (bf16[112,384]{1,0:T(8,128)(2,1)S(1)}, bf16[112,384]{1,0:T(8,128)(2,1)S(1)}, u32[]{:S(2)}, u32[]{:S(2)}) collective-permute-start(bf16[112,384]{1,0:T(8,128)(2,1)S(1)} %get-tuple-element.32), channel_id=1, source_target_pairs={{32,0},{33,1},{34,2},{35,3},{36,4},{37,5},{38,6},{39,7},{40,8},{41... | collective-permute-start | bytes 258056 | tf_op jit(solution)/shard_map/ppermute | solution.py:517
  13.2 1.1 copy-start.1
  29.2 5.2 %collective-permute-start.2 = (bf16[112,1024]{1,0:T(8,128)(2,1)S(1)}, bf16[112,1024]{1,0:T(8,128)(2,1)S(1)}, u32[]{:S(2)}, u32[]{:S(2)}) collective-permute-start(bf16[112,1024]{1,0:T(8,128)(2,1)S(1)} %get-tuple-element.38), channel_id=1, source_target_pairs={{0,4},{1,5},{2,6},{3,7},{4,8},{5,9},{6,10},{7,11},{8,12},{9,13},{1... | collective-permute-start | bytes 688136 | tf_op jit(solution)/shard_map/ppermute | solution.py:522
  31.5 7.3 %collective-permute-start.3 = (bf16[112,1024]{1,0:T(8,128)(2,1)S(1)}, bf16[112,1024]{1,0:T(8,128)(2,1)S(1)}, u32[]{:S(2)}, u32[]{:S(2)}) collective-permute-start(bf16[112,1024]{1,0:T(8,128)(2,1)S(1)} %get-tuple-element.39), channel_id=1, source_target_pairs={{4,0},{5,1},{6,2},{7,3},{8,4},{9,5},{10,6},{11,7},{12,8},{13,9},{1... | collective-permute-start | bytes 688136 | tf_op jit(solution)/shard_map/ppermute | solution.py:523
  39.0 10.2 %collective-permute-start.4 = (bf16[96,512]{1,0:T(8,128)(2,1)S(1)}, bf16[96,512]{1,0:T(8,128)(2,1)S(1)}, u32[]{:S(2)}, u32[]{:S(2)}) collective-permute-start(bf16[96,512]{1,0:T(8,128)(2,1)S(1)} %get-tuple-element.40), channel_id=1, source_target_pairs={{0,3},{4,7},{8,11},{12,15},{16,19},{20,23},{24,27},{28,31},{32,35}... | collective-permute-start | bytes 294920 | tf_op jit(solution)/shard_map/ppermute | solution.py:525
  43.6 8.0 %collective-permute-start.8 = (bf16[96,512]{1,0:T(8,128)(2,1)S(1)}, bf16[96,512]{1,0:T(8,128)(2,1)S(1)}, u32[]{:S(2)}, u32[]{:S(2)}) collective-permute-start(bf16[96,512]{1,0:T(8,128)(2,1)S(1)} %get-tuple-element.45), channel_id=1, source_target_pairs={{0,3},{4,7},{8,11},{12,15},{16,19},{20,23},{24,27},{28,31},{32,35}... | collective-permute-start | bytes 294920 | tf_op jit(solution)/shard_map/ppermute | solution.py:525
  50.9 2.7 %collective-permute-start.5 = (bf16[96,1024]{1,0:T(8,128)(2,1)S(1)}, bf16[96,1024]{1,0:T(8,128)(2,1)S(1)}, u32[]{:S(2)}, u32[]{:S(2)}) collective-permute-start(bf16[96,1024]{1,0:T(8,128)(2,1)S(1)} %shard_map.64.refs_7_.refs_0_), channel_id=1, source_target_pairs={{3,2},{7,6},{11,10},{15,14},{19,18},{23,22},{27,26},{31,30},{35,34... | collective-permute-start | bytes 589832 | tf_op jit(solution)/shard_map/ppermute | solution.py:542
  52.9 2.6 %collective-permute-start.9 = (bf16[96,768]{1,0:T(8,128)(2,1)S(1)}, bf16[96,768]{1,0:T(8,128)(2,1)S(1)}, u32[]{:S(2)}, u32[]{:S(2)}) collective-permute-start(bf16[96,768]{1,0:T(8,128)(2,1)S(1)} %shard_map.67.refs_1_), channel_id=1, source_target_pairs={{3,2},{7,6},{11,10},{15,14},{19,18},{23,22},{27,26},{31,30},{35,34... | collective-permute-start | bytes 442376 | tf_op jit(solution)/shard_map/ppermute | solution.py:542
  54.8 2.6 %collective-permute-start.6 = (bf16[96,640]{1,0:T(8,128)(2,1)S(1)}, bf16[96,640]{1,0:T(8,128)(2,1)S(1)}, u32[]{:S(2)}, u32[]{:S(2)}) collective-permute-start(bf16[96,640]{1,0:T(8,128)(2,1)S(1)} %shard_map.65.refs_5_.refs_2_), channel_id=1, source_target_pairs={{2,1},{6,5},{10,9},{14,13},{18,17},{22,21},{26,25},{30,29},{34,33}... | collective-permute-start | bytes 368648 | tf_op jit(solution)/shard_map/ppermute | solution.py:542
  56.8 1.8 %collective-permute-start.10 = (bf16[96,640]{1,0:T(8,128)(2,1)S(1)}, bf16[96,640]{1,0:T(8,128)(2,1)S(1)}, u32[]{:S(2)}, u32[]{:S(2)}) collective-permute-start(bf16[96,640]{1,0:T(8,128)(2,1)S(1)} %shard_map.68.refs_3_), channel_id=1, source_target_pairs={{2,1},{6,5},{10,9},{14,13},{18,17},{22,21},{26,25},{30,29},{34,33}... | collective-permute-start | bytes 368648 | tf_op jit(solution)/shard_map/ppermute | solution.py:542
  60.0 11.1 %collective-permute-start.11 = (bf16[96,512]{1,0:T(8,128)(2,1)S(1)}, bf16[96,512]{1,0:T(8,128)(2,1)S(1)}, u32[]{:S(2)}, u32[]{:S(2)}) collective-permute-start(bf16[96,512]{1,0:T(8,128)(2,1)S(1)} %shard_map.69.refs_5_), channel_id=1, source_target_pairs={{1,0},{5,4},{9,8},{13,12},{17,16},{21,20},{25,24},{29,28},{33,32},... | collective-permute-start | bytes 294920 | tf_op jit(solution)/shard_map/ppermute | solution.py:542
  61.3 9.8 %collective-permute-start.7 = (bf16[96,384]{1,0:T(8,128)(2,1)S(1)}, bf16[96,384]{1,0:T(8,128)(2,1)S(1)}, u32[]{:S(2)}, u32[]{:S(2)}) collective-permute-start(bf16[96,384]{1,0:T(8,128)(2,1)S(1)} %shard_map.66.refs_5_.refs_4_), channel_id=1, source_target_pairs={{1,0},{5,4},{9,8},{13,12},{17,16},{21,20},{25,24},{29,28},{33,32},... | collective-permute-start | bytes 221192 | tf_op jit(solution)/shard_map/ppermute | solution.py:542
  65.6 0.7 copy-start.4
  72.3 0.7 copy-start.2
  90.8 0.7 copy-start
  91.5 24.0 %all-to-all-start.1 = ((bf16[8,128,128]{2,1,0:T(8,128)(2,1)}), bf16[8,128,128]{2,1,0:T(8,128)(2,1)S(1)}, u32[]{:S(2)}, u32[]{:S(2)}) async-start(bf16[8,128,128]{2,1,0:T(8,128)(2,1)} %copy-done), calls=%async_computation.1 | async-start | bytes 524288 | tf_op jit(solution)/shard_map/all_to_all | solution.py:602
  98.9 0.9 copy-start.3
  99.8 0.9 copy-start.5

commit v13 on v12

--- a/solution.py
+++ b/solution.py
@@ -322,7 +322,7 @@
     return join([spare, packed_ref[:, width * row : width * row + width], spare])
 
 
-TOP_PIECES = (2, 8, WIDE), (10, 6, WIDE)
+TOP_PIECES = (2, 8, 112), (10, 6, 112)
 MIDDLE_PIECES = (3, 6, 96), (9, 6, 96)
 LATE_PIECES = (4, 4, 80), (8, 6, 80)
 
@@ -353,13 +353,13 @@
 
 
 def top_kernel(
-    low, count, top_ref, halo_ref, left_ref, right_ref, slope_ref, mask_ref, bwd_ref,
+    low, count, width, top_ref, halo_ref, left_ref, right_ref, slope_ref, mask_ref, bwd_ref,
     result_ref, *scratch,
 ):
     def row_of(row):
         return top_row(top_ref, halo_ref, left_ref, right_ref, row)
 
-    step_part(row_of, low, count, WIDE, result_ref, slope_ref, mask_ref, bwd_ref, scratch)
+    step_part(row_of, low, count, width, result_ref, slope_ref, mask_ref, bwd_ref, scratch)
 
 
 def middle_kernel(pieces, low, count, width, *refs):
@@ -425,14 +425,14 @@
         grad = incoming_ref[:, lane(row + 1)].astype(F32) * slope_ref[:, lane(row + 4)]
         grads.append(grad_in[:, lane(row)] + grad.astype(BF16))
     grads = join([halves(grads[2 * pair], grads[2 * pair + 1]) for pair in range(4)])
+    whole = lax.dot_general(
+        all_ref[...], grads, (((1,), (1,)), ((), ())), preferred_element_type=F32
+    ).astype(BF16)
     for four in range(7):
         parts = []
         for tap in range(4 * four, 4 * four + 4):
             if tap < TAPS:
-                part = lax.dot_general(
-                    all_ref[C * tap : C * tap + C, :], grads, (((1,), (1,)), ((), ())),
-                    preferred_element_type=F32,
-                ).astype(BF16)
+                part = whole[C * tap : C * tap + C, :]
             else:
                 part = jnp.zeros((C, C), BF16)
             parts.append(part)
@@ -559,7 +559,7 @@
 
     rest = (slope, mask, bwd)
     tops, moved = parts_of(
-        [functools.partial(top_kernel, low, count) for low, count, _ in TOP_PIECES],
+        [functools.partial(top_kernel, *piece) for piece in TOP_PIECES],
         [(top, halo, left, right) + rest for halo in halos],
         TOP_PIECES,
         3,

time: 136 us -> 137 us (level)
  transfers between devices with their start and end apart: 13 -> 13, of which waited for: 5 -> 5; matrix products, arithmetic and copies ran while one was open for 0% -> 0% of each run, Pallas kernels for 12% -> 13%
where the time goes in v13:
time: 137 us; the launch traced here: 136 us
  waiting for transfers between devices  35.8 us (26%)
  blocking collectives  35.7 us (26%)
  starting transfers between devices  34.5 us (25%)
  Pallas kernels  23.4 us (17%)
  local copies, waits for them, and re-layouts  5 us (4%)
  between operations  1.57 us (1%)
    pallas_call x17, Pallas kernels, run(): inner(*[arg if arg.dtype == jnp.int32 else pltpu.with_memory_space_constr...  23.4 us
    all_to_all x1, blocking collectives, body(): whole = lax.all_to_all(copies, 'space', 0, 0, axis_index_groups=near)  18.4 us
    all_to_all x1, blocking collectives, body(): lax.all_to_all(terms.reshape(NEAR, CHUNK, WIDE), 'space', 0, 0, axis_inde...  17.3 us
    ppermute x1, waiting for transfers between devices, body(): after = lax.ppermute(down, both, between(-1, 0, same))  13.7 us
    all_to_all x1, waiting for transfers between devices, body(): parts = lax.all_to_all(copies, 'space', 0, 0, axis_index_groups=far)  12.6 us
    ppermute x1, starting transfers between devices, body(): before = lax.ppermute(up, both, between(1, 0, same))  9.65 us
    all_to_all x1, starting transfers between devices, body(): parts = lax.all_to_all(copies, 'space', 0, 0, axis_index_groups=far)  7.99 us
    ppermute x2, starting transfers between devices, body(): lax.ppermute(halo, both, between(0, 0, [(0, SECTIONS - 1)]))  5.83 us
  transfers between devices with their start and end apart: 13, of which 5 were waited for; matrix products, arithmetic and copies ran while one was open for 0% of the time, Pallas kernels for 13%

profile of v13, /device:TPU:1, one launch (start us, length us, event | category | flops | bytes accessed | tf_op | source)
XLA Modules:
  0.0 136.0 jit_solution(17005213067102719702)
XLA Ops:
  1.3 1.0 shard_map.59
  2.3 9.6 %collective-permute-start = (bf16[112,384]{1,0:T(8,128)(2,1)S(1)}, bf16[112,384]{1,0:T(8,128)(2,1)S(1)}, u32[]{:S(2)}, u32[]{:S(2)}) collective-permute-start(bf16[112,384]{1,0:T(8,128)(2,1)S(1)} %get-tuple-element.31), channel_id=1, source_target_pairs={{0,32},{1,33},{2,34},{3,35},{4,36},{5,37},{6,38},{7,39},{8,40},{9,... | collective-permute-start | bytes 258056 | tf_op jit(solution)/shard_map/ppermute | solution.py:516
  11.9 1.3 collective-permute-start.1
  13.2 0.0 copy-start.1
  13.2 1.1 copy-done.1
  14.3 0.7 shard_map.60
  15.1 0.0 collective-permute-done.before_ref
  15.1 13.7 %collective-permute-done.1.after_ref = bf16[112,384]{1,0:T(8,128)(2,1)S(1)} collective-permute-done((bf16[112,384]{1,0:T(8,128)(2,1)S(1)}, bf16[112,384]{1,0:T(8,128)(2,1)S(1)}, u32[]{:S(2)}, u32[]{:S(2)}) %collective-permute-start.1) | collective-permute-done | bytes 86048 | tf_op jit(solution)/shard_map/ppermute | solution.py:517
  28.8 0.5 shard_map.61
  29.2 2.3 %collective-permute-start.2 = (bf16[112,1024]{1,0:T(8,128)(2,1)S(1)}, bf16[112,1024]{1,0:T(8,128)(2,1)S(1)}, u32[]{:S(2)}, u32[]{:S(2)}) collective-permute-start(bf16[112,1024]{1,0:T(8,128)(2,1)S(1)} %get-tuple-element.38), channel_id=1, source_target_pairs={{0,4},{1,5},{2,6},{3,7},{4,8},{5,9},{6,10},{7,11},{8,12},{9,13},{1... | collective-permute-start | bytes 688136 | tf_op jit(solution)/shard_map/ppermute | solution.py:522
  31.5 2.1 %collective-permute-start.3 = (bf16[112,1024]{1,0:T(8,128)(2,1)S(1)}, bf16[112,1024]{1,0:T(8,128)(2,1)S(1)}, u32[]{:S(2)}, u32[]{:S(2)}) collective-permute-start(bf16[112,1024]{1,0:T(8,128)(2,1)S(1)} %get-tuple-element.39), channel_id=1, source_target_pairs={{4,0},{5,1},{6,2},{7,3},{8,4},{9,5},{10,6},{11,7},{12,8},{13,9},{1... | collective-permute-start | bytes 688136 | tf_op jit(solution)/shard_map/ppermute | solution.py:523
  33.6 0.9 collective-permute-done.2.left_ref.refs_2_
  34.4 4.4 %collective-permute-done.3.right_ref.refs_3_ = bf16[112,1024]{1,0:T(8,128)(2,1)S(1)} collective-permute-done((bf16[112,1024]{1,0:T(8,128)(2,1)S(1)}, bf16[112,1024]{1,0:T(8,128)(2,1)S(1)}, u32[]{:S(2)}, u32[]{:S(2)}) %collective-permute-start.3) | collective-permute-done | bytes 229408 | tf_op jit(solution)/shard_map/ppermute | solution.py:523
  38.8 0.2 shard_map.62
  39.0 4.5 %collective-permute-start.4 = (bf16[96,512]{1,0:T(8,128)(2,1)S(1)}, bf16[96,512]{1,0:T(8,128)(2,1)S(1)}, u32[]{:S(2)}, u32[]{:S(2)}) collective-permute-start(bf16[96,512]{1,0:T(8,128)(2,1)S(1)} %get-tuple-element.40), channel_id=1, source_target_pairs={{0,3},{4,7},{8,11},{12,15},{16,19},{20,23},{24,27},{28,31},{32,35}... | collective-permute-start | bytes 294920 | tf_op jit(solution)/shard_map/ppermute | solution.py:525
  43.6 1.3 collective-permute-start.8
  44.9 4.3 %shard_map.63 = (f32[96,2048]{1,0:T(8,128)S(1)}, bf16[27,16,2048]{2,1,0:T(8,128)(2,1)S(1)}, bf16[96,1280]{1,0:T(8,128)(2,1)S(1)}) custom-call(bf16[96,512]{1,0:T(8,128)(2,1)S(1)} %get-tuple-element.37.x_ref, s32[1]{0:T(128)S(6)} %copy.6.height_ref, bf16[112,384]{1,0:T(8,128)(2,1)S(1)} %collective-permute-done.before_ref, ...), custom_call_target="tpu_custom_call" | custom-call | tf_op jit(solution)/shard_map/pallas_call | solution.py:50
  49.2 0.0 collective-permute-done.4.halo_ref
  49.2 1.7 %shard_map.64.refs_7_.refs_0_ = bf16[96,896]{1,0:T(8,128)(2,1)S(1)} custom-call(bf16[96,512]{1,0:T(8,128)(2,1)S(1)} %get-tuple-element.30.top_ref.refs_0_, bf16[96,512]{1,0:T(8,128)(2,1)S(1)} %collective-permute-done.4.halo_ref, bf16[112,1024]{1,0:T(8,128)(2,1)S(1)} %collective-permute-done.2.left_ref.refs_2_, ...), custom_call_target="tpu_custom_call" | custom-call | tf_op jit(solution)/shard_map/pallas_call | solution.py:50
  50.9 0.7 collective-permute-start.5
  51.6 0.0 collective-permute-done.8.refs_1_
  51.6 1.4 %shard_map.67.refs_1_ = bf16[96,768]{1,0:T(8,128)(2,1)S(1)} custom-call(bf16[96,512]{1,0:T(8,128)(2,1)S(1)} %get-tuple-element.30.top_ref.refs_0_, bf16[96,512]{1,0:T(8,128)(2,1)S(1)} %collective-permute-done.8.refs_1_, bf16[112,1024]{1,0:T(8,128)(2,1)S(1)} %collective-permute-done.2.left_ref.refs_2_, ...), custom_call_target="tpu_custom_call" | custom-call | tf_op jit(solution)/shard_map/pallas_call | solution.py:50
  53.0 0.7 collective-permute-start.9
  53.7 0.0 collective-permute-done.5.refs_0_.refs_6_
  53.7 1.5 %shard_map.65.refs_5_.refs_2_ = bf16[96,640]{1,0:T(8,128)(2,1)S(1)} custom-call(bf16[96,896]{1,0:T(8,128)(2,1)S(1)} %collective-permute-done.5.refs_0_.refs_6_, f32[96,2048]{1,0:T(8,128)S(1)} %get-tuple-element.42.slope_ref.refs_1_.refs_4_.refs_2_, bf16[27,16,2048]{2,1,0:T(8,128)(2,1)S(1)} %get-tuple-element.43.mask_ref.refs_2_.refs_5_.refs_3_, ...), custom_call_target="tpu_custom_call" | custom-call | tf_op jit(solution)/shard_map/pallas_call | solution.py:50
  55.1 0.7 collective-permute-start.6
  55.8 0.0 collective-permute-done.9.refs_1_.refs_7_
  55.8 1.5 %shard_map.68.refs_3_ = bf16[96,640]{1,0:T(8,128)(2,1)S(1)} custom-call(bf16[96,896]{1,0:T(8,128)(2,1)S(1)} %collective-permute-done.5.refs_0_.refs_6_, bf16[96,768]{1,0:T(8,128)(2,1)S(1)} %collective-permute-done.9.refs_1_.refs_7_, f32[96,2048]{1,0:T(8,128)S(1)} %get-tuple-element.42.slope_ref.refs_1_.refs_4_.refs_2_, ...), custom_call_target="tpu_custom_call" | custom-call | tf_op jit(solution)/shard_map/pallas_call | solution.py:50
  57.3 0.7 collective-permute-start.10
  58.0 0.0 collective-permute-done.6.refs_0_.refs_8_
  58.0 1.1 shard_map.66.refs_5_.refs_4_
  59.1 0.0 collective-permute-done.10.refs_1_.refs_9_
  59.1 1.4 %shard_map.69.refs_5_ = bf16[96,512]{1,0:T(8,128)(2,1)S(1)} custom-call(bf16[96,640]{1,0:T(8,128)(2,1)S(1)} %collective-permute-done.6.refs_0_.refs_8_, bf16[96,640]{1,0:T(8,128)(2,1)S(1)} %collective-permute-done.10.refs_1_.refs_9_, f32[96,2048]{1,0:T(8,128)S(1)} %get-tuple-element.42.slope_ref.refs_1_.refs_4_.refs_2_, ...), custom_call_target="tpu_custom_call" | custom-call | tf_op jit(solution)/shard_map/pallas_call | solution.py:50
  60.6 1.3 collective-permute-start.11
  61.9 1.5 %collective-permute-start.7 = (bf16[96,384]{1,0:T(8,128)(2,1)S(1)}, bf16[96,384]{1,0:T(8,128)(2,1)S(1)}, u32[]{:S(2)}, u32[]{:S(2)}) collective-permute-start(bf16[96,384]{1,0:T(8,128)(2,1)S(1)} %shard_map.66.refs_5_.refs_4_), channel_id=1, source_target_pairs={{1,0},{5,4},{9,8},{13,12},{17,16},{21,20},{25,24},{29,28},{33,32},... | collective-permute-start | bytes 221192 | tf_op jit(solution)/shard_map/ppermute | solution.py:542
  63.3 2.9 %shard_map.70 = (bf16[2592,512]{1,0:T(8,128)(2,1)S(1)}, bf16[96,1024]{1,0:T(8,128)(2,1)S(1)}, bf16[96,1024]{1,0:T(8,128)(2,1)S(1)}) custom-call(bf16[96,512]{1,0:T(8,128)(2,1)S(1)} %get-tuple-element.30.top_ref.refs_0_, bf16[96,512]{1,0:T(8,128)(2,1)S(1)} %collective-permute-done.4.halo_ref, bf16[112,1024]{1,0:T(8,128)(2,1)S(1)} %collective-permute-done.2.left_ref.refs_2_, ...), custom_call_target="tpu_custom_call" | custom-call | tf_op jit(solution)/shard_map/pallas_call | solution.py:50
  66.3 0.0 copy-start.4
  66.3 0.7 copy-done.4
  67.0 4.3 %collective-permute-done.7.first_ref = bf16[96,384]{1,0:T(8,128)(2,1)S(1)} collective-permute-done((bf16[96,384]{1,0:T(8,128)(2,1)S(1)}, bf16[96,384]{1,0:T(8,128)(2,1)S(1)}, u32[]{:S(2)}, u32[]{:S(2)}) %collective-permute-start.7) | collective-permute-done | bytes 73760 | tf_op jit(solution)/shard_map/ppermute | solution.py:542
  71.2 0.0 collective-permute-done.11.second_ref
  71.2 1.2 shard_map.71
  72.4 0.0 copy-start.2
  72.4 0.7 copy-done.2
  73.1 17.3 %all_to_all.15.parts_ref = bf16[16,128,128]{2,1,0:T(8,128)(2,1)S(1)} all-to-all(bf16[16,128,128]{2,1,0:T(8,128)(2,1)S(1)} %bitcast.9), channel_id=1, replica_groups={{0,4,8,12,128,132,136,140,256,260,264,268,384,388,392,396},{16,20,24,28..., dimensions={0} | all-to-all | bytes 1048576 | tf_op jit(solution)/shard_map/all_to_all | solution.py:591
  90.4 0.1 shard_map.72
  90.5 0.0 copy-start
  90.5 0.7 copy-done
  91.2 8.0 %all-to-all-start.1 = ((bf16[8,128,128]{2,1,0:T(8,128)(2,1)}), bf16[8,128,128]{2,1,0:T(8,128)(2,1)S(1)}, u32[]{:S(2)}, u32[]{:S(2)}) async-start(bf16[8,128,128]{2,1,0:T(8,128)(2,1)} %copy-done), calls=%async_computation.1 | async-start | bytes 524288 | tf_op jit(solution)/shard_map/all_to_all | solution.py:602
  99.2 0.0 copy-start.3
  99.2 0.9 copy-done.3
  100.1 0.0 copy-start.5
  100.1 0.9 copy-done.5
  101.1 2.1 %shard_map.73 = bf16[96,512]{1,0:T(8,128)(2,1)} custom-call(bf16[96,1280]{1,0:T(8,128)(2,1)S(1)} %copy-done.3, f32[96,2048]{1,0:T(8,128)S(1)} %get-tuple-element.42.slope_ref.refs_1_.refs_4_.refs_2_, bf16[27,16,2048]{2,1,0:T(8,128)(2,1)S(1)} %get-tuple-element.43.mask_ref.refs_2_.refs_5_.refs_3_, ...), custom_call_target="tpu_custom_call" | custom-call | tf_op jit(solution)/shard_map/pallas_call | solution.py:50
  103.2 12.6 %all-to-all-done.1.parts_ref = bf16[8,128,128]{2,1,0:T(8,128)(2,1)S(1)} async-done(((bf16[8,128,128]{2,1,0:T(8,128)(2,1)}), bf16[8,128,128]{2,1,0:T(8,128)(2,1)S(1)}, u32[]{:S(2)}, u32[]{:S(2)}) %all-to-all-start.1) | async-done | bytes 262176 | tf_op jit(solution)/shard_map/all_to_all | solution.py:602
  115.7 0.1 shard_map.74
  115.8 18.4 %all_to_all.16 = bf16[16,128,128]{2,1,0:T(8,128)(2,1)S(1)} all-to-all(bf16[16,128,128]{2,1,0:T(8,128)(2,1)S(1)} %shard_map.74), channel_id=1, replica_groups={{0,4,8,12,128,132,136,140,256,260,264,268,384,388,392,396},{16,20,24,28..., dimensions={0} | all-to-all | bytes 1048576 | tf_op jit(solution)/shard_map/all_to_all | solution.py:605
  134.2 1.8 %shard_map.75 = f32[2592,96]{1,0:T(8,128)} custom-call(bf16[2048,128]{1,0:T(8,128)(2,1)S(1)} %bitcast.7), custom_call_target="tpu_custom_call" | custom-call | tf_op jit(solution)/shard_map/pallas_call | solution.py:50
Async XLA Ops:
  2.3 12.8 %collective-permute-start = (bf16[112,384]{1,0:T(8,128)(2,1)S(1)}, bf16[112,384]{1,0:T(8,128)(2,1)S(1)}, u32[]{:S(2)}, u32[]{:S(2)}) collective-permute-start(bf16[112,384]{1,0:T(8,128)(2,1)S(1)} %get-tuple-element.31), channel_id=1, source_target_pairs={{0,32},{1,33},{2,34},{3,35},{4,36},{5,37},{6,38},{7,39},{8,40},{9,... | collective-permute-start | bytes 258056 | tf_op jit(solution)/shard_map/ppermute | solution.py:516
  11.9 16.9 %collective-permute-start.1 = (bf16[112,384]{1,0:T(8,128)(2,1)S(1)}, bf16[112,384]{1,0:T(8,128)(2,1)S(1)}, u32[]{:S(2)}, u32[]{:S(2)}) collective-permute-start(bf16[112,384]{1,0:T(8,128)(2,1)S(1)} %get-tuple-element.32), channel_id=1, source_target_pairs={{32,0},{33,1},{34,2},{35,3},{36,4},{37,5},{38,6},{39,7},{40,8},{41... | collective-permute-start | bytes 258056 | tf_op jit(solution)/shard_map/ppermute | solution.py:517
  13.2 1.1 copy-start.1
  29.2 5.2 %collective-permute-start.2 = (bf16[112,1024]{1,0:T(8,128)(2,1)S(1)}, bf16[112,1024]{1,0:T(8,128)(2,1)S(1)}, u32[]{:S(2)}, u32[]{:S(2)}) collective-permute-start(bf16[112,1024]{1,0:T(8,128)(2,1)S(1)} %get-tuple-element.38), channel_id=1, source_target_pairs={{0,4},{1,5},{2,6},{3,7},{4,8},{5,9},{6,10},{7,11},{8,12},{9,13},{1... | collective-permute-start | bytes 688136 | tf_op jit(solution)/shard_map/ppermute | solution.py:522
  31.5 7.3 %collective-permute-start.3 = (bf16[112,1024]{1,0:T(8,128)(2,1)S(1)}, bf16[112,1024]{1,0:T(8,128)(2,1)S(1)}, u32[]{:S(2)}, u32[]{:S(2)}) collective-permute-start(bf16[112,1024]{1,0:T(8,128)(2,1)S(1)} %get-tuple-element.39), channel_id=1, source_target_pairs={{4,0},{5,1},{6,2},{7,3},{8,4},{9,5},{10,6},{11,7},{12,8},{13,9},{1... | collective-permute-start | bytes 688136 | tf_op jit(solution)/shard_map/ppermute | solution.py:523
  39.0 10.2 %collective-permute-start.4 = (bf16[96,512]{1,0:T(8,128)(2,1)S(1)}, bf16[96,512]{1,0:T(8,128)(2,1)S(1)}, u32[]{:S(2)}, u32[]{:S(2)}) collective-permute-start(bf16[96,512]{1,0:T(8,128)(2,1)S(1)} %get-tuple-element.40), channel_id=1, source_target_pairs={{0,3},{4,7},{8,11},{12,15},{16,19},{20,23},{24,27},{28,31},{32,35}... | collective-permute-start | bytes 294920 | tf_op jit(solution)/shard_map/ppermute | solution.py:525
  43.6 8.0 %collective-permute-start.8 = (bf16[96,512]{1,0:T(8,128)(2,1)S(1)}, bf16[96,512]{1,0:T(8,128)(2,1)S(1)}, u32[]{:S(2)}, u32[]{:S(2)}) collective-permute-start(bf16[96,512]{1,0:T(8,128)(2,1)S(1)} %get-tuple-element.45), channel_id=1, source_target_pairs={{0,3},{4,7},{8,11},{12,15},{16,19},{20,23},{24,27},{28,31},{32,35}... | collective-permute-start | bytes 294920 | tf_op jit(solution)/shard_map/ppermute | solution.py:525
  50.9 2.7 %collective-permute-start.5 = (bf16[96,896]{1,0:T(8,128)(2,1)S(1)}, bf16[96,896]{1,0:T(8,128)(2,1)S(1)}, u32[]{:S(2)}, u32[]{:S(2)}) collective-permute-start(bf16[96,896]{1,0:T(8,128)(2,1)S(1)} %shard_map.64.refs_7_.refs_0_), channel_id=1, source_target_pairs={{3,2},{7,6},{11,10},{15,14},{19,18},{23,22},{27,26},{31,30},{35,34... | collective-permute-start | bytes 516104 | tf_op jit(solution)/shard_map/ppermute | solution.py:542
  53.0 2.8 %collective-permute-start.9 = (bf16[96,768]{1,0:T(8,128)(2,1)S(1)}, bf16[96,768]{1,0:T(8,128)(2,1)S(1)}, u32[]{:S(2)}, u32[]{:S(2)}) collective-permute-start(bf16[96,768]{1,0:T(8,128)(2,1)S(1)} %shard_map.67.refs_1_), channel_id=1, source_target_pairs={{3,2},{7,6},{11,10},{15,14},{19,18},{23,22},{27,26},{31,30},{35,34... | collective-permute-start | bytes 442376 | tf_op jit(solution)/shard_map/ppermute | solution.py:542
  55.1 2.8 %collective-permute-start.6 = (bf16[96,640]{1,0:T(8,128)(2,1)S(1)}, bf16[96,640]{1,0:T(8,128)(2,1)S(1)}, u32[]{:S(2)}, u32[]{:S(2)}) collective-permute-start(bf16[96,640]{1,0:T(8,128)(2,1)S(1)} %shard_map.65.refs_5_.refs_2_), channel_id=1, source_target_pairs={{2,1},{6,5},{10,9},{14,13},{18,17},{22,21},{26,25},{30,29},{34,33}... | collective-permute-start | bytes 368648 | tf_op jit(solution)/shard_map/ppermute | solution.py:542
  57.3 1.8 %collective-permute-start.10 = (bf16[96,640]{1,0:T(8,128)(2,1)S(1)}, bf16[96,640]{1,0:T(8,128)(2,1)S(1)}, u32[]{:S(2)}, u32[]{:S(2)}) collective-permute-start(bf16[96,640]{1,0:T(8,128)(2,1)S(1)} %shard_map.68.refs_3_), channel_id=1, source_target_pairs={{2,1},{6,5},{10,9},{14,13},{18,17},{22,21},{26,25},{30,29},{34,33}... | collective-permute-start | bytes 368648 | tf_op jit(solution)/shard_map/ppermute | solution.py:542
  60.6 10.7 %collective-permute-start.11 = (bf16[96,512]{1,0:T(8,128)(2,1)S(1)}, bf16[96,512]{1,0:T(8,128)(2,1)S(1)}, u32[]{:S(2)}, u32[]{:S(2)}) collective-permute-start(bf16[96,512]{1,0:T(8,128)(2,1)S(1)} %shard_map.69.refs_5_), channel_id=1, source_target_pairs={{1,0},{5,4},{9,8},{13,12},{17,16},{21,20},{25,24},{29,28},{33,32},... | collective-permute-start | bytes 294920 | tf_op jit(solution)/shard_map/ppermute | solution.py:542
  61.9 9.4 %collective-permute-start.7 = (bf16[96,384]{1,0:T(8,128)(2,1)S(1)}, bf16[96,384]{1,0:T(8,128)(2,1)S(1)}, u32[]{:S(2)}, u32[]{:S(2)}) collective-permute-start(bf16[96,384]{1,0:T(8,128)(2,1)S(1)} %shard_map.66.refs_5_.refs_4_), channel_id=1, source_target_pairs={{1,0},{5,4},{9,8},{13,12},{17,16},{21,20},{25,24},{29,28},{33,32},... | collective-permute-start | bytes 221192 | tf_op jit(solution)/shard_map/ppermute | solution.py:542
  66.3 0.7 copy-start.4
  72.4 0.7 copy-start.2
  90.5 0.7 copy-start
  91.2 24.6 %all-to-all-start.1 = ((bf16[8,128,128]{2,1,0:T(8,128)(2,1)}), bf16[8,128,128]{2,1,0:T(8,128)(2,1)S(1)}, u32[]{:S(2)}, u32[]{:S(2)}) async-start(bf16[8,128,128]{2,1,0:T(8,128)(2,1)} %copy-done), calls=%async_computation.1 | async-start | bytes 524288 | tf_op jit(solution)/shard_map/all_to_all | solution.py:602
  99.2 0.9 copy-start.3
  100.1 0.9 copy-start.5

commit v14 on v13

--- a/solution.py
+++ b/solution.py
@@ -322,7 +322,7 @@
     return join([spare, packed_ref[:, width * row : width * row + width], spare])
 
 
-TOP_PIECES = (2, 8, 112), (10, 6, 112)
+TOP_PIECES = (2, 8, WIDE), (10, 6, WIDE)
 MIDDLE_PIECES = (3, 6, 96), (9, 6, 96)
 LATE_PIECES = (4, 4, 80), (8, 6, 80)
 
@@ -353,13 +353,13 @@
 
 
 def top_kernel(
-    low, count, width, top_ref, halo_ref, left_ref, right_ref, slope_ref, mask_ref, bwd_ref,
+    low, count, top_ref, halo_ref, left_ref, right_ref, slope_ref, mask_ref, bwd_ref,
     result_ref, *scratch,
 ):
     def row_of(row):
         return top_row(top_ref, halo_ref, left_ref, right_ref, row)
 
-    step_part(row_of, low, count, width, result_ref, slope_ref, mask_ref, bwd_ref, scratch)
+    step_part(row_of, low, count, WIDE, result_ref, slope_ref, mask_ref, bwd_ref, scratch)
 
 
 def middle_kernel(pieces, low, count, width, *refs):
@@ -559,7 +559,7 @@
 
     rest = (slope, mask, bwd)
     tops, moved = parts_of(
-        [functools.partial(top_kernel, *piece) for piece in TOP_PIECES],
+        [functools.partial(top_kernel, low, count) for low, count, _ in TOP_PIECES],
         [(top, halo, left, right) + rest for halo in halos],
         TOP_PIECES,
         3,

time: 137 us -> 136 us (level)
  transfers between devices with their start and end apart: 13 -> 13, of which waited for: 5 -> 5; matrix products, arithmetic and copies ran while one was open for 0% -> 0% of each run, Pallas kernels for 13% -> 12%
where the time goes in v14:
time: 136 us
  waiting for transfers between devices  36.5 us (27%)
  blocking collectives  36.1 us (27%)
  starting transfers between devices  33.9 us (25%)
  Pallas kernels  22.6 us (17%)
  local copies, waits for them, and re-layouts  5 us (4%)
  between operations  1.57 us (1%)
    pallas_call x17, Pallas kernels, run(): inner(*[arg if arg.dtype == jnp.int32 else pltpu.with_memory_space_constr...  22.6 us
    all_to_all x1, blocking collectives, body(): whole = lax.all_to_all(copies, 'space', 0, 0, axis_index_groups=near)  18.4 us
    all_to_all x1, blocking collectives, body(): lax.all_to_all(terms.reshape(NEAR, CHUNK, WIDE), 'space', 0, 0, axis_inde...  17.7 us
    ppermute x1, waiting for transfers between devices, body(): after = lax.ppermute(down, both, between(-1, 0, same))  13.7 us
    all_to_all x1, waiting for transfers between devices, body(): parts = lax.all_to_all(copies, 'space', 0, 0, axis_index_groups=far)  12.6 us
    ppermute x1, starting transfers between devices, body(): before = lax.ppermute(up, both, between(1, 0, same))  9.65 us
    all_to_all x1, starting transfers between devices, body(): parts = lax.all_to_all(copies, 'space', 0, 0, axis_index_groups=far)  7.4 us
    ppermute x2, starting transfers between devices, body(): lax.ppermute(halo, both, between(0, 0, [(0, SECTIONS - 1)]))  5.83 us
  transfers between devices with their start and end apart: 13, of which 5 were waited for; matrix products, arithmetic and copies ran while one was open for 0% of the time, Pallas kernels for 12%

profile of v14, /device:TPU:1, one launch (start us, length us, event | category | flops | bytes accessed | tf_op | source)
XLA Modules:
  0.0 135.7 jit_solution(912054362268081246)
XLA Ops:
  1.3 1.0 shard_map.59
  2.3 9.6 %collective-permute-start = (bf16[112,384]{1,0:T(8,128)(2,1)S(1)}, bf16[112,384]{1,0:T(8,128)(2,1)S(1)}, u32[]{:S(2)}, u32[]{:S(2)}) collective-permute-start(bf16[112,384]{1,0:T(8,128)(2,1)S(1)} %get-tuple-element.31), channel_id=1, source_target_pairs={{0,32},{1,33},{2,34},{3,35},{4,36},{5,37},{6,38},{7,39},{8,40},{9,... | collective-permute-start | bytes 258056 | tf_op jit(solution)/shard_map/ppermute | solution.py:516
  11.9 1.3 collective-permute-start.1
  13.2 0.0 copy-start.1
  13.2 1.1 copy-done.1
  14.3 0.7 shard_map.60
  15.1 0.0 collective-permute-done.before_ref
  15.1 13.7 %collective-permute-done.1.after_ref = bf16[112,384]{1,0:T(8,128)(2,1)S(1)} collective-permute-done((bf16[112,384]{1,0:T(8,128)(2,1)S(1)}, bf16[112,384]{1,0:T(8,128)(2,1)S(1)}, u32[]{:S(2)}, u32[]{:S(2)}) %collective-permute-start.1) | collective-permute-done | bytes 86048 | tf_op jit(solution)/shard_map/ppermute | solution.py:517
  28.8 0.5 shard_map.61
  29.2 2.3 %collective-permute-start.2 = (bf16[112,1024]{1,0:T(8,128)(2,1)S(1)}, bf16[112,1024]{1,0:T(8,128)(2,1)S(1)}, u32[]{:S(2)}, u32[]{:S(2)}) collective-permute-start(bf16[112,1024]{1,0:T(8,128)(2,1)S(1)} %get-tuple-element.38), channel_id=1, source_target_pairs={{0,4},{1,5},{2,6},{3,7},{4,8},{5,9},{6,10},{7,11},{8,12},{9,13},{1... | collective-permute-start | bytes 688136 | tf_op jit(solution)/shard_map/ppermute | solution.py:522
  31.5 2.1 %collective-permute-start.3 = (bf16[112,1024]{1,0:T(8,128)(2,1)S(1)}, bf16[112,1024]{1,0:T(8,128)(2,1)S(1)}, u32[]{:S(2)}, u32[]{:S(2)}) collective-permute-start(bf16[112,1024]{1,0:T(8,128)(2,1)S(1)} %get-tuple-element.39), channel_id=1, source_target_pairs={{4,0},{5,1},{6,2},{7,3},{8,4},{9,5},{10,6},{11,7},{12,8},{13,9},{1... | collective-permute-start | bytes 688136 | tf_op jit(solution)/shard_map/ppermute | solution.py:523
  33.6 0.9 collective-permute-done.2.left_ref.refs_2_
  34.4 4.4 %collective-permute-done.3.right_ref.refs_3_ = bf16[112,1024]{1,0:T(8,128)(2,1)S(1)} collective-permute-done((bf16[112,1024]{1,0:T(8,128)(2,1)S(1)}, bf16[112,1024]{1,0:T(8,128)(2,1)S(1)}, u32[]{:S(2)}, u32[]{:S(2)}) %collective-permute-start.3) | collective-permute-done | bytes 229408 | tf_op jit(solution)/shard_map/ppermute | solution.py:523
  38.8 0.2 shard_map.62
  39.0 4.5 %collective-permute-start.4 = (bf16[96,512]{1,0:T(8,128)(2,1)S(1)}, bf16[96,512]{1,0:T(8,128)(2,1)S(1)}, u32[]{:S(2)}, u32[]{:S(2)}) collective-permute-start(bf16[96,512]{1,0:T(8,128)(2,1)S(1)} %get-tuple-element.40), channel_id=1, source_target_pairs={{0,3},{4,7},{8,11},{12,15},{16,19},{20,23},{24,27},{28,31},{32,35}... | collective-permute-start | bytes 294920 | tf_op jit(solution)/shard_map/ppermute | solution.py:525
  43.6 1.3 collective-permute-start.8
  44.9 4.3 %shard_map.63 = (f32[96,2048]{1,0:T(8,128)S(1)}, bf16[27,16,2048]{2,1,0:T(8,128)(2,1)S(1)}, bf16[96,1280]{1,0:T(8,128)(2,1)S(1)}) custom-call(bf16[96,512]{1,0:T(8,128)(2,1)S(1)} %get-tuple-element.37.x_ref, s32[1]{0:T(128)S(6)} %copy.6.height_ref, bf16[112,384]{1,0:T(8,128)(2,1)S(1)} %collective-permute-done.before_ref, ...), custom_call_target="tpu_custom_call" | custom-call | tf_op jit(solution)/shard_map/pallas_call | solution.py:50
  49.2 0.0 collective-permute-done.4.halo_ref
  49.2 1.6 %shard_map.64.refs_7_.refs_0_ = bf16[96,1024]{1,0:T(8,128)(2,1)S(1)} custom-call(bf16[96,512]{1,0:T(8,128)(2,1)S(1)} %get-tuple-element.30.top_ref.refs_0_, bf16[96,512]{1,0:T(8,128)(2,1)S(1)} %collective-permute-done.4.halo_ref, bf16[112,1024]{1,0:T(8,128)(2,1)S(1)} %collective-permute-done.2.left_ref.refs_2_, ...), custom_call_target="tpu_custom_call" | custom-call | tf_op jit(solution)/shard_map/pallas_call | solution.py:50
  50.9 0.7 collective-permute-start.5
  51.6 0.0 collective-permute-done.8.refs_1_
  51.6 1.3 shard_map.67.refs_1_
  52.9 0.7 collective-permute-start.9
  53.5 0.0 collective-permute-done.5.refs_0_.refs_6_
  53.6 1.3 shard_map.65.refs_5_.refs_2_
  54.8 0.7 collective-permute-start.6
  55.5 0.0 collective-permute-done.9.refs_1_.refs_7_
  55.5 1.2 shard_map.68.refs_3_
  56.8 0.7 collective-permute-start.10
  57.4 0.0 collective-permute-done.6.refs_0_.refs_8_
  57.5 1.1 shard_map.66.refs_5_.refs_4_
  58.6 0.0 collective-permute-done.10.refs_1_.refs_9_
  58.6 1.4 %shard_map.69.refs_5_ = bf16[96,512]{1,0:T(8,128)(2,1)S(1)} custom-call(bf16[96,640]{1,0:T(8,128)(2,1)S(1)} %collective-permute-done.6.refs_0_.refs_8_, bf16[96,640]{1,0:T(8,128)(2,1)S(1)} %collective-permute-done.10.refs_1_.refs_9_, f32[96,2048]{1,0:T(8,128)S(1)} %get-tuple-element.42.slope_ref.refs_1_.refs_4_.refs_2_, ...), custom_call_target="tpu_custom_call" | custom-call | tf_op jit(solution)/shard_map/pallas_call | solution.py:50
  60.0 1.3 collective-permute-start.11
  61.3 1.5 %collective-permute-start.7 = (bf16[96,384]{1,0:T(8,128)(2,1)S(1)}, bf16[96,384]{1,0:T(8,128)(2,1)S(1)}, u32[]{:S(2)}, u32[]{:S(2)}) collective-permute-start(bf16[96,384]{1,0:T(8,128)(2,1)S(1)} %shard_map.66.refs_5_.refs_4_), channel_id=1, source_target_pairs={{1,0},{5,4},{9,8},{13,12},{17,16},{21,20},{25,24},{29,28},{33,32},... | collective-permute-start | bytes 221192 | tf_op jit(solution)/shard_map/ppermute | solution.py:542
  62.8 2.8 %shard_map.70 = (bf16[2592,512]{1,0:T(8,128)(2,1)S(1)}, bf16[96,1024]{1,0:T(8,128)(2,1)S(1)}, bf16[96,1024]{1,0:T(8,128)(2,1)S(1)}) custom-call(bf16[96,512]{1,0:T(8,128)(2,1)S(1)} %get-tuple-element.30.top_ref.refs_0_, bf16[96,512]{1,0:T(8,128)(2,1)S(1)} %collective-permute-done.4.halo_ref, bf16[112,1024]{1,0:T(8,128)(2,1)S(1)} %collective-permute-done.2.left_ref.refs_2_, ...), custom_call_target="tpu_custom_call" | custom-call | tf_op jit(solution)/shard_map/pallas_call | solution.py:50
  65.6 0.0 copy-start.4
  65.6 0.7 copy-done.4
  66.2 4.9 %collective-permute-done.7.first_ref = bf16[96,384]{1,0:T(8,128)(2,1)S(1)} collective-permute-done((bf16[96,384]{1,0:T(8,128)(2,1)S(1)}, bf16[96,384]{1,0:T(8,128)(2,1)S(1)}, u32[]{:S(2)}, u32[]{:S(2)}) %collective-permute-start.7) | collective-permute-done | bytes 73760 | tf_op jit(solution)/shard_map/ppermute | solution.py:542
  71.2 0.0 collective-permute-done.11.second_ref
  71.2 1.2 shard_map.71
  72.3 0.0 copy-start.2
  72.3 0.7 copy-done.2
  73.0 17.7 %all_to_all.15.parts_ref = bf16[16,128,128]{2,1,0:T(8,128)(2,1)S(1)} all-to-all(bf16[16,128,128]{2,1,0:T(8,128)(2,1)S(1)} %bitcast.9), channel_id=1, replica_groups={{0,4,8,12,128,132,136,140,256,260,264,268,384,388,392,396},{16,20,24,28..., dimensions={0} | all-to-all | bytes 1048576 | tf_op jit(solution)/shard_map/all_to_all | solution.py:591
  90.7 0.1 shard_map.72
  90.8 0.0 copy-start
  90.8 0.7 copy-done
  91.5 7.4 %all-to-all-start.1 = ((bf16[8,128,128]{2,1,0:T(8,128)(2,1)}), bf16[8,128,128]{2,1,0:T(8,128)(2,1)S(1)}, u32[]{:S(2)}, u32[]{:S(2)}) async-start(bf16[8,128,128]{2,1,0:T(8,128)(2,1)} %copy-done), calls=%async_computation.1 | async-start | bytes 524288 | tf_op jit(solution)/shard_map/all_to_all | solution.py:602
  98.9 0.0 copy-start.3
  98.9 0.9 copy-done.3
  99.8 0.0 copy-start.5
  99.8 0.9 copy-done.5
  100.8 2.1 %shard_map.73 = bf16[96,512]{1,0:T(8,128)(2,1)} custom-call(bf16[96,1280]{1,0:T(8,128)(2,1)S(1)} %copy-done.3, f32[96,2048]{1,0:T(8,128)S(1)} %get-tuple-element.42.slope_ref.refs_1_.refs_4_.refs_2_, bf16[27,16,2048]{2,1,0:T(8,128)(2,1)S(1)} %get-tuple-element.43.mask_ref.refs_2_.refs_5_.refs_3_, ...), custom_call_target="tpu_custom_call" | custom-call | tf_op jit(solution)/shard_map/pallas_call | solution.py:50
  102.9 12.6 %all-to-all-done.1.parts_ref = bf16[8,128,128]{2,1,0:T(8,128)(2,1)S(1)} async-done(((bf16[8,128,128]{2,1,0:T(8,128)(2,1)}), bf16[8,128,128]{2,1,0:T(8,128)(2,1)S(1)}, u32[]{:S(2)}, u32[]{:S(2)}) %all-to-all-start.1) | async-done | bytes 262176 | tf_op jit(solution)/shard_map/all_to_all | solution.py:602
  115.5 0.1 shard_map.74
  115.5 18.4 %all_to_all.16 = bf16[16,128,128]{2,1,0:T(8,128)(2,1)S(1)} all-to-all(bf16[16,128,128]{2,1,0:T(8,128)(2,1)S(1)} %shard_map.74), channel_id=1, replica_groups={{0,4,8,12,128,132,136,140,256,260,264,268,384,388,392,396},{16,20,24,28..., dimensions={0} | all-to-all | bytes 1048576 | tf_op jit(solution)/shard_map/all_to_all | solution.py:605
  133.9 1.8 %shard_map.75 = f32[2592,96]{1,0:T(8,128)} custom-call(bf16[2048,128]{1,0:T(8,128)(2,1)S(1)} %bitcast.7), custom_call_target="tpu_custom_call" | custom-call | tf_op jit(solution)/shard_map/pallas_call | solution.py:50
Async XLA Ops:
  2.3 12.8 %collective-permute-start = (bf16[112,384]{1,0:T(8,128)(2,1)S(1)}, bf16[112,384]{1,0:T(8,128)(2,1)S(1)}, u32[]{:S(2)}, u32[]{:S(2)}) collective-permute-start(bf16[112,384]{1,0:T(8,128)(2,1)S(1)} %get-tuple-element.31), channel_id=1, source_target_pairs={{0,32},{1,33},{2,34},{3,35},{4,36},{5,37},{6,38},{7,39},{8,40},{9,... | collective-permute-start | bytes 258056 | tf_op jit(solution)/shard_map/ppermute | solution.py:516
  11.9 16.9 %collective-permute-start.1 = (bf16[112,384]{1,0:T(8,128)(2,1)S(1)}, bf16[112,384]{1,0:T(8,128)(2,1)S(1)}, u32[]{:S(2)}, u32[]{:S(2)}) collective-permute-start(bf16[112,384]{1,0:T(8,128)(2,1)S(1)} %get-tuple-element.32), channel_id=1, source_target_pairs={{32,0},{33,1},{34,2},{35,3},{36,4},{37,5},{38,6},{39,7},{40,8},{41... | collective-permute-start | bytes 258056 | tf_op jit(solution)/shard_map/ppermute | solution.py:517
  13.2 1.1 copy-start.1
  29.2 5.2 %collective-permute-start.2 = (bf16[112,1024]{1,0:T(8,128)(2,1)S(1)}, bf16[112,1024]{1,0:T(8,128)(2,1)S(1)}, u32[]{:S(2)}, u32[]{:S(2)}) collective-permute-start(bf16[112,1024]{1,0:T(8,128)(2,1)S(1)} %get-tuple-element.38), channel_id=1, source_target_pairs={{0,4},{1,5},{2,6},{3,7},{4,8},{5,9},{6,10},{7,11},{8,12},{9,13},{1... | collective-permute-start | bytes 688136 | tf_op jit(solution)/shard_map/ppermute | solution.py:522
  31.5 7.3 %collective-permute-start.3 = (bf16[112,1024]{1,0:T(8,128)(2,1)S(1)}, bf16[112,1024]{1,0:T(8,128)(2,1)S(1)}, u32[]{:S(2)}, u32[]{:S(2)}) collective-permute-start(bf16[112,1024]{1,0:T(8,128)(2,1)S(1)} %get-tuple-element.39), channel_id=1, source_target_pairs={{4,0},{5,1},{6,2},{7,3},{8,4},{9,5},{10,6},{11,7},{12,8},{13,9},{1... | collective-permute-start | bytes 688136 | tf_op jit(solution)/shard_map/ppermute | solution.py:523
  39.0 10.2 %collective-permute-start.4 = (bf16[96,512]{1,0:T(8,128)(2,1)S(1)}, bf16[96,512]{1,0:T(8,128)(2,1)S(1)}, u32[]{:S(2)}, u32[]{:S(2)}) collective-permute-start(bf16[96,512]{1,0:T(8,128)(2,1)S(1)} %get-tuple-element.40), channel_id=1, source_target_pairs={{0,3},{4,7},{8,11},{12,15},{16,19},{20,23},{24,27},{28,31},{32,35}... | collective-permute-start | bytes 294920 | tf_op jit(solution)/shard_map/ppermute | solution.py:525
  43.6 8.0 %collective-permute-start.8 = (bf16[96,512]{1,0:T(8,128)(2,1)S(1)}, bf16[96,512]{1,0:T(8,128)(2,1)S(1)}, u32[]{:S(2)}, u32[]{:S(2)}) collective-permute-start(bf16[96,512]{1,0:T(8,128)(2,1)S(1)} %get-tuple-element.45), channel_id=1, source_target_pairs={{0,3},{4,7},{8,11},{12,15},{16,19},{20,23},{24,27},{28,31},{32,35}... | collective-permute-start | bytes 294920 | tf_op jit(solution)/shard_map/ppermute | solution.py:525
  50.9 2.7 %collective-permute-start.5 = (bf16[96,1024]{1,0:T(8,128)(2,1)S(1)}, bf16[96,1024]{1,0:T(8,128)(2,1)S(1)}, u32[]{:S(2)}, u32[]{:S(2)}) collective-permute-start(bf16[96,1024]{1,0:T(8,128)(2,1)S(1)} %shard_map.64.refs_7_.refs_0_), channel_id=1, source_target_pairs={{3,2},{7,6},{11,10},{15,14},{19,18},{23,22},{27,26},{31,30},{35,34... | collective-permute-start | bytes 589832 | tf_op jit(solution)/shard_map/ppermute | solution.py:542
  52.9 2.6 %collective-permute-start.9 = (bf16[96,768]{1,0:T(8,128)(2,1)S(1)}, bf16[96,768]{1,0:T(8,128)(2,1)S(1)}, u32[]{:S(2)}, u32[]{:S(2)}) collective-permute-start(bf16[96,768]{1,0:T(8,128)(2,1)S(1)} %shard_map.67.refs_1_), channel_id=1, source_target_pairs={{3,2},{7,6},{11,10},{15,14},{19,18},{23,22},{27,26},{31,30},{35,34... | collective-permute-start | bytes 442376 | tf_op jit(solution)/shard_map/ppermute | solution.py:542
  54.8 2.6 %collective-permute-start.6 = (bf16[96,640]{1,0:T(8,128)(2,1)S(1)}, bf16[96,640]{1,0:T(8,128)(2,1)S(1)}, u32[]{:S(2)}, u32[]{:S(2)}) collective-permute-start(bf16[96,640]{1,0:T(8,128)(2,1)S(1)} %shard_map.65.refs_5_.refs_2_), channel_id=1, source_target_pairs={{2,1},{6,5},{10,9},{14,13},{18,17},{22,21},{26,25},{30,29},{34,33}... | collective-permute-start | bytes 368648 | tf_op jit(solution)/shard_map/ppermute | solution.py:542
  56.8 1.8 %collective-permute-start.10 = (bf16[96,640]{1,0:T(8,128)(2,1)S(1)}, bf16[96,640]{1,0:T(8,128)(2,1)S(1)}, u32[]{:S(2)}, u32[]{:S(2)}) collective-permute-start(bf16[96,640]{1,0:T(8,128)(2,1)S(1)} %shard_map.68.refs_3_), channel_id=1, source_target_pairs={{2,1},{6,5},{10,9},{14,13},{18,17},{22,21},{26,25},{30,29},{34,33}... | collective-permute-start | bytes 368648 | tf_op jit(solution)/shard_map/ppermute | solution.py:542
  60.0 11.1 %collective-permute-start.11 = (bf16[96,512]{1,0:T(8,128)(2,1)S(1)}, bf16[96,512]{1,0:T(8,128)(2,1)S(1)}, u32[]{:S(2)}, u32[]{:S(2)}) collective-permute-start(bf16[96,512]{1,0:T(8,128)(2,1)S(1)} %shard_map.69.refs_5_), channel_id=1, source_target_pairs={{1,0},{5,4},{9,8},{13,12},{17,16},{21,20},{25,24},{29,28},{33,32},... | collective-permute-start | bytes 294920 | tf_op jit(solution)/shard_map/ppermute | solution.py:542
  61.3 9.8 %collective-permute-start.7 = (bf16[96,384]{1,0:T(8,128)(2,1)S(1)}, bf16[96,384]{1,0:T(8,128)(2,1)S(1)}, u32[]{:S(2)}, u32[]{:S(2)}) collective-permute-start(bf16[96,384]{1,0:T(8,128)(2,1)S(1)} %shard_map.66.refs_5_.refs_4_), channel_id=1, source_target_pairs={{1,0},{5,4},{9,8},{13,12},{17,16},{21,20},{25,24},{29,28},{33,32},... | collective-permute-start | bytes 221192 | tf_op jit(solution)/shard_map/ppermute | solution.py:542
  65.6 0.7 copy-start.4
  72.3 0.7 copy-start.2
  90.8 0.7 copy-start
  91.5 24.0 %all-to-all-start.1 = ((bf16[8,128,128]{2,1,0:T(8,128)(2,1)}), bf16[8,128,128]{2,1,0:T(8,128)(2,1)S(1)}, u32[]{:S(2)}, u32[]{:S(2)}) async-start(bf16[8,128,128]{2,1,0:T(8,128)(2,1)} %copy-done), calls=%async_computation.1 | async-start | bytes 524288 | tf_op jit(solution)/shard_map/all_to_all | solution.py:602
  98.9 0.9 copy-start.3
  99.8 0.9 copy-start.5
